TPU v7x, 32 devices: a whole 2x2x4 slice. The times are simulated.
32 devices in a mesh: dp: 4 (over x, core), fsdp: 8 (over z, y).
Axes of the slice: x: 2, y: 2, z: 4, core: 2. Of those that a mesh axis runs over, the one named last changes fastest.
Arguments:
- hidden: float32 [32, 128, 2048], P(('dp', 'fsdp')), may hold values from -6 to 6
- cotangent: float32 [32, 128, 2048], P(('dp', 'fsdp')), may hold values from -6 to 6
- groups: int32 [32], P(('dp', 'fsdp')), may hold values from 0 to 7, never falling along the last dimension, each value on 1 to 8 neighbouring positions
- group_weights: float32 [8], replicated, may hold values from 0.5 to 20
- input_weight: bfloat16 [2, 2048, 8192], P(None, ('dp', 'fsdp')), may hold values from -0.125 to 0.125
- select_weight: bfloat16 [2, 4096, 160], P(None, ('dp', 'fsdp')), may hold values from -0.09375 to 0.09375
- rate_weight: bfloat16 [2, 128, 4096], P(None, None, ('dp', 'fsdp')), may hold values from -0.5 to 0.5
- output_weight: bfloat16 [2, 4096, 2048], P(None, ('dp', 'fsdp')), may hold values from -0.375 to 0.375
- norm_gain: bfloat16 [2, 2048], P(None, ('dp', 'fsdp')), may hold values from 0.099609375 to 1.8984375
- conv_taps: bfloat16 [2, 4, 4096], P(None, None, ('dp', 'fsdp')), may hold values from -3 to 3
- conv_shift: bfloat16 [2, 4096], P(None, ('dp', 'fsdp')), may hold values from -3 to 3
- rate_shift: bfloat16 [2, 4096], P(None, ('dp', 'fsdp')), may hold values from -4 to 4
- skip_gain: bfloat16 [2, 4096], P(None, ('dp', 'fsdp')), may hold values from 0.099609375 to 1.8984375
Outputs:
- hidden_out: float32 [32, 128, 2048], P(('dp', 'fsdp'))
- hidden_gradient: float32 [32, 128, 2048], P(('dp', 'fsdp'))
- gradient_input_weight: float32 [2, 2048, 8192], P(None, ('dp', 'fsdp'))
- gradient_select_weight: float32 [2, 4096, 160], P(None, ('dp', 'fsdp'))
- gradient_rate_weight: float32 [2, 128, 4096], P(None, None, ('dp', 'fsdp'))
- gradient_output_weight: float32 [2, 4096, 2048], P(None, ('dp', 'fsdp'))
- gradient_norm_gain: float32 [2, 2048], P(None, ('dp', 'fsdp'))
- gradient_conv_taps: float32 [2, 4, 4096], P(None, None, ('dp', 'fsdp'))
- gradient_conv_shift: float32 [2, 4096], P(None, ('dp', 'fsdp'))
- gradient_rate_shift: float32 [2, 4096], P(None, ('dp', 'fsdp'))
- gradient_skip_gain: float32 [2, 4096], P(None, ('dp', 'fsdp'))
- beta_mean: float32 [2], replicated
- beta_max: float32 [2], replicated
Inputs may be any that keep to these rules, and one draw needn't show every extreme that they name: `groups`: the group numbers never fall from one sequence to the next.
All inputs are finite; a program needn't handle non-finite values.
Results may differ from a plain program's by a relative error of at most 0.017.
The roundings to bfloat16 on the way count: a program that leaves them out, or rounds other values in their place, can miss the bound.
Values may be sent and summed in bfloat16 or wider, within the bound.
A program may use at most 448 MiB of HBM per device.

v0:
```python
import jax
import jax.numpy as jnp
from jax import lax
from jax.sharding import PartitionSpec as P

INNER = 4096
STATE = 16
RANK = 128
CONV = 4
LAYERS = 2
BLOCK = 32


eps = 1e-05


def rms_scale(stream_rows, gain_float):
    return (
        stream_rows
        * lax.rsqrt(jnp.mean(jnp.square(stream_rows), axis=-1, keepdims=True) + eps)
        * gain_float
    )


def causal_conv(inner_part, taps_float, shift_float):
    length = inner_part.shape[1]
    padded = jnp.pad(inner_part, ((0, 0), (CONV - 1, 0), (0, 0)))
    summed = shift_float + jnp.zeros_like(inner_part)
    for offset in range(CONV):
        summed = summed + taps_float[offset] * padded[:, offset : offset + length]
    return jax.nn.silu(summed)


def block_steps(carried, inputs):
    act_blk, step_blk, key_blk, query_blk = inputs
    outputs = []
    for offset in range(act_blk.shape[1]):
        key_now = key_blk[:, offset, None, :]
        decayed = 1.0 - step_blk[:, offset, :, None] * jnp.square(key_now)
        carried = (
            decayed * carried + (step_blk[:, offset] * act_blk[:, offset])[:, :, None] * key_now
        )
        outputs.append(jnp.sum(carried * query_blk[:, offset, None, :], axis=-1))
    return (carried, jnp.stack(outputs, axis=1))


def recurrence(activated, step_size, keys_part, query_part):
    seq_count, length, channels = activated.shape
    block_count = length // BLOCK

    def regroup(values):
        return jnp.moveaxis(values.reshape(seq_count, block_count, BLOCK, values.shape[-1]), 1, 0)

    initial = jnp.zeros((seq_count, channels, keys_part.shape[-1]), jnp.float32)
    finished, outputs = lax.scan(
        jax.checkpoint(block_steps),
        initial,
        (regroup(activated), regroup(step_size), regroup(keys_part), regroup(query_part)),
    )
    return jnp.moveaxis(outputs, 0, 1).reshape(seq_count, length, channels)


def mixer_core(activated, keys_part, query_part, rate_pre, rate_float, skip_float, gate_part):
    beta_rate = jax.nn.sigmoid(rate_pre + rate_float)
    step_size = beta_rate / (
        1.0 + beta_rate * jnp.sum(jnp.square(keys_part), axis=-1, keepdims=True)
    )
    scanned = recurrence(activated, step_size, keys_part, query_part)
    return (scanned + skip_float * activated) * jax.nn.silu(gate_part)


def fetch_forward(pieces):
    (
        input_piece,
        select_piece,
        rate_piece,
        output_piece,
        gain_piece,
        taps_piece,
        shift_piece,
        rate_shift_piece,
        skip_piece,
    ) = pieces
    return (
        lax.all_gather(input_piece, ("dp", "fsdp"), axis=0, tiled=True),
        lax.all_gather(select_piece, ("dp", "fsdp"), axis=0, tiled=True),
        lax.all_gather(rate_piece, ("dp", "fsdp"), axis=1, tiled=True),
        lax.all_gather(output_piece, ("dp", "fsdp"), axis=0, tiled=True),
        lax.all_gather(gain_piece, ("dp", "fsdp"), axis=0, tiled=True),
        lax.all_gather(taps_piece, ("dp", "fsdp"), axis=1, tiled=True),
        lax.all_gather(shift_piece, ("dp", "fsdp"), axis=0, tiled=True),
        lax.all_gather(rate_shift_piece, ("dp", "fsdp"), axis=0, tiled=True),
        lax.all_gather(skip_piece, ("dp", "fsdp"), axis=0, tiled=True),
    )


def fetch_backward(pieces):
    (
        input_piece,
        select_piece,
        rate_piece,
        output_piece,
        gain_piece,
        taps_piece,
        shift_piece,
        rate_shift_piece,
        skip_piece,
    ) = pieces
    return (
        lax.all_gather(input_piece, ("dp", "fsdp"), axis=0, tiled=True),
        lax.all_gather(select_piece, ("dp", "fsdp"), axis=0, tiled=True),
        lax.all_gather(rate_piece, ("dp", "fsdp"), axis=1, tiled=True),
        lax.all_gather(output_piece, ("dp", "fsdp"), axis=0, tiled=True),
        lax.all_gather(gain_piece, ("dp", "fsdp"), axis=0, tiled=True),
        lax.all_gather(taps_piece, ("dp", "fsdp"), axis=1, tiled=True),
        lax.all_gather(shift_piece, ("dp", "fsdp"), axis=0, tiled=True),
        lax.all_gather(rate_shift_piece, ("dp", "fsdp"), axis=0, tiled=True),
        lax.all_gather(skip_piece, ("dp", "fsdp"), axis=0, tiled=True),
    )


def forward_layer(stream_rows, gathered):
    (
        input_weight,
        select_weight,
        rate_weight,
        output_weight,
        norm_gain,
        conv_taps,
        conv_shift,
        rate_shift,
        skip_gain,
    ) = gathered
    normed = rms_scale(stream_rows, norm_gain.astype(jnp.float32)).astype(jnp.bfloat16)
    entry_rows = jnp.dot(normed, input_weight, preferred_element_type=jnp.float32)
    activated = causal_conv(
        entry_rows[None, :, :INNER], conv_taps.astype(jnp.float32), conv_shift.astype(jnp.float32)
    )[0].astype(jnp.bfloat16)
    projected = jnp.dot(activated, select_weight, preferred_element_type=jnp.float32)
    rate_pre = jnp.dot(
        projected[:, :RANK].astype(jnp.bfloat16), rate_weight, preferred_element_type=jnp.float32
    )
    beta_rate = jax.nn.sigmoid(rate_pre + rate_shift.astype(jnp.float32))
    beta_stats = (jnp.sum(beta_rate), jnp.max(beta_rate))
    mixed = mixer_core(
        activated.astype(jnp.float32)[None],
        projected[None, :, RANK : RANK + STATE],
        projected[None, :, RANK + STATE :],
        rate_pre[None],
        rate_shift.astype(jnp.float32),
        skip_gain.astype(jnp.float32),
        entry_rows[None, :, INNER:],
    )[0].astype(jnp.bfloat16)
    result = stream_rows + jnp.dot(mixed, output_weight, preferred_element_type=jnp.float32)
    return (
        result,
        (stream_rows, normed, entry_rows, activated, projected, rate_pre, mixed),
        beta_stats,
    )


def backward_layer(back_rows, stored, gathered):
    stream_rows, normed, entry_rows, activated, projected, rate_pre, mixed = stored
    (
        input_weight,
        select_weight,
        rate_weight,
        output_weight,
        norm_gain,
        conv_taps,
        conv_shift,
        rate_shift,
        skip_gain,
    ) = gathered
    back_low = back_rows.astype(jnp.bfloat16)
    slope_output = jnp.einsum("le,ld->ed", mixed, back_low, preferred_element_type=jnp.float32)
    back_mixed = jnp.einsum(
        "ld,ed->le", back_low, output_weight, preferred_element_type=jnp.float32
    )
    unused, core_pull = jax.vjp(
        mixer_core,
        activated.astype(jnp.float32)[None],
        projected[None, :, RANK : RANK + STATE],
        projected[None, :, RANK + STATE :],
        rate_pre[None],
        rate_shift.astype(jnp.float32),
        skip_gain.astype(jnp.float32),
        entry_rows[None, :, INNER:],
    )
    back_core, back_keys, back_query, back_rate, slope_rate_shift, slope_skip, back_gate = (
        core_pull(back_mixed[None])
    )
    back_rate_low = back_rate[0].astype(jnp.bfloat16)
    low_rank = projected[:, :RANK].astype(jnp.bfloat16)
    slope_rate = jnp.einsum(
        "lr,le->re", low_rank, back_rate_low, preferred_element_type=jnp.float32
    )
    back_rank = jnp.einsum(
        "le,re->lr", back_rate_low, rate_weight, preferred_element_type=jnp.float32
    )
    back_proj = jnp.concatenate([back_rank, back_keys[0], back_query[0]], axis=1).astype(
        jnp.bfloat16
    )
    slope_select = jnp.einsum("le,lx->ex", activated, back_proj, preferred_element_type=jnp.float32)
    back_act = back_core[0] + jnp.einsum(
        "lx,ex->le", back_proj, select_weight, preferred_element_type=jnp.float32
    )
    unused, conv_pull = jax.vjp(
        causal_conv,
        entry_rows[None, :, :INNER],
        conv_taps.astype(jnp.float32),
        conv_shift.astype(jnp.float32),
    )
    back_inner, slope_taps, slope_shift = conv_pull(back_act[None])
    back_entry = jnp.concatenate([back_inner[0], back_gate[0]], axis=1).astype(jnp.bfloat16)
    slope_input = jnp.einsum("ld,lk->dk", normed, back_entry, preferred_element_type=jnp.float32)
    back_normed = jnp.einsum(
        "lk,dk->ld", back_entry, input_weight, preferred_element_type=jnp.float32
    )
    unused, norm_pull = jax.vjp(rms_scale, stream_rows, norm_gain.astype(jnp.float32))
    back_stream, slope_gain = norm_pull(back_normed)
    shares = (
        lax.psum_scatter(slope_input, ("dp", "fsdp"), scatter_dimension=0, tiled=True),
        lax.psum_scatter(slope_select, ("dp", "fsdp"), scatter_dimension=0, tiled=True),
        lax.psum_scatter(slope_rate, ("dp", "fsdp"), scatter_dimension=1, tiled=True),
        lax.psum_scatter(slope_output, ("dp", "fsdp"), scatter_dimension=0, tiled=True),
        lax.psum_scatter(slope_gain, ("dp", "fsdp"), scatter_dimension=0, tiled=True),
        lax.psum_scatter(slope_taps, ("dp", "fsdp"), scatter_dimension=1, tiled=True),
        lax.psum_scatter(slope_shift, ("dp", "fsdp"), scatter_dimension=0, tiled=True),
        lax.psum_scatter(slope_rate_shift, ("dp", "fsdp"), scatter_dimension=0, tiled=True),
        lax.psum_scatter(slope_skip, ("dp", "fsdp"), scatter_dimension=0, tiled=True),
    )
    return (back_rows + back_stream, shares)


def on_device(
    hidden,
    cotangent,
    groups,
    group_weights,
    input_weight,
    select_weight,
    rate_weight,
    output_weight,
    norm_gain,
    conv_taps,
    conv_shift,
    rate_shift,
    skip_gain,
):
    device_count = lax.axis_size("dp") * lax.axis_size("fsdp")
    labels = jnp.arange(group_weights.shape[0])
    own_weight = jnp.sum(jnp.where(groups[:, None] == labels[None, :], group_weights[None, :], 0.0))
    weight_total = lax.psum(own_weight, ("dp", "fsdp"))
    own_scale = own_weight * device_count / weight_total
    shards = (
        input_weight,
        select_weight,
        rate_weight,
        output_weight,
        norm_gain,
        conv_taps,
        conv_shift,
        rate_shift,
        skip_gain,
    )
    stream_rows = hidden[0]
    stored_all = []
    fetched_all = []
    beta_sums = []
    beta_peaks = []
    for which_layer in range(LAYERS):
        gathered = fetch_forward(tuple((tensor[which_layer] for tensor in shards)))
        stream_rows, stored, beta_stats = forward_layer(stream_rows, gathered)
        stored_all.append(stored)
        fetched_all.append(gathered)
        beta_sums.append(beta_stats[0] * own_scale)
        beta_peaks.append(beta_stats[1] * own_scale)
    beta_total = lax.psum(jnp.stack(beta_sums), ("dp", "fsdp"))
    beta_peak = lax.pmax(jnp.stack(beta_peaks), ("dp", "fsdp"))
    beta_mean = beta_total / (device_count * hidden.shape[1] * rate_shift.shape[1] * device_count)
    back_rows = cotangent[0] * own_scale
    shares_all = []
    for which_layer in reversed(range(LAYERS)):
        gathered = fetch_backward(tuple((tensor[which_layer] for tensor in shards)))
        back_rows, shares = backward_layer(back_rows, stored_all[which_layer], gathered)
        shares_all = [shares] + shares_all
    stacked = tuple(
        (
            jnp.stack([layer_shares[member] for layer_shares in shares_all], axis=0)
            for member in range(9)
        )
    )
    return (stream_rows[None], back_rows[None]) + stacked + (beta_mean, beta_peak)


def solution(mesh):
    placed = (
        P(("dp", "fsdp"), None, None),
        P(("dp", "fsdp"), None, None),
        P(("dp", "fsdp")),
        P(),
        P(None, ("dp", "fsdp"), None),
        P(None, ("dp", "fsdp"), None),
        P(None, None, ("dp", "fsdp")),
        P(None, ("dp", "fsdp"), None),
        P(None, ("dp", "fsdp")),
        P(None, None, ("dp", "fsdp")),
        P(None, ("dp", "fsdp")),
        P(None, ("dp", "fsdp")),
        P(None, ("dp", "fsdp")),
    )
    return jax.shard_map(
        on_device,
        mesh=mesh,
        in_specs=placed,
        out_specs=(
            P(("dp", "fsdp"), None, None),
            P(("dp", "fsdp"), None, None),
            P(None, ("dp", "fsdp"), None),
            P(None, ("dp", "fsdp"), None),
            P(None, None, ("dp", "fsdp")),
            P(None, ("dp", "fsdp"), None),
            P(None, ("dp", "fsdp")),
            P(None, None, ("dp", "fsdp")),
            P(None, ("dp", "fsdp")),
            P(None, ("dp", "fsdp")),
            P(None, ("dp", "fsdp")),
            P(),
            P(),
        ),
        check_vma=False,
    )
```

profile of v0, /device:TPU:0, one launch (start us, length us, event | category | flops | bytes accessed | tf_op | source)
XLA Modules:
  0.0 6642.6 jit_solution(5355265086191140020)
XLA Ops:
  7.3 3.1 fusion.225
  16.4 43.4 all-reduce.349
  60.5 67.3 %all-gather.1 = bf16[1,4,4096]{2,1,0:T(4,128)(2,1)S(1)} all-gather(bf16[1,4,128]{2,1,0:T(4,128)(2,1)S(1)} %get-tuple-element.3057), channel_id=3, replica_groups=mesh['dp'=4,'fsdp'=8] {'dp','fsdp'}, dimensions={2}, use_global_device_ids=true | all-gather | bytes 33792 | tf_op jit(solution)/shard_map/all_gather | solution.py:90
  127.9 64.0 all-gather
  191.9 65.1 all-gather.6
  257.1 63.1 all-gather.7
  322.7 38.7 psum.14
  362.1 67.1 %all-gather.10 = bf16[1,4,4096]{2,1,0:T(4,128)(2,1)S(1)} all-gather(bf16[1,4,128]{2,1,0:T(4,128)(2,1)S(1)} %get-tuple-element.3056), channel_id=12, replica_groups=mesh['dp'=4,'fsdp'=8] {'dp','fsdp'}, dimensions={2}, use_global_device_ids=true | all-gather | bytes 33792 | tf_op jit(solution)/shard_map/all_gather | solution.py:90
  429.8 63.8 all-gather.9
  494.2 66.1 all-gather.15
  560.9 63.9 all-gather.16
  626.2 13.4 fusion.74
  648.2 4.3 multiply_divide_fusion.1
  654.0 145.2 %while.102 = (s32[]{:T(128)}, f32[1,4096,16]{1,2,0:T(8,128)S(1)}, f32[4,1,32,4096]{3,2,1,0:T(8,128)}, f32[4,1,32,4096]{3,2,1,0:T(8,128)}, f32[4,1,32,16]{3,2,1,0...) while((s32[]{:T(128)}, f32[1,4096,16]{1,2,0:T(8,128)S(1)}, ...), condition=%wide.region_35.36_spmd.clone, body=%wide.region_2.35_spmd.clone.sunk | while | flops 20054532 | bytes 19125108 | solution.py:55
  799.2 5.0 fusion.109
  804.2 9.5 multiply_reduce_fusion.461
  814.7 13.5 fusion.70
  831.8 13.5 fusion.112
  850.4 4.4 multiply_divide_fusion
  857.3 79.7 %while.104 = (s32[]{:T(128)}, f32[1,4096,16]{1,2,0:T(8,128)S(1)}, f32[4,1,32,4096]{3,2,1,0:T(8,128)}, f32[4,1,4096,16]{2,3,1,0:T(8,128)}, f32[4,1,32,4096]{3,2,1...) while((s32[]{:T(128)}, f32[1,4096,16]{1,2,0:T(8,128)S(1)}, ...), condition=%wide.region_107.108_spmd.clone, body=%wide.region_74.107_spmd.clone.sunk | while | flops 20120068 | bytes 19584352 | solution.py:55
  940.1 120.9 %while.105 = (s32[]{:T(128)}, f32[1,4096,16]{1,2,0:T(8,128)S(1)}, f32[4,1,32,4096]{3,2,1,0:T(8,128)}, f32[4,1,32,4096]{3,2,1,0:T(8,128)}, f32[4,1,32,16]{3,2,1,0...) while((s32[]{:T(128)}, f32[1,4096,16]{1,2,0:T(8,128)S(1)}, ...), condition=%wide.region_269.270_spmd.clone, body=%wide.region_108.269_spmd.clone.sunk | while | flops 68320768 | bytes 57278844 | solution.py:55
  947.7 4.3 multiply_reduce_fusion.615
  965.5 2.9 bitcast_dynamic-update-slice_fusion.33
  977.8 4.3 multiply_reduce_fusion.615
  1007.9 4.3 multiply_reduce_fusion.615
  1038.0 4.3 multiply_reduce_fusion.615
  1061.1 5.7 fusion.195
  1069.6 93.5 %while.103 = (s32[]{:T(128)}, f32[1,4096,16]{1,2,0:T(8,128)S(1)}, f32[4,1,32,4096]{3,2,1,0:T(8,128)}, f32[4,1,32,4096]{3,2,1,0:T(8,128)}, f32[4,1,32,16]{3,2,1,0...) while((s32[]{:T(128)}, f32[1,4096,16]{1,2,0:T(8,128)S(1)}, ...), condition=%wide.region_71.72_spmd.clone, body=%wide.region_38.71_spmd.clone.sunk | while | flops 20054532 | bytes 18666160 | solution.py:55
  1164.8 7.7 fusion.118
  1174.5 3.4 multiply_reduce_fusion.450
  1179.8 17.9 multiply_reduce_fusion.458
  1199.9 78.0 %while.106 = (s32[]{:T(128)}, f32[1,4096,16]{1,2,0:T(8,128)S(1)}, f32[4,1,32,4096]{3,2,1,0:T(8,128)}, f32[4,1,4096,16]{2,3,1,0:T(8,128)S(1)}, f32[4,1,32,4096]{3...) while((s32[]{:T(128)}, f32[1,4096,16]{1,2,0:T(8,128)S(1)}, ...), condition=%wide.region_305.306_spmd.clone, body=%wide.region_272.305_spmd.clone.sunk | while | flops 20120068 | bytes 19583844 | solution.py:55
  1278.8 3.0 bitcast_add_fusion.4
  1281.8 15.8 fusion.111
  1300.7 114.6 %while.107 = (s32[]{:T(128)}, f32[1,4096,16]{1,2,0:T(8,128)S(1)}, f32[4,1,32,4096]{3,2,1,0:T(8,128)}, f32[4,1,32,4096]{3,2,1,0:T(8,128)}, f32[4,1,32,16]{3,2,1,0...) while((s32[]{:T(128)}, f32[1,4096,16]{1,2,0:T(8,128)S(1)}, ...), condition=%wide.region_467.468_spmd.clone, body=%wide.region_306.467_spmd.clone.sunk | while | flops 68320768 | bytes 40501568 | solution.py:55
  1306.6 4.3 multiply_reduce_fusion.648
  1335.1 4.3 multiply_reduce_fusion.648
  1363.6 4.3 multiply_reduce_fusion.648
  1392.1 4.3 multiply_reduce_fusion.648
  1409.8 2.9 bitcast_dynamic-update-slice_fusion.39
  1415.3 4.8 fusion.193
  1421.5 3.9 bitcast_add_fusion
  1427.8 6.5 multiply_reduce_fusion.454
  1436.2 19.6 multiply_reduce_fusion.459
  1460.3 3.0 fusion.163
  1463.4 3.0 fusion.166
  1473.2 13.2 fusion.171
  1487.9 13.2 fusion.161
  1502.3 24.5 fusion.135
  1528.1 24.7 fusion.136
  1554.2 38.5 pmax.7
  1595.5 9.2 fusion.102
  1611.1 109.5 %reduce-scatter.31.cloned.1.call-done = f32[128,4]{1,0:T(8,128)} async-done(((f32[4096,4]{1,0:T(8,128)}), f32[128,4]{1,0:T(8,128)}) %reduce-scatter.31.cloned.1.call-update) | async-done | bytes 2064
  1721.6 135.7 %reduce-scatter.33.cloned.1.call-done = f32[128,4]{1,0:T(8,128)} async-done(((f32[4096,4]{1,0:T(8,128)}), f32[128,4]{1,0:T(8,128)}) %reduce-scatter.33.cloned.1.call-update) | async-done | bytes 2064
  1858.8 135.0 %reduce-scatter.23.cloned.1.call-done = f32[128,128]{1,0:T(8,128)} async-done(((f32[128,4096]{1,0:T(8,128)}), f32[128,128]{1,0:T(8,128)}) %reduce-scatter.23.cloned.1.call-update) | async-done | bytes 65552 | tf_op jit(solution)/shard_map/reduce_scatter | solution.py:225
  1993.8 137.2 %reduce-scatter.25.cloned.1.call-done = f32[128,128]{1,0:T(8,128)} async-done(((f32[128,4096]{1,0:T(8,128)}), f32[128,128]{1,0:T(8,128)}) %reduce-scatter.25.cloned.1.call-update) | async-done | bytes 65552 | tf_op jit(solution)/shard_map/reduce_scatter | solution.py:225
  2132.5 136.6 %reduce-scatter.19.cloned.1.call-done = f32[128,160]{0,1:T(8,128)} async-done(((f32[4096,160]{0,1:T(8,128)}), f32[128,160]{0,1:T(8,128)}) %reduce-scatter.19.cloned.1.call-update) | async-done | bytes 81936 | tf_op jit(solution)/shard_map/reduce_scatter | solution.py:224
  2269.0 139.0 %reduce-scatter.21.cloned.1.call-done = f32[128,160]{0,1:T(8,128)} async-done(((f32[4096,160]{0,1:T(8,128)}), f32[128,160]{0,1:T(8,128)}) %reduce-scatter.21.cloned.1.call-update) | async-done | bytes 81936 | tf_op jit(solution)/shard_map/reduce_scatter | solution.py:224
  2409.6 703.5 %reduce-scatter.27.cloned.1.call-done = f32[128,2048]{1,0:T(8,128)} async-done(((f32[4096,2048]{1,0:T(8,128)}), f32[128,2048]{1,0:T(8,128)}) %reduce-scatter.27.cloned.1.call-update) | async-done | bytes 1048592 | tf_op jit(solution)/shard_map/reduce_scatter | solution.py:226
  3113.2 708.2 %reduce-scatter.29.cloned.1.call-done = f32[128,2048]{1,0:T(8,128)} async-done(((f32[4096,2048]{1,0:T(8,128)}), f32[128,2048]{1,0:T(8,128)}) %reduce-scatter.29.cloned.1.call-update) | async-done | bytes 1048592 | tf_op jit(solution)/shard_map/reduce_scatter | solution.py:226
  3821.4 3.1 pad_maximum_fusion.3
  3824.4 1401.8 %reduce-scatter.15.cloned.1.call-done = f32[64,8192]{1,0:T(8,128)} async-done(((f32[2048,8192]{1,0:T(8,128)}), f32[64,8192]{1,0:T(8,128)}) %reduce-scatter.15.cloned.1.call-update) | async-done | bytes 2097168 | tf_op jit(solution)/shard_map/reduce_scatter | solution.py:223
  5226.2 1405.0 %reduce-scatter.17.cloned.1.call-done = f32[64,8192]{1,0:T(8,128)} async-done(((f32[2048,8192]{1,0:T(8,128)}), f32[64,8192]{1,0:T(8,128)}) %reduce-scatter.17.cloned.1.call-update) | async-done | bytes 2097168 | tf_op jit(solution)/shard_map/reduce_scatter | solution.py:223
  6631.2 4.6 pad_maximum_fusion
  (3200 shorter events, 657.8 us)
Async XLA Ops:
  7.2 618.9 %all-gather.27.cloned.1.call-start = ((), (), s32[]{:S(2)}) async-start(), calls=%async_computation.18 | async-start | bytes 34603008 | tf_op jit(solution)/shard_map/all_gather | solution.py:85
  10.4 633.8 %all-gather.29.cloned.1.call-start = ((), (), s32[]{:S(2)}) async-start(), calls=%async_computation.19 | async-start | bytes 1351680 | tf_op jit(solution)/shard_map/all_gather | solution.py:86
  11.2 637.0 %all-gather.31.cloned.1.call-start = ((), (), s32[]{:S(2)}) async-start(), calls=%async_computation.20 | async-start | bytes 1081344 | tf_op jit(solution)/shard_map/all_gather | solution.py:87
  11.9 47.9 copy-start.4
  11.9 792.2 %all-gather.33.cloned.1.call-start = ((), (), s32[]{:S(2)}) async-start(), calls=%async_computation.21 | async-start | bytes 17301504 | tf_op jit(solution)/shard_map/all_gather | solution.py:88
  13.1 47.4 copy-start.236
  13.1 114.7 %copy-start.238 = (bf16[2,128]{1,0:T(2,128)(2,1)S(1)}, bf16[2,128]{1,0:T(2,128)(2,1)}, u32[]{:S(2)}) copy-start(bf16[2,128]{1,0:T(2,128)(2,1)} %param.35) | copy-start | bytes 1540
  13.1 178.8 %copy-start.239 = (bf16[2,128]{1,0:T(2,128)(2,1)S(1)}, bf16[2,128]{1,0:T(2,128)(2,1)}, u32[]{:S(2)}) copy-start(bf16[2,128]{1,0:T(2,128)(2,1)} %param.36) | copy-start | bytes 1540
  13.1 244.0 %copy-start.240 = (bf16[2,128]{1,0:T(2,128)(2,1)S(1)}, bf16[2,128]{1,0:T(2,128)(2,1)}, u32[]{:S(2)}) copy-start(bf16[2,128]{1,0:T(2,128)(2,1)} %param.37) | copy-start | bytes 1540
  13.1 308.4 %copy-start.245 = (f32[8]{0:T(128)S(1)}, f32[8]{0:T(128)}, u32[]{:S(2)}) copy-start(f32[8]{0:T(128)} %param.28) | copy-start | bytes 100
  13.1 801.1 %all-gather.35.cloned.1.call-start = ((), (), s32[]{:S(2)}) async-start(), calls=%async_computation.22 | async-start | bytes 34603008 | tf_op jit(solution)/shard_map/all_gather | solution.py:85
  13.7 816.7 %all-gather.41.cloned.1.call-start = ((), (), s32[]{:S(2)}) async-start(), calls=%async_computation.25 | async-start | bytes 17301504 | tf_op jit(solution)/shard_map/all_gather | solution.py:88
  14.3 832.4 %all-gather.37.cloned.1.call-start = ((), (), s32[]{:S(2)}) async-start(), calls=%async_computation.23 | async-start | bytes 1351680 | tf_op jit(solution)/shard_map/all_gather | solution.py:86
  15.0 835.3 %all-gather.39.cloned.1.call-start = ((), (), s32[]{:S(2)}) async-start(), calls=%async_computation.24 | async-start | bytes 1081344 | tf_op jit(solution)/shard_map/all_gather | solution.py:87
  15.8 1588.8 %all-reduce.352.cloned.1.call-start = ((), (), s32[]{:S(2)}) async-start(), calls=%async_computation.28 | async-start | bytes 230400
  15.9 610.3 %copy-start.72 = (bf16[4,1,32,16]{3,2,1,0:T(8,128)(2,1)}, bf16[4,1,32,16]{3,2,1,0:T(8,128)(2,1)S(1)}, u32[]{:S(2)}) copy-start(bf16[4,1,32,16]{3,2,1,0:T(8,128)(2,1)S(1)} %fusion.230) | copy-start | bytes 12292
  59.8 566.3 %copy-start.63 = (f32[2048]{0:T(1024)}, f32[2048]{0:T(1024)S(1)}, u32[]{:S(2)}) copy-start(f32[2048]{0:T(1024)S(1)} %convert_element_type.189) | copy-start | bytes 24580
  60.5 565.7 %copy-start.209 = (f32[128]{0:T(128)}, f32[128]{0:T(128)S(1)}, u32[]{:S(2)}) copy-start(f32[128]{0:T(128)S(1)} %fusion.177) | copy-start | bytes 1540
  127.8 511.9 %copy-start.128 = (f32[1,1,4096]{2,1,0:T(1,128)}, f32[1,1,4096]{2,1,0:T(1,128)S(1)}, u32[]{:S(2)}) copy-start(f32[1,1,4096]{2,1,0:T(1,128)S(1)} %get-tuple-element.3051) | copy-start | bytes 49156
  127.8 511.9 %copy-start.130 = (f32[1,1,4096]{2,1,0:T(1,128)}, f32[1,1,4096]{2,1,0:T(1,128)S(1)}, u32[]{:S(2)}) copy-start(f32[1,1,4096]{2,1,0:T(1,128)S(1)} %get-tuple-element.3052) | copy-start | bytes 49156
  127.8 511.9 %copy-start.132 = (f32[1,1,4096]{2,1,0:T(1,128)}, f32[1,1,4096]{2,1,0:T(1,128)S(1)}, u32[]{:S(2)}) copy-start(f32[1,1,4096]{2,1,0:T(1,128)S(1)} %get-tuple-element.3053) | copy-start | bytes 49156
  127.8 511.9 %copy-start.134 = (f32[1,1,4096]{2,1,0:T(1,128)}, f32[1,1,4096]{2,1,0:T(1,128)S(1)}, u32[]{:S(2)}) copy-start(f32[1,1,4096]{2,1,0:T(1,128)S(1)} %get-tuple-element.3054) | copy-start | bytes 49156
  659.7 18.2 copy-start.83
  659.7 18.2 copy-start.84
  659.7 18.2 copy-start.91
  659.7 18.2 copy-start.92
  659.7 18.2 copy-start.97
  659.8 18.2 copy-start.101
  659.8 18.2 copy-start.105
  659.8 18.2 copy-start.109
  659.8 18.2 copy-start.119
  659.8 18.2 copy-start.120
  732.1 18.2 copy-start.83
  732.1 18.2 copy-start.84
  732.1 18.2 copy-start.91
  732.1 18.2 copy-start.92
  732.1 18.2 copy-start.97
  732.1 18.2 copy-start.101
  732.1 18.2 copy-start.105
  732.1 18.2 copy-start.109
  732.1 18.2 copy-start.119
  732.1 18.2 copy-start.120
  732.2 18.2 copy-start.121
  732.2 18.2 copy-start.122
  732.2 18.2 copy-start.151
  732.2 18.2 copy-start.152
  732.2 18.2 copy-start.153
  732.2 18.2 copy-start.154
  732.2 18.2 copy-start.155
  732.2 18.2 copy-start.156
  732.2 18.2 copy-start.157
  940.1 121.0 %copy-start.235 = (f32[128]{0:T(128)S(1)}, f32[128]{0:T(128)}, u32[]{:S(2)}) copy-start(f32[128]{0:T(128)} %copy-done.234) | copy-start | bytes 1540
  1300.7 114.6 %copy-start.233 = (f32[128]{0:T(128)S(1)}, f32[128]{0:T(128)}, u32[]{:S(2)}) copy-start(f32[128]{0:T(128)} %copy-done.232) | copy-start | bytes 1540
  1455.8 264.8 %reduce-scatter.31.cloned.1.call-start = ((), (), s32[]{:S(2)}) async-start(), calls=%async_computation.26 | async-start | bytes 2162688
  1458.0 399.3 %reduce-scatter.33.cloned.1.call-start = ((), (), s32[]{:S(2)}) async-start(), calls=%async_computation.27 | async-start | bytes 2162688
  1460.2 533.6 %reduce-scatter.23.cloned.1.call-start = ((), (), s32[]{:S(2)}) async-start(), calls=%async_computation.14 | async-start | bytes 2162688 | tf_op jit(solution)/shard_map/reduce_scatter | solution.py:225
  1463.3 667.6 %reduce-scatter.25.cloned.1.call-start = ((), (), s32[]{:S(2)}) async-start(), calls=%async_computation.15 | async-start | bytes 2162688 | tf_op jit(solution)/shard_map/reduce_scatter | solution.py:225
  1466.3 802.7 %reduce-scatter.19.cloned.1.call-start = ((), (), s32[]{:S(2)}) async-start(), calls=%async_computation.12 | async-start | bytes 2703360 | tf_op jit(solution)/shard_map/reduce_scatter | solution.py:224
  1468.5 939.6 %reduce-scatter.21.cloned.1.call-start = ((), (), s32[]{:S(2)}) async-start(), calls=%async_computation.13 | async-start | bytes 2703360 | tf_op jit(solution)/shard_map/reduce_scatter | solution.py:224
  1471.7 1641.5 %reduce-scatter.27.cloned.1.call-start = ((), (), s32[]{:S(2)}) async-start(), calls=%async_computation.16 | async-start | bytes 34603008 | tf_op jit(solution)/shard_map/reduce_scatter | solution.py:226
  1486.4 2334.9 %reduce-scatter.29.cloned.1.call-start = ((), (), s32[]{:S(2)}) async-start(), calls=%async_computation.17 | async-start | bytes 34603008 | tf_op jit(solution)/shard_map/reduce_scatter | solution.py:226
  1501.1 3725.1 %reduce-scatter.15.cloned.1.call-start = ((), (), s32[]{:S(2)}) async-start(), calls=%async_computation.10 | async-start | bytes 69206016 | tf_op jit(solution)/shard_map/reduce_scatter | solution.py:223
  1526.9 5104.3 %reduce-scatter.17.cloned.1.call-start = ((), (), s32[]{:S(2)}) async-start(), calls=%async_computation.11 | async-start | bytes 69206016 | tf_op jit(solution)/shard_map/reduce_scatter | solution.py:223
  1552.8 39.9 copy-start.242
  (649 other events, 4589.4 us)
Sparse Core Ops, SparseCore 0:
  11.6 199.2 all-gather.26
  214.3 48.0 all-gather.28
  265.8 47.8 all-gather.30
  316.7 115.7 all-gather.32
  435.8 193.3 all-gather.34
  632.2 113.1 all-gather.40
  748.8 47.8 all-gather.36
  799.6 47.8 all-gather.38
  1456.0 124.0 all-reduce.351
  1582.3 138.3 reduce-scatter.30
  1722.9 134.3 reduce-scatter.32
  1859.5 134.2 reduce-scatter.22
  1996.6 134.2 reduce-scatter.24
  2133.2 135.8 reduce-scatter.18
  2271.8 136.1 reduce-scatter.20
  2410.3 702.8 reduce-scatter.26
  3115.4 705.8 reduce-scatter.28
  3823.7 1402.4 reduce-scatter.14
  5228.7 1402.4 reduce-scatter.16
where the time goes:
time: 6680 us; the launch traced here: 6640 us
  waiting for transfers between devices  5010 us (75%)
  blocking collectives  641 us (10%)
  other arithmetic  517 us (8%)
  matrix products  223 us (3%)
  local copies, waits for them, and re-layouts  208 us (3%)
    reduce_scatter x2, waiting for transfers between devices, backward_layer(): lax.psum_scatter(slope_input, ('dp', 'fsdp'), scatter_dimension=0, tiled=...  2810 us
    reduce_scatter x2, waiting for transfers between devices, backward_layer(): lax.psum_scatter(slope_output, ('dp', 'fsdp'), scatter_dimension=0, tiled...  1410 us
    reduce_scatter x2, waiting for transfers between devices, backward_layer(): lax.psum_scatter(slope_select, ('dp', 'fsdp'), scatter_dimension=0, tiled...  276 us
    reduce_scatter x2, waiting for transfers between devices, backward_layer(): lax.psum_scatter(slope_rate, ('dp', 'fsdp'), scatter_dimension=1, tiled=T...  272 us
    unnamed x22, waiting for transfers between devices  248 us
    mul x824, other arithmetic, block_steps(): step_blk[:, offset] * act_blk[:, offset]  157 us
    all_gather x2, blocking collectives, fetch_forward(): lax.all_gather(taps_piece, ('dp', 'fsdp'), axis=1, tiled=True)  134 us
  transfers between devices with their start and end apart: 19, of which 10 were waited for; matrix products, arithmetic and copies ran while one was open for 5% of the time, Pallas kernels for 0%

commit v1 on v0

v1 whole, which is shorter than its diff:
```python
import functools

import jax
import jax.numpy as jnp
from jax import lax
from jax.sharding import PartitionSpec as P
import jax.experimental.pallas as pl
import jax.experimental.pallas.tpu as pltpu

INNER = 4096
STATE = 16
RANK = 128
CONV = 4
LAYERS = 2
WAYS = 4
TP = 8
STEPS = 16

eps = 1e-05
MESH = pl.DeviceIdType.MESH
f32 = jnp.float32
bf16 = jnp.bfloat16
VM = pl.BlockSpec(memory_space=pltpu.VMEM)
HB = pl.BlockSpec(memory_space=pl.ANY)


def place():
    dp, fs = lax.axis_index("dp"), lax.axis_index("fsdp")
    return dp // 2, lax.rem(dp, 2), fs // WAYS, lax.rem(fs, WAYS)


def device(x, core, zh, q):
    return (x * 2 + core, zh * WAYS + q)


def remote(src, dst, send, recv, target):
    return pltpu.make_async_remote_copy(
        src_ref=src, dst_ref=dst, send_sem=send, recv_sem=recv, device_id=target, device_id_type=MESH
    )


def greet(targets):
    barrier = pltpu.get_barrier_semaphore()
    for target in targets:
        pl.semaphore_signal(barrier, inc=1, device_id=target, device_id_type=MESH)
    pl.semaphore_wait(barrier, len(targets))


def tp_peers():
    x, core, zh, q = place()
    peers = []
    for dc in (0, 1):
        for dq in (1, 3, 2, 0):
            if dc == 0 and dq == 0:
                continue
            other_core = lax.rem(core + dc, 2)
            to_q, from_q = lax.rem(q + dq, WAYS), lax.rem(q + WAYS - dq, WAYS)
            peers.append(
                (device(x, other_core, zh, to_q), other_core * WAYS + to_q, other_core * WAYS + from_q)
            )
    return peers


def dp_peers(zh_size):
    x, core, zh, q = place()
    side = device(1 - x, core, zh, q)
    far = []
    for dz in range(1, zh_size):
        to_z, from_z = lax.rem(zh + dz, zh_size), lax.rem(zh + zh_size - dz, zh_size)
        far.append((device(x, core, to_z, q), to_z, from_z))
    return side, far


def weights_kernel(
    zh_size, win, wout, mats, small, misc, o_win, o_wout, o_mats, o_small, o_misc,
    tp_send, tp_recv, z_send, z_recv, x_send, x_recv, own_sem,
):
    x, core, zh, q = place()
    me = core * WAYS + q
    peers = tp_peers()
    side, far = dp_peers(zh_size)
    greet([p[0] for p in peers] + [side] + [f[0] for f in far])

    def row(xx, zz, rank):
        return ((xx * 2 + rank // WAYS) * zh_size + zz) * WAYS + lax.rem(rank, WAYS)

    waits = []
    own = []
    for i, (src, dst) in enumerate(
        (
            (win.at[me], o_win.at[row(x, zh, me)]),
            (misc, o_misc.at[row(x, zh, me)]),
            (wout, o_wout.at[x * zh_size + zh]),
            (mats, o_mats.at[x * zh_size + zh]),
            (small, o_small.at[x * zh_size + zh]),
        )
    ):
        copy = pltpu.make_async_copy(src, dst, own_sem.at[i])
        copy.start()
        own.append(copy)
    arrive = []
    for i, (target, rank, source) in enumerate(peers):
        for j, (src, dst) in enumerate(
            ((win.at[rank], o_win.at[row(x, zh, me)]), (misc, o_misc.at[row(x, zh, me)]))
        ):
            copy = remote(src, dst, tp_send.at[i, j], tp_recv.at[i, j], target)
            copy.start()
            arrive.append((copy, source, j))
            waits.append(copy)

    onward = []

    def spread(item, src, view):
        for k, (target, to_z, from_z) in enumerate(far):
            copy = remote(src, view(x, zh), z_send.at[item, k], z_recv.at[item, k], target)
            copy.start()
            waits.append(copy)
            onward.append((copy, item, k, view, from_z))
        copy = remote(src, view(x, zh), x_send.at[item, 0], x_recv.at[item, 0], side)
        copy.start()
        waits.append(copy)

    spread(0, win.at[me], lambda xx, zz: o_win.at[row(xx, zz, me)])
    spread(1, misc, lambda xx, zz: o_misc.at[row(xx, zz, me)])
    spread(2, small, lambda xx, zz: o_small.at[xx * zh_size + zz])
    spread(3, mats, lambda xx, zz: o_mats.at[xx * zh_size + zz])
    recv_done = set()
    item = 4
    for copy, source, j in arrive:
        copy.wait_recv()
        recv_done.add(id(copy))
        out = (o_win, o_misc)[j]
        view = functools.partial(lambda out, source, xx, zz: out.at[row(xx, zz, source)], out, source)
        spread(item, view(x, zh), view)
        item += 1
    spread(item, wout, lambda xx, zz: o_wout.at[xx * zh_size + zz])
    for copy, it, k, view, from_z in onward:
        copy.wait_recv()
        recv_done.add(id(copy))
        again = remote(view(x, from_z), view(x, from_z), x_send.at[it, k + 1], x_recv.at[it, k + 1], side)
        again.start()
        waits.append(again)
    for copy in waits:
        copy.wait_send()
        if id(copy) not in recv_done:
            copy.wait_recv()
    for copy in own:
        copy.wait()


def gather_weights(zh_size, call, win, wout, mats, small, misc):
    groups = 2 * zh_size
    count = groups * TP
    items = 5 + 2 * (TP - 1)
    dma = pltpu.SemaphoreType.DMA
    many = lambda a, n: jax.ShapeDtypeStruct((n,) + a.shape, a.dtype)
    return pl.pallas_call(
        functools.partial(weights_kernel, zh_size),
        out_shape=[
            jax.ShapeDtypeStruct((count,) + win.shape[1:], win.dtype),
            many(wout, groups), many(mats, groups), many(small, groups), many(misc, count),
        ],
        in_specs=[HB] * 5,
        out_specs=[HB] * 5,
        scratch_shapes=[
            dma((TP - 1, 2)), dma((TP - 1, 2)),
            dma((items, max(1, zh_size - 1))), dma((items, max(1, zh_size - 1))),
            dma((items, zh_size)), dma((items, zh_size)), dma((5,)),
        ],
        compiler_params=pltpu.CompilerParams(collective_id=1, has_side_effects=True),
        name="gather_weights",
    )(win, wout, mats, small, misc)


def tp_gather_kernel(x_ref, o_ref, f_send, f_recv, s_send, s_recv, own_sem):
    x, core, zh, q = place()
    sibling = device(x, 1 - core, zh, q)
    far = []
    for dq in (1, 3, 2):
        far.append((device(x, core, zh, lax.rem(q + dq, WAYS)), lax.rem(q + WAYS - dq, WAYS)))
    greet([t for t, _ in far] + [sibling])
    me = core * WAYS + q
    first = []
    for i, (target, _) in enumerate(far):
        copy = remote(x_ref, o_ref.at[me], f_send.at[i], f_recv.at[i], target)
        copy.start()
        first.append(copy)
    near = [remote(x_ref, o_ref.at[me], s_send.at[3], s_recv.at[3], sibling)]
    near[0].start()
    own = pltpu.make_async_copy(x_ref, o_ref.at[me], own_sem)
    own.start()
    for i, (_, source) in enumerate(far):
        first[i].wait_recv()
        slot = core * WAYS + source
        copy = remote(o_ref.at[slot], o_ref.at[slot], s_send.at[i], s_recv.at[i], sibling)
        copy.start()
        near.append(copy)
    for copy in first:
        copy.wait_send()
    for copy in near:
        copy.wait()
    own.wait()


def tp_gather(rows):
    dma = pltpu.SemaphoreType.DMA
    return pl.pallas_call(
        tp_gather_kernel,
        out_shape=jax.ShapeDtypeStruct((TP,) + rows.shape, rows.dtype),
        in_specs=[HB],
        out_specs=HB,
        scratch_shapes=[dma((3,)), dma((3,)), dma((4,)), dma((4,)), dma],
        compiler_params=pltpu.CompilerParams(collective_id=2, has_side_effects=True),
        name="tp_gather",
    )(rows)


def tp_scatter_kernel(p_ref, o_ref, near_buf, far_out, far_in, s_send, s_recv, f_send, f_recv):
    x, core, zh, q = place()
    sibling = device(x, 1 - core, zh, q)
    far = []
    for dq in (1, 3, 2):
        far.append((device(x, core, zh, lax.rem(q + dq, WAYS)), lax.rem(q + dq, WAYS)))
    greet([t for t, _ in far] + [sibling])
    near = []
    for i, to_q in enumerate([t for _, t in far] + [q]):
        copy = remote(
            p_ref.at[(1 - core) * WAYS + to_q], near_buf.at[i], s_send.at[i], s_recv.at[i], sibling
        )
        copy.start()
        near.append(copy)
    first = []
    for i, (target, to_q) in enumerate(far):
        near[i].wait_recv()
        far_out[i] = (
            p_ref[core * WAYS + to_q].astype(f32) + near_buf[i].astype(f32)
        ).astype(bf16)
        copy = remote(far_out.at[i], far_in.at[i], f_send.at[i], f_recv.at[i], target)
        copy.start()
        first.append(copy)
    near[3].wait_recv()
    o_ref[...] = p_ref[core * WAYS + q].astype(f32) + near_buf[3].astype(f32)
    for i in range(3):
        first[i].wait_recv()
        o_ref[...] += far_in[i].astype(f32)
    for copy in near + first:
        copy.wait_send()


def tp_scatter(partial):
    dma = pltpu.SemaphoreType.DMA
    block = partial.shape[1:]
    return pl.pallas_call(
        tp_scatter_kernel,
        out_shape=jax.ShapeDtypeStruct(block, f32),
        in_specs=[VM],
        out_specs=VM,
        scratch_shapes=[
            pltpu.VMEM((4,) + block, bf16), pltpu.VMEM((3,) + block, bf16), pltpu.VMEM((3,) + block, bf16),
            dma((4,)), dma((4,)), dma((3,)), dma((3,)),
        ],
        compiler_params=pltpu.CompilerParams(
            collective_id=3, has_side_effects=True, vmem_limit_bytes=40 * 2**20
        ),
        name="tp_scatter",
    )(partial)


def tp_sum_kernel(p_ref, own_ref, o_ref, all_ref, parts, a_send, a_recv, b_send, b_recv, c_send, c_recv):
    x, core, zh, q = place()
    me = core * WAYS + q
    peers = tp_peers()
    greet([p[0] for p in peers])
    one, two = [], []
    for i, (target, rank, _) in enumerate(peers):
        copy = remote(p_ref.at[rank], parts.at[i], a_send.at[i], a_recv.at[i], target)
        copy.start()
        one.append(copy)
        copy = remote(own_ref, all_ref.at[me], c_send.at[i], c_recv.at[i], target)
        copy.start()
        two.append(copy)
    all_ref[me] = own_ref[...]
    total = p_ref[me]
    for i in range(TP - 1):
        one[i].wait_recv()
        total = total + parts[i]
    o_ref[me] = total
    for i, (target, rank, _) in enumerate(peers):
        copy = remote(o_ref.at[me], o_ref.at[me], b_send.at[i], b_recv.at[i], target)
        copy.start()
        two.append(copy)
    for copy in one:
        copy.wait_send()
    for copy in two:
        copy.wait()


def tp_sum(partial, own):
    dma = pltpu.SemaphoreType.DMA
    return pl.pallas_call(
        tp_sum_kernel,
        out_shape=[
            jax.ShapeDtypeStruct(partial.shape, f32),
            jax.ShapeDtypeStruct((TP,) + own.shape, f32),
        ],
        in_specs=[VM, VM],
        out_specs=[VM, VM],
        scratch_shapes=[pltpu.VMEM((TP - 1,) + partial.shape[1:], f32)] + [dma((TP - 1,))] * 6,
        compiler_params=pltpu.CompilerParams(
            collective_id=4, has_side_effects=True, vmem_limit_bytes=40 * 2**20
        ),
        name="tp_sum",
    )(partial, own)


def gradients_kernel(
    zh_size, win, wout, mats, small, stats, gain, o_win, o_wout, o_mats, o_small, o_stats,
    win_x, wout_x, mats_x, small_x, stats_x, win_s, wout_s, mats_s, small_s, stats_s,
    win_z, wout_z, mats_z, small_z, stats_z, win_t, gain_t, vectors,
    x_send, x_recv, z_send, z_recv, t_send, t_recv, g_send, g_recv,
):
    x, core, zh, q = place()
    me = core * WAYS + q
    peers = tp_peers()
    side, far = dp_peers(zh_size)
    greet([p[0] for p in peers] + [side] + [f[0] for f in far])
    waits = []
    gains = []
    for i, (target, rank, _) in enumerate(peers):
        copy = remote(gain.at[rank], gain_t.at[i], g_send.at[i], g_recv.at[i], target)
        copy.start()
        gains.append(copy)

    add = lambda a, b: a + b
    chunks = [
        (win.at[:, 0], win_x.at[0], win_s.at[0], win_z.at[0], add),
        (win.at[:, 1], win_x.at[1], win_s.at[1], win_z.at[1], add),
        (wout, wout_x, wout_s, wout_z, add),
        (mats, mats_x, mats_s, mats_z, add),
        (vectors, small_x, small_s, small_z, add),
        (stats, stats_x, stats_s, stats_z, None),
    ]

    def join(a, b, op):
        a, b = a.astype(f32), b.astype(f32)
        if op is None:
            line = lax.broadcasted_iota(jnp.int32, a.shape, len(a.shape) - 2)
            return jnp.where(line < 4, a + b, jnp.maximum(a, b))
        return op(a, b)

    sends = []

    def to_side(c):
        src, near = chunks[c][:2]
        copy = remote(src.at[1 - x], near, x_send.at[c], x_recv.at[c], side)
        copy.start()
        sends.append(copy)

    to_side(0)
    to_side(1)
    total = gain[me]
    for i in range(TP - 1):
        gains[i].wait_recv()
        total = total + gain_t[i]
    vectors[...] = small[...]
    for g in range(2 * zh_size):
        vectors[g // zh_size, g % zh_size, 8:9, :] = total[g : g + 1, :]
    passed = []
    for c in range(len(chunks)):
        src, near, mine, buf, op = chunks[c]
        sends[c].wait_recv()
        mine[...] = join(src[x], near[...], op).astype(mine.dtype)
        moved = []
        for k, (target, to_z, _) in enumerate(far):
            copy = remote(mine.at[to_z], buf.at[k], z_send.at[c, k], z_recv.at[c, k], target)
            copy.start()
            moved.append(copy)
        passed.append(moved)
        if c + 2 < len(chunks):
            to_side(c + 2)
    outs = [None, None, o_wout, o_mats, o_small, o_stats]
    turn = []
    for c in range(len(chunks)):
        src, near, mine, buf, op = chunks[c]
        value = join(src[x, zh], near[zh], op)
        for k in range(zh_size - 1):
            passed[c][k].wait_recv()
            value = join(value, buf[k], op)
        if c < 2:
            win_t[c] = value.astype(bf16).reshape(win_t.shape[1:])
        else:
            outs[c][...] = value
        if c == 1:
            for i, (target, rank, _) in enumerate(peers):
                copy = remote(
                    win_t.at[rank // WAYS, lax.rem(rank, WAYS)], o_win.at[me], t_send.at[i], t_recv.at[i], target
                )
                copy.start()
                turn.append(copy)
    o_win[me] = win_t[core, q]
    for copy in gains + sends:
        copy.wait_send()
    for moved in passed:
        for copy in moved:
            copy.wait_send()
    for copy in turn:
        copy.wait()


def scatter_gradients(zh_size, win, wout, mats, small, stats, gain):
    dma = pltpu.SemaphoreType.DMA
    far = max(1, zh_size - 1)
    v = lambda shape, dtype: pltpu.VMEM(shape, dtype)
    rows = win.shape[3] // WAYS
    tail = lambda a: a.shape[1:]
    deep = lambda a: (far,) + a.shape[2:]
    ins = (win, wout, mats, small, stats)
    win_deep = (2, far) + win.shape[3:]
    near = [v((2,) + win.shape[2:], bf16)] + [v(tail(a), a.dtype) for a in ins[1:]]
    held = [v((2,) + win.shape[2:], bf16)] + [v(tail(a), a.dtype) for a in ins[1:]]
    buf = [v(win_deep, bf16)] + [v(deep(a), a.dtype) for a in ins[1:]]
    return pl.pallas_call(
        functools.partial(gradients_kernel, zh_size),
        out_shape=[jax.ShapeDtypeStruct((TP, rows, win.shape[4]), bf16)]
        + [jax.ShapeDtypeStruct(a.shape[2:], f32) for a in ins[1:]],
        in_specs=[VM] * 6,
        out_specs=[VM] * 5,
        scratch_shapes=near + held + buf
        + [v((2, WAYS, rows, win.shape[4]), bf16), v((TP - 1,) + gain.shape[1:], f32), v(small.shape, f32)]
        + [dma((6,)), dma((6,)), dma((6, far)), dma((6, far))]
        + [dma((TP - 1,))] * 4,
        input_output_aliases={},
        compiler_params=pltpu.CompilerParams(
            collective_id=5, has_side_effects=True, vmem_limit_bytes=56 * 2**20
        ),
        name="scatter_gradients",
    )(*ins, gain)


def spread_keys(kq, lane):
    a = kq.astype(bf16).astype(f32)
    rest = kq - a
    b = rest.astype(bf16).astype(f32)
    c = rest - b
    return jnp.where(lane < 32, a, jnp.where(lane < 64, b, c)).astype(bf16)


def forward_kernel(act_ref, step_ref, kq_ref, e_ref, y_ref, keep_ref, state, wide):
    tokens, seqs, channels = act_ref.shape
    parts = channels // 128
    rows_of = STEPS * seqs
    lane = lax.broadcasted_iota(jnp.int32, (rows_of, 128), 1)
    state[...] = jnp.zeros_like(state)

    def block(b, carry):
        keep_ref[b] = state[...]
        rows = pl.ds(pl.multiple_of(b * rows_of, rows_of), rows_of)
        wide[...] = jnp.dot(spread_keys(kq_ref[rows, :], lane), e_ref[...], preferred_element_type=f32)

        def one(j, carry):
            t = b * STEPS + j
            r = pl.ds(pl.multiple_of(j * seqs, seqs), seqs)
            acts = [act_ref[t, :, c * 128 : (c + 1) * 128] for c in range(parts)]
            steps = [step_ref[t, :, c * 128 : (c + 1) * 128] for c in range(parts)]
            sums = [None] * parts
            for n in range(STATE):
                key = wide[r, n * 128 : (n + 1) * 128]
                query = wide[r, (STATE + n) * 128 : (STATE + n + 1) * 128]
                for c in range(parts):
                    s = state[n, c]
                    s = s + (steps[c] * key) * (acts[c] - key * s)
                    state[n, c] = s
                    sums[c] = s * query if sums[c] is None else sums[c] + s * query
            for c in range(parts):
                y_ref[t, :, c * 128 : (c + 1) * 128] = sums[c]
            return carry

        return lax.fori_loop(0, STEPS, one, carry)

    lax.fori_loop(0, tokens // STEPS, block, 0)


def spreader():
    one = jnp.repeat(jnp.eye(32, dtype=bf16), 128, axis=1)
    return jnp.concatenate([one, one, one, jnp.zeros_like(one)], axis=0)


def recur_forward(act, step, kq):
    tokens, seqs, channels = act.shape
    parts = channels // 128
    return pl.pallas_call(
        forward_kernel,
        out_shape=[
            jax.ShapeDtypeStruct(act.shape, f32),
            jax.ShapeDtypeStruct((tokens // STEPS, STATE, parts, seqs, 128), f32),
        ],
        in_specs=[VM] * 4,
        out_specs=[VM] * 2,
        scratch_shapes=[
            pltpu.VMEM((STATE, parts, seqs, 128), f32),
            pltpu.VMEM((STEPS * seqs, 32 * 128), f32),
        ],
        compiler_params=pltpu.CompilerParams(vmem_limit_bytes=56 * 2**20),
        name="recur_forward",
    )(act, step, kq, spreader())


def backward_kernel(
    act_ref, step_ref, kq_ref, e_ref, et_ref, gsum_ref, keep_ref, gstep_ref, gact_ref, gkq_ref,
    states, lam, wide, terms,
):
    tokens, seqs, channels = act_ref.shape
    parts = channels // 128
    rows_of = STEPS * seqs
    lane = lax.broadcasted_iota(jnp.int32, (rows_of, 128), 1)
    lam[...] = jnp.zeros_like(lam)

    def cut(ref, t):
        return [ref[t, :, c * 128 : (c + 1) * 128] for c in range(parts)]

    def plus(a, b):
        return b if a is None else a + b

    def block(bi, carry):
        b = tokens // STEPS - 1 - bi
        states[0] = keep_ref[b]
        rows = pl.ds(pl.multiple_of(b * rows_of, rows_of), rows_of)
        wide[...] = jnp.dot(spread_keys(kq_ref[rows, :], lane), e_ref[...], preferred_element_type=f32)

        def again(j, carry):
            t = b * STEPS + j
            r = pl.ds(pl.multiple_of(j * seqs, seqs), seqs)
            acts, steps = cut(act_ref, t), cut(step_ref, t)
            for n in range(STATE):
                key = wide[r, n * 128 : (n + 1) * 128]
                for c in range(parts):
                    s = states[j, n, c]
                    states[j + 1, n, c] = s + (steps[c] * key) * (acts[c] - key * s)
            return carry

        lax.fori_loop(0, STEPS, again, 0)

        def back(jj, carry):
            j = STEPS - 1 - jj
            t = b * STEPS + j
            r = pl.ds(pl.multiple_of(j * seqs, seqs), seqs)
            acts, steps, gsums = cut(act_ref, t), cut(step_ref, t), cut(gsum_ref, t)
            first, second = [None] * parts, [None] * parts
            for n in range(STATE):
                key = wide[r, n * 128 : (n + 1) * 128]
                query = wide[r, (STATE + n) * 128 : (STATE + n + 1) * 128]
                key_term, query_term = None, None
                for c in range(parts):
                    before, after = states[j, n, c], states[j + 1, n, c]
                    grad = lam[n, c] + gsums[c] * query
                    w = key * before
                    d = acts[c] - w
                    gk = grad * key
                    first[c] = plus(first[c], gk * d)
                    second[c] = plus(second[c], gk)
                    key_term = plus(key_term, (steps[c] * grad) * (d - w))
                    query_term = plus(query_term, gsums[c] * after)
                    lam[n, c] = grad - (steps[c] * key) * gk
                terms[r, n * 128 : (n + 1) * 128] = key_term
                terms[r, (STATE + n) * 128 : (STATE + n + 1) * 128] = query_term
            for c in range(parts):
                gstep_ref[t, :, c * 128 : (c + 1) * 128] = first[c]
                gact_ref[t, :, c * 128 : (c + 1) * 128] = steps[c] * second[c]
            return carry

        lax.fori_loop(0, STEPS, back, 0)
        p = terms[...]
        high = p.astype(bf16)
        low = (p - high.astype(f32)).astype(bf16)
        gkq_ref[rows, :] = jnp.dot(high, et_ref[...], preferred_element_type=f32) + jnp.dot(
            low, et_ref[...], preferred_element_type=f32
        )
        return carry

    lax.fori_loop(0, tokens // STEPS, block, 0)


def recur_backward(act, step, kq, gsum, keep):
    tokens, seqs, channels = act.shape
    parts = channels // 128
    fold = jnp.pad(jnp.repeat(jnp.eye(32, dtype=bf16), 128, axis=0), ((0, 0), (0, 96)))
    return pl.pallas_call(
        backward_kernel,
        out_shape=[
            jax.ShapeDtypeStruct(act.shape, f32),
            jax.ShapeDtypeStruct(act.shape, f32),
            jax.ShapeDtypeStruct((tokens * seqs, 128), f32),
        ],
        in_specs=[VM] * 7,
        out_specs=[VM] * 3,
        scratch_shapes=[
            pltpu.VMEM((STEPS + 1, STATE, parts, seqs, 128), f32),
            pltpu.VMEM((STATE, parts, seqs, 128), f32),
            pltpu.VMEM((STEPS * seqs, 32 * 128), f32),
            pltpu.VMEM((STEPS * seqs, 32 * 128), f32),
        ],
        compiler_params=pltpu.CompilerParams(vmem_limit_bytes=60 * 2**20),
        name="recur_backward",
    )(act, step, kq, spreader(), fold, gsum, keep)


def dot(a, b, contract, out=f32):
    return lax.dot_general(a, b, (contract, ((), ())), preferred_element_type=out)


def rms(stream):
    return lax.rsqrt(jnp.mean(jnp.square(stream), axis=-1, keepdims=True) + eps)


def shifted(values, by):
    length = values.shape[0]
    if by == 0:
        return values
    if by > 0:
        return jnp.pad(values, ((by, 0), (0, 0), (0, 0)))[:length]
    return jnp.pad(values, ((0, -by), (0, 0), (0, 0)))[-by:]


def forward_layer(stream, w):
    tokens = stream.shape[0]
    normed = (stream * rms(stream) * w["gain"]).astype(bf16)
    rows = tp_gather(normed).reshape(TP * tokens, -1)
    entry = dot(rows, w["win"], ((1,), (0,))).reshape(TP, tokens, -1).transpose(1, 0, 2)
    half = entry.shape[-1] // 2
    inner, gate = entry[..., :half], entry[..., half:]
    conv = w["shift"] + sum(w["taps"][j] * shifted(inner, CONV - 1 - j) for j in range(CONV))
    act = jax.nn.silu(conv).astype(bf16)
    flat = act.reshape(tokens * TP, half)
    projected = dot(flat, w["select"], ((1,), (0,)))
    low = projected[:, :RANK]
    kq = projected[:, RANK:]
    whole = jnp.concatenate([low, kq, kq, kq, jnp.zeros_like(kq)], axis=1)
    summed, _ = tp_sum(whole.reshape(TP, tokens, -1), jnp.zeros((8, 128), f32))
    summed = summed.reshape(tokens * TP, -1)
    low16 = summed[:, :RANK].astype(bf16)
    kq = summed[:, RANK:]
    rate_pre = dot(low16, w["rate"], ((1,), (1,))).reshape(tokens, TP, half)
    beta = jax.nn.sigmoid(rate_pre + w["rate_shift"])
    norm = jnp.sum(jnp.square(kq[:, :STATE]), axis=-1).reshape(tokens, TP, 1)
    step = beta / (1.0 + beta * norm)
    act32 = act.astype(f32)
    recurrent, keep = recur_forward(act32, step, kq)
    mixed = ((recurrent + w["skip"] * act32) * jax.nn.silu(gate)).astype(bf16)
    mixed = mixed.transpose(1, 0, 2).reshape(TP * tokens, half)
    partial = dot(mixed, w["wout"], ((1,), (0,)), bf16).reshape(TP, tokens, -1)
    result = stream + tp_scatter(partial)
    beta_sums = jnp.sum(beta, axis=(0, 2))
    beta_peaks = jnp.max(beta, axis=(0, 2))
    kept = (stream, rows, inner, gate, conv, act, low16, kq, beta, norm, step, recurrent, keep, mixed)
    return result, kept, (beta_sums, beta_peaks)


def backward_layer(grad, kept, w, stats):
    stream, rows, inner, gate, conv, act, low16, kq, beta, norm, step, recurrent, keep, mixed = kept
    tokens = stream.shape[0]
    half = gate.shape[-1]
    gout = tp_gather(grad.astype(bf16)).reshape(TP * tokens, -1)
    slope_out = dot(mixed, gout, ((0,), (0,)), bf16)
    gmixed = dot(gout, w["wout"], ((1,), (1,))).reshape(TP, tokens, half).transpose(1, 0, 2)
    act32 = act.astype(f32)
    sig = jax.nn.sigmoid(gate)
    gsum = gmixed * (gate * sig)
    ggate = gmixed * (recurrent + w["skip"] * act32) * (sig * (1.0 + gate * (1.0 - sig)))
    slope_skip = jnp.sum(gsum * act32, axis=(0, 1))
    gstep, gact, gkq = recur_backward(act32, step, kq, gsum, keep)
    gact = gact + w["skip"] * gsum
    inverse = 1.0 / jnp.square(1.0 + beta * norm)
    gnorm = -jnp.sum(gstep * jnp.square(beta) * inverse, axis=-1).reshape(tokens * TP, 1)
    grate = gstep * inverse * beta * (1.0 - beta)
    slope_rate_shift = jnp.sum(grate, axis=(0, 1))
    grate16 = grate.astype(bf16).reshape(tokens * TP, half)
    slope_rate = dot(grate16, low16, ((0,), (0,)), bf16)
    grank = dot(grate16, w["rate"], ((1,), (0,)))
    gkeys = gkq[:, :STATE] + 2.0 * kq[:, :STATE] * gnorm
    whole = jnp.concatenate([grank, gkeys, gkq[:, STATE:]], axis=1)
    summed, stats = tp_sum(whole.reshape(TP, tokens, -1), stats)
    gproj = summed.reshape(tokens * TP, -1)[:, : RANK + 2 * STATE].astype(bf16)
    slope_select = dot(act.reshape(tokens * TP, half), gproj, ((0,), (0,)), bf16)
    gact = gact + dot(gproj, w["select"], ((1,), (1,))).reshape(tokens, TP, half)
    sig = jax.nn.sigmoid(conv)
    gconv = gact * (sig * (1.0 + conv * (1.0 - sig)))
    slope_shift = jnp.sum(gconv, axis=(0, 1))
    slope_taps = [jnp.sum(gconv * shifted(inner, CONV - 1 - j), axis=(0, 1)) for j in range(CONV)]
    ginner = sum(w["taps"][j] * shifted(gconv, j - CONV + 1) for j in range(CONV))
    gentry = jnp.concatenate([ginner, ggate], axis=-1).astype(bf16)
    gentry = gentry.transpose(1, 0, 2).reshape(TP * tokens, 2 * half)
    slope_in = dot(rows, gentry, ((0,), (0,)), bf16)
    partial = dot(gentry, w["win"], ((1,), (1,)), bf16).reshape(TP, tokens, -1)
    gnormed = tp_scatter(partial)
    r = rms(stream)
    slope_gain = jnp.sum(gnormed * stream * r, axis=0)
    scaled = gnormed * w["gain"]
    grad = grad + r * scaled - stream * (r * r * r) * jnp.mean(stream * scaled, axis=-1, keepdims=True)
    vectors = jnp.stack(slope_taps + [slope_shift, slope_rate_shift, slope_skip])
    return grad, (slope_in, slope_out, slope_rate, slope_select, vectors, slope_gain), stats


def on_device(
    hidden, cotangent, groups, group_weights, input_weight, select_weight, rate_weight,
    output_weight, norm_gain, conv_taps, conv_shift, rate_shift, skip_gain,
):
    fsdp = lax.axis_size("fsdp")
    zh_size = fsdp // WAYS
    count = 2 * 2 * fsdp
    group_count = 2 * zh_size
    share = conv_shift.shape[1]
    gains = norm_gain.shape[1]
    depth = input_weight.shape[1]
    x, core, zh, q = place()

    labels = jnp.arange(group_weights.shape[0])
    own_weight = jnp.sum(jnp.where(groups[:, None] == labels[None, :], group_weights[None, :], 0.0))

    weights = []
    for l in range(LAYERS):
        win = input_weight[l].reshape(depth, 2, 2, 2, zh_size, WAYS, share)
        win = win.transpose(3, 5, 0, 1, 2, 4, 6).reshape(TP, depth, 2 * group_count * share)
        mats = jnp.concatenate([rate_weight[l].T, select_weight[l]], axis=1)
        small = jnp.concatenate(
            [conv_taps[l], conv_shift[l][None], rate_shift[l][None], skip_gain[l][None], skip_gain[l][None]]
        ).astype(f32)
        small = jnp.pad(small, ((0, 0), (0, 128 - share)))
        misc = jnp.pad(norm_gain[l].astype(f32)[None], ((0, 7), (0, 128 - gains)))
        misc = misc.at[1, :].set(own_weight)
        win, wout, mats, small, misc = gather_weights(zh_size, l, win, output_weight[l], mats, small, misc)
        mats = mats.reshape(group_count * share, -1)
        small = small[:, :, :share].transpose(1, 0, 2).reshape(8, group_count * share)
        weights.append(
            dict(
                win=win.reshape(count * depth, -1), wout=wout.reshape(group_count * share, -1),
                rate=mats[:, :RANK], select=mats[:, RANK:], taps=small[:CONV], shift=small[CONV],
                rate_shift=small[CONV + 1], skip=small[CONV + 2],
                gain=misc[:, 0, :gains].reshape(count * gains),
            )
        )
        if l == 0:
            all_weights = misc[:, 1, 0]
    scales = all_weights / jnp.mean(all_weights)
    table = scales.reshape(2, 2, zh_size, WAYS)
    own_scale = table[x, core, zh, q]
    group_scale = table[x, :, zh, :].reshape(TP)

    stream = hidden[0]
    kept_all, stat_rows = [], []
    for l in range(LAYERS):
        stream, kept, (sums, peaks) = forward_layer(stream, weights[l])
        kept_all.append(kept)
        stat_rows.append((jnp.sum(sums * group_scale), jnp.max(peaks * group_scale)))
    rows = [s for s, _ in stat_rows] + [jnp.zeros((), f32)] * (4 - LAYERS)
    rows += [p for _, p in stat_rows] + [jnp.zeros((), f32)] * (4 - LAYERS)
    own_stats = jnp.broadcast_to(jnp.stack(rows)[:, None], (8, 128))

    grad = cotangent[0] * own_scale
    shares = [None] * LAYERS
    for l in reversed(range(LAYERS)):
        grad, slopes, stats = backward_layer(grad, kept_all[l], weights[l], own_stats)
        slope_in, slope_out, slope_rate, slope_select, vectors, slope_gain = slopes
        stats = jnp.concatenate([jnp.sum(stats[:, :4], axis=0), jnp.max(stats[:, 4:], axis=0)])
        stats = jnp.broadcast_to(stats, (2, zh_size, 8, 128))
        win = slope_in.reshape(2, 2, zh_size, WAYS * depth, -1)
        wout = slope_out.reshape(2, zh_size, share, -1)
        mats = jnp.concatenate([slope_rate, slope_select], axis=1).reshape(2, zh_size, share, -1)
        small = vectors.reshape(7, group_count, share).transpose(1, 0, 2)
        small = jnp.pad(small, ((0, 0), (0, 9), (0, 128 - share))).reshape(2, zh_size, 16, 128)
        gain = slope_gain.reshape(2, 2, zh_size, WAYS, gains).transpose(1, 3, 0, 2, 4)
        gain = gain.reshape(TP, group_count, gains)
        gain = jnp.pad(gain, ((0, 0), (0, -group_count % 8), (0, 128 - gains)))
        shares[l] = scatter_gradients(zh_size, win, wout, mats, small, stats, gain)
    outs = [[] for _ in range(9)]
    for l in range(LAYERS):
        win, wout, mats, small, stats = shares[l]
        win = win.reshape(2, WAYS, depth, 2, 2, zh_size, share).transpose(2, 3, 4, 0, 5, 1, 6)
        outs[0].append(win.reshape(depth, -1).astype(f32))
        outs[1].append(mats[:, RANK:])
        outs[2].append(mats[:, :RANK].T)
        outs[3].append(wout)
        outs[4].append(small[8, :gains])
        outs[5].append(small[:CONV, :share])
        outs[6].append(small[CONV, :share])
        outs[7].append(small[CONV + 1, :share])
        outs[8].append(small[CONV + 2, :share])
    stacked = tuple(jnp.stack(o) for o in outs)
    beta_mean = stats[:LAYERS, 0] / (count * hidden.shape[1] * INNER)
    beta_max = stats[4 : 4 + LAYERS, 0]
    return (stream[None], grad[None]) + stacked + (beta_mean, beta_max)


def solution(mesh):
    both = ("dp", "fsdp")
    placed = (
        P(both, None, None), P(both, None, None), P(both), P(),
        P(None, both, None), P(None, both, None), P(None, None, both), P(None, both, None),
        P(None, both), P(None, None, both), P(None, both), P(None, both), P(None, both),
    )
    return jax.shard_map(
        on_device,
        mesh=mesh,
        in_specs=placed,
        out_specs=(P(both, None, None), P(both, None, None)) + placed[4:] + (P(), P()),
        check_vma=False,
    )
```

time: 6680 us -> 1140 us (0.17)
  waiting for transfers between devices: 5010 us -> 0 us
  Pallas kernels: 0 us -> 862 us
  blocking collectives: 641 us -> 0 us
  other arithmetic: 517 us -> 62.8 us
  matrix products: 223 us -> 106 us
  local copies, waits for them, and re-layouts: 208 us -> 91.1 us
    reduce_scatter x8 -> x0, waiting for transfers between devices: 4770 us -> none  [the longest x2 2810 us: backward_layer(): lax.psum_scatter(slope_input, ('dp', 'fsdp'), scatter_dimension=0, tiled=...]
    pallas_call x0 -> x20, Pallas kernels: none -> 862 us  [the longest x2 211 us: scatter_gradients(): pl.pallas_call(functools.partial(gradients_kernel, zh_size), out_shape=[j...]
    all_gather x8 -> x0, blocking collectives: 520 us -> none  [the longest x2 134 us: fetch_forward(): lax.all_gather(taps_piece, ('dp', 'fsdp'), axis=1, tiled=True)]
    unnamed x22 -> x0, waiting for transfers between devices: 248 us -> none
    reduce_sum x403 -> x15, other arithmetic: 255 us -> 19.7 us  [the longest x2 8.87 us: backward_layer(): jnp.sum(gconv * shifted(inner, CONV - 1 - j), axis=(0, 1))]
    mul x932 -> x4, other arithmetic: 170 us -> 1.1 us  [the longest x2 1.09 us: backward_layer(): r * r * r]
    dot_general x24, matrix products: 223 us -> 106 us  [dot(): lax.dot_general(a, b, (contract, ((), ())), preferred_element_type=out)]
  transfers between devices with their start and end apart: 19 -> 0, of which waited for: 10 -> 0; matrix products, arithmetic and copies ran while one was open for 5% -> 0% of each run, Pallas kernels for 0% -> 0%
where the time goes in v1:
time: 1140 us; the launch traced here: 1130 us
  Pallas kernels  862 us (76%)
  matrix products  106 us (9%)
  local copies, waits for them, and re-layouts  91.1 us (8%)
  other arithmetic  62.8 us (6%)
    pallas_call x2, Pallas kernels, scatter_gradients(): pl.pallas_call(functools.partial(gradients_kernel, zh_size), out_shape=[j...  211 us
    pallas_call x2, Pallas kernels, gather_weights(): pl.pallas_call(functools.partial(weights_kernel, zh_size), out_shape=[jax...  188 us
    pallas_call x4, Pallas kernels, tp_gather(): pl.pallas_call(tp_gather_kernel, out_shape=jax.ShapeDtypeStruct((TP,) + r...  118 us
    pallas_call x4, Pallas kernels, tp_sum(): pl.pallas_call(tp_sum_kernel, out_shape=[jax.ShapeDtypeStruct(partial.sha...  116 us
    pallas_call x4, Pallas kernels, tp_scatter(): pl.pallas_call(tp_scatter_kernel, out_shape=jax.ShapeDtypeStruct(block, f...  116 us
    dot_general x24, matrix products, dot(): lax.dot_general(a, b, (contract, ((), ())), preferred_element_type=out)  106 us
    pallas_call x2, Pallas kernels, recur_backward(): pl.pallas_call(backward_kernel, out_shape=[jax.ShapeDtypeStruct(act.shape...  80.3 us
    pallas_call x2, Pallas kernels, recur_forward(): pl.pallas_call(forward_kernel, out_shape=[jax.ShapeDtypeStruct(act.shape,...  33.2 us

profile of v1, /device:TPU:0, one launch (start us, length us, event | category | flops | bytes accessed | tf_op | source)
XLA Modules:
  0.0 1126.2 jit_solution(17076642756590787)
XLA Ops:
  24.6 96.0 %gather_weights.2 = (bf16[32,64,1024]{2,1,0:T(8,128)(2,1)}, bf16[4,128,2048]{2,1,0:T(8,128)(2,1)}, bf16[4,128,288]{2,1,0:T(8,128)(2,1)}, f32[4,8,128]{2,1,0:T(8,128)}, f32[32,8,128]{2,1,0:T(8,128)}) custom-call(bf16[8,64,1024]{2,1,0:T(8,128)(2,1)} %reshape.433.win, bf16[128,2048]{1,0:T(8,128)(2,1)} %get-tuple-element.204.wout, ...), custom_call_target="tpu_custom_call" | custom-call | tf_op jit(solution)/shard_map/gather_weights/pallas_call | solution.py:157
  124.1 1.6 fusion.113
  127.9 29.6 %tp_gather.6 = bf16[8,128,2048]{2,1,0:T(8,128)(2,1)} custom-call(bf16[128,2048]{1,0:T(8,128)(2,1)} %bitcast_convert_fusion.x_ref), custom_call_target="tpu_custom_call" | custom-call | tf_op jit(solution)/shard_map/tp_gather/pallas_call | solution.py:207
  157.5 91.6 %gather_weights.3 = (bf16[32,64,1024]{2,1,0:T(8,128)(2,1)}, bf16[4,128,2048]{2,1,0:T(8,128)(2,1)}, bf16[4,128,288]{2,1,0:T(8,128)(2,1)}, f32[4,8,128]{2,1,0:T(8,128)}, f32[32,8,128]{2,1,0:T(8,128)}) custom-call(bf16[8,64,1024]{2,1,0:T(8,128)(2,1)} %reshape.442.win, bf16[128,2048]{1,0:T(8,128)(2,1)} %get-tuple-element.203.wout, ...), custom_call_target="tpu_custom_call" | custom-call | tf_op jit(solution)/shard_map/gather_weights/pallas_call | solution.py:157
  250.2 1.6 fusion.112
  252.9 29.2 %tp_gather.4 = bf16[8,128,2048]{2,1,0:T(8,128)(2,1)} custom-call(bf16[128,2048]{1,0:T(8,128)(2,1)} %fusion.65.x_ref), custom_call_target="tpu_custom_call" | custom-call | tf_op jit(solution)/shard_map/tp_gather/pallas_call | solution.py:207
  282.1 10.5 fusion.8
  292.6 1.8 slice.442
  294.4 7.2 copy.130
  301.7 3.7 fusion.108
  306.8 29.8 %tp_sum.4 = (f32[8,128,256]{2,1,0:T(8,128)S(1)}, f32[8,8,128]{2,1,0:T(8,128)}) custom-call(f32[8,128,256]{2,1,0:T(8,128)S(1)} %bitcast.312, f32[8,128]{1,0:T(8,128)S(1)} %broadcast_16_own_ref.2.own_ref), custom_call_target="tpu_custom_call" | custom-call | tf_op jit(solution)/shard_map/tp_sum/pallas_call | solution.py:300
  337.8 2.3 multiply_divide_fusion.3
  343.8 16.6 %recur_forward.2 = (f32[128,8,512]{2,1,0:T(8,128)}, f32[8,16,4,8,128]{4,3,2,1,0:T(8,128)}) custom-call(f32[128,8,512]{2,1,0:T(8,128)} %get-tuple-element.188.act_ref, f32[128,8,512]{2,1,0:T(8,128)} %get-tuple-element.243.step_ref, f32[1024,128]{1,0:T(8,128)} %slice.452.kq_ref, bf16[128,4096]{1,0:T(8,128)(2,1)} %maximum_maximum_fusion.1.e_ref), custom_call_target="tpu_custom_call" | custom-call | tf_op jit(solution)/shard_map/recur_forward/pallas_call | solution.py:491
  360.3 2.9 fusion.44
  364.5 1.7 copy.158
  366.3 4.3 fusion.98.p_ref
  370.5 28.5 %tp_scatter.4 = f32[128,2048]{1,0:T(8,128)S(1)} custom-call(bf16[8,128,2048]{2,1,0:T(8,128)(2,1)S(1)} %fusion.98.p_ref), custom_call_target="tpu_custom_call" | custom-call | tf_op jit(solution)/shard_map/tp_scatter/pallas_call | solution.py:253
  400.8 29.0 %tp_gather.5 = bf16[8,128,2048]{2,1,0:T(8,128)(2,1)} custom-call(bf16[128,2048]{1,0:T(8,128)(2,1)} %multiply_convert_fusion.4.x_ref), custom_call_target="tpu_custom_call" | custom-call | tf_op jit(solution)/shard_map/tp_gather/pallas_call | solution.py:207
  429.8 10.4 fusion.11
  440.2 3.1 slice.457
  443.3 6.6 copy.137
  449.9 13.3 %multiply_reduce_fusion = (f32[512]{0:T(512)}, f32[128,8,512]{2,1,0:T(8,128)}, bf16[128,8,512]{2,1,0:T(8,128)(2,1)S(1)}, f32[128,8,512]{2,1,0:T(8,128)}, f32[8,128,512]{2,0,1:T(8,128)}) fusion(f32[128,8,1024]{2,1,0:T(8,128)} %fusion.11, f32[128,8,512]{2,1,0:T(8,128)} %slice.457, f32[512]{0:T(512)S(1)} %bitcast.392, f32[512]{0:T(512)S(1)} %bitcast.394, ...), kind=kOutput, calls=%fused_computation.60 | convolution fusion | flops 2158493184 | bytes 17838080 | tf_op jit(solution)/shard_map/dot_general | solution.py:608
  465.0 1.6 copy.112
  466.6 29.0 %tp_sum.5 = (f32[8,128,256]{2,1,0:T(8,128)S(1)}, f32[8,8,128]{2,1,0:T(8,128)}) custom-call(f32[8,128,256]{2,1,0:T(8,128)S(1)} %bitcast.313, f32[8,128]{1,0:T(8,128)S(1)} %broadcast_16_own_ref.2.own_ref), custom_call_target="tpu_custom_call" | custom-call | tf_op jit(solution)/shard_map/tp_sum/pallas_call | solution.py:300
  497.4 1.6 convert_element_type.147.act_ref
  499.0 2.4 multiply_divide_fusion.2
  505.2 2.6 stack.123
  507.9 16.6 %recur_forward.3 = (f32[128,8,512]{2,1,0:T(8,128)}, f32[8,16,4,8,128]{4,3,2,1,0:T(8,128)}) custom-call(f32[128,8,512]{2,1,0:T(8,128)} %convert_element_type.147.act_ref, f32[128,8,512]{2,1,0:T(8,128)} %get-tuple-element.246.step_ref, f32[1024,128]{1,0:T(8,128)} %slice.467.kq_ref, bf16[128,4096]{1,0:T(8,128)(2,1)} %maximum_maximum_fusion.1.e_ref), custom_call_target="tpu_custom_call" | custom-call | tf_op jit(solution)/shard_map/recur_forward/pallas_call | solution.py:491
  524.5 40.2 %recur_backward.2 = (f32[128,8,512]{2,1,0:T(8,128)}, f32[128,8,512]{2,1,0:T(8,128)}, f32[1024,128]{1,0:T(8,128)}) custom-call(f32[128,8,512]{2,1,0:T(8,128)} %convert_element_type.147.act_ref, f32[128,8,512]{2,1,0:T(8,128)} %get-tuple-element.246.step_ref, f32[1024,128]{1,0:T(8,128)} %slice.467.kq_ref, bf16[128,4096]{1,0:T(8,128)(2,1)} %maximum_maximum_fusion.1.e_ref, ...), custom_call_target="tpu_custom_call" | custom-call | tf_op jit(solution)/shard_map/recur_backward/pallas_call | solution.py:587
  564.7 3.3 fusion.105
  568.5 2.1 multiply_add_fusion.5
  570.6 2.3 fusion.52
  576.0 28.3 %tp_sum.6 = (f32[8,128,256]{2,1,0:T(8,128)S(1)}, f32[8,8,128]{2,1,0:T(8,128)S(1)}) custom-call(f32[8,128,256]{2,1,0:T(8,128)S(1)} %bitcast.315, f32[8,128]{1,0:T(8,128)S(1)} %broadcast_in_dim.26.own_ref), custom_call_target="tpu_custom_call" | custom-call | tf_op jit(solution)/shard_map/tp_sum/pallas_call | solution.py:300
  604.4 3.4 fusion.31
  608.8 5.4 multiply_reduce_fusion.2
  618.8 6.3 fusion.123.wout
  625.1 2.4 fusion.96.p_ref
  627.5 29.0 %tp_scatter.5 = f32[128,2048]{1,0:T(8,128)S(1)} custom-call(bf16[8,128,2048]{2,1,0:T(8,128)(2,1)S(1)} %fusion.96.p_ref), custom_call_target="tpu_custom_call" | custom-call | tf_op jit(solution)/shard_map/tp_scatter/pallas_call | solution.py:253
  656.9 1.9 copy-done.90
  658.8 7.8 fusion.102.p_ref
  666.6 28.6 %tp_scatter.6 = f32[128,2048]{1,0:T(8,128)S(1)} custom-call(bf16[8,128,2048]{2,1,0:T(8,128)(2,1)S(1)} %fusion.102.p_ref), custom_call_target="tpu_custom_call" | custom-call | tf_op jit(solution)/shard_map/tp_scatter/pallas_call | solution.py:253
  697.4 6.0 fusion.122.win
  704.6 2.6 fusion.106
  707.9 105.6 %scatter_gradients.3 = (bf16[8,64,1024]{2,1,0:T(8,128)(2,1)}, f32[128,2048]{1,0:T(8,128)}, f32[128,288]{1,0:T(8,128)}, f32[16,128]{1,0:T(8,128)}, f32[8,128]{1,0:T(8,128)}) custom-call(bf16[2,2,2,256,1024]{4,3,2,1,0:T(8,128)(2,1)} %fusion.122.win, bf16[2,2,128,2048]{3,2,1,0:T(8,128)(2,1)} %fusion.123.wout, bf16[2,2,128,288]{3,2,1,0:T(8,128)(2,1)} %bitcast.331, ...), custom_call_target="tpu_custom_call" | custom-call | tf_op jit(solution)/shard_map/scatter_gradients/pallas_call | solution.py:422
  813.5 1.8 convert_element_type.156
  816.7 1.8 convert_element_type.158
  820.8 30.2 %tp_gather.7 = bf16[8,128,2048]{2,1,0:T(8,128)(2,1)} custom-call(bf16[128,2048]{1,0:T(8,128)(2,1)} %get-tuple-element.184.x_ref), custom_call_target="tpu_custom_call" | custom-call | tf_op jit(solution)/shard_map/tp_gather/pallas_call | solution.py:207
  851.1 10.0 multiply_reduce_fusion.5
  861.1 40.1 %recur_backward.3 = (f32[128,8,512]{2,1,0:T(8,128)}, f32[128,8,512]{2,1,0:T(8,128)}, f32[1024,128]{1,0:T(8,128)}) custom-call(f32[128,8,512]{2,1,0:T(8,128)} %get-tuple-element.188.act_ref, f32[128,8,512]{2,1,0:T(8,128)} %get-tuple-element.243.step_ref, f32[1024,128]{1,0:T(8,128)} %slice.452.kq_ref, bf16[128,4096]{1,0:T(8,128)(2,1)} %maximum_maximum_fusion.1.e_ref, ...), custom_call_target="tpu_custom_call" | custom-call | tf_op jit(solution)/shard_map/recur_backward/pallas_call | solution.py:587
  901.2 3.3 fusion.104
  905.0 3.7 fusion.121.wout
  909.1 2.1 multiply_add_fusion.4
  911.1 2.2 fusion.48
  916.5 29.1 %tp_sum.7 = (f32[8,128,256]{2,1,0:T(8,128)S(1)}, f32[8,8,128]{2,1,0:T(8,128)S(1)}) custom-call(f32[8,128,256]{2,1,0:T(8,128)S(1)} %bitcast.314, f32[8,128]{1,0:T(8,128)S(1)} %broadcast_in_dim.26.own_ref), custom_call_target="tpu_custom_call" | custom-call | tf_op jit(solution)/shard_map/tp_sum/pallas_call | solution.py:300
  945.8 3.4 fusion.28
  949.3 3.4 multiply_reduce_fusion.7
  955.9 1.9 copy-done.89
  957.8 7.4 fusion.100.p_ref
  965.2 29.4 %tp_scatter.7 = f32[128,2048]{1,0:T(8,128)S(1)} custom-call(bf16[8,128,2048]{2,1,0:T(8,128)(2,1)S(1)} %fusion.100.p_ref), custom_call_target="tpu_custom_call" | custom-call | tf_op jit(solution)/shard_map/tp_scatter/pallas_call | solution.py:253
  996.8 6.0 fusion.120.win
  1006.1 105.4 %scatter_gradients.2 = (bf16[8,64,1024]{2,1,0:T(8,128)(2,1)}, f32[128,2048]{1,0:T(8,128)}, f32[128,288]{1,0:T(8,128)}, f32[16,128]{1,0:T(8,128)}, f32[8,128]{1,0:T(8,128)}) custom-call(bf16[2,2,2,256,1024]{4,3,2,1,0:T(8,128)(2,1)} %fusion.120.win, bf16[2,2,128,2048]{3,2,1,0:T(8,128)(2,1)} %fusion.121.wout, bf16[2,2,128,288]{3,2,1,0:T(8,128)(2,1)} %bitcast.332, ...), custom_call_target="tpu_custom_call" | custom-call | tf_op jit(solution)/shard_map/scatter_gradients/pallas_call | solution.py:422
  1111.4 2.0 convert_element_type.153
  1115.7 3.2 pad_maximum_fusion
  1123.5 2.3 maximum_convert_fusion
  (343 shorter events, 83.6 us)
Async XLA Ops:
  5.9 246.1 %copy-start.71 = (f32[128]{0:T(128)}, f32[128]{0:T(128)S(1)}, u32[]{:S(2)}) copy-start(f32[128]{0:T(128)S(1)} %get-tuple-element.232) | copy-start | bytes 1540
  10.8 5.1 copy-start.55
  10.9 5.1 copy-start.54
  23.1 103.3 %copy-start.16 = (f32[1,128,2048]{2,1,0:T(8,128)S(1)}, f32[1,128,2048]{2,1,0:T(8,128)}, u32[]{:S(2)}) copy-start(f32[1,128,2048]{2,1,0:T(8,128)} %param.18) | copy-start | bytes 3145732
  125.8 31.7 %copy-start.70 = (f32[2,2,2,4]{3,2,1,0:T(2,128)}, f32[2,2,2,4]{3,2,1,0:T(2,128)S(1)}, u32[]{:S(2)}) copy-start(f32[2,2,2,4]{3,2,1,0:T(2,128)S(1)} %div.103) | copy-start | bytes 388
  157.5 94.4 %copy-start = (f32[1,128,2048]{2,1,0:T(8,128)S(1)}, f32[1,128,2048]{2,1,0:T(8,128)}, u32[]{:S(2)}) copy-start(f32[1,128,2048]{2,1,0:T(8,128)} %param.17) | copy-start | bytes 3145732
  252.0 30.2 %copy-start.45 = (f32[2048]{0:T(1024)}, f32[2048]{0:T(1024)S(1)}, u32[]{:S(2)}) copy-start(f32[2048]{0:T(1024)S(1)} %mul.530) | copy-start | bytes 24580
  294.4 7.3 copy-start.2
  294.4 7.3 copy-start.49
  301.6 3.7 copy-start.35
  343.8 16.6 %copy-start.7 = (bf16[128,8,512]{2,1,0:T(8,128)(2,1)S(1)}, bf16[128,8,512]{2,1,0:T(8,128)(2,1)}, u32[]{:S(2)}) copy-start(bf16[128,8,512]{2,1,0:T(8,128)(2,1)} %copy-done.6) | copy-start | bytes 3145732
  343.8 16.6 %copy-start.58 = (f32[1,4,128]{2,0,1:T(1,128)S(1)}, f32[1,4,128]{2,0,1:T(1,128)}, u32[]{:S(2)}) copy-start(f32[1,4,128]{2,0,1:T(1,128)} %get-tuple-element.216) | copy-start | bytes 6148
  399.2 30.5 %copy-start.4 = (f32[128,2048]{1,0:T(8,128)}, f32[128,2048]{1,0:T(8,128)S(1)}, u32[]{:S(2)}) copy-start(f32[128,2048]{1,0:T(8,128)S(1)} %get-tuple-element.187) | copy-start | bytes 3145732
  399.8 29.9 %copy-start.73 = (f32[128]{0:T(128)}, f32[128]{0:T(128)S(1)}, u32[]{:S(2)}) copy-start(f32[128]{0:T(128)S(1)} %get-tuple-element.234) | copy-start | bytes 1540
  443.3 6.6 copy-start.62
  443.3 6.6 copy-start.64
  443.3 6.6 copy-start.66
  443.3 6.6 copy-start.68
  443.3 6.6 copy-start.75
  449.9 13.3 %copy-start.37 = (bf16[4,128,288]{2,1,0:T(8,128)(2,1)S(1)}, bf16[4,128,288]{2,1,0:T(8,128)(2,1)}, u32[]{:S(2)}) copy-start(bf16[4,128,288]{2,1,0:T(8,128)(2,1)} %get-tuple-element.82) | copy-start | bytes 884740
  463.2 3.4 copy-start.9
  524.5 40.2 %copy-start.42 = (f32[128,8]{1,0:T(8,128)S(1)}, f32[128,8]{1,0:T(8,128)}, u32[]{:S(2)}) copy-start(f32[128,8]{1,0:T(8,128)} %mul.570) | copy-start | bytes 12292
  524.5 40.2 %copy-start.48 = (f32[1,4,128]{2,0,1:T(1,128)S(1)}, f32[1,4,128]{2,0,1:T(1,128)}, u32[]{:S(2)}) copy-start(f32[1,4,128]{2,0,1:T(1,128)} %get-tuple-element.210) | copy-start | bytes 6148
  570.6 3.5 copy-start.27
  575.6 28.7 %copy-start.61 = (f32[1,4,128]{2,0,1:T(1,128)S(1)}, f32[1,4,128]{2,0,1:T(1,128)}, u32[]{:S(2)}) copy-start(f32[1,4,128]{2,0,1:T(1,128)} %get-tuple-element.209) | copy-start | bytes 6148
  575.9 28.4 %copy-start.29 = (f32[128,8,512]{2,1,0:T(8,128)S(1)}, f32[128,8,512]{2,1,0:T(8,128)}, u32[]{:S(2)}) copy-start(f32[128,8,512]{2,1,0:T(8,128)} %get-tuple-element.179.gsum_ref) | copy-start | bytes 6291460
  575.9 28.4 %copy-start.38 = (bf16[4,128,288]{2,1,0:T(8,128)(2,1)S(1)}, bf16[4,128,288]{2,1,0:T(8,128)(2,1)}, u32[]{:S(2)}) copy-start(bf16[4,128,288]{2,1,0:T(8,128)(2,1)} %get-tuple-element.82) | copy-start | bytes 884740
  604.4 3.5 copy-start.11
  604.4 3.5 copy-start.14
  604.4 3.8 copy-start.30
  604.4 4.4 copy-start.31
  604.4 4.4 copy-start.63
  604.4 4.4 copy-start.65
  604.4 4.4 copy-start.67
  604.4 4.4 copy-start.69
  618.8 6.3 copy-start.91
  627.5 29.1 %copy-start.23 = (bf16[128,8,512]{2,1,0:T(8,128)(2,1)S(1)}, bf16[128,8,512]{2,1,0:T(8,128)(2,1)}, u32[]{:S(2)}) copy-start(bf16[128,8,512]{2,1,0:T(8,128)(2,1)} %get-tuple-element.197) | copy-start | bytes 3145732
  627.5 29.1 %copy-start.24 = (bf16[128,8,512]{2,1,0:T(8,128)(2,1)S(1)}, bf16[128,8,512]{2,1,0:T(8,128)(2,1)}, u32[]{:S(2)}) copy-start(bf16[128,8,512]{2,1,0:T(8,128)(2,1)} %get-tuple-element.199) | copy-start | bytes 3145732
  697.4 6.0 copy-start.5
  697.4 6.0 copy-start.74
  815.3 3.7 copy-start.83
  815.3 5.5 copy-start.44
  820.8 30.3 %copy-start.8 = (bf16[128,8,512]{2,1,0:T(8,128)(2,1)S(1)}, bf16[128,8,512]{2,1,0:T(8,128)(2,1)}, u32[]{:S(2)}) copy-start(bf16[128,8,512]{2,1,0:T(8,128)(2,1)} %copy-done.6) | copy-start | bytes 3145732
  820.8 30.3 %copy-start.59 = (f32[1,4,128]{2,0,1:T(1,128)S(1)}, f32[1,4,128]{2,0,1:T(1,128)}, u32[]{:S(2)}) copy-start(f32[1,4,128]{2,0,1:T(1,128)} %get-tuple-element.216) | copy-start | bytes 6148
  861.1 40.2 %copy-start.40 = (f32[128,8]{1,0:T(8,128)S(1)}, f32[128,8]{1,0:T(8,128)}, u32[]{:S(2)}) copy-start(f32[128,8]{1,0:T(8,128)} %copy-done.39) | copy-start | bytes 12292
  901.2 3.4 copy-start.18
  901.2 3.7 copy-start.33
  911.1 3.4 copy-start.26
  916.5 29.2 %copy-start.25 = (f32[128,8,512]{2,1,0:T(8,128)S(1)}, f32[128,8,512]{2,1,0:T(8,128)}, u32[]{:S(2)}) copy-start(f32[128,8,512]{2,1,0:T(8,128)} %get-tuple-element.190) | copy-start | bytes 6291460
  916.5 29.2 %copy-start.36 = (bf16[4,128,288]{2,1,0:T(8,128)(2,1)S(1)}, bf16[4,128,288]{2,1,0:T(8,128)(2,1)}, u32[]{:S(2)}) copy-start(bf16[4,128,288]{2,1,0:T(8,128)(2,1)} %get-tuple-element.75) | copy-start | bytes 884740
  945.7 3.5 copy-start.3
  945.7 3.5 copy-start.50
  945.8 3.5 copy-start.51
  945.8 3.5 copy-start.52
  945.8 3.5 copy-start.53
  996.8 6.0 copy-start.1
  996.8 6.0 copy-start.46
  996.8 6.0 copy-start.72
  1115.7 3.8 copy-start.60
  1115.7 4.4 copy-start.78
  1115.7 5.0 copy-start.77
  1115.7 5.6 copy-start.76
  1115.7 6.1 copy-start.43
  1115.7 7.7 copy-start.21
  (28 other events, 53.2 us)

commit v2 on v1

--- a/solution.py
+++ b/solution.py
@@ -37,6 +37,10 @@
     return pltpu.make_async_remote_copy(
         src_ref=src, dst_ref=dst, send_sem=send, recv_sem=recv, device_id=target, device_id_type=MESH
     )
+
+
+def cost(us):
+    return pl.CostEstimate(flops=int(us * 1.1e9), bytes_accessed=0, transcendentals=0)
 
 
 def greet(targets):
@@ -72,7 +76,7 @@
 
 
 def weights_kernel(
-    zh_size, win, wout, mats, small, misc, o_win, o_wout, o_mats, o_small, o_misc,
+    zh_size, win, late, small, misc, o_win, o_late, o_small, o_misc,
     tp_send, tp_recv, z_send, z_recv, x_send, x_recv, own_sem,
 ):
     x, core, zh, q = place()
@@ -90,15 +94,15 @@
         (
             (win.at[me], o_win.at[row(x, zh, me)]),
             (misc, o_misc.at[row(x, zh, me)]),
-            (wout, o_wout.at[x * zh_size + zh]),
-            (mats, o_mats.at[x * zh_size + zh]),
             (small, o_small.at[x * zh_size + zh]),
+            (late.at[me], o_late.at[me]),
         )
     ):
         copy = pltpu.make_async_copy(src, dst, own_sem.at[i])
         copy.start()
         own.append(copy)
     arrive = []
+    last = []
     for i, (target, rank, source) in enumerate(peers):
         for j, (src, dst) in enumerate(
             ((win.at[rank], o_win.at[row(x, zh, me)]), (misc, o_misc.at[row(x, zh, me)]))
@@ -123,9 +127,8 @@
     spread(0, win.at[me], lambda xx, zz: o_win.at[row(xx, zz, me)])
     spread(1, misc, lambda xx, zz: o_misc.at[row(xx, zz, me)])
     spread(2, small, lambda xx, zz: o_small.at[xx * zh_size + zz])
-    spread(3, mats, lambda xx, zz: o_mats.at[xx * zh_size + zz])
     recv_done = set()
-    item = 4
+    item = 3
     for copy, source, j in arrive:
         copy.wait_recv()
         recv_done.add(id(copy))
@@ -133,7 +136,10 @@
         view = functools.partial(lambda out, source, xx, zz: out.at[row(xx, zz, source)], out, source)
         spread(item, view(x, zh), view)
         item += 1
-    spread(item, wout, lambda xx, zz: o_wout.at[xx * zh_size + zz])
+    for i, (target, rank, source) in enumerate(peers):
+        copy = remote(late.at[rank], o_late.at[me], tp_send.at[i, 2], tp_recv.at[i, 2], target)
+        copy.start()
+        waits.append(copy)
     for copy, it, k, view, from_z in onward:
         copy.wait_recv()
         recv_done.add(id(copy))
@@ -148,28 +154,69 @@
         copy.wait()
 
 
-def gather_weights(zh_size, call, win, wout, mats, small, misc):
+def gather_weights(zh_size, win, late, small, misc):
     groups = 2 * zh_size
     count = groups * TP
-    items = 5 + 2 * (TP - 1)
+    items = 3 + 2 * (TP - 1)
     dma = pltpu.SemaphoreType.DMA
     many = lambda a, n: jax.ShapeDtypeStruct((n,) + a.shape, a.dtype)
     return pl.pallas_call(
         functools.partial(weights_kernel, zh_size),
         out_shape=[
             jax.ShapeDtypeStruct((count,) + win.shape[1:], win.dtype),
-            many(wout, groups), many(mats, groups), many(small, groups), many(misc, count),
+            jax.ShapeDtypeStruct(late.shape, late.dtype),
+            many(small, groups), many(misc, count),
         ],
-        in_specs=[HB] * 5,
-        out_specs=[HB] * 5,
+        in_specs=[HB] * 4,
+        out_specs=[HB] * 4,
         scratch_shapes=[
-            dma((TP - 1, 2)), dma((TP - 1, 2)),
+            dma((TP - 1, 3)), dma((TP - 1, 3)),
             dma((items, max(1, zh_size - 1))), dma((items, max(1, zh_size - 1))),
-            dma((items, zh_size)), dma((items, zh_size)), dma((5,)),
+            dma((items, zh_size)), dma((items, zh_size)), dma((4,)),
         ],
         compiler_params=pltpu.CompilerParams(collective_id=1, has_side_effects=True),
         name="gather_weights",
-    )(win, wout, mats, small, misc)
+        cost_estimate=cost(90),
+    )(win, late, small, misc)
+
+
+def swap(value, zh_size, turn_x, turn_z):
+    fsdp = zh_size * WAYS
+    pairs = []
+    for x in (0, 1):
+        for core in (0, 1):
+            for zh in range(zh_size):
+                for q in range(WAYS):
+                    a = (x * 2 + core) * fsdp + zh * WAYS + q
+                    b = ((x + turn_x) % 2 * 2 + core) * fsdp + (zh + turn_z) % zh_size * WAYS + q
+                    pairs.append((a, b))
+    return lax.ppermute(value, ("dp", "fsdp"), pairs)
+
+
+def dp_gather(piece, zh_size):
+    x, core, zh, q = place()
+    blocks = [piece] + [swap(piece, zh_size, 0, k) for k in range(1, zh_size)]
+    other = [swap(block, zh_size, 1, 0) for block in blocks]
+    out = jnp.zeros((2, piece.shape[0], zh_size) + piece.shape[1:], piece.dtype)
+    zero = (0,) * (piece.ndim - 1)
+    for k in range(zh_size):
+        at = lax.rem(zh + zh_size - k, zh_size)
+        for xx, block in ((x, blocks[k]), (1 - x, other[k])):
+            out = lax.dynamic_update_slice(out, block[None, :, None], (xx, 0, at) + zero)
+    return out
+
+
+def dp_scatter(partial, zh_size, near=None):
+    x, core, zh, q = place()
+    pick = lambda a, i: lax.dynamic_index_in_dim(a, i, 0, keepdims=False)
+    if near is None:
+        near = swap(pick(partial, 1 - x), zh_size, 1, 0)
+    half = pick(partial, x).astype(f32) + near.astype(f32)
+    total = pick(half, zh)
+    half = half.astype(bf16)
+    for k in range(1, zh_size):
+        total = total + swap(pick(half, lax.rem(zh + k, zh_size)), zh_size, 0, k).astype(f32)
+    return total
 
 
 def tp_gather_kernel(x_ref, o_ref, f_send, f_recv, s_send, s_recv, own_sem):
@@ -212,6 +259,7 @@
         scratch_shapes=[dma((3,)), dma((3,)), dma((4,)), dma((4,)), dma],
         compiler_params=pltpu.CompilerParams(collective_id=2, has_side_effects=True),
         name="tp_gather",
+        cost_estimate=cost(28),
     )(rows)
 
 
@@ -263,19 +311,44 @@
             collective_id=3, has_side_effects=True, vmem_limit_bytes=40 * 2**20
         ),
         name="tp_scatter",
+        cost_estimate=cost(28),
     )(partial)
 
 
-def tp_sum_kernel(p_ref, own_ref, o_ref, all_ref, parts, a_send, a_recv, b_send, b_recv, c_send, c_recv):
+def lanes_of(shape):
+    return lax.broadcasted_iota(jnp.int32, shape, 1)
+
+
+def encode(v):
+    tail = v[:, RANK:]
+    lane = lanes_of(tail.shape)
+    high = tail.astype(bf16).astype(f32)
+    low = pltpu.roll(tail - high, 32, 1)
+    both = jnp.where(lane < 32, high, jnp.where(lane < 64, low, 0.0))
+    return jnp.concatenate([v[:, :RANK].astype(bf16), both.astype(bf16)], axis=1)
+
+
+def decode(v):
+    tail = v[:, RANK:].astype(f32)
+    lane = lanes_of(tail.shape)
+    tail = jnp.where(lane < 32, tail + pltpu.roll(tail, 96, 1), 0.0)
+    return jnp.concatenate([v[:, :RANK].astype(f32), tail], axis=1)
+
+
+def tp_sum_kernel(
+    p_ref, own_ref, o_ref, all_ref, out, parts, a_send, a_recv, b_send, b_recv, c_send, c_recv
+):
     x, core, zh, q = place()
     me = core * WAYS + q
     peers = tp_peers()
     greet([p[0] for p in peers])
     one, two = [], []
     for i, (target, rank, _) in enumerate(peers):
-        copy = remote(p_ref.at[rank], parts.at[i], a_send.at[i], a_recv.at[i], target)
+        out[i] = encode(p_ref[rank])
+        copy = remote(out.at[i], parts.at[i], a_send.at[i], a_recv.at[i], target)
         copy.start()
         one.append(copy)
+    for i, (target, rank, _) in enumerate(peers):
         copy = remote(own_ref, all_ref.at[me], c_send.at[i], c_recv.at[i], target)
         copy.start()
         two.append(copy)
@@ -283,8 +356,8 @@
     total = p_ref[me]
     for i in range(TP - 1):
         one[i].wait_recv()
-        total = total + parts[i]
-    o_ref[me] = total
+        total = total + decode(parts[i])
+    o_ref[me] = encode(total)
     for i, (target, rank, _) in enumerate(peers):
         copy = remote(o_ref.at[me], o_ref.at[me], b_send.at[i], b_recv.at[i], target)
         copy.start()
@@ -297,56 +370,54 @@
 
 def tp_sum(partial, own):
     dma = pltpu.SemaphoreType.DMA
+    part = pltpu.VMEM((TP - 1,) + partial.shape[1:], bf16)
     return pl.pallas_call(
         tp_sum_kernel,
         out_shape=[
-            jax.ShapeDtypeStruct(partial.shape, f32),
+            jax.ShapeDtypeStruct(partial.shape, bf16),
             jax.ShapeDtypeStruct((TP,) + own.shape, f32),
         ],
         in_specs=[VM, VM],
         out_specs=[VM, VM],
-        scratch_shapes=[pltpu.VMEM((TP - 1,) + partial.shape[1:], f32)] + [dma((TP - 1,))] * 6,
+        scratch_shapes=[part, part] + [dma((TP - 1,))] * 6,
         compiler_params=pltpu.CompilerParams(
             collective_id=4, has_side_effects=True, vmem_limit_bytes=40 * 2**20
         ),
         name="tp_sum",
+        cost_estimate=cost(18),
     )(partial, own)
 
 
 def gradients_kernel(
-    zh_size, win, wout, mats, small, stats, gain, o_win, o_wout, o_mats, o_small, o_stats,
-    win_x, wout_x, mats_x, small_x, stats_x, win_s, wout_s, mats_s, small_s, stats_s,
-    win_z, wout_z, mats_z, small_z, stats_z, win_t, gain_t, vectors,
-    x_send, x_recv, z_send, z_recv, t_send, t_recv, g_send, g_recv,
+    zh_size, win, small, stats, gain, late, o_win, o_small, o_stats, o_late,
+    win_x, small_x, stats_x, win_s, small_s, stats_s, win_z, small_z, stats_z, win_t, gain_t, vectors,
+    x_send, x_recv, z_send, z_recv, t_send, t_recv, l_send, l_recv, g_send, g_recv,
 ):
     x, core, zh, q = place()
     me = core * WAYS + q
     peers = tp_peers()
     side, far = dp_peers(zh_size)
     greet([p[0] for p in peers] + [side] + [f[0] for f in far])
-    waits = []
     gains = []
+    turn = []
     for i, (target, rank, _) in enumerate(peers):
         copy = remote(gain.at[rank], gain_t.at[i], g_send.at[i], g_recv.at[i], target)
         copy.start()
         gains.append(copy)
 
-    add = lambda a, b: a + b
     chunks = [
-        (win.at[:, 0], win_x.at[0], win_s.at[0], win_z.at[0], add),
-        (win.at[:, 1], win_x.at[1], win_s.at[1], win_z.at[1], add),
-        (wout, wout_x, wout_s, wout_z, add),
-        (mats, mats_x, mats_s, mats_z, add),
-        (vectors, small_x, small_s, small_z, add),
-        (stats, stats_x, stats_s, stats_z, None),
+        (win.at[:, 0], win_x.at[0], win_s.at[0], win_z.at[0], False),
+        (win.at[:, 1], win_x.at[1], win_s.at[1], win_z.at[1], False),
+        (vectors, small_x, small_s, small_z, False),
+        (stats, stats_x, stats_s, stats_z, True),
     ]
 
-    def join(a, b, op):
+    def join(a, b, peaks):
         a, b = a.astype(f32), b.astype(f32)
-        if op is None:
+        if peaks:
             line = lax.broadcasted_iota(jnp.int32, a.shape, len(a.shape) - 2)
             return jnp.where(line < 4, a + b, jnp.maximum(a, b))
-        return op(a, b)
+        return a + b
 
     sends = []
 
@@ -358,18 +429,25 @@
 
     to_side(0)
     to_side(1)
+    for i, (target, rank, _) in enumerate(peers):
+        copy = remote(late.at[rank], o_late.at[me], l_send.at[i], l_recv.at[i], target)
+        copy.start()
+        turn.append(copy)
+    o_late[me] = late[me]
     total = gain[me]
     for i in range(TP - 1):
         gains[i].wait_recv()
         total = total + gain_t[i]
     vectors[...] = small[...]
-    for g in range(2 * zh_size):
-        vectors[g // zh_size, g % zh_size, 8:9, :] = total[g : g + 1, :]
+    for l in range(LAYERS):
+        for g in range(2 * zh_size):
+            at = l * 2 * zh_size + g
+            vectors[g // zh_size, g % zh_size, l * 16 + 8 : l * 16 + 9, :] = total[at : at + 1, :]
     passed = []
     for c in range(len(chunks)):
-        src, near, mine, buf, op = chunks[c]
+        src, near, mine, buf, peaks = chunks[c]
         sends[c].wait_recv()
-        mine[...] = join(src[x], near[...], op).astype(mine.dtype)
+        mine[...] = join(src[x], near[...], peaks).astype(mine.dtype)
         moved = []
         for k, (target, to_z, _) in enumerate(far):
             copy = remote(mine.at[to_z], buf.at[k], z_send.at[c, k], z_recv.at[c, k], target)
@@ -378,14 +456,13 @@
         passed.append(moved)
         if c + 2 < len(chunks):
             to_side(c + 2)
-    outs = [None, None, o_wout, o_mats, o_small, o_stats]
-    turn = []
+    outs = [None, None, o_small, o_stats]
     for c in range(len(chunks)):
-        src, near, mine, buf, op = chunks[c]
-        value = join(src[x, zh], near[zh], op)
+        src, near, mine, buf, peaks = chunks[c]
+        value = join(src[x, zh], near[zh], peaks)
         for k in range(zh_size - 1):
             passed[c][k].wait_recv()
-            value = join(value, buf[k], op)
+            value = join(value, buf[k], peaks)
         if c < 2:
             win_t[c] = value.astype(bf16).reshape(win_t.shape[1:])
         else:
@@ -407,34 +484,30 @@
         copy.wait()
 
 
-def scatter_gradients(zh_size, win, wout, mats, small, stats, gain):
+def scatter_gradients(zh_size, win, small, stats, gain, late):
     dma = pltpu.SemaphoreType.DMA
     far = max(1, zh_size - 1)
     v = lambda shape, dtype: pltpu.VMEM(shape, dtype)
     rows = win.shape[3] // WAYS
-    tail = lambda a: a.shape[1:]
-    deep = lambda a: (far,) + a.shape[2:]
-    ins = (win, wout, mats, small, stats)
-    win_deep = (2, far) + win.shape[3:]
-    near = [v((2,) + win.shape[2:], bf16)] + [v(tail(a), a.dtype) for a in ins[1:]]
-    held = [v((2,) + win.shape[2:], bf16)] + [v(tail(a), a.dtype) for a in ins[1:]]
-    buf = [v(win_deep, bf16)] + [v(deep(a), a.dtype) for a in ins[1:]]
+    ins = (small, stats)
+    near = [v((2,) + win.shape[2:], bf16)] + [v(a.shape[1:], a.dtype) for a in ins]
+    buf = [v((2, far) + win.shape[3:], bf16)] + [v((far,) + a.shape[2:], a.dtype) for a in ins]
+    block = jax.ShapeDtypeStruct((TP, rows, win.shape[4]), bf16)
     return pl.pallas_call(
         functools.partial(gradients_kernel, zh_size),
-        out_shape=[jax.ShapeDtypeStruct((TP, rows, win.shape[4]), bf16)]
-        + [jax.ShapeDtypeStruct(a.shape[2:], f32) for a in ins[1:]],
-        in_specs=[VM] * 6,
-        out_specs=[VM] * 5,
-        scratch_shapes=near + held + buf
+        out_shape=[block] + [jax.ShapeDtypeStruct(a.shape[2:], f32) for a in ins] + [block],
+        in_specs=[VM] * 5,
+        out_specs=[VM] * 4,
+        scratch_shapes=near + near + buf
         + [v((2, WAYS, rows, win.shape[4]), bf16), v((TP - 1,) + gain.shape[1:], f32), v(small.shape, f32)]
-        + [dma((6,)), dma((6,)), dma((6, far)), dma((6, far))]
-        + [dma((TP - 1,))] * 4,
-        input_output_aliases={},
+        + [dma((4,)), dma((4,)), dma((4, far)), dma((4, far))]
+        + [dma((TP - 1,))] * 6,
         compiler_params=pltpu.CompilerParams(
             collective_id=5, has_side_effects=True, vmem_limit_bytes=56 * 2**20
         ),
         name="scatter_gradients",
-    )(*ins, gain)
+        cost_estimate=cost(90),
+    )(win, *ins, gain, late)
 
 
 def spread_keys(kq, lane):
@@ -502,13 +575,19 @@
         ],
         compiler_params=pltpu.CompilerParams(vmem_limit_bytes=56 * 2**20),
         name="recur_forward",
+        cost_estimate=cost(16),
     )(act, step, kq, spreader())
 
 
 def backward_kernel(
-    act_ref, step_ref, kq_ref, e_ref, et_ref, gsum_ref, keep_ref, gstep_ref, gact_ref, gkq_ref,
-    states, lam, wide, terms,
+    act_ref, step_ref, kq_ref, e_ref, et_ref, gsum_ref, keep_ref, slope_ref, gstep_ref, gact_ref, gkq_ref,
+    near_ref, states, lam, wide, terms, send, recv,
 ):
+    x, core, zh, q = place()
+    side = device(1 - x, core, zh, q)
+    greet([side])
+    swap_half = remote(slope_ref.at[1 - x], near_ref, send, recv, side)
+    swap_half.start()
     tokens, seqs, channels = act_ref.shape
     parts = channels // 128
     rows_of = STEPS * seqs
@@ -578,9 +657,10 @@
         return carry
 
     lax.fori_loop(0, tokens // STEPS, block, 0)
-
-
-def recur_backward(act, step, kq, gsum, keep):
+    swap_half.wait()
+
+
+def recur_backward(act, step, kq, gsum, keep, slope):
     tokens, seqs, channels = act.shape
     parts = channels // 128
     fold = jnp.pad(jnp.repeat(jnp.eye(32, dtype=bf16), 128, axis=0), ((0, 0), (0, 96)))
@@ -590,18 +670,23 @@
             jax.ShapeDtypeStruct(act.shape, f32),
             jax.ShapeDtypeStruct(act.shape, f32),
             jax.ShapeDtypeStruct((tokens * seqs, 128), f32),
+            jax.ShapeDtypeStruct(slope.shape[1:], slope.dtype),
         ],
-        in_specs=[VM] * 7,
-        out_specs=[VM] * 3,
+        in_specs=[VM] * 7 + [HB],
+        out_specs=[VM] * 3 + [HB],
         scratch_shapes=[
             pltpu.VMEM((STEPS + 1, STATE, parts, seqs, 128), f32),
             pltpu.VMEM((STATE, parts, seqs, 128), f32),
             pltpu.VMEM((STEPS * seqs, 32 * 128), f32),
             pltpu.VMEM((STEPS * seqs, 32 * 128), f32),
+            pltpu.SemaphoreType.DMA, pltpu.SemaphoreType.DMA,
         ],
-        compiler_params=pltpu.CompilerParams(vmem_limit_bytes=60 * 2**20),
+        compiler_params=pltpu.CompilerParams(
+            collective_id=6, has_side_effects=True, vmem_limit_bytes=60 * 2**20
+        ),
         name="recur_backward",
-    )(act, step, kq, spreader(), fold, gsum, keep)
+        cost_estimate=cost(40),
+    )(act, step, kq, spreader(), fold, gsum, keep, slope)
 
 
 def dot(a, b, contract, out=f32):
@@ -631,14 +716,12 @@
     conv = w["shift"] + sum(w["taps"][j] * shifted(inner, CONV - 1 - j) for j in range(CONV))
     act = jax.nn.silu(conv).astype(bf16)
     flat = act.reshape(tokens * TP, half)
-    projected = dot(flat, w["select"], ((1,), (0,)))
-    low = projected[:, :RANK]
-    kq = projected[:, RANK:]
-    whole = jnp.concatenate([low, kq, kq, kq, jnp.zeros_like(kq)], axis=1)
+    whole = dot(flat, jnp.pad(w["select"], ((0, 0), (0, 96))), ((1,), (0,)))
     summed, _ = tp_sum(whole.reshape(TP, tokens, -1), jnp.zeros((8, 128), f32))
     summed = summed.reshape(tokens * TP, -1)
-    low16 = summed[:, :RANK].astype(bf16)
-    kq = summed[:, RANK:]
+    low16 = summed[:, :RANK]
+    kq = summed[:, RANK : RANK + 32].astype(f32) + summed[:, RANK + 32 : RANK + 64].astype(f32)
+    kq = jnp.concatenate([kq, kq, kq, jnp.zeros_like(kq)], axis=1)
     rate_pre = dot(low16, w["rate"], ((1,), (1,))).reshape(tokens, TP, half)
     beta = jax.nn.sigmoid(rate_pre + w["rate_shift"])
     norm = jnp.sum(jnp.square(kq[:, :STATE]), axis=-1).reshape(tokens, TP, 1)
@@ -667,7 +750,9 @@
     gsum = gmixed * (gate * sig)
     ggate = gmixed * (recurrent + w["skip"] * act32) * (sig * (1.0 + gate * (1.0 - sig)))
     slope_skip = jnp.sum(gsum * act32, axis=(0, 1))
-    gstep, gact, gkq = recur_backward(act32, step, kq, gsum, keep)
+    slope_out = slope_out.reshape(2, lax.axis_size("fsdp") // WAYS, -1, slope_out.shape[1])
+    gstep, gact, gkq, slope_near = recur_backward(act32, step, kq, gsum, keep, slope_out)
+    slope_out = (slope_out, slope_near)
     gact = gact + w["skip"] * gsum
     inverse = 1.0 / jnp.square(1.0 + beta * norm)
     gnorm = -jnp.sum(gstep * jnp.square(beta) * inverse, axis=-1).reshape(tokens * TP, 1)
@@ -679,7 +764,7 @@
     gkeys = gkq[:, :STATE] + 2.0 * kq[:, :STATE] * gnorm
     whole = jnp.concatenate([grank, gkeys, gkq[:, STATE:]], axis=1)
     summed, stats = tp_sum(whole.reshape(TP, tokens, -1), stats)
-    gproj = summed.reshape(tokens * TP, -1)[:, : RANK + 2 * STATE].astype(bf16)
+    gproj = summed.reshape(tokens * TP, -1)[:, : RANK + 2 * STATE]
     slope_select = dot(act.reshape(tokens * TP, half), gproj, ((0,), (0,)), bf16)
     gact = gact + dot(gproj, w["select"], ((1,), (1,))).reshape(tokens, TP, half)
     sig = jax.nn.sigmoid(conv)
@@ -716,30 +801,33 @@
     labels = jnp.arange(group_weights.shape[0])
     own_weight = jnp.sum(jnp.where(groups[:, None] == labels[None, :], group_weights[None, :], 0.0))
 
-    weights = []
+    wins, mats, smalls, misc = [], [], [], []
     for l in range(LAYERS):
         win = input_weight[l].reshape(depth, 2, 2, 2, zh_size, WAYS, share)
-        win = win.transpose(3, 5, 0, 1, 2, 4, 6).reshape(TP, depth, 2 * group_count * share)
-        mats = jnp.concatenate([rate_weight[l].T, select_weight[l]], axis=1)
+        wins.append(win.transpose(3, 5, 0, 1, 2, 4, 6).reshape(TP, depth, 2 * group_count * share))
+        mats.append(jnp.concatenate([rate_weight[l].T, output_weight[l], select_weight[l]], axis=1))
         small = jnp.concatenate(
             [conv_taps[l], conv_shift[l][None], rate_shift[l][None], skip_gain[l][None], skip_gain[l][None]]
         ).astype(f32)
-        small = jnp.pad(small, ((0, 0), (0, 128 - share)))
-        misc = jnp.pad(norm_gain[l].astype(f32)[None], ((0, 7), (0, 128 - gains)))
-        misc = misc.at[1, :].set(own_weight)
-        win, wout, mats, small, misc = gather_weights(zh_size, l, win, output_weight[l], mats, small, misc)
-        mats = mats.reshape(group_count * share, -1)
-        small = small[:, :, :share].transpose(1, 0, 2).reshape(8, group_count * share)
+        smalls.append(jnp.pad(small, ((0, 0), (0, 128 - share))))
+        misc.append(jnp.pad(norm_gain[l].astype(f32)[None], ((0, 0), (0, 128 - gains))))
+    misc = jnp.concatenate(misc + [jnp.full((8 - LAYERS, 128), own_weight)])
+    win, late, small, misc = gather_weights(zh_size, wins[0], wins[1], jnp.concatenate(smalls), misc)
+    all_weights = misc[:, LAYERS, 0]
+    small = small[:, :, :share].transpose(1, 0, 2).reshape(LAYERS, 8, group_count * share)
+    late = late.reshape(2, WAYS * depth, -1)
+    wins = [win.reshape(count * depth, -1), dp_gather(late, zh_size).reshape(count * depth, -1)]
+    weights = []
+    width = output_weight.shape[2]
+    for l in range(LAYERS):
+        m = dp_gather(mats[l][None], zh_size).reshape(group_count * share, -1)
         weights.append(
             dict(
-                win=win.reshape(count * depth, -1), wout=wout.reshape(group_count * share, -1),
-                rate=mats[:, :RANK], select=mats[:, RANK:], taps=small[:CONV], shift=small[CONV],
-                rate_shift=small[CONV + 1], skip=small[CONV + 2],
-                gain=misc[:, 0, :gains].reshape(count * gains),
+                win=wins[l], rate=m[:, :RANK], wout=m[:, RANK : RANK + width], select=m[:, RANK + width :],
+                taps=small[l, :CONV], shift=small[l, CONV], rate_shift=small[l, CONV + 1],
+                skip=small[l, CONV + 2], gain=misc[:, l, :gains].reshape(count * gains),
             )
         )
-        if l == 0:
-            all_weights = misc[:, 1, 0]
     scales = all_weights / jnp.mean(all_weights)
     table = scales.reshape(2, 2, zh_size, WAYS)
     own_scale = table[x, core, zh, q]
@@ -756,34 +844,42 @@
     own_stats = jnp.broadcast_to(jnp.stack(rows)[:, None], (8, 128))
 
     grad = cotangent[0] * own_scale
-    shares = [None] * LAYERS
+    shares, smalls, gain_sums = [None] * LAYERS, [None] * LAYERS, [None] * LAYERS
     for l in reversed(range(LAYERS)):
         grad, slopes, stats = backward_layer(grad, kept_all[l], weights[l], own_stats)
         slope_in, slope_out, slope_rate, slope_select, vectors, slope_gain = slopes
-        stats = jnp.concatenate([jnp.sum(stats[:, :4], axis=0), jnp.max(stats[:, 4:], axis=0)])
-        stats = jnp.broadcast_to(stats, (2, zh_size, 8, 128))
-        win = slope_in.reshape(2, 2, zh_size, WAYS * depth, -1)
-        wout = slope_out.reshape(2, zh_size, share, -1)
-        mats = jnp.concatenate([slope_rate, slope_select], axis=1).reshape(2, zh_size, share, -1)
+        m = jnp.concatenate([slope_rate, slope_select], axis=1)
+        m = dp_scatter(m.reshape(2, zh_size, share, -1), zh_size)
+        shares[l] = (
+            slope_in.reshape(2, 2, zh_size, WAYS * depth, -1), m,
+            dp_scatter(slope_out[0], zh_size, slope_out[1]),
+        )
         small = vectors.reshape(7, group_count, share).transpose(1, 0, 2)
-        small = jnp.pad(small, ((0, 0), (0, 9), (0, 128 - share))).reshape(2, zh_size, 16, 128)
+        smalls[l] = jnp.pad(small, ((0, 0), (0, 9), (0, 128 - share)))
         gain = slope_gain.reshape(2, 2, zh_size, WAYS, gains).transpose(1, 3, 0, 2, 4)
-        gain = gain.reshape(TP, group_count, gains)
-        gain = jnp.pad(gain, ((0, 0), (0, -group_count % 8), (0, 128 - gains)))
-        shares[l] = scatter_gradients(zh_size, win, wout, mats, small, stats, gain)
+        gain_sums[l] = gain.reshape(TP, group_count, gains)
+    stats = jnp.concatenate([jnp.sum(stats[:, :4], axis=0), jnp.max(stats[:, 4:], axis=0)])
+    stats = jnp.broadcast_to(stats, (2, zh_size, 8, 128))
+    small = jnp.concatenate(smalls, axis=1).reshape(2, zh_size, 16 * LAYERS, 128)
+    gain = jnp.concatenate(gain_sums, axis=1)
+    gain = jnp.pad(gain, ((0, 0), (0, -gain.shape[1] % 8), (0, 128 - gains)))
+    late = shares[1][0].swapaxes(1, 2).reshape(2, zh_size, TP * depth, -1)
+    late = dp_scatter(late, zh_size).astype(bf16).reshape(TP, depth, -1)
+    first, small, stats, late = scatter_gradients(zh_size, shares[0][0], small, stats, gain, late)
     outs = [[] for _ in range(9)]
-    for l in range(LAYERS):
-        win, wout, mats, small, stats = shares[l]
+    for l, win in enumerate((first, late)):
+        m = shares[l][1]
         win = win.reshape(2, WAYS, depth, 2, 2, zh_size, share).transpose(2, 3, 4, 0, 5, 1, 6)
         outs[0].append(win.reshape(depth, -1).astype(f32))
-        outs[1].append(mats[:, RANK:])
-        outs[2].append(mats[:, :RANK].T)
-        outs[3].append(wout)
-        outs[4].append(small[8, :gains])
-        outs[5].append(small[:CONV, :share])
-        outs[6].append(small[CONV, :share])
-        outs[7].append(small[CONV + 1, :share])
-        outs[8].append(small[CONV + 2, :share])
+        outs[1].append(m[:, RANK:])
+        outs[2].append(m[:, :RANK].T)
+        outs[3].append(shares[l][2])
+        vec = small[16 * l : 16 * (l + 1)]
+        outs[4].append(vec[8, :gains])
+        outs[5].append(vec[:CONV, :share])
+        outs[6].append(vec[CONV, :share])
+        outs[7].append(vec[CONV + 1, :share])
+        outs[8].append(vec[CONV + 2, :share])
     stacked = tuple(jnp.stack(o) for o in outs)
     beta_mean = stats[:LAYERS, 0] / (count * hidden.shape[1] * INNER)
     beta_max = stats[4 : 4 + LAYERS, 0]

time: 1140 us -> 1040 us (0.912)
  Pallas kernels: 862 us -> 600 us
  waiting for transfers between devices: 0 us -> 106 us
  starting transfers between devices: 0 us -> 23.4 us
  local copies, waits for them, and re-layouts: 91.1 us -> 109 us
    pallas_call x2 -> x1, Pallas kernels: 211 us -> 87.7 us  [scatter_gradients(): pl.pallas_call(functools.partial(gradients_kernel, zh_size), out_shape=[b...]
    ppermute x0 -> x17, waiting for transfers between devices: none -> 106 us  [swap(): return lax.ppermute(value, ('dp', 'fsdp'), pairs)]
    pallas_call x2 -> x1, Pallas kernels: 188 us -> 91.7 us  [gather_weights(): pl.pallas_call(functools.partial(weights_kernel, zh_size), out_shape=[jax...]
    pallas_call x4, Pallas kernels: 116 us -> 73.7 us  [tp_sum(): pl.pallas_call(tp_sum_kernel, out_shape=[jax.ShapeDtypeStruct(partial.sha...]
    ppermute x0 -> x17, starting transfers between devices: none -> 23.4 us  [swap(): return lax.ppermute(value, ('dp', 'fsdp'), pairs)]
    dynamic_update_slice x0 -> x11, local copies, waits for them, and re-layouts: none -> 14.2 us  [dp_gather(): lax.dynamic_update_slice(out, block[None, :, None], (xx, 0, at) + zero)]
    broadcast_in_dim x0 -> x8, local copies, waits for them, and re-layouts: none -> 11.4 us  [the longest x6 8.21 us: dp_gather(): block[None, :, None]]
  transfers between devices with their start and end apart: 0 -> 17, of which waited for: 0 -> 4; matrix products, arithmetic and copies ran while one was open for 0% -> 13% of each run, Pallas kernels for 0% -> 26%
where the time goes in v2:
time: 1040 us; the launch traced here: 1030 us
  Pallas kernels  600 us (58%)
  matrix products  111 us (11%)
  local copies, waits for them, and re-layouts  109 us (10%)
  waiting for transfers between devices  106 us (10%)
  other arithmetic  73.5 us (7%)
  starting transfers between devices  23.4 us (2%)
    pallas_call x4, Pallas kernels, tp_scatter(): pl.pallas_call(tp_scatter_kernel, out_shape=jax.ShapeDtypeStruct(block, f...  115 us
    pallas_call x4, Pallas kernels, tp_gather(): pl.pallas_call(tp_gather_kernel, out_shape=jax.ShapeDtypeStruct((TP,) + r...  114 us
    dot_general x24, matrix products, dot(): lax.dot_general(a, b, (contract, ((), ())), preferred_element_type=out)  111 us
    ppermute x17, waiting for transfers between devices, swap(): return lax.ppermute(value, ('dp', 'fsdp'), pairs)  106 us
    pallas_call x1, Pallas kernels, gather_weights(): pl.pallas_call(functools.partial(weights_kernel, zh_size), out_shape=[jax...  91.7 us
    pallas_call x1, Pallas kernels, scatter_gradients(): pl.pallas_call(functools.partial(gradients_kernel, zh_size), out_shape=[b...  87.7 us
    pallas_call x2, Pallas kernels, recur_backward(): pl.pallas_call(backward_kernel, out_shape=[jax.ShapeDtypeStruct(act.shape...  84.3 us
    pallas_call x4, Pallas kernels, tp_sum(): pl.pallas_call(tp_sum_kernel, out_shape=[jax.ShapeDtypeStruct(partial.sha...  73.7 us
  transfers between devices with their start and end apart: 17, of which 4 were waited for; matrix products, arithmetic and copies ran while one was open for 13% of the time, Pallas kernels for 26%

profile of v2, /device:TPU:0, one launch (start us, length us, event | category | flops | bytes accessed | tf_op | source)
XLA Modules:
  0.0 1027.9 jit_solution(16655339858473613125)
XLA Ops:
  3.5 2.9 collective-permute-start.6
  6.4 2.6 collective-permute-start.7
  22.3 91.7 %gather_weights.1 = (bf16[32,64,1024]{2,1,0:T(8,128)(2,1)}, bf16[8,64,1024]{2,1,0:T(8,128)(2,1)}, f32[4,16,128]{2,1,0:T(8,128)}, f32[32,8,128]{2,1,0:T(8,128)}) custom-call(bf16[8,64,1024]{2,1,0:T(8,128)(2,1)} %reshape.373.win, bf16[8,64,1024]{2,1,0:T(8,128)(2,1)} %reshape.374.late, f32[16,128]{1,0:T(8,128)} %concatenate.61.small, ...), custom_call_target="tpu_custom_call" | custom-call | flops 99000000512 | tf_op jit(solution)/shard_map/gather_weights/pallas_call | solution.py:163
  120.5 27.5 %tp_gather.4 = bf16[8,128,2048]{2,1,0:T(8,128)(2,1)} custom-call(bf16[128,2048]{1,0:T(8,128)(2,1)} %fusion.67.x_ref), custom_call_target="tpu_custom_call" | custom-call | flops 30799998976 | tf_op jit(solution)/shard_map/tp_gather/pallas_call | solution.py:254
  153.2 29.5 %tp_gather.6 = bf16[8,128,2048]{2,1,0:T(8,128)(2,1)} custom-call(bf16[128,2048]{1,0:T(8,128)(2,1)} %bitcast_convert_fusion.x_ref), custom_call_target="tpu_custom_call" | custom-call | flops 30799998976 | tf_op jit(solution)/shard_map/tp_gather/pallas_call | solution.py:254
  187.6 11.9 %fusion.8 = f32[128,8,1024]{2,1,0:T(8,128)} fusion(bf16[2048,1024,1]{1,0,2:T(8,128)(2,1)} %bitcast.492, bf16[8,128,2048]{2,1,0:T(8,128)(2,1)S(1)} %copy-done.41), kind=kOutput, calls=%fused_computation.9 | convolution fusion | flops 4294967296 | bytes 12582912 | tf_op jit(solution)/shard_map/dot_general | solution.py:693
  200.8 2.5 broadcast_in_dim.90
  203.3 2.3 constant_dynamic-update-slice_fusion.4
  208.1 6.7 copy.213
  216.2 2.9 fusion.126
  219.1 3.0 collective-permute-start.4
  233.1 35.4 %collective-permute-done.4 = bf16[2,256,1024]{2,1,0:T(8,128)(2,1)} collective-permute-done((bf16[2,256,1024]{2,1,0:T(8,128)(2,1)}, bf16[2,256,1024]{2,1,0:T(8,128)(2,1)}, u32[]{:S(2)}, u32[]{:S(2)}) %collective-permute-start.4) | collective-permute-done | bytes 1048608 | tf_op jit(solution)/shard_map/ppermute | solution.py:193
  269.1 2.3 bitcast_dynamic-update-slice_fusion.2
  271.4 2.3 bitcast_dynamic-update-slice_fusion.1
  279.8 18.8 %tp_sum.4 = (bf16[8,128,256]{2,1,0:T(8,128)(2,1)S(1)}, f32[8,8,128]{2,1,0:T(8,128)}) custom-call(f32[8,128,256]{2,1,0:T(8,128)S(1)} %fusion.90.p_ref, f32[8,128]{1,0:T(8,128)S(1)} %broadcast_18_own_ref.2.own_ref), custom_call_target="tpu_custom_call" | custom-call | flops 19800000512 | tf_op jit(solution)/shard_map/tp_sum/pallas_call | solution.py:374
  300.2 3.8 multiply_divide_fusion.3
  304.0 16.7 %recur_forward.2 = (f32[128,8,512]{2,1,0:T(8,128)}, f32[8,16,4,8,128]{4,3,2,1,0:T(8,128)}) custom-call(f32[128,8,512]{2,1,0:T(8,128)} %get-tuple-element.105.act_ref, f32[128,8,512]{2,1,0:T(8,128)} %get-tuple-element.170.step_ref, f32[1024,128]{1,0:T(8,128)} %maximum_maximum_fusion.1.kq_ref, bf16[128,4096]{1,0:T(8,128)(2,1)} %maximum_maximum_fusion.e_ref), custom_call_target="tpu_custom_call" | custom-call | flops 17600000000 | tf_op jit(solution)/shard_map/recur_forward/pallas_call | solution.py:564
  320.7 2.3 fusion.47
  323.1 4.0 fusion.45.p_ref
  327.1 29.4 %tp_scatter.4 = f32[128,2048]{1,0:T(8,128)S(1)} custom-call(bf16[8,128,2048]{2,1,0:T(8,128)(2,1)S(1)} %fusion.45.p_ref), custom_call_target="tpu_custom_call" | custom-call | flops 30799998976 | tf_op jit(solution)/shard_map/tp_scatter/pallas_call | solution.py:301
  358.7 28.3 %tp_gather.5 = bf16[8,128,2048]{2,1,0:T(8,128)(2,1)} custom-call(bf16[128,2048]{1,0:T(8,128)(2,1)} %multiply_convert_fusion.4.x_ref), custom_call_target="tpu_custom_call" | custom-call | flops 30799998976 | tf_op jit(solution)/shard_map/tp_gather/pallas_call | solution.py:254
  389.9 6.4 copy.217
  398.7 8.7 fusion.11
  409.5 2.3 copy-done.122
  411.8 11.5 %multiply_reduce_fusion = (f32[512]{0:T(512)}, f32[128,8,512]{2,1,0:T(8,128)}, bf16[128,8,512]{2,1,0:T(8,128)(2,1)S(1)}, f32[128,8,512]{2,1,0:T(8,128)}, f32[8,128,512]{2,0,1:T(8,128)}) fusion(f32[128,8,1024]{2,1,0:T(8,128)S(1)} %fusion.11, f32[128,8,512]{2,1,0:T(8,128)S(1)} %slice.422, f32[512]{0:T(512)S(1)} %bitcast.467, f32[512]{0:T(512)S(1)} %bitcast.469, ...), kind=kOutput, calls=%fused_computation.70 | convolution fusion | flops 2158493184 | bytes 17838080 | tf_op jit(solution)/shard_map/dot_general | solution.py:693
  423.8 19.0 %tp_sum.5 = (bf16[8,128,256]{2,1,0:T(8,128)(2,1)S(1)}, f32[8,8,128]{2,1,0:T(8,128)}) custom-call(f32[8,128,256]{2,1,0:T(8,128)S(1)} %fusion.88.p_ref, f32[8,128]{1,0:T(8,128)S(1)} %broadcast_18_own_ref.2.own_ref), custom_call_target="tpu_custom_call" | custom-call | flops 19800000512 | tf_op jit(solution)/shard_map/tp_sum/pallas_call | solution.py:374
  446.0 3.8 multiply_divide_fusion.2
  449.8 16.7 %recur_forward.3 = (f32[128,8,512]{2,1,0:T(8,128)}, f32[8,16,4,8,128]{4,3,2,1,0:T(8,128)}) custom-call(f32[128,8,512]{2,1,0:T(8,128)} %convert_element_type.231.act_ref, f32[128,8,512]{2,1,0:T(8,128)} %get-tuple-element.173.step_ref, f32[1024,128]{1,0:T(8,128)} %maximum_maximum_fusion.2.kq_ref, bf16[128,4096]{1,0:T(8,128)(2,1)} %maximum_maximum_fusion.e_ref), custom_call_target="tpu_custom_call" | custom-call | flops 17600000000 | tf_op jit(solution)/shard_map/recur_forward/pallas_call | solution.py:564
  466.4 4.3 fusion.34
  472.1 6.2 fusion.46.p_ref
  479.5 2.5 copy.238
  481.9 6.2 fusion.136.slope_ref
  488.1 42.4 %recur_backward.2 = (f32[128,8,512]{2,1,0:T(8,128)}, f32[128,8,512]{2,1,0:T(8,128)}, f32[1024,128]{1,0:T(8,128)}, bf16[2,128,2048]{2,1,0:T(8,128)(2,1)}) custom-call(f32[128,8,512]{2,1,0:T(8,128)} %convert_element_type.231.act_ref, f32[128,8,512]{2,1,0:T(8,128)} %get-tuple-element.173.step_ref, f32[1024,128]{1,0:T(8,128)} %maximum_maximum_fusion.2.kq_ref, ...), custom_call_target="tpu_custom_call" | custom-call | flops 44000002048 | tf_op jit(solution)/shard_map/recur_backward/pallas_call | solution.py:667
  530.5 3.3 fusion.123
  538.9 2.6 stack.123
  541.6 18.2 %tp_sum.6 = (bf16[8,128,256]{2,1,0:T(8,128)(2,1)S(1)}, f32[8,8,128]{2,1,0:T(8,128)}) custom-call(f32[8,128,256]{2,1,0:T(8,128)S(1)} %bitcast.399, f32[8,128]{1,0:T(8,128)S(1)} %broadcast_in_dim.100.own_ref), custom_call_target="tpu_custom_call" | custom-call | flops 19800000512 | tf_op jit(solution)/shard_map/tp_sum/pallas_call | solution.py:374
  559.9 2.2 fusion.32
  563.0 2.9 multiply_reduce_fusion.2
  566.1 2.4 copy.204
  568.6 7.6 fusion.120.p_ref
  576.2 28.5 %tp_scatter.5 = f32[128,2048]{1,0:T(8,128)S(1)} custom-call(bf16[8,128,2048]{2,1,0:T(8,128)(2,1)S(1)} %copy-done.8), custom_call_target="tpu_custom_call" | custom-call | flops 30799998976 | tf_op jit(solution)/shard_map/tp_scatter/pallas_call | solution.py:301
  604.8 28.7 %tp_scatter.6 = f32[128,2048]{1,0:T(8,128)S(1)} custom-call(bf16[8,128,2048]{2,1,0:T(8,128)(2,1)S(1)} %fusion.120.p_ref), custom_call_target="tpu_custom_call" | custom-call | flops 30799998976 | tf_op jit(solution)/shard_map/tp_scatter/pallas_call | solution.py:301
  634.8 2.6 fusion.124
  637.4 28.9 %tp_gather.7 = bf16[8,128,2048]{2,1,0:T(8,128)(2,1)} custom-call(bf16[128,2048]{1,0:T(8,128)(2,1)} %get-tuple-element.101.x_ref), custom_call_target="tpu_custom_call" | custom-call | flops 30799998976 | tf_op jit(solution)/shard_map/tp_gather/pallas_call | solution.py:254
  666.4 9.5 multiply_reduce_fusion.5
  675.8 3.7 fusion.137.slope_ref
  679.6 41.9 %recur_backward.3 = (f32[128,8,512]{2,1,0:T(8,128)}, f32[128,8,512]{2,1,0:T(8,128)}, f32[1024,128]{1,0:T(8,128)}, bf16[2,128,2048]{2,1,0:T(8,128)(2,1)}) custom-call(f32[128,8,512]{2,1,0:T(8,128)} %get-tuple-element.105.act_ref, f32[128,8,512]{2,1,0:T(8,128)} %get-tuple-element.170.step_ref, f32[1024,128]{1,0:T(8,128)} %maximum_maximum_fusion.1.kq_ref, ...), custom_call_target="tpu_custom_call" | custom-call | flops 44000002048 | tf_op jit(solution)/shard_map/recur_backward/pallas_call | solution.py:667
  721.5 3.0 fusion.122
  725.4 2.2 fusion.58
  728.5 2.1 pad_maximum_fusion.2
  732.2 17.7 %tp_sum.7 = (bf16[8,128,256]{2,1,0:T(8,128)(2,1)S(1)}, f32[8,8,128]{2,1,0:T(8,128)S(1)}) custom-call(f32[8,128,256]{2,1,0:T(8,128)S(1)} %bitcast.400, f32[8,128]{1,0:T(8,128)S(1)} %copy-done.5), custom_call_target="tpu_custom_call" | custom-call | flops 19800000512 | tf_op jit(solution)/shard_map/tp_sum/pallas_call | solution.py:374
  752.9 2.9 multiply_reduce_fusion.7
  757.9 7.4 fusion.118.p_ref
  765.4 2.5 copy.212
  771.4 4.9 convolution_bitcast_fusion
  780.7 28.7 %tp_scatter.7 = f32[128,2048]{1,0:T(8,128)S(1)} custom-call(bf16[8,128,2048]{2,1,0:T(8,128)(2,1)S(1)} %fusion.118.p_ref), custom_call_target="tpu_custom_call" | custom-call | flops 30799998976 | tf_op jit(solution)/shard_map/tp_scatter/pallas_call | solution.py:301
  813.6 2.8 collective-permute-start.15
  825.3 9.5 fusion.138.win
  838.0 2.2 collective-permute-start.12
  841.2 26.5 %collective-permute-done.12 = bf16[128,288]{0,1:T(8,128)(2,1)S(1)} collective-permute-done((bf16[128,288]{0,1:T(8,128)(2,1)S(1)}, bf16[128,288]{0,1:T(8,128)(2,1)S(1)}, u32[]{:S(2)}, u32[]{:S(2)}) %collective-permute-start.12) | collective-permute-done | bytes 73760 | tf_op jit(solution)/shard_map/ppermute | solution.py:193
  870.3 3.1 convert_add_fusion
  878.8 43.0 %collective-permute-done.10 = bf16[512,1024]{1,0:T(8,128)(2,1)S(1)} collective-permute-done((bf16[512,1024]{1,0:T(8,128)(2,1)S(1)}, bf16[512,1024]{1,0:T(8,128)(2,1)S(1)}, u32[]{:S(2)}, u32[]{:S(2)}) %collective-permute-start.10) | collective-permute-done | bytes 1048608 | tf_op jit(solution)/shard_map/ppermute | solution.py:193
  923.8 87.7 %scatter_gradients.1 = (bf16[8,64,1024]{2,1,0:T(8,128)(2,1)}, f32[32,128]{1,0:T(8,128)}, f32[8,128]{1,0:T(8,128)}, bf16[8,64,1024]{2,1,0:T(8,128)(2,1)}) custom-call(bf16[2,2,2,256,1024]{4,3,2,1,0:T(8,128)(2,1)} %fusion.138.win, f32[2,2,32,128]{3,2,1,0:T(8,128)} %bitcast.437, f32[2,2,8,128]{3,2,1,0:T(8,128)} %broadcast_in_dim.102.stats, ...), custom_call_target="tpu_custom_call" | custom-call | flops 99000000512 | tf_op jit(solution)/shard_map/scatter_gradients/pallas_call | solution.py:496
  1025.2 2.3 maximum_convert_fusion
  (474 shorter events, 135.3 us)
Async XLA Ops:
  3.5 215.6 %collective-permute-start.6 = (bf16[1,128,2336]{1,2,0:T(8,128)(2,1)}, bf16[1,128,2336]{1,2,0:T(8,128)(2,1)}, u32[]{:S(2)}, u32[]{:S(2)}) collective-permute-start(bf16[1,128,2336]{1,2,0:T(8,128)(2,1)} %get-tuple-element.120), channel_id=1, source_target_pairs={{0,16},{1,17},{2,18},{3,19},{4,20},{5,21},{6,22},{7,23},{8,24},{9,... | collective-permute-start | bytes 1794056 | tf_op jit(solution)/shard_map/ppermute | solution.py:193
  6.4 217.1 %collective-permute-start.7 = (bf16[1,128,2336]{1,2,0:T(8,128)(2,1)}, bf16[1,128,2336]{1,2,0:T(8,128)(2,1)}, u32[]{:S(2)}, u32[]{:S(2)}) collective-permute-start(bf16[1,128,2336]{1,2,0:T(8,128)(2,1)} %get-tuple-element.120), channel_id=1, source_target_pairs={{0,4},{1,5},{2,6},{3,7},{4,0},{5,1},{6,2},{7,3},{8,12},{9,13},{10,... | collective-permute-start | bytes 1794056 | tf_op jit(solution)/shard_map/ppermute | solution.py:193
  10.4 214.5 %collective-permute-start = (bf16[1,128,2336]{1,2,0:T(8,128)(2,1)}, bf16[1,128,2336]{1,2,0:T(8,128)(2,1)}, u32[]{:S(2)}, u32[]{:S(2)}) collective-permute-start(bf16[1,128,2336]{1,2,0:T(8,128)(2,1)} %get-tuple-element.122), channel_id=1, source_target_pairs={{0,16},{1,17},{2,18},{3,19},{4,20},{5,21},{6,22},{7,23},{8,24},{9,... | collective-permute-start | bytes 1794056 | tf_op jit(solution)/shard_map/ppermute | solution.py:193
  10.9 215.3 %collective-permute-start.1 = (bf16[1,128,2336]{1,2,0:T(8,128)(2,1)}, bf16[1,128,2336]{1,2,0:T(8,128)(2,1)}, u32[]{:S(2)}, u32[]{:S(2)}) collective-permute-start(bf16[1,128,2336]{1,2,0:T(8,128)(2,1)} %get-tuple-element.122), channel_id=1, source_target_pairs={{0,4},{1,5},{2,6},{3,7},{4,0},{5,1},{6,2},{7,3},{8,12},{9,13},{10,... | collective-permute-start | bytes 1794056 | tf_op jit(solution)/shard_map/ppermute | solution.py:193
  22.2 96.0 %copy-start.47 = (bf16[1,1,1,128,2336]{3,4,2,1,0:T(8,128)(2,1)S(1)}, bf16[1,1,1,128,2336]{3,4,2,1,0:T(8,128)(2,1)}, u32[]{:S(2)}) copy-start(bf16[1,1,1,128,2336]{3,4,2,1,0:T(8,128)(2,1)} %get-tuple-element.121) | copy-start | bytes 1794052
  22.2 96.3 %copy-start.48 = (bf16[1,1,1,128,2336]{3,4,2,1,0:T(8,128)(2,1)S(1)}, bf16[1,1,1,128,2336]{3,4,2,1,0:T(8,128)(2,1)}, u32[]{:S(2)}) copy-start(bf16[1,1,1,128,2336]{3,4,2,1,0:T(8,128)(2,1)} %get-tuple-element.123) | copy-start | bytes 1794052
  114.0 155.2 %collective-permute-start.3 = (bf16[2,256,1024]{2,1,0:T(8,128)(2,1)}, bf16[2,256,1024]{2,1,0:T(8,128)(2,1)}, u32[]{:S(2)}, u32[]{:S(2)}) collective-permute-start(bf16[2,256,1024]{2,1,0:T(8,128)(2,1)} %bitcast.37), channel_id=1, source_target_pairs={{0,16},{1,17},{2,18},{3,19},{4,20},{5,21},{6,22},{7,23},{8,24},{9,... | collective-permute-start | bytes 3145736 | tf_op jit(solution)/shard_map/ppermute | solution.py:193
  118.9 29.1 %copy-start.63 = (f32[2048]{0:T(1024)}, f32[2048]{0:T(1024)S(1)}, u32[]{:S(2)}) copy-start(f32[2048]{0:T(1024)S(1)} %mul.530) | copy-start | bytes 24580
  119.6 28.5 %copy-start.103 = (f32[128]{0:T(128)}, f32[128]{0:T(128)S(1)}, u32[]{:S(2)}) copy-start(f32[128]{0:T(128)S(1)} %get-tuple-element.159) | copy-start | bytes 1540
  120.5 27.5 %copy-start.71 = (f32[4,16,128]{2,1,0:T(8,128)S(1)}, f32[4,16,128]{2,1,0:T(8,128)}, u32[]{:S(2)}) copy-start(f32[4,16,128]{2,1,0:T(8,128)} %get-tuple-element.38) | copy-start | bytes 98308
  120.5 31.1 %copy-start.38 = (f32[1,128,2048]{2,1,0:T(8,128)S(1)}, f32[1,128,2048]{2,1,0:T(8,128)}, u32[]{:S(2)}) copy-start(f32[1,128,2048]{2,1,0:T(8,128)} %param.14) | copy-start | bytes 3145732
  148.7 67.4 %copy-start.75 = (f32[1,1,512]{2,1,0:T(1,128)}, f32[1,1,512]{2,1,0:T(1,128)S(1)}, u32[]{:S(2)}) copy-start(f32[1,1,512]{2,1,0:T(1,128)S(1)} %get-tuple-element.141) | copy-start | bytes 6148
  148.7 67.4 %copy-start.77 = (f32[1,1,512]{2,1,0:T(1,128)}, f32[1,1,512]{2,1,0:T(1,128)S(1)}, u32[]{:S(2)}) copy-start(f32[1,1,512]{2,1,0:T(1,128)S(1)} %get-tuple-element.142) | copy-start | bytes 6148
  148.7 67.4 %copy-start.79 = (f32[1,1,512]{2,1,0:T(1,128)}, f32[1,1,512]{2,1,0:T(1,128)S(1)}, u32[]{:S(2)}) copy-start(f32[1,1,512]{2,1,0:T(1,128)S(1)} %get-tuple-element.143) | copy-start | bytes 6148
  148.8 67.4 %copy-start.81 = (f32[1,1,512]{2,1,0:T(1,128)}, f32[1,1,512]{2,1,0:T(1,128)S(1)}, u32[]{:S(2)}) copy-start(f32[1,1,512]{2,1,0:T(1,128)S(1)} %get-tuple-element.144) | copy-start | bytes 6148
  148.8 239.7 %copy-start.72 = (f32[1,1,512]{2,1,0:T(1,128)}, f32[1,1,512]{2,1,0:T(1,128)S(1)}, u32[]{:S(2)}) copy-start(f32[1,1,512]{2,1,0:T(1,128)S(1)} %get-tuple-element.140) | copy-start | bytes 6148
  151.1 31.6 %copy-start.102 = (f32[2,2,2,4]{3,2,1,0:T(2,128)}, f32[2,2,2,4]{3,2,1,0:T(2,128)S(1)}, u32[]{:S(2)}) copy-start(f32[2,2,2,4]{3,2,1,0:T(2,128)S(1)} %div.125) | copy-start | bytes 388
  208.1 149.2 %copy-start.65 = (f32[2048]{0:T(1024)}, f32[2048]{0:T(1024)S(1)}, u32[]{:S(2)}) copy-start(f32[2048]{0:T(1024)S(1)} %mul.556) | copy-start | bytes 24580
  219.1 101.6 %copy-start.22 = (bf16[128,8,512]{2,1,0:T(8,128)(2,1)}, bf16[128,8,512]{2,1,0:T(8,128)(2,1)S(1)}, u32[]{:S(2)}) copy-start(bf16[128,8,512]{2,1,0:T(8,128)(2,1)S(1)} %get-tuple-element.106) | copy-start | bytes 3145732
  219.1 49.4 %collective-permute-start.4 = (bf16[2,256,1024]{2,1,0:T(8,128)(2,1)}, bf16[2,256,1024]{2,1,0:T(8,128)(2,1)}, u32[]{:S(2)}, u32[]{:S(2)}) collective-permute-start(bf16[2,256,1024]{2,1,0:T(8,128)(2,1)} %bitcast.37), channel_id=1, source_target_pairs={{0,4},{1,5},{2,6},{3,7},{4,0},{5,1},{6,2},{7,3},{8,12},{9,13},{10,... | collective-permute-start | bytes 3145736 | tf_op jit(solution)/shard_map/ppermute | solution.py:193
  228.5 45.2 %collective-permute-start.2 = (bf16[1,128,2336]{1,2,0:T(8,128)(2,1)}, bf16[1,128,2336]{1,2,0:T(8,128)(2,1)S(1)}, u32[]{:S(2)}, u32[]{:S(2)}) collective-permute-start(bf16[1,128,2336]{1,2,0:T(8,128)(2,1)} %collective-permute-done.1), channel_id=1, source_target_pairs={{0,16},{1,17},{2,18},{3,19},{4,20},{5,21},{6,22},{7,23},{8,24},{9,... | collective-permute-start | bytes 1794056 | tf_op jit(solution)/shard_map/ppermute | solution.py:193
  229.1 46.8 %collective-permute-start.8 = (bf16[1,128,2336]{1,2,0:T(8,128)(2,1)}, bf16[1,128,2336]{1,2,0:T(8,128)(2,1)}, u32[]{:S(2)}, u32[]{:S(2)}) collective-permute-start(bf16[1,128,2336]{1,2,0:T(8,128)(2,1)} %collective-permute-done.7), channel_id=1, source_target_pairs={{0,16},{1,17},{2,18},{3,19},{4,20},{5,21},{6,22},{7,23},{8,24},{9,... | collective-permute-start | bytes 1794056 | tf_op jit(solution)/shard_map/ppermute | solution.py:193
  268.5 129.1 %collective-permute-start.5 = (bf16[2,256,1024]{2,1,0:T(8,128)(2,1)}, bf16[2,256,1024]{2,1,0:T(8,128)(2,1)S(1)}, u32[]{:S(2)}, u32[]{:S(2)}) collective-permute-start(bf16[2,256,1024]{2,1,0:T(8,128)(2,1)} %collective-permute-done.4), channel_id=1, source_target_pairs={{0,16},{1,17},{2,18},{3,19},{4,20},{5,21},{6,22},{7,23},{8,24},{9,... | collective-permute-start | bytes 3145736 | tf_op jit(solution)/shard_map/ppermute | solution.py:193
  279.8 19.3 %copy-start.108 = (f32[128]{0:T(128)S(1)}, f32[128]{0:T(128)}, u32[]{:S(2)}) copy-start(f32[128]{0:T(128)} %pad.158.clone) | copy-start | bytes 1540
  304.0 16.7 %copy-start.24 = (f32[128,8,1024]{2,1,0:T(8,128)S(1)}, f32[128,8,1024]{2,1,0:T(8,128)}, u32[]{:S(2)}) copy-start(f32[128,8,1024]{2,1,0:T(8,128)} %fusion.8) | copy-start | bytes 12582916
  304.0 16.7 %copy-start.83 = (f32[1,1,512]{2,1,0:T(1,128)S(1)}, f32[1,1,512]{2,1,0:T(1,128)}, u32[]{:S(2)}) copy-start(f32[1,1,512]{2,1,0:T(1,128)} %get-tuple-element.139) | copy-start | bytes 6148
  327.0 29.5 %copy-start.10 = (f32[1,128,2048]{2,1,0:T(8,128)S(1)}, f32[1,128,2048]{2,1,0:T(8,128)}, u32[]{:S(2)}) copy-start(f32[1,128,2048]{2,1,0:T(8,128)} %param.13) | copy-start | bytes 3145732
  357.3 29.7 %copy-start.106 = (f32[128]{0:T(128)}, f32[128]{0:T(128)S(1)}, u32[]{:S(2)}) copy-start(f32[128]{0:T(128)S(1)} %get-tuple-element.161) | copy-start | bytes 1540
  407.7 15.7 %copy-start.31 = (f32[128,8,512]{2,1,0:T(8,128)}, f32[128,8,512]{2,1,0:T(8,128)S(1)}, u32[]{:S(2)}) copy-start(f32[128,8,512]{2,1,0:T(8,128)S(1)} %slice.422) | copy-start | bytes 6291460
  423.3 43.1 %copy-start.17 = (bf16[128,8,512]{2,1,0:T(8,128)(2,1)}, bf16[128,8,512]{2,1,0:T(8,128)(2,1)S(1)}, u32[]{:S(2)}) copy-start(bf16[128,8,512]{2,1,0:T(8,128)(2,1)S(1)} %get-tuple-element.97) | copy-start | bytes 3145732
  449.8 16.7 %copy-start.20 = (f32[128,8,1024]{2,1,0:T(8,128)S(1)}, f32[128,8,1024]{2,1,0:T(8,128)}, u32[]{:S(2)}) copy-start(f32[128,8,1024]{2,1,0:T(8,128)} %copy-done.19) | copy-start | bytes 12582916
  449.8 16.7 %copy-start.85 = (f32[1,1,512]{2,1,0:T(1,128)S(1)}, f32[1,1,512]{2,1,0:T(1,128)}, u32[]{:S(2)}) copy-start(f32[1,1,512]{2,1,0:T(1,128)} %get-tuple-element.132) | copy-start | bytes 6148
  541.6 18.3 %copy-start.4 = (f32[8,128]{1,0:T(8,128)}, f32[8,128]{1,0:T(8,128)S(1)}, u32[]{:S(2)}) copy-start(f32[8,128]{1,0:T(8,128)S(1)} %broadcast_in_dim.100.own_ref) | copy-start | bytes 12292
  541.6 18.3 %copy-start.124 = (f32[128,8,512]{2,1,0:T(8,128)S(1)}, f32[128,8,512]{2,1,0:T(8,128)}, u32[]{:S(2)}) copy-start(f32[128,8,512]{2,1,0:T(8,128)} %get-tuple-element.96.gsum_ref) | copy-start | bytes 6291460
  541.6 18.3 %copy-start.125 = (f32[128,8,512]{2,1,0:T(8,128)S(1)}, f32[128,8,512]{2,1,0:T(8,128)}, u32[]{:S(2)}) copy-start(f32[128,8,512]{2,1,0:T(8,128)} %get-tuple-element.98) | copy-start | bytes 6291460
  541.6 18.3 %copy-start.126 = (f32[128,8,512]{2,1,0:T(8,128)S(1)}, f32[128,8,512]{2,1,0:T(8,128)}, u32[]{:S(2)}) copy-start(f32[128,8,512]{2,1,0:T(8,128)} %get-tuple-element.47) | copy-start | bytes 6291460
  604.8 28.7 %copy-start.15 = (f32[128,2048]{1,0:T(8,128)S(1)}, f32[128,2048]{1,0:T(8,128)}, u32[]{:S(2)}) copy-start(f32[128,2048]{1,0:T(8,128)} %copy-done.14) | copy-start | bytes 3145732
  604.8 28.7 %copy-start.66 = (f32[2048]{0:T(1024)S(1)}, f32[2048]{0:T(1024)}, u32[]{:S(2)}) copy-start(f32[2048]{0:T(1024)} %copy-done.65) | copy-start | bytes 24580
  604.8 28.7 %copy-start.107 = (f32[128]{0:T(128)S(1)}, f32[128]{0:T(128)}, u32[]{:S(2)}) copy-start(f32[128]{0:T(128)} %copy-done.106) | copy-start | bytes 1540
  637.4 29.0 %copy-start.23 = (bf16[128,8,512]{2,1,0:T(8,128)(2,1)S(1)}, bf16[128,8,512]{2,1,0:T(8,128)(2,1)}, u32[]{:S(2)}) copy-start(bf16[128,8,512]{2,1,0:T(8,128)(2,1)} %copy-done.22) | copy-start | bytes 3145732
  637.4 29.0 %copy-start.52 = (f32[128,8,512]{2,1,0:T(8,128)S(1)}, f32[128,8,512]{2,1,0:T(8,128)}, u32[]{:S(2)}) copy-start(f32[128,8,512]{2,1,0:T(8,128)} %get-tuple-element.42) | copy-start | bytes 6291460
  637.4 29.0 %copy-start.84 = (f32[1,1,512]{2,1,0:T(1,128)S(1)}, f32[1,1,512]{2,1,0:T(1,128)}, u32[]{:S(2)}) copy-start(f32[1,1,512]{2,1,0:T(1,128)} %get-tuple-element.139) | copy-start | bytes 6148
  666.3 9.5 copy-start.56
  666.3 9.5 copy-start.123
  679.6 41.9 %copy-start.27 = (f32[1024,512]{1,0:T(8,128)S(1)}, f32[1024,512]{1,0:T(8,128)}, u32[]{:S(2)}) copy-start(f32[1024,512]{1,0:T(8,128)} %get-tuple-element.171) | copy-start | bytes 6291460
  679.6 41.9 %copy-start.61 = (f32[128,8]{1,0:T(8,128)S(1)}, f32[128,8]{1,0:T(8,128)}, u32[]{:S(2)}) copy-start(f32[128,8]{1,0:T(8,128)} %copy-done.60) | copy-start | bytes 12292
  679.6 41.9 %copy-start.73 = (f32[1,1,512]{2,1,0:T(1,128)S(1)}, f32[1,1,512]{2,1,0:T(1,128)}, u32[]{:S(2)}) copy-start(f32[1,1,512]{2,1,0:T(1,128)} %copy-done.72) | copy-start | bytes 6148
  732.2 17.7 %copy-start.49 = (f32[128,8,512]{2,1,0:T(8,128)S(1)}, f32[128,8,512]{2,1,0:T(8,128)}, u32[]{:S(2)}) copy-start(f32[128,8,512]{2,1,0:T(8,128)} %get-tuple-element.107) | copy-start | bytes 6291460
  732.2 17.7 %copy-start.127 = (f32[128,8,512]{2,1,0:T(8,128)S(1)}, f32[128,8,512]{2,1,0:T(8,128)}, u32[]{:S(2)}) copy-start(f32[128,8,512]{2,1,0:T(8,128)} %get-tuple-element.92.gsum_ref) | copy-start | bytes 6291460
  732.2 17.7 %copy-start.128 = (f32[128,8,512]{2,1,0:T(8,128)S(1)}, f32[128,8,512]{2,1,0:T(8,128)}, u32[]{:S(2)}) copy-start(f32[128,8,512]{2,1,0:T(8,128)} %get-tuple-element.52) | copy-start | bytes 6291460
  779.4 30.1 %copy-start.11 = (f32[1,128,2048]{2,1,0:T(8,128)S(1)}, f32[1,128,2048]{2,1,0:T(8,128)}, u32[]{:S(2)}) copy-start(f32[1,128,2048]{2,1,0:T(8,128)} %param.13) | copy-start | bytes 3145732
  779.4 30.1 %copy-start.64 = (f32[2048]{0:T(1024)S(1)}, f32[2048]{0:T(1024)}, u32[]{:S(2)}) copy-start(f32[2048]{0:T(1024)} %copy-done.63) | copy-start | bytes 24580
  779.4 30.1 %copy-start.104 = (f32[128]{0:T(128)S(1)}, f32[128]{0:T(128)}, u32[]{:S(2)}) copy-start(f32[128]{0:T(128)} %copy-done.103) | copy-start | bytes 1540
  779.4 90.9 %collective-permute-start.9 = (bf16[2,512,1024]{2,1,0:T(8,128)(2,1)}, bf16[2,512,1024]{2,1,0:T(8,128)(2,1)}, u32[]{:S(2)}, u32[]{:S(2)}) collective-permute-start(bf16[2,512,1024]{2,1,0:T(8,128)(2,1)} %dynamic-slice_bitcast_fusion), channel_id=1, source_target_pairs={{0,16},{1,17},{2,18},{3,19},{4,20},{5,21},{6,22},{7,23},{8,24},{9,... | collective-permute-start | bytes 6291464 | tf_op jit(solution)/shard_map/ppermute | solution.py:193
  813.6 60.1 %collective-permute-start.15 = (bf16[128,2048]{1,0:T(8,128)(2,1)S(1)}, bf16[128,2048]{1,0:T(8,128)(2,1)}, u32[]{:S(2)}, u32[]{:S(2)}) collective-permute-start(bf16[128,2048]{1,0:T(8,128)(2,1)S(1)} %fusion.74), channel_id=1, source_target_pairs={{0,4},{1,5},{2,6},{3,7},{4,0},{5,1},{6,2},{7,3},{8,12},{9,13},{10,... | collective-permute-start | bytes 1572872 | tf_op jit(solution)/shard_map/ppermute | solution.py:193
  818.2 58.0 %collective-permute-start.16 = (bf16[128,2048]{1,0:T(8,128)(2,1)}, bf16[128,2048]{1,0:T(8,128)(2,1)}, u32[]{:S(2)}, u32[]{:S(2)}) collective-permute-start(bf16[128,2048]{1,0:T(8,128)(2,1)} %fusion.75), channel_id=1, source_target_pairs={{0,4},{1,5},{2,6},{3,7},{4,0},{5,1},{6,2},{7,3},{8,12},{9,13},{10,... | collective-permute-start | bytes 1572872 | tf_op jit(solution)/shard_map/ppermute | solution.py:193
  819.9 17.1 %collective-permute-start.11 = (bf16[2,128,288]{1,2,0:T(8,128)(2,1)}, bf16[2,128,288]{1,2,0:T(8,128)(2,1)}, u32[]{:S(2)}, u32[]{:S(2)}) collective-permute-start(bf16[2,128,288]{1,2,0:T(8,128)(2,1)} %bitcast.397), channel_id=1, source_target_pairs={{0,16},{1,17},{2,18},{3,19},{4,20},{5,21},{6,22},{7,23},{8,24},{9,... | collective-permute-start | bytes 442376 | tf_op jit(solution)/shard_map/ppermute | solution.py:193
  821.9 18.4 %collective-permute-start.13 = (bf16[2,128,288]{1,2,0:T(8,128)(2,1)S(1)}, bf16[2,128,288]{1,2,0:T(8,128)(2,1)S(1)}, u32[]{:S(2)}, u32[]{:S(2)}) collective-permute-start(bf16[2,128,288]{1,2,0:T(8,128)(2,1)S(1)} %bitcast.436), channel_id=1, source_target_pairs={{0,16},{1,17},{2,18},{3,19},{4,20},{5,21},{6,22},{7,23},{8,24},{9,... | collective-permute-start | bytes 442376 | tf_op jit(solution)/shard_map/ppermute | solution.py:193
  825.3 9.5 copy-start.37
  825.3 9.5 copy-start.105
  825.3 9.5 copy-start.118
  838.0 29.6 %collective-permute-start.12 = (bf16[128,288]{0,1:T(8,128)(2,1)S(1)}, bf16[128,288]{0,1:T(8,128)(2,1)S(1)}, u32[]{:S(2)}, u32[]{:S(2)}) collective-permute-start(bf16[128,288]{0,1:T(8,128)(2,1)S(1)} %fusion.108), channel_id=1, source_target_pairs={{0,4},{1,5},{2,6},{3,7},{4,0},{5,1},{6,2},{7,3},{8,12},{9,13},{10,... | collective-permute-start | bytes 221192 | tf_op jit(solution)/shard_map/ppermute | solution.py:193
  840.4 28.5 %collective-permute-start.14 = (bf16[128,288]{0,1:T(8,128)(2,1)S(1)}, bf16[128,288]{0,1:T(8,128)(2,1)S(1)}, u32[]{:S(2)}, u32[]{:S(2)}) collective-permute-start(bf16[128,288]{0,1:T(8,128)(2,1)S(1)} %fusion.109), channel_id=1, source_target_pairs={{0,4},{1,5},{2,6},{3,7},{4,0},{5,1},{6,2},{7,3},{8,12},{9,13},{10,... | collective-permute-start | bytes 221192 | tf_op jit(solution)/shard_map/ppermute | solution.py:193
  873.6 48.2 %collective-permute-start.10 = (bf16[512,1024]{1,0:T(8,128)(2,1)S(1)}, bf16[512,1024]{1,0:T(8,128)(2,1)S(1)}, u32[]{:S(2)}, u32[]{:S(2)}) collective-permute-start(bf16[512,1024]{1,0:T(8,128)(2,1)S(1)} %fusion.49), channel_id=1, source_target_pairs={{0,4},{1,5},{2,6},{3,7},{4,0},{5,1},{6,2},{7,3},{8,12},{9,13},{10,... | collective-permute-start | bytes 3145736 | tf_op jit(solution)/shard_map/ppermute | solution.py:193
  (82 other events, 250.3 us)

commit v3 on v2

v3 whole, which is shorter than its diff:
```python
import functools

import jax
import jax.numpy as jnp
from jax import lax
from jax.sharding import PartitionSpec as P
import jax.experimental.pallas as pl
import jax.experimental.pallas.tpu as pltpu

INNER = 4096
STATE = 16
RANK = 128
CONV = 4
LAYERS = 2
WAYS = 4
TP = 8
STEPS = 16

eps = 1e-05
MESH = pl.DeviceIdType.MESH
f32 = jnp.float32
bf16 = jnp.bfloat16
VM = pl.BlockSpec(memory_space=pltpu.VMEM)
HB = pl.BlockSpec(memory_space=pl.ANY)


def place():
    dp, fs = lax.axis_index("dp"), lax.axis_index("fsdp")
    return dp // 2, lax.rem(dp, 2), fs // WAYS, lax.rem(fs, WAYS)


def device(x, core, zh, q):
    return (x * 2 + core, zh * WAYS + q)


def remote(src, dst, send, recv, target):
    return pltpu.make_async_remote_copy(
        src_ref=src, dst_ref=dst, send_sem=send, recv_sem=recv, device_id=target, device_id_type=MESH
    )


def cost(us):
    return pl.CostEstimate(flops=int(us * 1.1e9), bytes_accessed=0, transcendentals=0)


def greet(targets):
    barrier = pltpu.get_barrier_semaphore()
    for target in targets:
        pl.semaphore_signal(barrier, inc=1, device_id=target, device_id_type=MESH)
    pl.semaphore_wait(barrier, len(targets))


def tp_peers():
    x, core, zh, q = place()
    peers = []
    for dc in (0, 1):
        for dq in (1, 3, 2, 0):
            if dc == 0 and dq == 0:
                continue
            other_core = lax.rem(core + dc, 2)
            to_q, from_q = lax.rem(q + dq, WAYS), lax.rem(q + WAYS - dq, WAYS)
            peers.append(
                (device(x, other_core, zh, to_q), other_core * WAYS + to_q, other_core * WAYS + from_q)
            )
    return peers


def dp_peers(zh_size):
    x, core, zh, q = place()
    side = device(1 - x, core, zh, q)
    far = []
    for dz in range(1, zh_size):
        to_z, from_z = lax.rem(zh + dz, zh_size), lax.rem(zh + zh_size - dz, zh_size)
        far.append((device(x, core, to_z, q), to_z, from_z))
    return side, far


def weights_kernel(
    zh_size, win, late, small, misc, mats, o_win, o_late, o_small, o_misc, o_mats,
    tp_send, tp_recv, z_send, z_recv, x_send, x_recv, own_sem,
):
    x, core, zh, q = place()
    me = core * WAYS + q
    peers = tp_peers()
    side, far = dp_peers(zh_size)
    greet([p[0] for p in peers] + [side] + [f[0] for f in far])

    def row(xx, zz, rank):
        return ((xx * 2 + rank // WAYS) * zh_size + zz) * WAYS + lax.rem(rank, WAYS)

    waits = []
    own = []
    for i, (src, dst) in enumerate(
        (
            (win.at[me], o_win.at[row(x, zh, me)]),
            (misc, o_misc.at[row(x, zh, me)]),
            (small, o_small.at[x * zh_size + zh]),
            (late.at[me], o_late.at[me]),
            (mats, o_mats.at[x * zh_size + zh]),
        )
    ):
        copy = pltpu.make_async_copy(src, dst, own_sem.at[i])
        copy.start()
        own.append(copy)
    arrive = []
    last = []
    for i, (target, rank, source) in enumerate(peers):
        for j, (src, dst) in enumerate(
            ((win.at[rank], o_win.at[row(x, zh, me)]), (misc, o_misc.at[row(x, zh, me)]))
        ):
            copy = remote(src, dst, tp_send.at[i, j], tp_recv.at[i, j], target)
            copy.start()
            arrive.append((copy, source, j))
            waits.append(copy)

    onward = []

    def spread(item, src, view):
        for k, (target, to_z, from_z) in enumerate(far):
            copy = remote(src, view(x, zh), z_send.at[item, k], z_recv.at[item, k], target)
            copy.start()
            waits.append(copy)
            onward.append((copy, item, k, view, from_z))
        copy = remote(src, view(x, zh), x_send.at[item, 0], x_recv.at[item, 0], side)
        copy.start()
        waits.append(copy)

    spread(0, win.at[me], lambda xx, zz: o_win.at[row(xx, zz, me)])
    spread(1, misc, lambda xx, zz: o_misc.at[row(xx, zz, me)])
    spread(2, small, lambda xx, zz: o_small.at[xx * zh_size + zz])
    spread(3, mats, lambda xx, zz: o_mats.at[xx * zh_size + zz])
    recv_done = set()
    item = 4
    for copy, source, j in arrive:
        copy.wait_recv()
        recv_done.add(id(copy))
        out = (o_win, o_misc)[j]
        view = functools.partial(lambda out, source, xx, zz: out.at[row(xx, zz, source)], out, source)
        spread(item, view(x, zh), view)
        item += 1
    for i, (target, rank, source) in enumerate(peers):
        copy = remote(late.at[rank], o_late.at[me], tp_send.at[i, 2], tp_recv.at[i, 2], target)
        copy.start()
        waits.append(copy)
    for copy, it, k, view, from_z in onward:
        copy.wait_recv()
        recv_done.add(id(copy))
        again = remote(view(x, from_z), view(x, from_z), x_send.at[it, k + 1], x_recv.at[it, k + 1], side)
        again.start()
        waits.append(again)
    for copy in waits:
        copy.wait_send()
        if id(copy) not in recv_done:
            copy.wait_recv()
    for copy in own:
        copy.wait()


def gather_weights(zh_size, win, late, small, misc, mats):
    groups = 2 * zh_size
    count = groups * TP
    items = 4 + 2 * (TP - 1)
    dma = pltpu.SemaphoreType.DMA
    many = lambda a, n: jax.ShapeDtypeStruct((n,) + a.shape, a.dtype)
    return pl.pallas_call(
        functools.partial(weights_kernel, zh_size),
        out_shape=[
            jax.ShapeDtypeStruct((count,) + win.shape[1:], win.dtype),
            jax.ShapeDtypeStruct(late.shape, late.dtype),
            many(small, groups), many(misc, count), many(mats, groups),
        ],
        in_specs=[HB] * 5,
        out_specs=[HB] * 5,
        scratch_shapes=[
            dma((TP - 1, 3)), dma((TP - 1, 3)),
            dma((items, max(1, zh_size - 1))), dma((items, max(1, zh_size - 1))),
            dma((items, zh_size)), dma((items, zh_size)), dma((5,)),
        ],
        compiler_params=pltpu.CompilerParams(collective_id=1, has_side_effects=True),
        name="gather_weights",
        cost_estimate=cost(90),
    )(win, late, small, misc, mats)


def tp_gather_kernel(x_ref, o_ref, f_send, f_recv, s_send, s_recv, own_sem):
    x, core, zh, q = place()
    sibling = device(x, 1 - core, zh, q)
    far = []
    for dq in (1, 3, 2):
        far.append((device(x, core, zh, lax.rem(q + dq, WAYS)), lax.rem(q + WAYS - dq, WAYS)))
    greet([t for t, _ in far] + [sibling])
    me = core * WAYS + q
    first = []
    for i, (target, _) in enumerate(far):
        copy = remote(x_ref, o_ref.at[me], f_send.at[i], f_recv.at[i], target)
        copy.start()
        first.append(copy)
    near = [remote(x_ref, o_ref.at[me], s_send.at[3], s_recv.at[3], sibling)]
    near[0].start()
    own = pltpu.make_async_copy(x_ref, o_ref.at[me], own_sem)
    own.start()
    for i, (_, source) in enumerate(far):
        first[i].wait_recv()
        slot = core * WAYS + source
        copy = remote(o_ref.at[slot], o_ref.at[slot], s_send.at[i], s_recv.at[i], sibling)
        copy.start()
        near.append(copy)
    for copy in first:
        copy.wait_send()
    for copy in near:
        copy.wait()
    own.wait()


def tp_gather(rows):
    dma = pltpu.SemaphoreType.DMA
    return pl.pallas_call(
        tp_gather_kernel,
        out_shape=jax.ShapeDtypeStruct((TP,) + rows.shape, rows.dtype),
        in_specs=[HB],
        out_specs=HB,
        scratch_shapes=[dma((3,)), dma((3,)), dma((4,)), dma((4,)), dma],
        compiler_params=pltpu.CompilerParams(collective_id=2, has_side_effects=True),
        name="tp_gather",
        cost_estimate=cost(28),
    )(rows)


def lanes_of(shape):
    return lax.broadcasted_iota(jnp.int32, shape, 1)


def encode(v):
    tail = v[:, RANK:]
    lane = lanes_of(tail.shape)
    high = tail.astype(bf16).astype(f32)
    low = pltpu.roll(tail - high, 32, 1)
    both = jnp.where(lane < 32, high, jnp.where(lane < 64, low, 0.0))
    return jnp.concatenate([v[:, :RANK].astype(bf16), both.astype(bf16)], axis=1)


def decode(v):
    tail = v[:, RANK:].astype(f32)
    lane = lanes_of(tail.shape)
    tail = jnp.where(lane < 32, tail + pltpu.roll(tail, 96, 1), 0.0)
    return jnp.concatenate([v[:, :RANK].astype(f32), tail], axis=1)


class Gather:
    sems = staticmethod(lambda dma: [dma((3,)), dma((3,)), dma((4,)), dma((4,)), dma])

    def __init__(self, src, out, sems):
        self.src, self.out = src, out
        self.f_send, self.f_recv, self.s_send, self.s_recv, self.own_sem = sems
        x, core, zh, q = place()
        self.core, self.me = core, core * WAYS + q
        self.sibling = device(x, 1 - core, zh, q)
        self.far = [
            (device(x, core, zh, lax.rem(q + dq, WAYS)), lax.rem(q + WAYS - dq, WAYS)) for dq in (1, 3, 2)
        ]

    def start(self):
        dst = self.out.at[self.me]
        self.first = [
            remote(self.src, dst, self.f_send.at[i], self.f_recv.at[i], target)
            for i, (target, _) in enumerate(self.far)
        ]
        self.near = [remote(self.src, dst, self.s_send.at[3], self.s_recv.at[3], self.sibling)]
        for copy in self.first + self.near:
            copy.start()
        self.own = pltpu.make_async_copy(self.src, dst, self.own_sem)
        self.own.start()

    def onward(self):
        for i, (_, source) in enumerate(self.far):
            self.first[i].wait_recv()
            slot = self.out.at[self.core * WAYS + source]
            copy = remote(slot, slot, self.s_send.at[i], self.s_recv.at[i], self.sibling)
            copy.start()
            self.near.append(copy)

    def finish(self):
        for copy in self.first:
            copy.wait_send()
        for copy in self.near:
            copy.wait()
        self.own.wait()


class Scatter:
    sems = staticmethod(lambda dma: [dma((4,)), dma((4,)), dma((3,)), dma((3,))])

    @staticmethod
    def buffers(block):
        return [pltpu.VMEM((4,) + block, bf16), pltpu.VMEM((3,) + block, bf16), pltpu.VMEM((3,) + block, bf16)]

    def __init__(self, partial, buffers, sems):
        self.partial = partial
        self.near_buf, self.far_out, self.far_in = buffers
        self.s_send, self.s_recv, self.f_send, self.f_recv = sems
        x, core, zh, q = place()
        self.core = core
        self.sibling = device(x, 1 - core, zh, q)
        self.turns = [lax.rem(q + dq, WAYS) for dq in (1, 3, 2, 0)]
        self.targets = [device(x, core, zh, t) for t in self.turns[:3]]
        self.near, self.first = [None] * 4, [None] * 3

    def to_sibling(self, i):
        slot = (1 - self.core) * WAYS + self.turns[i]
        self.near[i] = remote(
            self.partial.at[slot], self.near_buf.at[i], self.s_send.at[i], self.s_recv.at[i], self.sibling
        )
        self.near[i].start()

    def joined(self, i):
        self.near[i].wait_recv()
        return self.partial[self.core * WAYS + self.turns[i]].astype(f32) + self.near_buf[i].astype(f32)

    def across(self, i):
        self.far_out[i] = self.joined(i).astype(bf16)
        self.first[i] = remote(
            self.far_out.at[i], self.far_in.at[i], self.f_send.at[i], self.f_recv.at[i], self.targets[i]
        )
        self.first[i].start()

    def total(self):
        value = self.joined(3)
        for i in range(3):
            self.first[i].wait_recv()
            value = value + self.far_in[i].astype(f32)
        for copy in self.near + self.first:
            copy.wait_send()
        return value


class Spread:
    @staticmethod
    def sems(dma, zh_size):
        far = max(1, zh_size - 1)
        return [dma((far,)), dma((far,)), dma((zh_size,)), dma((zh_size,)), dma]

    def __init__(self, zh_size, src, view, sems):
        self.src, self.view = src, view
        self.z_send, self.z_recv, self.x_send, self.x_recv, self.own_sem = sems
        self.x, _, self.zh, _ = place()
        self.side, self.far = dp_peers(zh_size)

    def start(self):
        dst = self.view(self.x, self.zh)
        self.along = [
            remote(self.src, dst, self.z_send.at[k], self.z_recv.at[k], target)
            for k, (target, _, _) in enumerate(self.far)
        ]
        self.over = [remote(self.src, dst, self.x_send.at[0], self.x_recv.at[0], self.side)]
        for copy in self.along + self.over:
            copy.start()
        self.own = pltpu.make_async_copy(self.src, dst, self.own_sem)
        self.own.start()

    def onward(self):
        for k, (_, _, source) in enumerate(self.far):
            self.along[k].wait_recv()
            slot = self.view(self.x, source)
            copy = remote(slot, slot, self.x_send.at[k + 1], self.x_recv.at[k + 1], self.side)
            copy.start()
            self.over.append(copy)

    def finish(self):
        for copy in self.along:
            copy.wait_send()
        for copy in self.over:
            copy.wait()
        self.own.wait()


class Sum:
    sems = staticmethod(lambda dma: [dma((TP - 1,))] * 4)

    def __init__(self, payload, parts, out, sems):
        self.payload, self.parts, self.out = payload, parts, out
        self.a_send, self.a_recv, self.b_send, self.b_recv = sems
        x, core, zh, q = place()
        self.me = core * WAYS + q
        self.peers = tp_peers()

    def start(self):
        self.one = [
            remote(self.payload.at[rank], self.parts.at[i], self.a_send.at[i], self.a_recv.at[i], target)
            for i, (target, rank, _) in enumerate(self.peers)
        ]
        for copy in self.one:
            copy.start()

    def middle(self, own):
        total = own
        for i in range(TP - 1):
            self.one[i].wait_recv()
            total = total + decode(self.parts[i])
        self.out[self.me] = encode(total)
        self.two = [
            remote(self.out.at[self.me], self.out.at[self.me], self.b_send.at[i], self.b_recv.at[i], target)
            for i, (target, _, _) in enumerate(self.peers)
        ]
        for copy in self.two:
            copy.start()

    def finish(self):
        for copy in self.one:
            copy.wait_send()
        for copy in self.two:
            copy.wait()


def call(body, name, collective, ins, outs, scratch, **options):
    names = list(ins) + list(outs) + list(scratch)

    def kernel(*refs):
        named, refs = {}, list(refs)
        flat = []
        for key in names:
            kind = scratch.get(key)
            if isinstance(kind, list):
                named[key] = refs[: len(kind)]
                refs = refs[len(kind) :]
            else:
                named[key] = refs.pop(0)
        body(named)

    flat = []
    for kind in scratch.values():
        flat += kind if isinstance(kind, list) else [kind]
    values = pl.pallas_call(
        kernel,
        out_shape=[shape for shape, _ in outs.values()],
        in_specs=[spec for _, spec in ins.values()],
        out_specs=[spec for _, spec in outs.values()],
        scratch_shapes=flat,
        compiler_params=pltpu.CompilerParams(
            collective_id=collective, has_side_effects=True, vmem_limit_bytes=63 * 2**20
        ),
        name=name,
    )(*[array for array, _ in ins.values()])
    return dict(zip(outs, values))


def gradients_kernel(
    zh_size, win, near, mats, small, stats, gain, late, o_win, o_mats, o_small, o_stats, o_late,
    mats_x, small_x, stats_x, win_s, mats_s, small_s, stats_s, win_z, mats_z, small_z, stats_z, win_t, gain_t, stats_t, vectors, stats_v,
    x_send, x_recv, z_send, z_recv, t_send, t_recv, l_send, l_recv, g_send, g_recv, s_send, s_recv,
):
    x, core, zh, q = place()
    me = core * WAYS + q
    peers = tp_peers()
    side, far = dp_peers(zh_size)
    greet([p[0] for p in peers] + [side] + [f[0] for f in far])
    gains = []
    turn = []
    for i, (target, rank, _) in enumerate(peers):
        copy = remote(gain.at[rank], gain_t.at[i], g_send.at[i], g_recv.at[i], target)
        copy.start()
        gains.append(copy)
    shown = []
    for i, (target, rank, _) in enumerate(peers):
        copy = remote(stats, stats_t.at[i], s_send.at[i], s_recv.at[i], target)
        copy.start()
        shown.append(copy)

    chunks = [
        (win.at[:, 0], near.at[0], win_s.at[0], win_z.at[0], False),
        (win.at[:, 1], near.at[1], win_s.at[1], win_z.at[1], False),
        (mats, mats_x, mats_s, mats_z, False),
        (vectors, small_x, small_s, small_z, False),
        (stats_v, stats_x, stats_s, stats_z, True),
    ]

    def join(a, b, peaks):
        a, b = a.astype(f32), b.astype(f32)
        if peaks:
            line = lax.broadcasted_iota(jnp.int32, a.shape, len(a.shape) - 2)
            return jnp.where(line < 4, a + b, jnp.maximum(a, b))
        return a + b

    sends = [None, None]

    def to_side(c):
        src, arrived = chunks[c][:2]
        copy = remote(src.at[1 - x], arrived, x_send.at[c], x_recv.at[c], side)
        copy.start()
        sends.append(copy)

    passed = []

    def pass_on(c):
        src, arrived, mine, buf, peaks = chunks[c]
        if sends[c] is not None:
            sends[c].wait_recv()
        mine[...] = join(src[x], arrived[...], peaks).astype(mine.dtype)
        moved = []
        for k, (target, to_z, _) in enumerate(far):
            copy = remote(mine.at[to_z], buf.at[k], z_send.at[c, k], z_recv.at[c, k], target)
            copy.start()
            moved.append(copy)
        passed.append(moved)

    to_side(2)
    pass_on(0)
    pass_on(1)
    for i, (target, rank, _) in enumerate(peers):
        copy = remote(late.at[rank], o_late.at[me], l_send.at[i], l_recv.at[i], target)
        copy.start()
        turn.append(copy)
    o_late[me] = late[me]
    total = gain[me]
    for i in range(TP - 1):
        gains[i].wait_recv()
        total = total + gain_t[i]
    vectors[...] = small[...]
    for l in range(LAYERS):
        for g in range(2 * zh_size):
            at = l * 2 * zh_size + g
            vectors[g // zh_size, g % zh_size, l * 16 + 8 : l * 16 + 9, :] = total[at : at + 1, :]
    seen = stats[...]
    for i in range(TP - 1):
        shown[i].wait_recv()
        seen = join(seen, stats_t[i], True)
    stats_v[...] = jnp.broadcast_to(seen, stats_v.shape)
    to_side(3)
    to_side(4)
    for c in range(2, len(chunks)):
        pass_on(c)
    outs = [None, None, o_mats, o_small, o_stats]
    for c in range(len(chunks)):
        src, arrived, mine, buf, peaks = chunks[c]
        value = join(src[x, zh], arrived[zh], peaks)
        for k in range(zh_size - 1):
            passed[c][k].wait_recv()
            value = join(value, buf[k], peaks)
        if c < 2:
            win_t[c] = value.astype(bf16).reshape(win_t.shape[1:])
        else:
            outs[c][...] = value
        if c == 1:
            for i, (target, rank, _) in enumerate(peers):
                copy = remote(
                    win_t.at[rank // WAYS, lax.rem(rank, WAYS)], o_win.at[me], t_send.at[i], t_recv.at[i], target
                )
                copy.start()
                turn.append(copy)
    o_win[me] = win_t[core, q]
    for copy in gains + shown + sends[2:]:
        copy.wait_send()
    for moved in passed:
        for copy in moved:
            copy.wait_send()
    for copy in turn:
        copy.wait()


def scatter_gradients(zh_size, win, near, mats, small, stats, gain, late):
    dma = pltpu.SemaphoreType.DMA
    far = max(1, zh_size - 1)
    v = lambda shape, dtype: pltpu.VMEM(shape, dtype)
    rows = win.shape[3] // WAYS
    every = jax.ShapeDtypeStruct((2, zh_size) + stats.shape, f32)
    ins = (mats, small, every)
    held = [v(a.shape[1:], a.dtype) for a in ins]
    sums = [v((2,) + win.shape[2:], bf16)] + held
    buf = [v((2, far) + win.shape[3:], bf16)] + [v((far,) + a.shape[2:], a.dtype) for a in ins]
    block = jax.ShapeDtypeStruct((TP, rows, win.shape[4]), bf16)
    return pl.pallas_call(
        functools.partial(gradients_kernel, zh_size),
        out_shape=[block] + [jax.ShapeDtypeStruct(a.shape[2:], f32) for a in ins] + [block],
        in_specs=[VM] * 7,
        out_specs=[VM] * 5,
        scratch_shapes=held + sums + buf
        + [v((2, WAYS, rows, win.shape[4]), bf16), v((TP - 1,) + gain.shape[1:], f32)]
        + [v((TP - 1,) + stats.shape, f32), v(small.shape, f32), v(every.shape, f32)]
        + [dma((5,)), dma((5,)), dma((5, far)), dma((5, far))]
        + [dma((TP - 1,))] * 8,
        compiler_params=pltpu.CompilerParams(
            collective_id=5, has_side_effects=True, vmem_limit_bytes=56 * 2**20
        ),
        name="scatter_gradients",
        cost_estimate=cost(90),
    )(win, near, mats, small, stats, gain, late)


def spread_keys(kq, lane):
    a = kq.astype(bf16).astype(f32)
    rest = kq - a
    b = rest.astype(bf16).astype(f32)
    c = rest - b
    return jnp.where(lane < 32, a, jnp.where(lane < 64, b, c)).astype(bf16)


def spreader():
    one = jnp.repeat(jnp.eye(32, dtype=bf16), 128, axis=1)
    return jnp.concatenate([one, one, one, jnp.zeros_like(one)], axis=0)


def dot(a, b, contract, out=f32):
    return lax.dot_general(a, b, (contract, ((), ())), preferred_element_type=out)


def rms(stream):
    return lax.rsqrt(jnp.mean(jnp.square(stream), axis=-1, keepdims=True) + eps)


LANES = 128


def struct(*shape, dtype=f32):
    return jax.ShapeDtypeStruct(shape, dtype)


def at_block(b, size):
    return pl.ds(pl.multiple_of(b * size, size), size)


def conv_of(entry, vec, row, size, c):
    cols = slice(c * LANES, (c + 1) * LANES)
    conv = vec[CONV : CONV + 1, cols]
    for j in range(CONV):
        conv = conv + vec[j : j + 1, cols] * entry[c, pl.ds(pl.multiple_of(row + TP * j, TP), size), :]
    return conv


def wide_of(ref, rows, parts):
    return jnp.concatenate([ref[c, rows, :] for c in range(parts)], axis=1)


def row_sum(value):
    return jnp.sum(value.reshape(-1, TP, value.shape[1]), axis=0)


def square_sum(kq):
    lane = lanes_of(kq.shape)
    return jnp.sum(jnp.where(lane < STATE, kq * kq, 0.0), axis=1, keepdims=True)


def forward_layer(zh_size, xg, win, mats, wout, vec, scale, nxt=None):
    tokens, width = xg.shape[1], xg.shape[2]
    half = win.shape[1] // 2
    parts = half // LANES
    rows = tokens * TP
    size = STEPS * TP
    blocks = rows // size
    halo = (CONV - 1) * TP
    dma = pltpu.SemaphoreType.DMA
    last = nxt is None
    groups = 2 * zh_size
    ins = dict(
        xg=(xg, VM), win=(win, VM), mats=(mats, VM), wout=(wout, HB if not last else VM), vec=(vec, VM),
        scale=(scale, VM), e=(spreader(), VM),
    )
    outs = dict(
        entry=(struct(2 * parts, halo + rows, LANES), VM), beta=(struct(parts, rows, LANES), VM),
        kq=(struct(rows, LANES), VM), proj=(struct(TP, size, 2 * LANES, dtype=bf16), VM),
        y=(struct(parts, rows, LANES), VM), keep=(struct(blocks, STATE, parts, TP, LANES), VM),
        mixed=(struct(TP, tokens, half, dtype=bf16), VM), stats=(struct(2, TP, LANES), VM),
    )
    scratch = dict(
        act=pltpu.VMEM((parts, rows, LANES), f32), step=pltpu.VMEM((parts, rows, LANES), f32),
        payload=pltpu.VMEM((TP, size, 2 * LANES), bf16), parts=pltpu.VMEM((TP - 1, size, 2 * LANES), bf16),
        own=pltpu.VMEM((size, 2 * LANES), f32),
        state=pltpu.VMEM((STATE, parts, TP, LANES), f32), wide=pltpu.VMEM((size, 32 * LANES), f32),
        part=pltpu.VMEM((TP, tokens, width), bf16),
        scatter_buf=Scatter.buffers((tokens, width)),
        sum_sems=Sum.sems(dma), scatter_sems=Scatter.sems(dma),
    )
    outs["result"] = (struct(tokens, width), VM)
    if not last:
        ins.update(
            h=(nxt["h"], VM), gain=(nxt["gain"], VM), win1=(nxt["win"], HB), mats1=(nxt["mats"], HB), wout1=(nxt["wout"], HB)
        )
        outs.update(
            wout_all=(struct(groups, *wout.shape, dtype=bf16), VM),
            win1_all=(struct(2, 2, zh_size, *nxt["win"].shape[1:], dtype=bf16), HB),
            mats1_all=(struct(groups, *nxt["mats"].shape, dtype=bf16), HB),
            wout1_all=(struct(groups, *nxt["wout"].shape, dtype=bf16), HB),
            xg1=(struct(TP, tokens, width, dtype=bf16), HB),
        )
        scratch.update(
            normed=pltpu.VMEM((tokens, width), bf16), gather_sems=Gather.sems(dma),
            d0=Spread.sems(dma, zh_size), d1=Spread.sems(dma, zh_size), d2=Spread.sems(dma, zh_size),
            d3=Spread.sems(dma, zh_size),
        )

    def body(r):
        targets = [p[0] for p in tp_peers()]
        if not last:
            side, far = dp_peers(zh_size)
            targets += [side] + [f[0] for f in far]
        greet(targets)
        entry, act, step, beta, kq, y = r["entry"], r["act"], r["step"], r["beta"], r["kq"], r["y"]
        if not last:
            index = lambda ref: lambda xx, zz: ref.at[xx * zh_size + zz]
            early = Spread(zh_size, r["wout"], index(r["wout_all"]), r["d0"])
            moves = [
                Spread(zh_size, r["win1"], lambda xx, zz: r["win1_all"].at[xx, :, zz], r["d1"]),
                Spread(zh_size, r["wout1"], index(r["wout1_all"]), r["d2"]),
                Spread(zh_size, r["mats1"], index(r["mats1_all"]), r["d3"]),
            ]
            early.start()

        entry[:, :halo, :] = jnp.zeros((2 * parts, halo, LANES), f32)
        tile = 2 * LANES
        for p in range(TP // 2):

            def columns(n, carry, p=p):
                cols = at_block(n, tile)
                out = jnp.dot(
                    r["xg"][2 * p : 2 * p + 2].reshape(2 * tokens, width), r["win"][:, cols],
                    preferred_element_type=f32,
                )
                for j in range(2):
                    for c in range(2):
                        entry[2 * n + c, pl.ds(halo + 2 * p + j, tokens, stride=TP), :] = out[
                            j * tokens : (j + 1) * tokens, c * LANES : (c + 1) * LANES
                        ]
                return carry

            lax.fori_loop(0, 2 * half // tile, columns, 0)
        if not last:
            moves[0].start()

        total = Sum(r["payload"], r["parts"], r["proj"], r["sum_sems"])

        def project(b, carry):
            rs = at_block(b, size)
            for c in range(parts):
                conv = conv_of(entry, r["vec"], b * size, size, c)
                act[c, rs, :] = (conv * jax.nn.sigmoid(conv)).astype(bf16).astype(f32)
            out = jnp.dot(
                wide_of(act, rs, parts).astype(bf16), r["mats"][:, RANK:], preferred_element_type=f32
            )
            r["payload"][b] = encode(out)

            @pl.when(b == total.me)
            def _():
                r["own"][...] = out

            return carry

        lax.fori_loop(0, blocks, project, 0)
        total.start()
        total.middle(r["own"][...])
        total.finish()
        if not last:
            early.onward()
            moves[1].start()
            moves[2].start()

        r["stats"][...] = jnp.zeros((2, TP, LANES), f32)

        def rates(b, carry):
            rs = at_block(b, size)
            tail = decode(r["proj"][b])[:, RANK:]
            keys = tail + pltpu.roll(tail, 32, 1) + pltpu.roll(tail, 64, 1)
            kq[rs, :] = keys
            norm = square_sum(keys)
            pre = dot(r["proj"][b, :, :RANK], r["mats"][:, :RANK], ((1,), (1,)))
            for c in range(parts):
                cols = slice(c * LANES, (c + 1) * LANES)
                rate = jax.nn.sigmoid(pre[:, cols] + r["vec"][CONV + 1 : CONV + 2, cols])
                beta[c, rs, :] = rate
                step[c, rs, :] = rate / (1.0 + rate * norm)
                r["stats"][0] += row_sum(rate)
                r["stats"][1] = jnp.maximum(
                    r["stats"][1], jnp.max(rate.reshape(-1, TP, LANES), axis=0)
                )
            return carry

        lax.fori_loop(0, blocks, rates, 0)
        r["stats"][0] = r["stats"][0] * r["scale"][...]
        r["stats"][1] = r["stats"][1] * r["scale"][...]

        lane = lanes_of((size, LANES))
        state, wide = r["state"], r["wide"]
        state[...] = jnp.zeros_like(state)

        def block(b, carry):
            r["keep"][b] = state[...]
            wide[...] = jnp.dot(spread_keys(kq[at_block(b, size), :], lane), r["e"][...], preferred_element_type=f32)

            def one(j, carry):
                t = at_block(b * STEPS + j, TP)
                w = at_block(j, TP)
                acts = [act[c, t, :] for c in range(parts)]
                steps = [step[c, t, :] for c in range(parts)]
                sums = [None] * parts
                for n in range(STATE):
                    key = wide[w, n * LANES : (n + 1) * LANES]
                    query = wide[w, (STATE + n) * LANES : (STATE + n + 1) * LANES]
                    for c in range(parts):
                        s = state[n, c]
                        s = s + (steps[c] * key) * (acts[c] - key * s)
                        state[n, c] = s
                        sums[c] = s * query if sums[c] is None else sums[c] + s * query
                for c in range(parts):
                    y[c, t, :] = sums[c]
                return carry

            lax.fori_loop(0, STEPS, one, 0)
            rs = at_block(b, size)
            here = pl.ds(pl.multiple_of(b * STEPS, STEPS), STEPS)
            for c in range(parts):
                cols = slice(c * LANES, (c + 1) * LANES)
                gate = entry[parts + c, pl.ds(pl.multiple_of(b * size + halo, TP), size), :]
                skip = r["vec"][CONV + 2 : CONV + 3, cols]
                step[c, rs, :] = (y[c, rs, :] + skip * act[c, rs, :]) * (gate * jax.nn.sigmoid(gate))
                for s in range(TP):
                    r["mixed"][s, here, cols] = step[c, pl.ds(b * size + s, STEPS, stride=TP), :].astype(bf16)
            return carry

        lax.fori_loop(0, blocks, block, 0)
        if not last:
            early.finish()
            moves[0].onward()
        weight = r["wout_all"] if not last else r["wout"]
        scatter = Scatter(r["part"], r["scatter_buf"], r["scatter_sems"])
        down = (lambda: weight[...].reshape(half, width)) if not last else (lambda: weight[...])
        out_partial(scatter, r["part"], r["mixed"], down)
        if last:
            r["result"][...] = scatter.total()
            return
        stream = r["h"][...] + scatter.total()
        r["result"][...] = stream
        r["normed"][...] = (stream * rms(stream) * r["gain"][...]).astype(bf16)
        spread = Gather(r["normed"], r["xg1"], r["gather_sems"])
        spread.start()
        for move in moves[1:]:
            move.onward()
        spread.onward()
        spread.finish()
        for move in moves:
            move.finish()

    return call(body, "layer_forward_last" if last else "layer_forward", 7 if last else 6, ins, outs, scratch)


def out_partial(scatter, part, left, right, turned=False):
    contract = ((1,), (1,)) if turned else ((1,), (0,))
    for i in range(4):
        for core in (1 - scatter.core, scatter.core):
            slot = core * WAYS + scatter.turns[i]
            part[slot] = dot(left[slot], right(), contract).astype(bf16)
        scatter.to_sibling(i)
        if i >= 1:
            scatter.across(i - 1)


class Reduce:
    @staticmethod
    def sems(dma, zh_size):
        far = max(1, zh_size - 1)
        return [dma, dma, dma((far,)), dma((far,))]

    @staticmethod
    def buffers(zh_size, block):
        return [
            pltpu.VMEM((zh_size,) + block, bf16), pltpu.VMEM((zh_size,) + block, bf16),
            pltpu.VMEM((max(1, zh_size - 1),) + block, bf16),
        ]

    def __init__(self, zh_size, src, buffers, sems):
        self.zh_size, self.src = zh_size, src
        self.near, self.mine, self.buf = buffers
        self.x_send, self.x_recv, self.z_send, self.z_recv = sems
        self.x, _, self.zh, _ = place()
        self.side, self.far = dp_peers(zh_size)

    def start(self):
        half = self.src.at[pl.ds((1 - self.x) * self.zh_size, self.zh_size)]
        self.over = remote(half, self.near, self.x_send, self.x_recv, self.side)
        self.over.start()

    def middle(self):
        self.over.wait_recv()
        for k in range(self.zh_size):
            self.mine[k] = (
                self.src[self.x * self.zh_size + k].astype(f32) + self.near[k].astype(f32)
            ).astype(bf16)
        self.along = [
            remote(self.mine.at[to_z], self.buf.at[k], self.z_send.at[k], self.z_recv.at[k], target)
            for k, (target, to_z, _) in enumerate(self.far)
        ]
        for copy in self.along:
            copy.start()

    def total(self):
        value = self.src[self.x * self.zh_size + self.zh].astype(f32) + self.near[self.zh].astype(f32)
        for k in range(self.zh_size - 1):
            self.along[k].wait_recv()
            value = value + self.buf[k].astype(f32)
        self.over.wait_send()
        for copy in self.along:
            copy.wait_send()
        return value


def backward_layer(zh_size, kept, gog, wout, mats, vec, xg, win, gain, h, grad, late=None, onward=True):
    tokens, width = xg.shape[1], xg.shape[2]
    half = win.shape[1] // 2
    parts = half // LANES
    rows = tokens * TP
    size = STEPS * TP
    blocks = rows // size
    halo = (CONV - 1) * TP
    groups = 2 * zh_size
    share = half // groups
    deep = width // (2 * groups)
    far = max(1, zh_size - 1)
    dma = pltpu.SemaphoreType.DMA
    fold = jnp.pad(jnp.repeat(jnp.eye(32, dtype=bf16), LANES, axis=0), ((0, 0), (0, 96)))
    ins = {k: (kept[k], VM) for k in ("entry", "beta", "kq", "proj", "keep")}
    ins.update(
        mats=(mats, VM), wout=(wout, HB), vec=(vec, VM), gain=(gain, VM), h=(h, VM), grad=(grad, VM),
        mixed=(kept["mixed"], HB), e=(spreader(), VM), fold=(fold, VM), gouts=(gog, HB), y=(kept["y"], HB), xg=(xg, HB), win=(win, HB),
    )
    outs = dict(
        prev=(struct(tokens, width), VM), gwin=(struct(2 * groups, deep, 2 * half, dtype=bf16), VM),
        near=(struct(groups, deep, 2 * half, dtype=bf16), HB), gwout=(struct(share, width), VM),
        gmats=(struct(half, 3 * LANES, dtype=bf16), VM), gvec=(struct(8, half), VM),
        ggain=(struct(1, width), VM),
    )
    block_f32 = pltpu.VMEM((parts, rows, LANES), f32)
    scratch = dict(
        a=pltpu.VMEM((TP, tokens, width), bf16), b=pltpu.VMEM(win.shape, bf16),
        gs=block_f32, act=block_f32, gact=block_f32, ggate=block_f32,
        step=pltpu.VMEM((parts, rows + halo, LANES), f32),
        states=pltpu.VMEM((STEPS + 1, STATE, parts, TP, LANES), f32),
        lam=pltpu.VMEM((STATE, parts, TP, LANES), f32), wide=pltpu.VMEM((size, 32 * LANES), f32),
        gstep=pltpu.VMEM((parts, size, LANES), f32),
        gentry=pltpu.VMEM((TP, tokens, 2 * half), bf16),
        payload=pltpu.VMEM((TP, size, 2 * LANES), bf16), parts=pltpu.VMEM((TP - 1, size, 2 * LANES), bf16),
        total=pltpu.VMEM((TP, size, 2 * LANES), bf16), own=pltpu.VMEM((size, 2 * LANES), f32),
        sums=pltpu.VMEM((8, parts, TP, LANES), f32),
        grate=pltpu.VMEM((half, LANES), f32), gselect=pltpu.VMEM((half, 2 * LANES), f32),
        gwo=pltpu.VMEM((groups, share, width), bf16),
        scatter_buf=Scatter.buffers((tokens, width)), reduce_buf=Reduce.buffers(zh_size, (share, width)),
        sum_sems=Sum.sems(dma), scatter_sems=Scatter.sems(dma), reduce_sems=Reduce.sems(dma, zh_size),
        loads=dma((7,)), over=[dma, dma],
    )
    if onward:
        outs["gog"] = (struct(TP, tokens, width, dtype=bf16), HB)
        scratch.update(gout=pltpu.VMEM((tokens, width), bf16), gather_sems=Gather.sems(dma))
    if late is not None:
        ins["late"] = (late, HB)
        outs["late"] = (struct(far, 2, *late.shape[2:], dtype=bf16), HB)
        scratch.update(late_sems=[dma((far,)), dma((far,))])
        ins["late_in"] = ins.pop("late")

    def body(r):
        x, core, zh, q = place()
        side, far_ones = dp_peers(zh_size)
        greet([p[0] for p in tp_peers()] + [side] + [f[0] for f in far_ones])
        entry, act, step, beta, kq = r["entry"], r["act"], r["step"], r["beta"], r["kq"]
        gs, gact, ggate, vec, sums = r["gs"], r["gact"], r["ggate"], r["vec"], r["sums"]
        loads = [
            pltpu.make_async_copy(src, dst, r["loads"].at[i])
            for i, (src, dst) in enumerate(
                (
                    (r["gouts"], r["a"]), (r["mixed"], r["gentry"].at[:, :, :half]),
                    (r["wout"].at[:, : 2 * half], r["b"].at[:half]), (r["wout"].at[:, 2 * half :], r["b"].at[half : 2 * half]),
                    (r["y"], gact), (r["xg"], r["a"]), (r["win"], r["b"]),
                )
            )
        ]
        for copy in loads[:5]:
            copy.start()
        passed = []
        if late is not None:
            for k, (target, to_z, _) in enumerate(far_ones):
                copy = remote(
                    r["late_in"].at[:, to_z], r["late"].at[k], r["late_sems"][0].at[k], r["late_sems"][1].at[k], target
                )
                copy.start()
                passed.append(copy)
        sums[...] = jnp.zeros_like(sums)
        r["grate"][...] = jnp.zeros_like(r["grate"])
        r["gselect"][...] = jnp.zeros_like(r["gselect"])

        def again(b, carry):
            rs = at_block(b, size)
            norm = square_sum(kq[rs, :])
            for c in range(parts):
                conv = conv_of(entry, vec, b * size, size, c)
                act[c, rs, :] = (conv * jax.nn.sigmoid(conv)).astype(bf16).astype(f32)
                rate = beta[c, rs, :]
                step[c, rs, :] = rate / (1.0 + rate * norm)
            return carry

        lax.fori_loop(0, blocks, again, 0)
        loads[0].wait()
        loads[1].wait()

        def outer(c, carry):
            left = r["gentry"][:, :, at_block(c, LANES)].reshape(rows, LANES)
            out = dot(left, r["a"][...].reshape(rows, width), ((0,), (0,))).astype(bf16)
            each = LANES // share
            r["gwo"][pl.ds(c * each, each)] = out.reshape(each, share, width)
            return carry

        lax.fori_loop(0, parts, outer, 0)
        reduce = Reduce(zh_size, r["gwo"], r["reduce_buf"], r["reduce_sems"])
        reduce.start()
        loads[2].wait()
        loads[3].wait()
        for p in range(TP // 2):

            def columns(n, carry, p=p):
                out = 0.0
                for k in range(2):
                    left = r["a"][2 * p : 2 * p + 2, :, 2 * half * k : 2 * half * (k + 1)].reshape(2 * tokens, 2 * half)
                    right = r["b"][pl.ds(pl.multiple_of(half * k + n * 2 * LANES, 2 * LANES), 2 * LANES), :]
                    out = out + dot(left, right, ((1,), (1,)))
                for j in range(2):
                    for c in range(2):
                        gs[2 * n + c, pl.ds(2 * p + j, tokens, stride=TP), :] = out[
                            j * tokens : (j + 1) * tokens, c * LANES : (c + 1) * LANES
                        ]
                return carry

            lax.fori_loop(0, half // (2 * LANES), columns, 0)
        loads[5].start()
        loads[6].start()
        loads[4].wait()

        def gates(b, carry):
            rs = at_block(b, size)
            for c in range(parts):
                cols = slice(c * LANES, (c + 1) * LANES)
                gate = entry[parts + c, pl.ds(pl.multiple_of(b * size + halo, TP), size), :]
                sig = jax.nn.sigmoid(gate)
                g = gs[c, rs, :]
                a = act[c, rs, :]
                down = g * (gate * sig)
                ggate[c, rs, :] = g * (gact[c, rs, :] + vec[CONV + 2 : CONV + 3, cols] * a) * (
                    sig * (1.0 + gate * (1.0 - sig))
                )
                gs[c, rs, :] = down
                sums[CONV + 2, c] += row_sum(down * a)
            return carry

        lax.fori_loop(0, blocks, gates, 0)

        lane = lanes_of((size, LANES))
        states, lam, wide, gstep = r["states"], r["lam"], r["wide"], r["gstep"]
        lam[...] = jnp.zeros_like(lam)
        plus = lambda a, b: b if a is None else a + b
        total = Sum(r["payload"], r["parts"], r["total"], r["sum_sems"])

        def block(bi, carry):
            b = blocks - 1 - bi
            rs = at_block(b, size)
            states[0] = r["keep"][b]
            wide[...] = jnp.dot(spread_keys(kq[rs, :], lane), r["e"][...], preferred_element_type=f32)

            def replay(j, carry):
                t, w = at_block(b * STEPS + j, TP), at_block(j, TP)
                acts = [act[c, t, :] for c in range(parts)]
                steps = [step[c, t, :] for c in range(parts)]
                for n in range(STATE):
                    key = wide[w, n * LANES : (n + 1) * LANES]
                    for c in range(parts):
                        s = states[j, n, c]
                        states[j + 1, n, c] = s + (steps[c] * key) * (acts[c] - key * s)
                return carry

            lax.fori_loop(0, STEPS, replay, 0)

            def back(jj, carry):
                j = STEPS - 1 - jj
                t, w = at_block(b * STEPS + j, TP), at_block(j, TP)
                acts = [act[c, t, :] for c in range(parts)]
                steps = [step[c, t, :] for c in range(parts)]
                gsums = [gs[c, t, :] for c in range(parts)]
                first, second = [None] * parts, [None] * parts
                for n in range(STATE):
                    kcols, qcols = slice(n * LANES, (n + 1) * LANES), slice((STATE + n) * LANES, (STATE + n + 1) * LANES)
                    key, query = wide[w, kcols], wide[w, qcols]
                    key_term, query_term = None, None
                    for c in range(parts):
                        before, after = states[j, n, c], states[j + 1, n, c]
                        grad = lam[n, c] + gsums[c] * query
                        u = key * before
                        d = acts[c] - u
                        gk = grad * key
                        first[c] = plus(first[c], gk * d)
                        second[c] = plus(second[c], gk)
                        key_term = plus(key_term, (steps[c] * grad) * (d - u))
                        query_term = plus(query_term, gsums[c] * after)
                        lam[n, c] = grad - (steps[c] * key) * gk
                    wide[w, kcols] = key_term
                    wide[w, qcols] = query_term
                for c in range(parts):
                    gstep[c, w, :] = first[c]
                    gact[c, t, :] = steps[c] * second[c]
                return carry

            lax.fori_loop(0, STEPS, back, 0)
            terms = wide[...]
            high = terms.astype(bf16)
            low = (terms - high.astype(f32)).astype(bf16)
            gkq = jnp.dot(high, r["fold"][...], preferred_element_type=f32) + jnp.dot(
                low, r["fold"][...], preferred_element_type=f32
            )
            keys = kq[rs, :]
            norm = square_sum(keys)
            gnorm = jnp.zeros((size, 1), f32)
            grates = []
            for c in range(parts):
                cols = slice(c * LANES, (c + 1) * LANES)
                rate = beta[c, rs, :]
                g = gstep[c]
                inverse = 1.0 + rate * norm
                inverse = 1.0 / (inverse * inverse)
                gnorm = gnorm - jnp.sum(g * (rate * rate * inverse), axis=1, keepdims=True)
                grate = g * inverse * rate * (1.0 - rate)
                sums[CONV + 1, c] += row_sum(grate)
                grates.append(grate.astype(bf16))
                gact[c, rs, :] += vec[CONV + 2 : CONV + 3, cols] * gs[c, rs, :]
            grate = jnp.concatenate(grates, axis=1)
            r["grate"][...] += dot(grate, r["proj"][b, :, :RANK], ((0,), (0,)))
            grank = dot(grate, r["mats"][:, :RANK], ((1,), (0,)))
            gkq = gkq + jnp.where(lane < STATE, 2.0 * keys * gnorm, 0.0)
            out = jnp.concatenate([grank, gkq], axis=1)
            r["payload"][b] = encode(out)

            @pl.when(b == total.me)
            def _():
                r["own"][...] = out

            return carry

        lax.fori_loop(0, blocks, block, 0)
        total.start()
        reduce.middle()
        total.middle(r["own"][...])
        total.finish()
        step[:, rows:, :] = jnp.zeros((parts, halo, LANES), f32)
        gconv = step

        def convs(b, carry):
            rs = at_block(b, size)
            gp = r["total"][b]
            gp = jnp.where(lanes_of(gp.shape) < RANK + 2 * STATE, gp.astype(f32), 0.0).astype(bf16)
            r["gselect"][...] += dot(wide_of(act, rs, parts).astype(bf16), gp, ((0,), (0,)))
            more = dot(gp, r["mats"][:, RANK:], ((1,), (1,)))
            for c in range(parts):
                conv = conv_of(entry, vec, b * size, size, c)
                sig = jax.nn.sigmoid(conv)
                g = (gact[c, rs, :] + more[:, c * LANES : (c + 1) * LANES]) * (sig * (1.0 + conv * (1.0 - sig)))
                gconv[c, rs, :] = g
                sums[CONV, c] += row_sum(g)
                for j in range(CONV):
                    inner = entry[c, pl.ds(pl.multiple_of(b * size + TP * j, TP), size), :]
                    sums[j, c] += row_sum(g * inner)
            return carry

        lax.fori_loop(0, blocks, convs, 0)

        def inners(b, carry):
            rs = at_block(b, size)
            here = pl.ds(pl.multiple_of(b * STEPS, STEPS), STEPS)
            for c in range(parts):
                cols = slice(c * LANES, (c + 1) * LANES)
                value = None
                for j in range(CONV):
                    at = pl.ds(pl.multiple_of(b * size + TP * (CONV - 1 - j), TP), size)
                    value = plus(value, vec[j : j + 1, cols] * gconv[c, at, :])
                gs[c, rs, :] = value
                for s in range(TP):
                    at = pl.ds(b * size + s, STEPS, stride=TP)
                    r["gentry"][s, here, cols] = gs[c, at, :].astype(bf16)
                    r["gentry"][s, here, half + c * LANES : half + (c + 1) * LANES] = ggate[c, at, :].astype(bf16)
            return carry

        lax.fori_loop(0, blocks, inners, 0)
        loads[5].wait()
        tile = 2 * LANES

        def outer_in(i, carry):
            left = r["a"][:, :, at_block(i, tile)].reshape(rows, tile)
            out = dot(left, r["gentry"][...].reshape(rows, 2 * half), ((0,), (0,))).astype(bf16)
            each = tile // deep
            r["gwin"][pl.ds(i * each, each)] = out.reshape(each, deep, 2 * half)
            return carry

        lax.fori_loop(0, width // tile, outer_in, 0)
        over = remote(
            r["gwin"].at[pl.ds((1 - x) * groups, groups)], r["near"], r["over"][0], r["over"][1], side
        )
        over.start()
        loads[6].wait()
        scatter = Scatter(r["a"], r["scatter_buf"], r["scatter_sems"])
        out_partial(scatter, r["a"], r["gentry"], lambda: r["b"][...], turned=True)
        r["gmats"][:, :RANK] = r["grate"][...].astype(bf16)
        r["gmats"][:, RANK:] = r["gselect"][...].astype(bf16)
        for j in range(8):
            for c in range(parts):
                r["gvec"][j : j + 1, c * LANES : (c + 1) * LANES] = jnp.sum(sums[j, c], axis=0, keepdims=True)
        r["gwout"][...] = reduce.total()
        gnormed = scatter.total()
        stream = r["h"][...]
        scale = rms(stream)
        r["ggain"][...] = jnp.sum(gnormed * stream * scale, axis=0, keepdims=True)
        scaled = gnormed * r["gain"][...]
        grad = r["grad"][...] + scale * scaled - stream * (scale * scale * scale) * jnp.mean(
            stream * scaled, axis=-1, keepdims=True
        )
        r["prev"][...] = grad
        if onward:
            r["gout"][...] = grad.astype(bf16)
            spread = Gather(r["gout"], r["gog"], r["gather_sems"])
            spread.start()
            spread.onward()
            spread.finish()
        for copy in passed:
            copy.wait()
        over.wait()

    return call(body, "layer_backward", 9 if onward else 8, ins, outs, scratch)


def on_device(
    hidden, cotangent, groups, group_weights, input_weight, select_weight, rate_weight,
    output_weight, norm_gain, conv_taps, conv_shift, rate_shift, skip_gain,
):
    fsdp = lax.axis_size("fsdp")
    zh_size = fsdp // WAYS
    count = 2 * 2 * fsdp
    group_count = 2 * zh_size
    share = conv_shift.shape[1]
    gains = norm_gain.shape[1]
    depth = input_weight.shape[1]
    x, core, zh, q = place()

    labels = jnp.arange(group_weights.shape[0])
    own_weight = jnp.sum(jnp.where(groups[:, None] == labels[None, :], group_weights[None, :], 0.0))

    wins, mats, smalls, misc = [], [], [], []
    for l in range(LAYERS):
        win = input_weight[l].reshape(depth, 2, 2, 2, zh_size, WAYS, share)
        wins.append(win.transpose(3, 5, 0, 1, 2, 4, 6).reshape(TP, depth, 2 * group_count * share))
        both = jnp.concatenate([rate_weight[l].T, select_weight[l]], axis=1)
        mats.append(jnp.pad(both, ((0, 0), (0, 3 * LANES - both.shape[1]))))
        small = jnp.concatenate(
            [conv_taps[l], conv_shift[l][None], rate_shift[l][None], skip_gain[l][None], skip_gain[l][None]]
        ).astype(f32)
        smalls.append(jnp.pad(small, ((0, 0), (0, 128 - share))))
        misc.append(jnp.pad(norm_gain[l].astype(f32)[None], ((0, 0), (0, 128 - gains))))
    misc = jnp.concatenate(misc + [jnp.full((8 - LAYERS, 128), own_weight)])
    win, late, small, misc, mat = gather_weights(
        zh_size, wins[0], wins[1], jnp.concatenate(smalls), misc, mats[0]
    )
    all_weights = misc[:, LAYERS, 0]
    small = small[:, :, :share].transpose(1, 0, 2).reshape(LAYERS, 8, group_count * share)
    gain = [misc[:, l, :gains].reshape(1, count * gains) for l in range(LAYERS)]
    late = late.reshape(2, WAYS * depth, -1)
    width = output_weight.shape[2]
    scales = all_weights / jnp.mean(all_weights)
    table = scales.reshape(2, 2, zh_size, WAYS)
    own_scale = table[x, core, zh, q]
    group_scale = table[x, :, zh, :].reshape(TP)

    group_scale = jnp.broadcast_to(group_scale[:, None], (TP, LANES))

    h0 = hidden[0]
    xg0 = tp_gather((h0 * rms(h0) * gain[0]).astype(bf16))
    grad = cotangent[0] * own_scale
    gog1 = tp_gather(grad.astype(bf16))
    flat = lambda a: a.reshape(group_count * share, -1)
    win0, mat0 = win.reshape(count * depth, -1), flat(mat)
    one = forward_layer(
        zh_size, xg0, win0, mat0, output_weight[0], small[0], group_scale,
        dict(h=h0, gain=gain[1], win=late, mats=mats[1], wout=output_weight[1]),
    )
    win1, mat1 = one["win1_all"].reshape(count * depth, -1), flat(one["mats1_all"])
    wout0, wout1 = flat(one["wout_all"]), flat(one["wout1_all"])
    h1 = one["result"]
    two = forward_layer(zh_size, one["xg1"], win1, mat1, wout1, small[1], group_scale)
    stream = h1 + two["result"]
    sums = [jnp.sum(o["stats"][0]) for o in (one, two)]
    peaks = [jnp.max(o["stats"][1]) for o in (one, two)]
    pad = [jnp.zeros((), f32)] * (4 - LAYERS)
    own_stats = jnp.broadcast_to(jnp.stack(sums + pad + peaks + pad)[:, None], (8, 128))

    down1 = backward_layer(zh_size, two, gog1, wout1, mat1, small[1], one["xg1"], win1, gain[1], h1, grad)
    grid = (2, 2, zh_size, WAYS * depth, -1)
    pick = lambda a, i: lax.dynamic_index_in_dim(a, i, 0, keepdims=False)
    summed = pick(down1["gwin"].reshape(grid), x).astype(f32) + down1["near"].reshape(grid[1:]).astype(f32)
    down0 = backward_layer(
        zh_size, one, down1["gog"], wout0, mat0, small[0], xg0, win0, gain[0], h0, down1["prev"],
        late=summed.astype(bf16), onward=False,
    )
    grad = down0["prev"]
    late = lax.dynamic_index_in_dim(summed, zh, 1, keepdims=False)
    for k in range(zh_size - 1):
        late = late + down0["late"][k].astype(f32)
    late = late.astype(bf16).reshape(TP, depth, -1)
    smalls, gain_sums, mats = [], [], []
    for down in (down0, down1):
        vec = down["gvec"][:7].reshape(7, group_count, share).transpose(1, 0, 2)
        smalls.append(jnp.pad(vec, ((0, 0), (0, 9), (0, 128 - share))))
        part = down["ggain"].reshape(2, 2, zh_size, WAYS, gains).transpose(1, 3, 0, 2, 4)
        gain_sums.append(part.reshape(TP, group_count, gains))
        mats.append(down["gmats"])
    small = jnp.concatenate(smalls, axis=1).reshape(2, zh_size, 16 * LAYERS, 128)
    mats = jnp.concatenate(mats, axis=1).reshape(2, zh_size, share, -1)
    gain = jnp.concatenate(gain_sums, axis=1)
    gain = jnp.pad(gain, ((0, 0), (0, -gain.shape[1] % 8), (0, 128 - gains)))
    first, mats, small, stats, late = scatter_gradients(
        zh_size, down0["gwin"].reshape(grid), down0["near"].reshape(grid[1:]), mats, small, own_stats, gain, late
    )
    outs = [[] for _ in range(9)]
    for l, win in enumerate((first, late)):
        m = mats[:, 3 * LANES * l : 3 * LANES * (l + 1)]
        win = win.reshape(2, WAYS, depth, 2, 2, zh_size, share).transpose(2, 3, 4, 0, 5, 1, 6)
        outs[0].append(win.reshape(depth, -1).astype(f32))
        outs[1].append(m[:, RANK : RANK + select_weight.shape[2]])
        outs[2].append(m[:, :RANK].T)
        outs[3].append((down0, down1)[l]["gwout"])
        vec = small[16 * l : 16 * (l + 1)]
        outs[4].append(vec[8, :gains])
        outs[5].append(vec[:CONV, :share])
        outs[6].append(vec[CONV, :share])
        outs[7].append(vec[CONV + 1, :share])
        outs[8].append(vec[CONV + 2, :share])
    stacked = tuple(jnp.stack(o) for o in outs)
    beta_mean = stats[:LAYERS, 0] / (count * hidden.shape[1] * INNER)
    beta_max = stats[4 : 4 + LAYERS, 0]
    return (stream[None], grad[None]) + stacked + (beta_mean, beta_max)


def solution(mesh):
    both = ("dp", "fsdp")
    placed = (
        P(both, None, None), P(both, None, None), P(both), P(),
        P(None, both, None), P(None, both, None), P(None, None, both), P(None, both, None),
        P(None, both), P(None, None, both), P(None, both), P(None, both), P(None, both),
    )
    return jax.shard_map(
        on_device,
        mesh=mesh,
        in_specs=placed,
        out_specs=(P(both, None, None), P(both, None, None)) + placed[4:] + (P(), P()),
        check_vma=False,
    )
```

time: 1040 us -> 827 us (0.80)
  Pallas kernels: 600 us -> 743 us
  matrix products: 111 us -> 0 us
  waiting for transfers between devices: 106 us -> 0 us
  local copies, waits for them, and re-layouts: 109 us -> 35.7 us
  other arithmetic: 73.5 us -> 38.4 us
  starting transfers between devices: 23.4 us -> 0 us
    pallas_call x12 -> x4, Pallas kernels: 307 us -> 545 us  [call(): pl.pallas_call(kernel, out_shape=[shape for shape, _ in outs.values()], i...]
    dot_general x24 -> x0, matrix products: 111 us -> none  [dot(): lax.dot_general(a, b, (contract, ((), ())), preferred_element_type=out)]
    ppermute x17 -> x0, waiting for transfers between devices: 106 us -> none  [swap(): return lax.ppermute(value, ('dp', 'fsdp'), pairs)]
    pallas_call x4 -> x2, Pallas kernels: 114 us -> 58.2 us  [tp_gather(): pl.pallas_call(tp_gather_kernel, out_shape=jax.ShapeDtypeStruct((TP,) + r...]
    pallas_call x1, Pallas kernels: 91.7 us -> 67.6 us  [gather_weights(): pl.pallas_call(functools.partial(weights_kernel, zh_size), out_shape=[jax...]
    ppermute x17 -> x0, starting transfers between devices: 23.4 us -> none  [swap(): return lax.ppermute(value, ('dp', 'fsdp'), pairs)]
    dot_general x4 -> x0, local copies, waits for them, and re-layouts: 16.9 us -> none  [dot(): lax.dot_general(a, b, (contract, ((), ())), preferred_element_type=out)]
    pallas_call x1, Pallas kernels: 87.7 us -> 71.9 us  [scatter_gradients(): pl.pallas_call(functools.partial(gradients_kernel, zh_size), out_shape=[b...]
  transfers between devices with their start and end apart: 17 -> 0, of which waited for: 4 -> 0; matrix products, arithmetic and copies ran while one was open for 13% -> 0% of each run, Pallas kernels for 26% -> 0%
where the time goes in v3:
time: 827 us; the launch traced here: 819 us
  Pallas kernels  743 us (90%)
  other arithmetic  38.4 us (5%)
  local copies, waits for them, and re-layouts  35.7 us (4%)
    pallas_call x4, Pallas kernels, call(): pl.pallas_call(kernel, out_shape=[shape for shape, _ in outs.values()], i...  545 us
    pallas_call x1, Pallas kernels, scatter_gradients(): pl.pallas_call(functools.partial(gradients_kernel, zh_size), out_shape=[b...  71.9 us
    pallas_call x1, Pallas kernels, gather_weights(): pl.pallas_call(functools.partial(weights_kernel, zh_size), out_shape=[jax...  67.6 us
    pallas_call x2, Pallas kernels, tp_gather(): pl.pallas_call(tp_gather_kernel, out_shape=jax.ShapeDtypeStruct((TP,) + r...  58.2 us

profile of v3, /device:TPU:0, one launch (start us, length us, event | category | flops | bytes accessed | tf_op | source)
XLA Modules:
  0.0 819.5 jit_solution(12762116763447312006)
XLA Ops:
  1.3 1.3 fusion.8
  2.6 0.6 broadcast_in_dim.47
  3.3 1.4 multiply_reduce_fusion
  4.8 0.7 fusion.16
  5.5 0.7 fusion.19
  6.3 0.7 fusion.17
  7.0 0.7 slice_bitcast_fusion.12
  7.8 0.7 maximum_maximum_fusion.1.misc
  8.4 0.6 concatenate.33.small
  9.1 0.8 fusion.13
  10.1 0.8 fusion.12
  11.0 0.7 fusion.6.refs_10_
  11.8 0.7 fusion.5.mats
  12.8 1.2 maximum_maximum_fusion.refs_6_.refs_12_
  14.1 1.2 pad.42.refs_13_
  15.3 1.1 slice_bitcast_fusion
  16.6 0.8 reshape_squeeze.13
  17.3 0.8 copy.62
  18.2 1.5 reshape.174.late
  19.7 0.7 reshape_squeeze.12
  20.5 0.8 copy.63
  21.3 1.5 reshape.173.win
  22.8 67.6 %gather_weights.1 = (bf16[32,64,1024]{2,1,0:T(8,128)(2,1)}, bf16[8,64,1024]{2,1,0:T(8,128)(2,1)}, f32[4,16,128]{2,1,0:T(8,128)}, f32[32,8,128]{2,1,0:T(8,128)}, bf16[4,128,384]{2,1,0:T(8,128)(2,1)}) custom-call(bf16[8,64,1024]{2,1,0:T(8,128)(2,1)} %reshape.173.win, bf16[8,64,1024]{2,1,0:T(8,128)(2,1)} %reshape.174.late, f32[16,128]{1,0:T(8,128)} %concatenate.33.small, ...), custom_call_target="tpu_custom_call" | custom-call | flops 99000000512 | tf_op jit(solution)/shard_map/gather_weights/pallas_call | solution.py:165
  90.4 1.6 slice_reduce_fusion.1
  92.7 1.2 divide_reduce_fusion
  94.7 0.7 broadcast_in_dim.49.refs_5_
  95.4 1.3 slice_bitcast_fusion.6
  96.7 1.1 slice_reduce_fusion
  97.8 0.7 reshape_squeeze.14.refs_8_
  98.5 0.7 reshape_squeeze.15.refs_8_
  99.2 0.9 multiply_convert_fusion.x_ref
  100.2 2.0 fusion.10
  102.1 28.8 %tp_gather.2.refs_0_.refs_16_ = bf16[8,128,2048]{2,1,0:T(8,128)(2,1)} custom-call(bf16[128,2048]{1,0:T(8,128)(2,1)} %multiply_convert_fusion.x_ref), custom_call_target="tpu_custom_call" | custom-call | flops 30799998976 | tf_op jit(solution)/shard_map/tp_gather/pallas_call | solution.py:217
  131.0 29.4 %tp_gather.3.refs_14_ = bf16[8,128,2048]{2,1,0:T(8,128)(2,1)} custom-call(bf16[128,2048]{1,0:T(8,128)(2,1)} %get-tuple-element.147.x_ref), custom_call_target="tpu_custom_call" | custom-call | flops 30799998976 | tf_op jit(solution)/shard_map/tp_gather/pallas_call | solution.py:217
  160.4 165.1 %layer_forward.1 = (f32[8,1048,128]{2,1,0:T(8,128)}, f32[4,1024,128]{2,1,0:T(8,128)}, f32[1024,128]{1,0:T(8,128)}, bf16[8,128,256]{2,1,0:T(8,128)(2,1)}, f32[4,1...) custom-call(bf16[8,128,2048]{2,1,0:T(8,128)(2,1)} %tp_gather.2.refs_, ...), custom_call_target="tpu_custom_call" | custom-call | tf_op jit(solution)/shard_map/layer_forward/pallas_call | solution.py:432
  325.4 1.3 slice_reduce_fusion.3
  326.7 81.8 %layer_forward_last.1 = (f32[8,1048,128]{2,1,0:T(8,128)}, f32[4,1024,128]{2,1,0:T(8,128)}, f32[1024,128]{1,0:T(8,128)}, bf16[8,128,256]{2,1,0:T(8,128)(2,1)}, f3...) custom-call(bf16[8,128,2048]{2,1,0:T(8,128)(2,1)} %get-tuple-element, ...), custom_call_target="tpu_custom_call" | custom-call | tf_op jit(solution)/shard_map/layer_forward_last/pallas_call | solution.py:432
  408.5 160.7 %layer_backward.2 = (f32[128,2048]{1,0:T(8,128)}, bf16[8,256,1024]{2,1,0:T(8,128)(2,1)}, bf16[4,256,1024]{2,1,0:T(8,128)(2,1)}, f32[128,2048]{1,0:T(8,128)}, bf1...) custom-call(f32[8,1048,128]{2,1,0:T(8,128)} %get-tuple-element.79.refs_0_, ...), custom_call_target="tpu_custom_call" | custom-call | tf_op jit(solution)/shard_map/layer_backward/pallas_call | solution.py:432
  569.3 2.8 add_bitcast_fusion
  572.7 2.7 stack.75
  575.4 0.7 broadcast_in_dim.54.stats
  576.5 0.7 reduce.33
  577.3 5.4 fusion.9
  582.7 137.5 %layer_backward.3 = (f32[128,2048]{1,0:T(8,128)}, bf16[8,256,1024]{2,1,0:T(8,128)(2,1)}, bf16[4,256,1024]{2,1,0:T(8,128)(2,1)}, f32[128,2048]{1,0:T(8,128)}, bf1...) custom-call(f32[8,1048,128]{2,1,0:T(8,128)} %get-tuple-element.73.refs_0_, ...), custom_call_target="tpu_custom_call" | custom-call | tf_op jit(solution)/shard_map/layer_backward/pallas_call | solution.py:432
  720.2 1.5 reduce.34
  721.8 0.6 select_maximum_fusion.1.gain
  722.4 0.7 slice_bitcast_fusion.9
  723.1 0.6 select_maximum_fusion
  723.8 2.0 pad_maximum_fusion.1
  725.7 2.9 pad_maximum_fusion
  728.9 1.0 copy-done.9
  729.8 1.3 fusion.late
  731.2 71.9 %scatter_gradients.1 = (bf16[8,64,1024]{2,1,0:T(8,128)(2,1)}, f32[128,768]{1,0:T(8,128)}, f32[32,128]{1,0:T(8,128)}, f32[8,128]{1,0:T(8,128)}, bf16[8,64,1024]{2,1,0:T(8,128)(2,1)}) custom-call(bf16[2,2,2,256,1024]{4,3,2,1,0:T(8,128)(2,1)} %bitcast.142, bf16[2,2,256,1024]{3,2,1,0:T(8,128)(2,1)} %bitcast.143, bf16[2,2,128,768]{3,2,1,0:T(8,128)(2,1)} %bitcast.132, ...), custom_call_target="tpu_custom_call" | custom-call | flops 99000000512 | tf_op jit(solution)/shard_map/scatter_gradients/pallas_call | solution.py:570
  803.1 1.8 convert_element_type.111
  804.9 1.4 copy.50
  806.3 0.8 convert_element_type.113
  807.1 1.4 slice_reduce_fusion.6
  811.5 0.8 copy.52
  812.3 0.8 copy.53
  813.1 0.7 convert_element_type.114
  813.8 1.4 copy.51
  815.2 0.8 convert_element_type.116
  816.0 2.3 maximum_convert_fusion
  818.3 1.0 copy.67
  (72 shorter events, 6.7 us)
Async XLA Ops:
  12.8 2.6 copy-start.4
  14.1 2.3 copy-start.2
  22.8 76.4 %copy-start = (f32[1,128,2048]{2,1,0:T(8,128)S(1)}, f32[1,128,2048]{2,1,0:T(8,128)}, u32[]{:S(2)}) copy-start(f32[1,128,2048]{2,1,0:T(8,128)} %param.13) | copy-start | bytes 3145732
  90.4 9.8 %copy-start.5 = (f32[1,128,2048]{2,1,0:T(8,128)S(1)}, f32[1,128,2048]{2,1,0:T(8,128)}, u32[]{:S(2)}) copy-start(f32[1,128,2048]{2,1,0:T(8,128)} %param.14) | copy-start | bytes 3145732
  569.3 2.8 copy-start.13
  569.3 7.3 copy-start.14
  569.3 8.0 copy-start.12
  569.3 8.0 copy-start.3
  582.7 141.1 %copy-start.11 = (bf16[512,384]{1,0:T(8,128)(2,1)S(1)}, bf16[512,384]{1,0:T(8,128)(2,1)}, u32[]{:S(2)}) copy-start(bf16[512,384]{1,0:T(8,128)(2,1)} %get-tuple-element.96) | copy-start | bytes 1179652
  720.2 5.5 copy-start.8
  725.7 2.9 copy-start.1
  728.6 1.2 copy-start.9
  804.9 3.6 copy-start.15
  804.9 6.5 copy-start.10
  806.3 6.8 copy-start.7
  816.0 2.3 copy-start.6

commit v4 on v3

v4 whole, which is shorter than its diff:
```python
import jax
import jax.numpy as jnp
import numpy as np
from jax import lax
from jax.sharding import PartitionSpec as P
import jax.experimental.pallas as pl
import jax.experimental.pallas.tpu as pltpu

INNER = 4096
STATE = 16
RANK = 128
CONV = 4
LAYERS = 2
WAYS = 4
TP = 8
STEPS = 16

eps = 1e-05
MESH = pl.DeviceIdType.MESH
f32 = jnp.float32
bf16 = jnp.bfloat16
VM = pl.BlockSpec(memory_space=pltpu.VMEM)
HB = pl.BlockSpec(memory_space=pl.ANY)


def place():
    dp, fs = lax.axis_index("dp"), lax.axis_index("fsdp")
    return dp // 2, lax.rem(dp, 2), fs // WAYS, lax.rem(fs, WAYS)


def device(x, core, zh, q):
    return (x * 2 + core, zh * WAYS + q)


def remote(src, dst, send, recv, target):
    return pltpu.make_async_remote_copy(
        src_ref=src, dst_ref=dst, send_sem=send, recv_sem=recv, device_id=target, device_id_type=MESH
    )


def greet(targets):
    barrier = pltpu.get_barrier_semaphore()
    for target in targets:
        pl.semaphore_signal(barrier, inc=1, device_id=target, device_id_type=MESH)
    pl.semaphore_wait(barrier, len(targets))


def tp_peers():
    x, core, zh, q = place()
    peers = []
    for dc in (0, 1):
        for dq in (1, 3, 2, 0):
            if dc == 0 and dq == 0:
                continue
            other_core = lax.rem(core + dc, 2)
            to_q, from_q = lax.rem(q + dq, WAYS), lax.rem(q + WAYS - dq, WAYS)
            peers.append(
                (device(x, other_core, zh, to_q), other_core * WAYS + to_q, other_core * WAYS + from_q)
            )
    return peers


def neighbour(q, da, db):
    a, b = lax.rem(q, 2), q // 2
    return (1 - b if db else b) * 2 + (1 - a if da else a)


def total_rank():
    _, core, _, q = place()
    return core * WAYS + q


def dp_peers(zh_size):
    x, core, zh, q = place()
    side = device(1 - x, core, zh, q)
    far = []
    for dz in range(1, zh_size):
        to_z, from_z = lax.rem(zh + dz, zh_size), lax.rem(zh + zh_size - dz, zh_size)
        far.append((device(x, core, to_z, q), to_z, from_z))
    return side, far


def lanes_of(shape):
    return lax.broadcasted_iota(jnp.int32, shape, 1)


def encode(v):
    tail = v[:, RANK:]
    lane = lanes_of(tail.shape)
    high = tail.astype(bf16).astype(f32)
    low = pltpu.roll(tail - high, 32, 1)
    both = jnp.where(lane < 32, high, jnp.where(lane < 64, low, 0.0))
    return jnp.concatenate([v[:, :RANK].astype(bf16), both.astype(bf16)], axis=1)


def decode(v):
    tail = v[:, RANK:].astype(f32)
    lane = lanes_of(tail.shape)
    tail = jnp.where(lane < 32, tail + pltpu.roll(tail, 96, 1), 0.0)
    return jnp.concatenate([v[:, :RANK].astype(f32), tail], axis=1)


def halves(rows):
    return pl.ds(0, rows // 2), pl.ds(rows // 2, rows // 2)


class Gather:
    sems = staticmethod(lambda dma: [dma((6,)), dma((6,)), dma((4,)), dma((4,)), dma])

    def __init__(self, src, out, sems):
        self.src, self.out = src, out
        self.f_send, self.f_recv, self.s_send, self.s_recv, self.own_sem = sems
        x, core, zh, q = place()
        self.core, self.me = core, core * WAYS + q
        self.sibling = device(x, 1 - core, zh, q)
        self.chips = [neighbour(q, 0, 1), neighbour(q, 1, 0), neighbour(q, 1, 1)]
        self.b, self.a = [device(x, core, zh, c) for c in self.chips[:2]]
        self.top, self.low = halves(src.shape[0])

    def send(self, i, src, slot, rows, target):
        copy = remote(src, self.out.at[slot, rows], self.f_send.at[i], self.f_recv.at[i], target)
        copy.start()
        return copy

    def to_sibling(self, i, src, slot):
        copy = remote(src, self.out.at[slot], self.s_send.at[i], self.s_recv.at[i], self.sibling)
        copy.start()
        self.near.append(copy)

    def start(self):
        self.near = []
        self.first = [
            self.send(i, self.src.at[rows], self.me, rows, target)
            for i, (rows, target) in enumerate(
                ((self.top, self.b), (self.low, self.a), (self.low, self.b), (self.top, self.a))
            )
        ]
        self.to_sibling(3, self.src, self.me)
        self.own = pltpu.make_async_copy(self.src, self.out.at[self.me], self.own_sem)
        self.own.start()

    def relay(self):
        for i, rows, target in ((0, self.top, self.a), (1, self.low, self.b)):
            self.first[i].wait_recv()
            slot = self.core * WAYS + self.chips[i]
            self.first.append(self.send(4 + i, self.out.at[slot, rows], slot, rows, target))

    def rest(self):
        for i, ends in enumerate(((2,), (3,), (4, 5))):
            for k in ends:
                self.first[k].wait_recv()
            slot = self.core * WAYS + self.chips[i]
            self.to_sibling(i, self.out.at[slot], slot)

    def finish(self):
        for copy in self.first:
            copy.wait_send()
        for copy in self.near:
            copy.wait()
        self.own.wait()


class Scatter:
    sems = staticmethod(lambda dma: [dma((4,)), dma((4,)), dma((6,)), dma((6,))])

    @staticmethod
    def buffers(block):
        return [pltpu.VMEM((4,) + block, bf16), pltpu.VMEM((3,) + block, bf16), pltpu.VMEM((3,) + block, bf16)]

    def __init__(self, partial, buffers, sems):
        self.partial = partial
        self.near_buf, self.out, self.into = buffers
        self.s_send, self.s_recv, self.f_send, self.f_recv = sems
        x, core, zh, q = place()
        self.core = core
        self.sibling = device(x, 1 - core, zh, q)
        self.turns = [neighbour(q, 1, 1), neighbour(q, 1, 0), neighbour(q, 0, 1), q]
        self.a, self.b = [device(x, core, zh, t) for t in self.turns[1:3]]
        self.top, self.low = halves(partial.shape[1])
        self.near, self.first = [None] * 4, {}

    def to_sibling(self, i):
        slot = (1 - self.core) * WAYS + self.turns[i]
        self.near[i] = remote(
            self.partial.at[slot], self.near_buf.at[i], self.s_send.at[i], self.s_recv.at[i], self.sibling
        )
        self.near[i].start()

    def joined(self, i, rows=slice(None)):
        own = self.partial[self.core * WAYS + self.turns[i], rows]
        return own.astype(f32) + self.near_buf[i, rows].astype(f32)

    def send(self, k, i, rows, target):
        self.first[k] = remote(
            self.out.at[i, rows], self.into.at[i, rows], self.f_send.at[k], self.f_recv.at[k], target
        )
        self.first[k].start()

    def across(self, i):
        self.near[i].wait_recv()
        if i == 0:
            self.out[0] = self.joined(0).astype(bf16)
            self.send(0, 0, self.top, self.a)
            self.send(1, 0, self.low, self.b)
        else:
            rows, target = ((self.top, self.a), (self.low, self.b))[i - 1]
            self.out[i, rows] = self.joined(i, rows).astype(bf16)
            self.send(1 + i, i, rows, target)

    def sums(self):
        for k, i, rows, target in ((1, 1, self.low, self.a), (0, 2, self.top, self.b)):
            self.first[k].wait_recv()
            self.out[i, rows] = (self.joined(i, rows) + self.into[0, rows].astype(f32)).astype(bf16)
            self.send(3 + i, i, rows, target)

    def total(self):
        self.near[3].wait_recv()
        value = self.joined(3)
        for k in (2, 3, 4, 5):
            self.first[k].wait_recv()
        value = value + self.into[1].astype(f32) + self.into[2].astype(f32)
        for copy in self.near + list(self.first.values()):
            copy.wait_send()
        return value


class Spread:
    @staticmethod
    def sems(dma, zh_size):
        far = max(1, zh_size - 1)
        return [dma((far,)), dma((far,)), dma((zh_size,)), dma((zh_size,)), dma]

    def __init__(self, zh_size, src, view, sems, keep=True):
        self.src, self.view, self.keep = src, view, keep
        self.z_send, self.z_recv, self.x_send, self.x_recv, self.own_sem = sems
        self.x, _, self.zh, _ = place()
        self.side, self.far = dp_peers(zh_size)

    def start(self):
        dst = self.view(self.x, self.zh)
        self.along = [
            remote(self.src, dst, self.z_send.at[k], self.z_recv.at[k], target)
            for k, (target, _, _) in enumerate(self.far)
        ]
        self.over = [remote(self.src, dst, self.x_send.at[0], self.x_recv.at[0], self.side)]
        for copy in self.along + self.over:
            copy.start()
        if self.keep:
            self.own = pltpu.make_async_copy(self.src, dst, self.own_sem)
            self.own.start()

    def onward(self):
        for k, (_, _, source) in enumerate(self.far):
            self.along[k].wait_recv()
            slot = self.view(self.x, source)
            copy = remote(slot, slot, self.x_send.at[k + 1], self.x_recv.at[k + 1], self.side)
            copy.start()
            self.over.append(copy)

    def finish(self):
        for copy in self.along:
            copy.wait_send()
        for copy in self.over:
            copy.wait()
        if self.keep:
            self.own.wait()


class Sum:
    sems = staticmethod(lambda dma: [dma((TP - 1,))] * 4)

    def __init__(self, payload, parts, out, sems):
        self.payload, self.parts, self.out = payload, parts, out
        self.a_send, self.a_recv, self.b_send, self.b_recv = sems
        x, core, zh, q = place()
        self.me = core * WAYS + q
        self.peers = tp_peers()

    def start(self):
        self.one = [
            remote(self.payload.at[rank], self.parts.at[i], self.a_send.at[i], self.a_recv.at[i], target)
            for i, (target, rank, _) in enumerate(self.peers)
        ]
        for copy in self.one:
            copy.start()

    def middle(self, own):
        total = own
        for i in range(TP - 1):
            self.one[i].wait_recv()
            total = total + decode(self.parts[i])
        self.out[self.me] = encode(total)
        self.two = [
            remote(self.out.at[self.me], self.out.at[self.me], self.b_send.at[i], self.b_recv.at[i], target)
            for i, (target, _, _) in enumerate(self.peers)
        ]
        for copy in self.two:
            copy.start()

    def finish(self):
        for copy in self.one:
            copy.wait_send()
        for copy in self.two:
            copy.wait()


def call(body, name, collective, ins, outs, scratch, **options):
    names = list(ins) + list(outs) + list(scratch)

    def kernel(*refs):
        named, refs = {}, list(refs)
        flat = []
        for key in names:
            kind = scratch.get(key)
            if isinstance(kind, list):
                named[key] = refs[: len(kind)]
                refs = refs[len(kind) :]
            else:
                named[key] = refs.pop(0)
        body(named)

    flat = []
    for kind in scratch.values():
        flat += kind if isinstance(kind, list) else [kind]
    values = pl.pallas_call(
        kernel,
        out_shape=[shape for shape, _ in outs.values()],
        in_specs=[spec for _, spec in ins.values()],
        out_specs=[spec for _, spec in outs.values()],
        scratch_shapes=flat,
        compiler_params=pltpu.CompilerParams(
            collective_id=collective, has_side_effects=True, vmem_limit_bytes=63 * 2**20
        ),
        name=name,
    )(*[array for array, _ in ins.values()])
    return dict(zip(outs, values))


def spread_keys(kq, lane):
    a = kq.astype(bf16).astype(f32)
    rest = kq - a
    b = rest.astype(bf16).astype(f32)
    c = rest - b
    return jnp.where(lane < 32, a, jnp.where(lane < 64, b, c)).astype(bf16)


def spreader():
    one = np.repeat(np.eye(32, dtype=np.float32), 128, axis=1)
    return jnp.asarray(np.concatenate([one, one, one, np.zeros_like(one)], axis=0), bf16)


def folder():
    return jnp.asarray(np.pad(np.repeat(np.eye(32, dtype=np.float32), 128, axis=0), ((0, 0), (0, 96))), bf16)


def dot(a, b, contract, out=f32):
    return lax.dot_general(a, b, (contract, ((), ())), preferred_element_type=out)


def rms(stream):
    return lax.rsqrt(jnp.mean(jnp.square(stream), axis=-1, keepdims=True) + eps)


LANES = 128


def struct(*shape, dtype=f32):
    return jax.ShapeDtypeStruct(shape, dtype)


def side_by_side(pieces, lanes):
    each = LANES // lanes
    out = []
    for i in range(0, len(pieces), each):
        tile = pieces[i]
        for j in range(1, each):
            tile = tile + pltpu.roll(pieces[i + j], j * lanes, 1)
        out.append(tile)
    return jnp.concatenate(out, axis=1)


def opening(zh_size, gains, share, win, small, misc, mats, h, cot):
    groups = 2 * zh_size
    count = groups * TP
    tokens, width = h.shape
    half = groups * share
    dma = pltpu.SemaphoreType.DMA
    ins = dict(
        win=(win, HB), small=(small, VM), misc=(misc, VM), mats=(mats, HB), h=(h, VM), cot=(cot, VM)
    )
    outs = dict(
        win_all=(struct(count, *win.shape[1:], dtype=bf16), HB),
        mats_all=(struct(groups, *mats.shape, dtype=bf16), HB), vec=(struct(8 * LAYERS, half), VM),
        gains=(struct(8, width), VM), scale=(struct(TP, LANES), VM), grad=(struct(tokens, width), VM),
        gout=(struct(tokens, width, dtype=bf16), VM), xg=(struct(TP, tokens, width, dtype=bf16), HB),
    )
    spread = lambda: Spread.sems(dma, zh_size)
    scratch = dict(
        misc_all=pltpu.VMEM((count,) + misc.shape, f32), small_all=pltpu.VMEM((groups,) + small.shape, f32),
        normed=pltpu.VMEM((tokens, width), bf16), gather_sems=Gather.sems(dma),
        m_sems=[dma((TP - 1,))] * 2, w_sems=[dma((TP - 1,))] * 2,
        s0=spread(), s1=spread(),
    )
    for i in range(TP):
        scratch["sm%d" % i] = spread()
        scratch["sw%d" % i] = spread()

    def body(r):
        x, core, zh, q = place()
        me = core * WAYS + q
        peers = tp_peers()
        side, far = dp_peers(zh_size)
        greet([p[0] for p in peers] + [side] + [f[0] for f in far])

        def row(xx, zz, rank):
            return ((xx * 2 + rank // WAYS) * zh_size + zz) * WAYS + lax.rem(rank, WAYS)

        def views(out, rank):
            return lambda xx, zz: out.at[row(xx, zz, rank)]

        def exchange(src, out, slot, sems):
            copies = []
            for i, (target, rank, _) in enumerate(peers):
                copies.append(remote(src(rank), out.at[slot], sems[0].at[i], sems[1].at[i], target))
                copies[-1].start()
            return copies

        here = row(x, zh, me)
        miscs = exchange(lambda rank: r["misc"], r["misc_all"], here, r["m_sems"])
        misc_moves = [Spread(zh_size, r["misc"], views(r["misc_all"], me), r["sm0"])]
        misc_moves[0].start()
        smalls = Spread(zh_size, r["small"], lambda xx, zz: r["small_all"].at[xx * zh_size + zz], r["s0"])
        smalls.start()
        wins = exchange(lambda rank: r["win"].at[rank], r["win_all"], here, r["w_sems"])
        win_moves = [Spread(zh_size, r["win"].at[me], views(r["win_all"], me), r["sw0"])]
        for i, (_, _, source) in enumerate(peers):
            view = views(r["win_all"], source)
            win_moves.append(Spread(zh_size, view(x, zh), view, r["sw%d" % (i + 1)], keep=False))
        mats_move = Spread(zh_size, r["mats"], lambda xx, zz: r["mats_all"].at[xx * zh_size + zz], r["s1"])

        def step(i):
            if i >= 1:
                wins[i - 1].wait_recv()
            if i >= 2:
                win_moves[i - 2].onward()
            win_moves[i].start()

        step(0)
        for i, (_, _, source) in enumerate(peers):
            miscs[i].wait_recv()
            view = views(r["misc_all"], source)
            misc_moves.append(Spread(zh_size, view(x, zh), view, r["sm%d" % (i + 1)], keep=False))
            misc_moves[-1].start()
        step(1)
        for move in misc_moves:
            move.onward()
        smalls.onward()
        for move in misc_moves:
            move.finish()
        for l in range(LAYERS):
            r["gains"][l : l + 1, :] = side_by_side(
                [r["misc_all"][d, l : l + 1, :] for d in range(count)], gains
            )
        r["gains"][LAYERS:, :] = jnp.zeros((8 - LAYERS, width), f32)
        stream = r["h"][...]
        r["normed"][...] = (stream * rms(stream) * r["gains"][0:1, :]).astype(bf16)
        rows = Gather(r["normed"], r["xg"], r["gather_sems"])
        rows.start()
        step(2)
        mats_move.start()
        total = r["misc_all"][0, LAYERS : LAYERS + 1, :]
        for d in range(1, count):
            total = total + r["misc_all"][d, LAYERS : LAYERS + 1, :]
        inverse = count / total
        for rank in range(TP):
            r["scale"][rank : rank + 1, :] = r["misc_all"][row(x, zh, rank), LAYERS : LAYERS + 1, :] * inverse
        own = (r["misc"][LAYERS : LAYERS + 1, :] * inverse)[:, :1]
        grad = r["cot"][...] * own
        r["grad"][...] = grad
        r["gout"][...] = grad.astype(bf16)
        step(3)
        smalls.finish()
        for l in range(LAYERS):
            r["vec"][8 * l : 8 * (l + 1), :] = side_by_side(
                [r["small_all"][g, 8 * l : 8 * (l + 1), :] for g in range(groups)], share
            )
        step(4)
        mats_move.onward()
        rows.relay()
        step(5)
        step(6)
        rows.rest()
        step(7)
        win_moves[6].onward()
        win_moves[7].onward()
        for copy in miscs + wins:
            copy.wait_send()
        for move in win_moves + [mats_move]:
            move.finish()
        rows.finish()

    return call(body, "opening", 1, ins, outs, scratch)


def at_block(b, size):
    return pl.ds(pl.multiple_of(b * size, size), size)


def conv_of(entry, vec, row, size, c):
    cols = slice(c * LANES, (c + 1) * LANES)
    conv = vec[CONV : CONV + 1, cols]
    for j in range(CONV):
        conv = conv + vec[j : j + 1, cols] * entry[c, pl.ds(pl.multiple_of(row + TP * j, TP), size), :]
    return conv


def wide_of(ref, rows, parts):
    return jnp.concatenate([ref[c, rows, :] for c in range(parts)], axis=1)


def row_sum(value):
    return jnp.sum(value.reshape(-1, TP, value.shape[1]), axis=0)


def square_sum(kq):
    lane = lanes_of(kq.shape)
    return jnp.sum(jnp.where(lane < STATE, kq * kq, 0.0), axis=1, keepdims=True)


def forward_layer(zh_size, layer, xg, win, mats, wout, vec, scale, gout=None, nxt=None):
    tokens, width = xg.shape[1], xg.shape[2]
    half = win.shape[1] // 2
    parts = half // LANES
    rows = tokens * TP
    size = STEPS * TP
    blocks = rows // size
    halo = (CONV - 1) * TP
    dma = pltpu.SemaphoreType.DMA
    last = nxt is None
    groups = 2 * zh_size
    ins = dict(
        xg=(xg, VM), win=(win, VM), mats=(mats, VM), wout=(wout, HB), vec=(vec, VM),
        scale=(scale, VM), e=(spreader(), VM),
    )
    outs = dict(
        entry=(struct(2 * parts, halo + rows, LANES), VM), beta=(struct(parts, rows, LANES), VM),
        kq=(struct(rows, LANES), VM), proj=(struct(TP, size, 2 * LANES, dtype=bf16), VM),
        y=(struct(parts, rows, LANES), VM), keep=(struct(blocks, STATE, parts, TP, LANES), VM),
        mixed=(struct(TP, tokens, half, dtype=bf16), VM), stats=(struct(2, TP, LANES), VM),
    )
    scratch = dict(
        act=pltpu.VMEM((parts, rows, LANES), f32), step=pltpu.VMEM((parts, rows, LANES), f32),
        payload=pltpu.VMEM((TP, size, 2 * LANES), bf16), parts=pltpu.VMEM((TP - 1, size, 2 * LANES), bf16),
        own=pltpu.VMEM((size, 2 * LANES), f32),
        state=pltpu.VMEM((STATE, parts, TP, LANES), f32), wide=pltpu.VMEM((size, 32 * LANES), f32),
        part=pltpu.VMEM((TP, tokens, width), bf16),
        scatter_buf=Scatter.buffers((tokens, width)),
        sum_sems=Sum.sems(dma), scatter_sems=Scatter.sems(dma),
    )
    outs["wout_all"] = (struct(groups, *wout.shape, dtype=bf16), VM)
    scratch["d0"] = Spread.sems(dma, zh_size)
    if last:
        ins["gout"] = (gout, VM)
        outs["gog"] = (struct(TP, tokens, width, dtype=bf16), HB)
        scratch["gather_sems"] = Gather.sems(dma)
        outs["part"] = (struct(TP, tokens, width, dtype=bf16), VM)
        del scratch["part"], scratch["scatter_buf"], scratch["scatter_sems"]
    if not last:
        win1 = nxt["win"]
        ins.update(h=(nxt["h"], VM), gain=(nxt["gain"], VM), win1=(win1, HB), mats1=(nxt["mats"], HB))
        outs.update(
            result=(struct(tokens, width), VM),
            win1_all=(struct(2, 2, zh_size, WAYS, *win1.shape[1:], dtype=bf16), HB),
            mats1_all=(struct(groups, *nxt["mats"].shape, dtype=bf16), HB),
            xg1=(struct(TP, tokens, width, dtype=bf16), HB),
        )
        scratch.update(
            normed=pltpu.VMEM((tokens, width), bf16), gather_sems=Gather.sems(dma),
            turned=pltpu.VMEM(win1.shape, bf16), l_sems=[dma((TP - 1,)), dma((TP - 1,)), dma],
            d1=Spread.sems(dma, zh_size), d2=Spread.sems(dma, zh_size), d3=Spread.sems(dma, zh_size),
        )

    def body(r):
        side, far = dp_peers(zh_size)
        greet([p[0] for p in tp_peers()] + [side] + [f[0] for f in far])
        entry, act, step, beta, kq, y = r["entry"], r["act"], r["step"], r["beta"], r["kq"], r["y"]
        vec = r["vec"].at[8 * layer : 8 * (layer + 1)]
        index = lambda ref: lambda xx, zz: ref.at[xx * zh_size + zz]
        early = Spread(zh_size, r["wout"], index(r["wout_all"]), r["d0"])
        early.start()
        if last:
            gouts = Gather(r["gout"], r["gog"], r["gather_sems"])
        else:
            me = total_rank()
            turned = [pltpu.make_async_copy(r["win1"].at[me], r["turned"].at[me], r["l_sems"][2])]
            for i, (target, rank, _) in enumerate(tp_peers()):
                turned.append(
                    remote(r["win1"].at[rank], r["turned"].at[me], r["l_sems"][0].at[i], r["l_sems"][1].at[i], target)
                )
            for copy in turned:
                copy.start()
            moves = [Spread(zh_size, r["mats1"], index(r["mats1_all"]), r["d3"])]
            for k in range(2):
                view = lambda xx, zz, k=k: r["win1_all"].at[xx, k, zz]
                src = r["turned"].at[k * WAYS : (k + 1) * WAYS]
                moves.append(Spread(zh_size, src, view, r["d1" if k == 0 else "d2"]))

        entry[:, :halo, :] = jnp.zeros((2 * parts, halo, LANES), f32)
        tile = 2 * LANES
        for p in range(TP // 2):

            def columns(n, carry, p=p):
                cols = at_block(n, tile)
                out = jnp.dot(
                    r["xg"][2 * p : 2 * p + 2].reshape(2 * tokens, width), r["win"][:, cols],
                    preferred_element_type=f32,
                )
                for j in range(2):
                    for c in range(2):
                        entry[2 * n + c, pl.ds(halo + 2 * p + j, tokens, stride=TP), :] = out[
                            j * tokens : (j + 1) * tokens, c * LANES : (c + 1) * LANES
                        ]
                return carry

            lax.fori_loop(0, 2 * half // tile, columns, 0)
        if not last:
            for copy in turned:
                copy.wait()

        total = Sum(r["payload"], r["parts"], r["proj"], r["sum_sems"])

        def project(b, carry):
            rs = at_block(b, size)
            for c in range(parts):
                conv = conv_of(entry, vec, b * size, size, c)
                act[c, rs, :] = (conv * jax.nn.sigmoid(conv)).astype(bf16).astype(f32)
            out = jnp.dot(
                wide_of(act, rs, parts).astype(bf16), r["mats"][:, RANK:], preferred_element_type=f32
            )
            r["payload"][b] = encode(out)

            @pl.when(b == total.me)
            def _():
                r["own"][...] = out

            return carry

        lax.fori_loop(0, blocks, project, 0)
        total.start()
        total.middle(r["own"][...])
        total.finish()
        early.onward()
        if last:
            gouts.start()
        else:
            moves[0].start()
            moves[1].start()

        r["stats"][...] = jnp.zeros((2, TP, LANES), f32)

        def rates(b, carry):
            rs = at_block(b, size)
            tail = decode(r["proj"][b])[:, RANK:]
            keys = tail + pltpu.roll(tail, 32, 1) + pltpu.roll(tail, 64, 1)
            kq[rs, :] = keys
            norm = square_sum(keys)
            pre = dot(r["proj"][b, :, :RANK], r["mats"][:, :RANK], ((1,), (1,)))
            for c in range(parts):
                cols = slice(c * LANES, (c + 1) * LANES)
                rate = jax.nn.sigmoid(pre[:, cols] + vec[CONV + 1 : CONV + 2, cols])
                beta[c, rs, :] = rate
                step[c, rs, :] = rate / (1.0 + rate * norm)
                r["stats"][0] += row_sum(rate)
                r["stats"][1] = jnp.maximum(
                    r["stats"][1], jnp.max(rate.reshape(-1, TP, LANES), axis=0)
                )
            return carry

        lax.fori_loop(0, blocks, rates, 0)
        r["stats"][0] = r["stats"][0] * r["scale"][...]
        r["stats"][1] = r["stats"][1] * r["scale"][...]

        lane = lanes_of((size, LANES))
        state, wide = r["state"], r["wide"]
        state[...] = jnp.zeros_like(state)

        def block(b, carry):
            r["keep"][b] = state[...]
            wide[...] = jnp.dot(spread_keys(kq[at_block(b, size), :], lane), r["e"][...], preferred_element_type=f32)

            def one(j, carry):
                t = at_block(b * STEPS + j, TP)
                w = at_block(j, TP)
                acts = [act[c, t, :] for c in range(parts)]
                steps = [step[c, t, :] for c in range(parts)]
                sums = [None] * parts
                for n in range(STATE):
                    key = wide[w, n * LANES : (n + 1) * LANES]
                    query = wide[w, (STATE + n) * LANES : (STATE + n + 1) * LANES]
                    for c in range(parts):
                        s = state[n, c]
                        s = s + (steps[c] * key) * (acts[c] - key * s)
                        state[n, c] = s
                        sums[c] = s * query if sums[c] is None else sums[c] + s * query
                for c in range(parts):
                    y[c, t, :] = sums[c]
                return carry

            lax.fori_loop(0, STEPS, one, 0)
            rs = at_block(b, size)
            here = pl.ds(pl.multiple_of(b * STEPS, STEPS), STEPS)
            for c in range(parts):
                cols = slice(c * LANES, (c + 1) * LANES)
                gate = entry[parts + c, pl.ds(pl.multiple_of(b * size + halo, TP), size), :]
                skip = vec[CONV + 2 : CONV + 3, cols]
                step[c, rs, :] = (y[c, rs, :] + skip * act[c, rs, :]) * (gate * jax.nn.sigmoid(gate))
                for s in range(TP):
                    r["mixed"][s, here, cols] = step[c, pl.ds(b * size + s, STEPS, stride=TP), :].astype(bf16)
            return carry

        if last:
            lax.fori_loop(0, blocks, block, 0)
            gouts.relay()
        else:
            lax.fori_loop(0, blocks // 2, block, 0)
            moves[0].onward()
            moves[2].start()
            lax.fori_loop(blocks // 2, blocks, block, 0)
        early.finish()
        weight = lambda: r["wout_all"][...].reshape(half, width)
        if last:

            def plain(s, carry):
                r["part"][s] = dot(r["mixed"][s], weight(), ((1,), (0,))).astype(bf16)
                return carry

            lax.fori_loop(0, TP // 2, plain, 0)
            gouts.rest()
            lax.fori_loop(TP // 2, TP, plain, 0)
            gouts.finish()
            return
        moves[1].onward()
        scatter = Scatter(r["part"], r["scatter_buf"], r["scatter_sems"])
        out_partial(scatter, r["part"], r["mixed"], weight)
        moves[2].onward()
        stream = r["h"][...] + scatter.total()
        r["result"][...] = stream
        r["normed"][...] = (stream * rms(stream) * r["gain"][layer + 1 : layer + 2, :]).astype(bf16)
        spread = Gather(r["normed"], r["xg1"], r["gather_sems"])
        spread.start()
        spread.relay()
        spread.rest()
        spread.finish()
        for move in moves:
            move.finish()

    return call(body, "layer_forward_last" if last else "layer_forward", 7 if last else 6, ins, outs, scratch)


def out_partial(scatter, part, left, right, turned=False):
    contract = ((1,), (1,)) if turned else ((1,), (0,))
    for i in range(4):
        for core in (1 - scatter.core, scatter.core):
            slot = core * WAYS + scatter.turns[i]
            part[slot] = dot(left[slot], right(), contract).astype(bf16)
        scatter.to_sibling(i)
        if i >= 1:
            scatter.across(i - 1)
    scatter.sums()


class Reduce:
    @staticmethod
    def sems(dma, zh_size):
        far = max(1, zh_size - 1)
        return [dma, dma, dma((far,)), dma((far,))]

    @staticmethod
    def buffers(zh_size, block):
        return [
            pltpu.VMEM((zh_size,) + block, bf16), pltpu.VMEM((zh_size,) + block, bf16),
            pltpu.VMEM((max(1, zh_size - 1),) + block, bf16),
        ]

    def __init__(self, zh_size, src, buffers, sems):
        self.zh_size, self.src = zh_size, src
        self.near, self.mine, self.buf = buffers
        self.x_send, self.x_recv, self.z_send, self.z_recv = sems
        self.x, _, self.zh, _ = place()
        self.side, self.far = dp_peers(zh_size)

    def start(self):
        half = self.src.at[pl.ds((1 - self.x) * self.zh_size, self.zh_size)]
        self.over = remote(half, self.near, self.x_send, self.x_recv, self.side)
        self.over.start()

    def middle(self):
        self.over.wait_recv()
        for k in range(self.zh_size):
            self.mine[k] = (
                self.src[self.x * self.zh_size + k].astype(f32) + self.near[k].astype(f32)
            ).astype(bf16)
        self.along = [
            remote(self.mine.at[to_z], self.buf.at[k], self.z_send.at[k], self.z_recv.at[k], target)
            for k, (target, to_z, _) in enumerate(self.far)
        ]
        for copy in self.along:
            copy.start()

    def total(self):
        value = self.src[self.x * self.zh_size + self.zh].astype(f32) + self.near[self.zh].astype(f32)
        for k in range(self.zh_size - 1):
            self.along[k].wait_recv()
            value = value + self.buf[k].astype(f32)
        self.over.wait_send()
        for copy in self.along:
            copy.wait_send()
        return value


def backward_layer(zh_size, layer, kept, gog, wout, mats, vec, xg, win, gain, h, grad, late=None, part=None):
    tokens, width = xg.shape[1], xg.shape[2]
    half = win.shape[1] // 2
    parts = half // LANES
    rows = tokens * TP
    size = STEPS * TP
    blocks = rows // size
    halo = (CONV - 1) * TP
    groups = 2 * zh_size
    share = half // groups
    deep = width // (2 * groups)
    far = max(1, zh_size - 1)
    dma = pltpu.SemaphoreType.DMA
    onward = part is not None
    ins = {k: (kept[k], VM) for k in ("entry", "beta", "kq", "proj")}
    ins.update(
        mats=(mats, VM), wout=(wout, HB), vec=(vec, VM), gain=(gain, VM), h=(h, VM), grad=(grad, VM),
        mixed=(kept["mixed"], HB), e=(spreader(), VM), fold=(folder(), VM), keep=(kept["keep"], HB), gouts=(gog, HB), y=(kept["y"], HB), xg=(xg, HB), win=(win, HB),
    )
    outs = dict(
        prev=(struct(tokens, width), VM), ginner=(struct(groups, 2, deep, half, dtype=bf16), VM),
        near=(struct(zh_size, 2, deep, half, dtype=bf16), HB), ggate=(struct(2, deep, half, dtype=bf16), VM), gwout=(struct(share, width), VM),
        gmats=(struct(half, 3 * LANES, dtype=bf16), VM), gvec=(struct(8, half), VM),
        ggain=(struct(1, width), VM),
    )
    block_f32 = pltpu.VMEM((parts, rows, LANES), f32)
    scratch = dict(
        a=pltpu.VMEM((TP, tokens, width), bf16), b=pltpu.VMEM(win.shape, bf16),
        gs=block_f32, act=block_f32, gact=block_f32,
        step=pltpu.VMEM((parts, rows + halo, LANES), f32),
        states=pltpu.VMEM((STEPS + 1, STATE, parts, TP, LANES), f32),
        lam=pltpu.VMEM((STATE, parts, TP, LANES), f32), wide=pltpu.VMEM((size, 32 * LANES), f32),
        gstep=pltpu.VMEM((parts, size, LANES), f32),
        gentry=pltpu.VMEM((TP, tokens, 2 * half), bf16),
        payload=pltpu.VMEM((TP, size, 2 * LANES), bf16), parts=pltpu.VMEM((TP - 1, size, 2 * LANES), bf16),
        total=pltpu.VMEM((TP, size, 2 * LANES), bf16), own=pltpu.VMEM((size, 2 * LANES), f32),
        sums=pltpu.VMEM((8, parts, TP, LANES), f32),
        grate=pltpu.VMEM((half, LANES), f32), gselect=pltpu.VMEM((half, 2 * LANES), f32),
        gwo=pltpu.VMEM((groups, share, width), bf16), gwg=pltpu.VMEM((groups, 2, deep, half), bf16),
        gate_buf=Reduce.buffers(zh_size, (2, deep, half)), gate_sems=Reduce.sems(dma, zh_size),
        keeps=pltpu.VMEM((2, STATE, parts, TP, LANES), f32), keep_sems=dma((2,)),
        scatter_buf=Scatter.buffers((tokens, width)), reduce_buf=Reduce.buffers(zh_size, (share, width)),
        sum_sems=Sum.sems(dma), scatter_sems=Scatter.sems(dma), reduce_sems=Reduce.sems(dma, zh_size),
        loads=dma((7,)), over=[dma, dma],
    )
    if onward:
        outs["gog"] = (struct(TP, tokens, width, dtype=bf16), HB)
        ins["part"] = (part, HB)
        outs["parts_all"] = (struct(*part.shape, dtype=bf16), HB)
        scratch.update(part_sems=[dma((TP - 1,)), dma((TP - 1,)), dma])
        scratch.update(gout=pltpu.VMEM((tokens, width), bf16), gather_sems=Gather.sems(dma))
    if late is not None:
        ins["late"] = (late, HB)
        outs["late"] = (struct(far, *late.shape[1:], dtype=bf16), HB)
        scratch.update(late_sems=[dma((far,)), dma((far,))])
        ins["late_in"] = ins.pop("late")

    def body(r):
        x, core, zh, q = place()
        side, far_ones = dp_peers(zh_size)
        greet([p[0] for p in tp_peers()] + [side] + [f[0] for f in far_ones])
        entry, act, step, beta, kq = r["entry"], r["act"], r["step"], r["beta"], r["kq"]
        gs, gact, sums, gstep = r["gs"], r["gact"], r["sums"], r["gstep"]
        vec = r["vec"].at[8 * layer : 8 * (layer + 1)]
        loads = [
            pltpu.make_async_copy(src, dst, r["loads"].at[i])
            for i, (src, dst) in enumerate(
                (
                    (r["gouts"], r["a"]), (r["mixed"], r["gentry"].at[:, :, :half]),
                    (r["wout"].at[:, : 2 * half], r["b"].at[:half]), (r["wout"].at[:, 2 * half :], r["b"].at[half : 2 * half]),
                    (r["y"], gact), (r["xg"], r["a"]), (r["win"], r["b"]),
                )
            )
        ]
        for copy in loads[:5]:
            copy.start()
        passed = []
        if onward:
            me = core * WAYS + q
            for i, (target, rank, _) in enumerate(tp_peers()):
                copy = remote(
                    r["part"].at[rank], r["parts_all"].at[me], r["part_sems"][0].at[i], r["part_sems"][1].at[i], target
                )
                copy.start()
                passed.append(copy)
            passed.append(pltpu.make_async_copy(r["part"].at[me], r["parts_all"].at[me], r["part_sems"][2]))
            passed[-1].start()
        if late is not None:
            for k, (target, to_z, _) in enumerate(far_ones):
                copy = remote(
                    r["late_in"].at[to_z], r["late"].at[k], r["late_sems"][0].at[k], r["late_sems"][1].at[k], target
                )
                copy.start()
                passed.append(copy)
        sums[...] = jnp.zeros_like(sums)
        r["grate"][...] = jnp.zeros_like(r["grate"])
        r["gselect"][...] = jnp.zeros_like(r["gselect"])

        def again(b, carry):
            rs = at_block(b, size)
            norm = square_sum(kq[rs, :])
            for c in range(parts):
                conv = conv_of(entry, vec, b * size, size, c)
                act[c, rs, :] = (conv * jax.nn.sigmoid(conv)).astype(bf16).astype(f32)
                rate = beta[c, rs, :]
                step[c, rs, :] = rate / (1.0 + rate * norm)
            return carry

        lax.fori_loop(0, blocks, again, 0)
        loads[0].wait()
        loads[1].wait()

        def outer(c, carry):
            left = r["gentry"][:, :, at_block(c, LANES)].reshape(rows, LANES)
            out = dot(left, r["a"][...].reshape(rows, width), ((0,), (0,))).astype(bf16)
            each = LANES // share
            r["gwo"][pl.ds(c * each, each)] = out.reshape(each, share, width)
            return carry

        lax.fori_loop(0, parts, outer, 0)
        reduce = Reduce(zh_size, r["gwo"], r["reduce_buf"], r["reduce_sems"])
        reduce.start()
        loads[2].wait()
        loads[3].wait()
        for p in range(TP // 2):

            def columns(n, carry, p=p):
                out = 0.0
                for k in range(2):
                    left = r["a"][2 * p : 2 * p + 2, :, 2 * half * k : 2 * half * (k + 1)].reshape(2 * tokens, 2 * half)
                    right = r["b"][pl.ds(pl.multiple_of(half * k + n * 2 * LANES, 2 * LANES), 2 * LANES), :]
                    out = out + dot(left, right, ((1,), (1,)))
                for j in range(2):
                    for c in range(2):
                        gs[2 * n + c, pl.ds(2 * p + j, tokens, stride=TP), :] = out[
                            j * tokens : (j + 1) * tokens, c * LANES : (c + 1) * LANES
                        ]
                return carry

            lax.fori_loop(0, half // (2 * LANES), columns, 0)
        loads[5].start()
        loads[6].start()
        loads[4].wait()

        def gates(b, carry):
            rs = at_block(b, size)
            here = pl.ds(pl.multiple_of(b * STEPS, STEPS), STEPS)
            for c in range(parts):
                cols = slice(c * LANES, (c + 1) * LANES)
                gate = entry[parts + c, pl.ds(pl.multiple_of(b * size + halo, TP), size), :]
                sig = jax.nn.sigmoid(gate)
                g = gs[c, rs, :]
                a = act[c, rs, :]
                down = g * (gate * sig)
                gstep[c] = g * (gact[c, rs, :] + vec[CONV + 2 : CONV + 3, cols] * a) * (
                    sig * (1.0 + gate * (1.0 - sig))
                )
                gs[c, rs, :] = down
                sums[CONV + 2, c] += row_sum(down * a)
                for s in range(TP):
                    r["gentry"][s, here, half + c * LANES : half + (c + 1) * LANES] = gstep[
                        c, pl.ds(s, STEPS, stride=TP), :
                    ].astype(bf16)
            return carry

        lax.fori_loop(0, blocks, gates, 0)
        loads[5].wait()
        tile = 2 * LANES

        def outer_in(out_ref, first, i, carry):
            left = r["a"][:, :, at_block(i, tile)].reshape(rows, tile)
            out = dot(left, r["gentry"][:, :, first : first + half].reshape(rows, half), ((0,), (0,))).astype(bf16)
            each = tile // deep
            for e in range(each):
                d = i * each + e
                xx, cc, zz = d // (2 * zh_size), lax.rem(d // zh_size, 2), lax.rem(d, zh_size)
                out_ref[xx * zh_size + zz, cc] = out[e * deep : (e + 1) * deep]
            return carry

        lax.fori_loop(0, width // tile, lambda i, k: outer_in(r["gwg"], half, i, k), 0)
        gate_reduce = Reduce(zh_size, r["gwg"], r["gate_buf"], r["gate_sems"])

        lane = lanes_of((size, LANES))
        states, lam, wide = r["states"], r["lam"], r["wide"]
        lam[...] = jnp.zeros_like(lam)
        plus = lambda a, b: b if a is None else a + b
        total = Sum(r["payload"], r["parts"], r["total"], r["sum_sems"])

        def block(bi, carry):
            b = blocks - 1 - bi
            rs = at_block(b, size)
            slot = lax.rem(b, 2)
            pltpu.make_async_copy(r["keep"].at[b], r["keeps"].at[slot], r["keep_sems"].at[slot]).wait()

            @pl.when(b > 0)
            def _():
                ahead = pltpu.make_async_copy(r["keep"].at[b - 1], r["keeps"].at[1 - slot], r["keep_sems"].at[1 - slot])
                ahead.start()

            states[0] = r["keeps"][slot]
            wide[...] = jnp.dot(spread_keys(kq[rs, :], lane), r["e"][...], preferred_element_type=f32)

            def replay(j, carry):
                t, w = at_block(b * STEPS + j, TP), at_block(j, TP)
                acts = [act[c, t, :] for c in range(parts)]
                steps = [step[c, t, :] for c in range(parts)]
                for n in range(STATE):
                    key = wide[w, n * LANES : (n + 1) * LANES]
                    for c in range(parts):
                        s = states[j, n, c]
                        states[j + 1, n, c] = s + (steps[c] * key) * (acts[c] - key * s)
                return carry

            lax.fori_loop(0, STEPS, replay, 0)

            def back(jj, carry):
                j = STEPS - 1 - jj
                t, w = at_block(b * STEPS + j, TP), at_block(j, TP)
                acts = [act[c, t, :] for c in range(parts)]
                steps = [step[c, t, :] for c in range(parts)]
                gsums = [gs[c, t, :] for c in range(parts)]
                first, second = [None] * parts, [None] * parts
                for n in range(STATE):
                    kcols, qcols = slice(n * LANES, (n + 1) * LANES), slice((STATE + n) * LANES, (STATE + n + 1) * LANES)
                    key, query = wide[w, kcols], wide[w, qcols]
                    key_term, query_term = None, None
                    for c in range(parts):
                        before, after = states[j, n, c], states[j + 1, n, c]
                        grad = lam[n, c] + gsums[c] * query
                        u = key * before
                        d = acts[c] - u
                        gk = grad * key
                        first[c] = plus(first[c], gk * d)
                        second[c] = plus(second[c], gk)
                        key_term = plus(key_term, (steps[c] * grad) * (d - u))
                        query_term = plus(query_term, gsums[c] * after)
                        lam[n, c] = grad - (steps[c] * key) * gk
                    wide[w, kcols] = key_term
                    wide[w, qcols] = query_term
                for c in range(parts):
                    gstep[c, w, :] = first[c]
                    gact[c, t, :] = steps[c] * second[c]
                return carry

            lax.fori_loop(0, STEPS, back, 0)
            terms = wide[...]
            high = terms.astype(bf16)
            low = (terms - high.astype(f32)).astype(bf16)
            gkq = jnp.dot(high, r["fold"][...], preferred_element_type=f32) + jnp.dot(
                low, r["fold"][...], preferred_element_type=f32
            )
            keys = kq[rs, :]
            norm = square_sum(keys)
            gnorm = jnp.zeros((size, 1), f32)
            grates = []
            for c in range(parts):
                cols = slice(c * LANES, (c + 1) * LANES)
                rate = beta[c, rs, :]
                g = gstep[c]
                inverse = 1.0 + rate * norm
                inverse = 1.0 / (inverse * inverse)
                gnorm = gnorm - jnp.sum(g * (rate * rate * inverse), axis=1, keepdims=True)
                grate = g * inverse * rate * (1.0 - rate)
                sums[CONV + 1, c] += row_sum(grate)
                grates.append(grate.astype(bf16))
                gact[c, rs, :] += vec[CONV + 2 : CONV + 3, cols] * gs[c, rs, :]
            grate = jnp.concatenate(grates, axis=1)
            r["grate"][...] += dot(grate, r["proj"][b, :, :RANK], ((0,), (0,)))
            grank = dot(grate, r["mats"][:, :RANK], ((1,), (0,)))
            gkq = gkq + jnp.where(lane < STATE, 2.0 * keys * gnorm, 0.0)
            out = jnp.concatenate([grank, gkq], axis=1)
            r["payload"][b] = encode(out)

            @pl.when(b == total.me)
            def _():
                r["own"][...] = out

            return carry

        last = (blocks - 1) % 2
        pltpu.make_async_copy(r["keep"].at[blocks - 1], r["keeps"].at[last], r["keep_sems"].at[last]).start()
        lax.fori_loop(0, blocks // 2, block, 0)
        reduce.middle()
        gate_reduce.start()
        lax.fori_loop(blocks // 2, blocks, block, 0)
        total.start()
        total.middle(r["own"][...])
        total.finish()
        gate_reduce.middle()
        step[:, rows:, :] = jnp.zeros((parts, halo, LANES), f32)
        gconv = step

        def convs(b, carry):
            rs = at_block(b, size)
            gp = r["total"][b]
            gp = jnp.where(lanes_of(gp.shape) < RANK + 2 * STATE, gp.astype(f32), 0.0).astype(bf16)
            r["gselect"][...] += dot(wide_of(act, rs, parts).astype(bf16), gp, ((0,), (0,)))
            more = dot(gp, r["mats"][:, RANK:], ((1,), (1,)))
            for c in range(parts):
                conv = conv_of(entry, vec, b * size, size, c)
                sig = jax.nn.sigmoid(conv)
                g = (gact[c, rs, :] + more[:, c * LANES : (c + 1) * LANES]) * (sig * (1.0 + conv * (1.0 - sig)))
                gconv[c, rs, :] = g
                sums[CONV, c] += row_sum(g)
                for j in range(CONV):
                    inner = entry[c, pl.ds(pl.multiple_of(b * size + TP * j, TP), size), :]
                    sums[j, c] += row_sum(g * inner)
            return carry

        lax.fori_loop(0, blocks, convs, 0)

        def inners(b, carry):
            rs = at_block(b, size)
            here = pl.ds(pl.multiple_of(b * STEPS, STEPS), STEPS)
            for c in range(parts):
                cols = slice(c * LANES, (c + 1) * LANES)
                value = None
                for j in range(CONV):
                    at = pl.ds(pl.multiple_of(b * size + TP * (CONV - 1 - j), TP), size)
                    value = plus(value, vec[j : j + 1, cols] * gconv[c, at, :])
                gs[c, rs, :] = value
                for s in range(TP):
                    at = pl.ds(b * size + s, STEPS, stride=TP)
                    r["gentry"][s, here, cols] = gs[c, at, :].astype(bf16)
            return carry

        lax.fori_loop(0, blocks, inners, 0)
        lax.fori_loop(0, width // tile, lambda i, k: outer_in(r["ginner"], 0, i, k), 0)
        over = remote(
            r["ginner"].at[pl.ds((1 - x) * zh_size, zh_size)], r["near"], r["over"][0], r["over"][1], side
        )
        over.start()
        loads[6].wait()
        scatter = Scatter(r["a"], r["scatter_buf"], r["scatter_sems"])
        out_partial(scatter, r["a"], r["gentry"], lambda: r["b"][...], turned=True)
        r["gmats"][:, :RANK] = r["grate"][...].astype(bf16)
        r["gmats"][:, RANK:] = r["gselect"][...].astype(bf16)
        for j in range(8):
            for c in range(parts):
                r["gvec"][j : j + 1, c * LANES : (c + 1) * LANES] = jnp.sum(sums[j, c], axis=0, keepdims=True)
        r["gwout"][...] = reduce.total()
        r["ggate"][...] = gate_reduce.total().astype(bf16)
        gnormed = scatter.total()
        stream = r["h"][...]
        scale = rms(stream)
        r["ggain"][...] = jnp.sum(gnormed * stream * scale, axis=0, keepdims=True)
        scaled = gnormed * r["gain"][layer : layer + 1, :]
        grad = r["grad"][...] + scale * scaled - stream * (scale * scale * scale) * jnp.mean(
            stream * scaled, axis=-1, keepdims=True
        )
        r["prev"][...] = grad
        if onward:
            r["gout"][...] = grad.astype(bf16)
            spread = Gather(r["gout"], r["gog"], r["gather_sems"])
            spread.start()
            spread.relay()
            spread.rest()
            spread.finish()
        for copy in passed:
            copy.wait()
        over.wait()

    return call(body, "layer_backward", 9 if onward else 8, ins, outs, scratch)


def closing(zh_size, inner, near, mats, small, stats, gain, turns, gwouts, select):
    groups = 2 * zh_size
    count = groups * TP
    far_n = max(1, zh_size - 1)
    dma = pltpu.SemaphoreType.DMA
    depth, half = inner.shape[3] // WAYS, inner.shape[4]
    share, width = gwouts[0].shape
    gains = width // count
    every = (2, zh_size) + stats.shape
    v = pltpu.VMEM
    ins = dict(
        inner=(inner, VM), near=(near, VM), mats=(mats, VM), small=(small, VM), stats=(stats, VM), gain=(gain, VM),
        t0=(turns[0], VM), t1=(turns[1], VM), t2=(turns[2], VM), w0=(gwouts[0], VM), w1=(gwouts[1], VM),
    )
    outs = dict(
        gin=(struct(LAYERS, depth, 2 * count * share), VM), gselect=(struct(LAYERS, share, select), VM),
        grate=(struct(LAYERS, RANK, share), VM), gwout=(struct(LAYERS, share, width), VM),
        ggain=(struct(LAYERS, gains), VM), gtaps=(struct(LAYERS, CONV, share), VM), gshift=(struct(LAYERS, share), VM),
        grate_shift=(struct(LAYERS, share), VM), gskip=(struct(LAYERS, share), VM), stats_all=(struct(*stats.shape), VM),
    )
    chunk = lambda shape, dtype: dict(
        s=v(shape[1:], dtype), z=v((far_n,) + shape[2:], dtype), z_sems=[dma((far_n,)), dma((far_n,))]
    )
    shapes = dict(
        c0=(inner.shape[:2] + inner.shape[3:], bf16), c1=(inner.shape[:2] + inner.shape[3:], bf16),
        mats=(mats.shape, bf16), small=(small.shape, f32), stats=(every, f32),
    )
    scratch = dict(
        vectors=v(small.shape, f32), stats_v=v(every, f32), stats_t=v((TP - 1,) + stats.shape, f32),
        gain_t=v((TP - 1,) + gain.shape[1:], f32), win_t=v((2, WAYS, depth, half), bf16),
        total=v(small.shape[2:], f32),
        g_sems=[dma((TP - 1,))] * 2, s_sems=[dma((TP - 1,))] * 2,
    )
    for i in range(4):
        scratch["b%d" % i] = v((TP, depth, half), bf16)
        scratch["b%d_sems" % i] = [dma((TP - 1,)), dma((TP - 1,))]
    for name, (shape, dtype) in shapes.items():
        for key, value in chunk(shape, dtype).items():
            scratch[name + "_" + key] = value
        if name not in ("c0", "c1"):
            scratch[name + "_near"] = v(shape[1:], dtype)
            scratch[name + "_x"] = [dma, dma]

    def body(r):
        x, core, zh, q = place()
        me = core * WAYS + q
        peers = tp_peers()
        side, far = dp_peers(zh_size)
        greet([p[0] for p in peers] + [side] + [f[0] for f in far])
        sent, full = [], []

        def join(a, b, peaks):
            a, b = a.astype(f32), b.astype(f32)
            if peaks:
                line = lax.broadcasted_iota(jnp.int32, a.shape, len(a.shape) - 2)
                return jnp.where(line < 4, a + b, jnp.maximum(a, b))
            return a + b

        class Chunk:
            def __init__(self, name, src, near=None):
                self.name, self.src, self.near, self.peaks = name, src, near, name == "stats"

            def start(self):
                self.near = r[self.name + "_near"]
                sems = r[self.name + "_x"]
                self.over = remote(self.src.at[1 - x], self.near, sems[0], sems[1], side)
                self.over.start()
                sent.append(self.over)

            def middle(self, arrived=False):
                if not arrived:
                    self.over.wait_recv()
                mine, buf, sems = r[self.name + "_s"], r[self.name + "_z"], r[self.name + "_z_sems"]
                mine[...] = join(self.src[x], self.near[...], self.peaks).astype(mine.dtype)
                self.along = [
                    remote(mine.at[to_z], buf.at[k], sems[0].at[k], sems[1].at[k], target)
                    for k, (target, to_z, _) in enumerate(far)
                ]
                for copy in self.along:
                    copy.start()
                    sent.append(copy)

            def total(self):
                value = join(self.src[x, zh], self.near[zh], self.peaks)
                for k, copy in enumerate(self.along):
                    copy.wait_recv()
                    value = join(value, r[self.name + "_z"][k], self.peaks)
                return value

        def turn(src, i):
            box, sems = r["b%d" % i], r["b%d_sems" % i]
            for k, (target, rank, _) in enumerate(peers):
                copy = remote(src(rank), box.at[me], sems[0].at[k], sems[1].at[k], target)
                copy.start()
                full.append(copy)
            box[me] = src(me)[...]

        cs = [Chunk("c%d" % c, r["inner"].at[:, :, c], r["near"].at[:, c]) for c in range(2)]
        cs[0].middle(arrived=True)
        cs[1].middle(arrived=True)
        gained, shown = [], []
        for i, (target, rank, _) in enumerate(peers):
            for src, buf, sems, copies in (
                (r["gain"].at[rank], r["gain_t"], r["g_sems"], gained),
                (r["stats"], r["stats_t"], r["s_sems"], shown),
            ):
                copy = remote(src, buf.at[i], sems[0].at[i], sems[1].at[i], target)
                copy.start()
                copies.append(copy)
                sent.append(copy)
        mats_c = Chunk("mats", r["mats"])
        mats_c.start()
        for l in range(LAYERS):
            r["gwout"][l] = r["w%d" % l][...]
        for i in range(3):
            turn(lambda rank, i=i: r["t%d" % i].at[rank], i + 1)
        total = r["gain"][me]
        seen = r["stats"][...]
        for i in range(TP - 1):
            gained[i].wait_recv()
            total = total + r["gain_t"][i]
            shown[i].wait_recv()
            seen = join(seen, r["stats_t"][i], True)
        r["vectors"][...] = r["small"][...]
        for l in range(LAYERS):
            for g in range(groups):
                at = l * groups + g
                r["vectors"][g // zh_size, g % zh_size, l * 16 + 8 : l * 16 + 9, :] = total[at : at + 1, :]
        r["stats_v"][...] = jnp.broadcast_to(seen, every)
        rest = [mats_c, Chunk("small", r["vectors"]), Chunk("stats", r["stats_v"])]
        for c in rest[1:]:
            c.start()
        for c in rest:
            c.middle()
        for c in range(2):
            r["win_t"][c] = cs[c].total().astype(bf16).reshape(WAYS, depth, half)
        turn(lambda rank: r["win_t"].at[rank // WAYS, lax.rem(rank, WAYS)], 0)
        m = rest[0].total()
        for l in range(LAYERS):
            base = 3 * LANES * l
            r["grate"][l] = m[:, base : base + RANK].T
            r["gselect"][l] = m[:, base + RANK : base + RANK + select]
        r["total"][...] = rest[1].total()
        for l in range(LAYERS):
            r["gtaps"][l] = r["total"][16 * l : 16 * l + CONV, :share]
            for name, j, size in (
                ("gshift", CONV, share), ("grate_shift", CONV + 1, share), ("gskip", CONV + 2, share), ("ggain", 8, gains)
            ):
                r[name][l : l + 1, :] = r["total"][16 * l + j : 16 * l + j + 1, :size]
        r["stats_all"][...] = rest[2].total()

        def lay(box, l, at):
            for rank in range(TP):
                for g in range(groups):
                    d = ((g // zh_size * 2 + rank // WAYS) * zh_size + g % zh_size) * WAYS + rank % WAYS
                    r["gin"][l, :, at + d * share : at + (d + 1) * share] = box[
                        rank, :, g * share : (g + 1) * share
                    ].astype(f32)

        boxes = {0: (0, 0), 1: (0, count * share), 2: (1, 0), 3: (1, count * share)}
        done = full[: 3 * (TP - 1)]
        for copy in done:
            copy.wait_recv()
        for i in (1, 2, 3):
            lay(r["b%d" % i], *boxes[i])
        late = full[3 * (TP - 1) :]
        for copy in late:
            copy.wait_recv()
        lay(r["b0"], *boxes[0])
        for copy in sent + done + late:
            copy.wait_send()

    return call(body, "closing", 5, ins, outs, scratch)


def on_device(
    hidden, cotangent, groups, group_weights, input_weight, select_weight, rate_weight,
    output_weight, norm_gain, conv_taps, conv_shift, rate_shift, skip_gain,
):
    fsdp = lax.axis_size("fsdp")
    zh_size = fsdp // WAYS
    count = 2 * 2 * fsdp
    group_count = 2 * zh_size
    share = conv_shift.shape[1]
    gains = norm_gain.shape[1]
    depth = input_weight.shape[1]
    half = group_count * share
    x, core, zh, q = place()

    labels = jnp.arange(group_weights.shape[0])
    own_weight = jnp.sum(jnp.where(groups[:, None] == labels[None, :], group_weights[None, :], 0.0))

    wins = input_weight.reshape(LAYERS, depth, 2, 2, 2, zh_size, WAYS, share)
    wins = wins.transpose(0, 4, 6, 1, 2, 3, 5, 7).reshape(LAYERS, TP, depth, 2 * half)
    mats = jnp.concatenate([rate_weight.swapaxes(1, 2), select_weight], axis=2)
    mats = jnp.pad(mats, ((0, 0), (0, 0), (0, 3 * LANES - mats.shape[2])))
    vectors = [conv_taps, conv_shift[:, None], rate_shift[:, None], skip_gain[:, None], skip_gain[:, None]]
    small = jnp.concatenate(vectors, axis=1).astype(f32).reshape(8 * LAYERS, share)
    small = jnp.pad(small, ((0, 0), (0, LANES - share)))
    misc = jnp.pad(norm_gain.astype(f32), ((0, 0), (0, LANES - gains)))
    misc = jnp.concatenate([misc, jnp.full((8 - LAYERS, LANES), own_weight)])

    flat = lambda a: a.reshape(half, -1)
    h0 = hidden[0]
    start = opening(zh_size, gains, share, wins[0], small, misc, mats[0], h0, cotangent[0])
    vec, gain, scale = start["vec"], start["gains"], start["scale"]
    win0, mat0 = start["win_all"].reshape(count * depth, -1), flat(start["mats_all"])
    one = forward_layer(
        zh_size, 0, start["xg"], win0, mat0, output_weight[0], vec, scale,
        nxt=dict(h=h0, gain=gain, win=wins[1], mats=mats[1]),
    )
    win1, mat1 = one["win1_all"].reshape(count * depth, -1), flat(one["mats1_all"])
    h1 = one["result"]
    two = forward_layer(zh_size, 1, one["xg1"], win1, mat1, output_weight[1], vec, scale, gout=start["gout"])

    down1 = backward_layer(
        zh_size, 1, two, two["gog"], flat(two["wout_all"]), mat1, vec, one["xg1"], win1, gain, h1, start["grad"],
        part=two["part"],
    )
    stream = h1 + jnp.sum(down1["parts_all"].astype(f32), axis=0)
    blocks = (2, zh_size) + down1["ginner"].shape[1:]
    pick = lambda a, i: lax.dynamic_index_in_dim(a, i, 0, keepdims=False)
    summed = pick(down1["ginner"].reshape(blocks), x).astype(f32) + down1["near"].astype(f32)
    down0 = backward_layer(
        zh_size, 0, one, down1["gog"], flat(one["wout_all"]), mat0, vec, start["xg"], win0, gain, h0, down1["prev"],
        late=summed.astype(bf16),
    )
    late = pick(summed, zh)
    for k in range(zh_size - 1):
        late = late + down0["late"][k].astype(f32)

    sums = [jnp.sum(o["stats"][0]) for o in (one, two)]
    peaks = [jnp.max(o["stats"][1]) for o in (one, two)]
    pad = [jnp.zeros((), f32)] * (4 - LAYERS)
    own_stats = jnp.broadcast_to(jnp.stack(sums + pad + peaks + pad)[:, None], (8, LANES))
    downs = (down0, down1)
    small = jnp.stack([down["gvec"] for down in downs]).reshape(LAYERS, 8, group_count, share)
    small = jnp.pad(small.transpose(2, 0, 1, 3), ((0, 0), (0, 0), (0, 8), (0, LANES - share)))
    small = small.reshape(2, zh_size, 16 * LAYERS, LANES)
    spread_gain = jnp.stack([down["ggain"][0] for down in downs]).reshape(LAYERS, 2, 2, zh_size, WAYS, gains)
    spread_gain = spread_gain.transpose(2, 4, 0, 1, 3, 5).reshape(TP, LAYERS * group_count, gains)
    spread_gain = jnp.pad(spread_gain, ((0, 0), (0, -LAYERS * group_count % 8), (0, LANES - gains)))
    mats = jnp.concatenate([down["gmats"] for down in downs], axis=1).reshape(2, zh_size, share, -1)
    turns = [down0["ggate"], late.astype(bf16), down1["ggate"]]
    end = closing(
        zh_size, down0["ginner"].reshape(blocks), down0["near"], mats, small, own_stats, spread_gain,
        [t.reshape(TP, depth, half) for t in turns], [down["gwout"] for down in downs], select_weight.shape[2],
    )
    stats = end["stats_all"]
    beta_mean = stats[:LAYERS, 0] / (count * hidden.shape[1] * INNER)
    beta_max = stats[4 : 4 + LAYERS, 0]
    names = ("gin", "gselect", "grate", "gwout", "ggain", "gtaps", "gshift", "grate_shift", "gskip")
    return (stream[None], down0["prev"][None]) + tuple(end[n] for n in names) + (beta_mean, beta_max)


def solution(mesh):
    both = ("dp", "fsdp")
    placed = (
        P(both, None, None), P(both, None, None), P(both), P(),
        P(None, both, None), P(None, both, None), P(None, None, both), P(None, both, None),
        P(None, both), P(None, None, both), P(None, both), P(None, both), P(None, both),
    )
    return jax.shard_map(
        on_device,
        mesh=mesh,
        in_specs=placed,
        out_specs=(P(both, None, None), P(both, None, None)) + placed[4:] + (P(), P()),
        check_vma=False,
    )
```

time: 827 us -> 668 us (0.81)
  Pallas kernels: 743 us -> 606 us
  other arithmetic: 38.4 us -> 15.5 us
    pallas_call x4 -> x0, Pallas kernels: 198 us -> none  [the longest x1 71.9 us: scatter_gradients(): pl.pallas_call(functools.partial(gradients_kernel, zh_size), out_shape=[b...]
    pallas_call x4 -> x6, Pallas kernels: 545 us -> 606 us  [call(): pl.pallas_call(kernel, out_shape=[shape for shape, _ in outs.values()], i...]
    unnamed x40 -> x46, local copies, waits for them, and re-layouts: 4.12 us -> 15.6 us
where the time goes in v4:
time: 668 us; the launch traced here: 660 us
  Pallas kernels  606 us (91%)
  local copies, waits for them, and re-layouts  36.8 us (6%)
  other arithmetic  15.5 us (2%)
    pallas_call x6, Pallas kernels, call(): pl.pallas_call(kernel, out_shape=[shape for shape, _ in outs.values()], i...  606 us
    unnamed x46, local copies, waits for them, and re-layouts  15.6 us

profile of v4, /device:TPU:0, one launch (start us, length us, event | category | flops | bytes accessed | tf_op | source)
XLA Modules:
  0.0 660.4 jit_solution(14747660488330693214)
XLA Ops:
  1.3 1.3 fusion.3
  2.6 0.7 pad_convert_fusion
  3.2 0.7 copy.44
  3.9 0.7 copy.45
  4.6 0.7 copy.46
  5.2 0.7 concatenate.13
  5.9 1.2 concatenate.14.refs_2_
  7.2 0.6 bitcast_convert_fusion.refs_1_
  7.8 0.9 copy.48
  8.7 1.0 copy.49
  9.8 0.7 slice_bitcast_fusion.2
  10.5 2.3 slice_bitcast_fusion
  12.7 3.2 reshape.103
  16.0 1.8 copy.55
  17.7 1.5 fusion.5
  19.2 1.5 squeeze.42.refs_9_
  20.8 1.5 squeeze.37.refs_0_
  22.3 77.2 %opening.1 = (bf16[32,64,1024]{2,1,0:T(8,128)(2,1)}, bf16[4,128,384]{2,1,0:T(8,128)(2,1)}, f32[16,512]{1,0:T(8,128)}, f32[8,2048]{1,0:T(8,128)}, f32[8,128]{1,0:...) custom-call(bf16[8,64,1024]{2,1,0:T(8,128)(2,1)} %squeeze.37.refs_0_, ...), custom_call_target="tpu_custom_call" | custom-call | tf_op jit(solution)/shard_map/opening/pallas_call | solution.py:325
  99.5 137.2 %layer_forward.1 = (f32[8,1048,128]{2,1,0:T(8,128)}, f32[4,1024,128]{2,1,0:T(8,128)}, f32[1024,128]{1,0:T(8,128)}, bf16[8,128,256]{2,1,0:T(8,128)(2,1)}, f32[4,1...) custom-call(bf16[8,128,2048]{2,1,0:T(8,128)(2,1)} %get-tuple-element, ...), custom_call_target="tpu_custom_call" | custom-call | tf_op jit(solution)/shard_map/layer_forward/pallas_call | solution.py:325
  236.7 1.3 slice_reduce_fusion.1
  238.0 74.3 %layer_forward_last.1 = (f32[8,1048,128]{2,1,0:T(8,128)}, f32[4,1024,128]{2,1,0:T(8,128)}, f32[1024,128]{1,0:T(8,128)}, bf16[8,128,256]{2,1,0:T(8,128)(2,1)}, f3...) custom-call(bf16[8,128,2048]{2,1,0:T(8,128)(2,1)} %get-tuple-element, ...), custom_call_target="tpu_custom_call" | custom-call | tf_op jit(solution)/shard_map/layer_forward_last/pallas_call | solution.py:325
  312.3 144.5 %layer_backward.2 = (f32[128,2048]{1,0:T(8,128)}, bf16[4,2,256,512]{3,2,1,0:T(8,128)(2,1)}, bf16[2,2,256,512]{3,2,1,0:T(8,128)(2,1)}, bf16[2,256,512]{2,1,0:T(8,...) custom-call(f32[8,1048,128]{2,1,0:T(8,128)} %get-tuple-element.85.re, ...), custom_call_target="tpu_custom_call" | custom-call | tf_op jit(solution)/shard_map/layer_backward/pallas_call | solution.py:325
  456.8 0.0 copy-start
  456.8 0.0 copy-start.9
  456.8 3.1 convert_reduce_fusion
  459.9 0.0 copy-done
  459.9 0.0 copy-start.2
  459.9 0.0 copy-start.3
  459.9 1.1 add_bitcast_fusion
  461.0 0.0 copy-done.9
  461.0 0.6 slice_reduce_fusion
  461.6 2.7 stack.34
  464.3 0.7 broadcast_in_dim.36.refs_4_
  465.0 0.0 copy-done.2
  465.0 0.0 copy-done.3
  465.0 2.1 fusion.4
  467.0 123.5 %layer_backward.3 = (f32[128,2048]{1,0:T(8,128)}, bf16[4,2,256,512]{3,2,1,0:T(8,128)(2,1)}, bf16[2,2,256,512]{3,2,1,0:T(8,128)(2,1)}, bf16[2,256,512]{2,1,0:T(8,...) custom-call(f32[8,1048,128]{2,1,0:T(8,128)} %get-tuple-element.97.re, ...), custom_call_target="tpu_custom_call" | custom-call | tf_op jit(solution)/shard_map/layer_backward/pallas_call | solution.py:325
  590.6 0.0 copy-start.10
  590.6 0.0 copy-start.11
  590.6 0.0 copy-start.7
  590.6 0.0 copy-start.8
  590.6 0.0 copy-start.4
  590.6 0.0 copy-start.5
  590.6 2.4 add_convert_fusion
  593.1 0.0 copy-done.10
  593.1 0.0 copy-done.11
  593.1 0.1 reshape.114
  593.2 0.6 pad.24.refs_5_
  593.8 0.0 copy-done.7
  593.9 0.6 pad.23
  594.5 0.9 pad_maximum_fusion
  595.4 49.5 %closing.1 = (f32[2,64,8192]{2,1,0:T(8,128)}, f32[2,128,160]{2,1,0:T(8,128)}, f32[2,128,128]{2,1,0:T(8,128)}, f32[2,128,2048]{2,1,0:T(8,128)}, f32[2,64]{1,0:T(2...) custom-call(bf16[2,2,2,256,512]{4,3,2,1,0:T(8,128)(2,1)} %bitcast.67, ...), custom_call_target="tpu_custom_call" | custom-call | tf_op jit(solution)/shard_map/closing/pallas_call | solution.py:325
  645.0 1.4 slice_reduce_fusion.4
  646.4 1.7 copy.53
  648.1 2.3 copy.66
  650.4 4.8 copy.67
  655.2 0.7 copy.68
  655.9 1.3 copy.69
  657.2 0.6 copy.70
  657.8 0.0 copy-done.12
  657.8 0.6 copy.71
  658.4 0.6 copy.72
  658.9 0.6 copy.73
  659.5 0.6 copy.74
  (21 shorter events, 0.1 us)
Async XLA Ops:
  456.8 3.1 copy-start
  456.8 4.2 copy-start.9
  459.9 5.1 copy-start.2
  459.9 5.1 copy-start.3
  590.6 2.5 copy-start.10
  590.6 2.5 copy-start.11
  590.6 3.2 copy-start.7
  590.6 3.2 copy-start.8
  590.6 3.9 copy-start.4
  590.6 3.9 copy-start.5
  650.4 4.8 copy-start.6
  650.4 5.4 copy-start.1
  655.9 1.4 copy-start.16
  655.9 1.9 copy-start.12
  655.9 2.5 copy-start.15
  655.9 3.1 copy-start.14
  655.9 3.6 copy-start.13

commit v5 on v4

--- a/solution.py
+++ b/solution.py
@@ -1,3 +1,5 @@
+import types
+
 import jax
 import jax.numpy as jnp
 import numpy as np
@@ -48,15 +50,10 @@
 def tp_peers():
     x, core, zh, q = place()
     peers = []
-    for dc in (0, 1):
-        for dq in (1, 3, 2, 0):
-            if dc == 0 and dq == 0:
-                continue
-            other_core = lax.rem(core + dc, 2)
-            to_q, from_q = lax.rem(q + dq, WAYS), lax.rem(q + WAYS - dq, WAYS)
-            peers.append(
-                (device(x, other_core, zh, to_q), other_core * WAYS + to_q, other_core * WAYS + from_q)
-            )
+    for dc, da, db in ((1, 0, 0), (0, 1, 0), (0, 0, 1), (1, 1, 0), (1, 0, 1), (0, 1, 1), (1, 1, 1)):
+        other_core, other_q = lax.rem(core + dc, 2), neighbour(q, da, db)
+        rank = other_core * WAYS + other_q
+        peers.append((device(x, other_core, zh, other_q), rank, rank))
     return peers
 
 
@@ -304,36 +301,30 @@
             copy.wait()
 
 
-def call(body, name, collective, ins, outs, scratch, **options):
-    names = list(ins) + list(outs) + list(scratch)
+def call(body, collective, ins, outs, scratch):
+    def flatten(kind):
+        return [leaf for each in kind for leaf in flatten(each)] if isinstance(kind, list) else [kind]
+
+    def rebuild(kind, refs):
+        return [rebuild(each, refs) for each in kind] if isinstance(kind, list) else refs.pop(0)
 
     def kernel(*refs):
-        named, refs = {}, list(refs)
-        flat = []
-        for key in names:
-            kind = scratch.get(key)
-            if isinstance(kind, list):
-                named[key] = refs[: len(kind)]
-                refs = refs[len(kind) :]
-            else:
-                named[key] = refs.pop(0)
-        body(named)
-
-    flat = []
-    for kind in scratch.values():
-        flat += kind if isinstance(kind, list) else [kind]
+        refs = list(refs)
+        named = {key: refs.pop(0) for key in list(ins) + list(outs)}
+        named.update({key: rebuild(kind, refs) for key, kind in scratch.items()})
+        body(types.SimpleNamespace(**named))
+
     values = pl.pallas_call(
         kernel,
         out_shape=[shape for shape, _ in outs.values()],
         in_specs=[spec for _, spec in ins.values()],
         out_specs=[spec for _, spec in outs.values()],
-        scratch_shapes=flat,
+        scratch_shapes=flatten(list(scratch.values())),
         compiler_params=pltpu.CompilerParams(
             collective_id=collective, has_side_effects=True, vmem_limit_bytes=63 * 2**20
         ),
-        name=name,
     )(*[array for array, _ in ins.values()])
-    return dict(zip(outs, values))
+    return types.SimpleNamespace(**dict(zip(outs, values)))
 
 
 def spread_keys(kq, lane):
@@ -379,18 +370,59 @@
     return jnp.concatenate(out, axis=1)
 
 
+def turn_pieces(zh_size, win, layer, out, rank):
+    if len(win.shape) == 4:
+        return [(win.at[layer, rank], out)]
+    groups = 2 * zh_size
+    share = win.shape[2] // (2 * groups * TP)
+    pieces = []
+    for part in range(2):
+        for g in range(groups):
+            d = ((g // zh_size * 2 + rank // WAYS) * zh_size + g % zh_size) * WAYS + lax.rem(rank, WAYS)
+            first = pl.multiple_of((part * groups * TP + d) * share, share)
+            pieces.append(
+                (win.at[layer, :, pl.ds(first, share)], out.at[:, pl.ds((part * groups + g) * share, share)])
+            )
+    return pieces
+
+
+class Turn:
+    def __init__(self, zh_size, win, layer, out, slot, sems):
+        self.out, self.slot, self.sems = out, slot, sems
+        self.me = total_rank()
+        self.peers = tp_peers()
+        self.pieces = lambda rank: turn_pieces(zh_size, win, layer, out.at[slot(self.me)], rank)
+
+    def start(self):
+        for i, (target, rank, _) in enumerate(self.peers):
+            for src, dst in self.pieces(rank):
+                remote(src, dst, self.sems[0].at[i], self.sems[1].at[i], target).start()
+
+    def whole(self, i, rank):
+        block = self.out.at[self.slot(rank)]
+        return remote(block, block, self.sems[0].at[i], self.sems[1].at[i], self.peers[i][0])
+
+    def arrived(self, i):
+        self.whole(i, self.peers[i][2]).wait_recv()
+
+    def sent(self):
+        for i in range(TP - 1):
+            self.whole(i, self.me).wait_send()
+
+
 def opening(zh_size, gains, share, win, small, misc, mats, h, cot):
     groups = 2 * zh_size
     count = groups * TP
     tokens, width = h.shape
     half = groups * share
+    depth = win.shape[-2]
     dma = pltpu.SemaphoreType.DMA
     ins = dict(
         win=(win, HB), small=(small, VM), misc=(misc, VM), mats=(mats, HB), h=(h, VM), cot=(cot, VM)
     )
     outs = dict(
-        win_all=(struct(count, *win.shape[1:], dtype=bf16), HB),
-        mats_all=(struct(groups, *mats.shape, dtype=bf16), HB), vec=(struct(8 * LAYERS, half), VM),
+        win_all=(struct(count, depth, 2 * half, dtype=bf16), HB),
+        mats_all=(struct(groups, *mats.shape[1:], dtype=bf16), HB), vec=(struct(8 * LAYERS, half), VM),
         gains=(struct(8, width), VM), scale=(struct(TP, LANES), VM), grad=(struct(tokens, width), VM),
         gout=(struct(tokens, width, dtype=bf16), VM), xg=(struct(TP, tokens, width, dtype=bf16), HB),
     )
@@ -398,12 +430,10 @@
     scratch = dict(
         misc_all=pltpu.VMEM((count,) + misc.shape, f32), small_all=pltpu.VMEM((groups,) + small.shape, f32),
         normed=pltpu.VMEM((tokens, width), bf16), gather_sems=Gather.sems(dma),
-        m_sems=[dma((TP - 1,))] * 2, w_sems=[dma((TP - 1,))] * 2,
-        s0=spread(), s1=spread(),
-    )
-    for i in range(TP):
-        scratch["sm%d" % i] = spread()
-        scratch["sw%d" % i] = spread()
+        m_sems=[dma((TP - 1,))] * 2, w_sems=[dma((TP - 1,))] * 2, own_sem=dma,
+        own=pltpu.VMEM((depth, 2 * half), bf16), s0=spread(), s1=spread(),
+        sm=[spread() for _ in range(TP)], sw=[spread() for _ in range(TP)],
+    )
 
     def body(r):
         x, core, zh, q = place()
@@ -418,29 +448,33 @@
         def views(out, rank):
             return lambda xx, zz: out.at[row(xx, zz, rank)]
 
-        def exchange(src, out, slot, sems):
-            copies = []
-            for i, (target, rank, _) in enumerate(peers):
-                copies.append(remote(src(rank), out.at[slot], sems[0].at[i], sems[1].at[i], target))
-                copies[-1].start()
-            return copies
-
         here = row(x, zh, me)
-        miscs = exchange(lambda rank: r["misc"], r["misc_all"], here, r["m_sems"])
-        misc_moves = [Spread(zh_size, r["misc"], views(r["misc_all"], me), r["sm0"])]
+        miscs = []
+        for i, (target, rank, _) in enumerate(peers):
+            miscs.append(remote(r.misc, r.misc_all.at[here], r.m_sems[0].at[i], r.m_sems[1].at[i], target))
+            miscs[-1].start()
+        misc_moves = [Spread(zh_size, r.misc, views(r.misc_all, me), r.sm[0])]
         misc_moves[0].start()
-        smalls = Spread(zh_size, r["small"], lambda xx, zz: r["small_all"].at[xx * zh_size + zz], r["s0"])
+        smalls = Spread(zh_size, r.small, lambda xx, zz: r.small_all.at[xx * zh_size + zz], r.s0)
         smalls.start()
-        wins = exchange(lambda rank: r["win"].at[rank], r["win_all"], here, r["w_sems"])
-        win_moves = [Spread(zh_size, r["win"].at[me], views(r["win_all"], me), r["sw0"])]
+        wins = Turn(zh_size, r.win, 0, r.win_all, lambda rank: row(x, zh, rank), r.w_sems)
+        wins.start()
+        own_pieces = [
+            pltpu.make_async_copy(src, dst, r.own_sem)
+            for src, dst in turn_pieces(zh_size, r.win, 0, r.own, me)
+        ]
+        for copy in own_pieces:
+            copy.start()
+        pltpu.make_async_copy(r.own, r.own, r.own_sem).wait()
+        win_moves = [Spread(zh_size, r.own, views(r.win_all, me), r.sw[0])]
         for i, (_, _, source) in enumerate(peers):
-            view = views(r["win_all"], source)
-            win_moves.append(Spread(zh_size, view(x, zh), view, r["sw%d" % (i + 1)], keep=False))
-        mats_move = Spread(zh_size, r["mats"], lambda xx, zz: r["mats_all"].at[xx * zh_size + zz], r["s1"])
+            view = views(r.win_all, source)
+            win_moves.append(Spread(zh_size, view(x, zh), view, r.sw[i + 1], keep=False))
+        mats_move = Spread(zh_size, r.mats.at[0], lambda xx, zz: r.mats_all.at[xx * zh_size + zz], r.s1)
 
         def step(i):
             if i >= 1:
-                wins[i - 1].wait_recv()
+                wins.arrived(i - 1)
             if i >= 2:
                 win_moves[i - 2].onward()
             win_moves[i].start()
@@ -448,8 +482,8 @@
         step(0)
         for i, (_, _, source) in enumerate(peers):
             miscs[i].wait_recv()
-            view = views(r["misc_all"], source)
-            misc_moves.append(Spread(zh_size, view(x, zh), view, r["sm%d" % (i + 1)], keep=False))
+            view = views(r.misc_all, source)
+            misc_moves.append(Spread(zh_size, view(x, zh), view, r.sm[i + 1], keep=False))
             misc_moves[-1].start()
         step(1)
         for move in misc_moves:
@@ -458,31 +492,31 @@
         for move in misc_moves:
             move.finish()
         for l in range(LAYERS):
-            r["gains"][l : l + 1, :] = side_by_side(
-                [r["misc_all"][d, l : l + 1, :] for d in range(count)], gains
+            r.gains[l : l + 1, :] = side_by_side(
+                [r.misc_all[d, l : l + 1, :] for d in range(count)], gains
             )
-        r["gains"][LAYERS:, :] = jnp.zeros((8 - LAYERS, width), f32)
-        stream = r["h"][...]
-        r["normed"][...] = (stream * rms(stream) * r["gains"][0:1, :]).astype(bf16)
-        rows = Gather(r["normed"], r["xg"], r["gather_sems"])
+        r.gains[LAYERS:, :] = jnp.zeros((8 - LAYERS, width), f32)
+        stream = r.h[...]
+        r.normed[...] = (stream * rms(stream) * r.gains[0:1, :]).astype(bf16)
+        rows = Gather(r.normed, r.xg, r.gather_sems)
         rows.start()
         step(2)
         mats_move.start()
-        total = r["misc_all"][0, LAYERS : LAYERS + 1, :]
+        total = r.misc_all[0, LAYERS : LAYERS + 1, :]
         for d in range(1, count):
-            total = total + r["misc_all"][d, LAYERS : LAYERS + 1, :]
+            total = total + r.misc_all[d, LAYERS : LAYERS + 1, :]
         inverse = count / total
         for rank in range(TP):
-            r["scale"][rank : rank + 1, :] = r["misc_all"][row(x, zh, rank), LAYERS : LAYERS + 1, :] * inverse
-        own = (r["misc"][LAYERS : LAYERS + 1, :] * inverse)[:, :1]
-        grad = r["cot"][...] * own
-        r["grad"][...] = grad
-        r["gout"][...] = grad.astype(bf16)
+            r.scale[rank : rank + 1, :] = r.misc_all[row(x, zh, rank), LAYERS : LAYERS + 1, :] * inverse
+        own = (r.misc[LAYERS : LAYERS + 1, :] * inverse)[:, :1]
+        grad = r.cot[...] * own
+        r.grad[...] = grad
+        r.gout[...] = grad.astype(bf16)
         step(3)
         smalls.finish()
         for l in range(LAYERS):
-            r["vec"][8 * l : 8 * (l + 1), :] = side_by_side(
-                [r["small_all"][g, 8 * l : 8 * (l + 1), :] for g in range(groups)], share
+            r.vec[8 * l : 8 * (l + 1), :] = side_by_side(
+                [r.small_all[g, 8 * l : 8 * (l + 1), :] for g in range(groups)], share
             )
         step(4)
         mats_move.onward()
@@ -493,13 +527,14 @@
         step(7)
         win_moves[6].onward()
         win_moves[7].onward()
-        for copy in miscs + wins:
+        wins.sent()
+        for copy in miscs:
             copy.wait_send()
         for move in win_moves + [mats_move]:
             move.finish()
         rows.finish()
 
-    return call(body, "opening", 1, ins, outs, scratch)
+    return call(body, 1, ins, outs, scratch)
 
 
 def at_block(b, size):
@@ -553,57 +588,54 @@
         payload=pltpu.VMEM((TP, size, 2 * LANES), bf16), parts=pltpu.VMEM((TP - 1, size, 2 * LANES), bf16),
         own=pltpu.VMEM((size, 2 * LANES), f32),
         state=pltpu.VMEM((STATE, parts, TP, LANES), f32), wide=pltpu.VMEM((size, 32 * LANES), f32),
-        part=pltpu.VMEM((TP, tokens, width), bf16),
-        scatter_buf=Scatter.buffers((tokens, width)),
-        sum_sems=Sum.sems(dma), scatter_sems=Scatter.sems(dma),
-    )
-    outs["wout_all"] = (struct(groups, *wout.shape, dtype=bf16), VM)
-    scratch["d0"] = Spread.sems(dma, zh_size)
+        sum_sems=Sum.sems(dma),
+    )
+    outs.update(wout_all=(struct(groups, *wout.shape[1:], dtype=bf16), VM))
+    scratch.update(d0=Spread.sems(dma, zh_size))
     if last:
-        ins["gout"] = (gout, VM)
-        outs["gog"] = (struct(TP, tokens, width, dtype=bf16), HB)
-        scratch["gather_sems"] = Gather.sems(dma)
-        outs["part"] = (struct(TP, tokens, width, dtype=bf16), VM)
-        del scratch["part"], scratch["scatter_buf"], scratch["scatter_sems"]
+        ins.update(gout=(gout, VM))
+        outs.update(
+            gog=(struct(TP, tokens, width, dtype=bf16), HB), part=(struct(TP, tokens, width, dtype=bf16), VM)
+        )
+        scratch.update(gather_sems=Gather.sems(dma))
     if not last:
-        win1 = nxt["win"]
-        ins.update(h=(nxt["h"], VM), gain=(nxt["gain"], VM), win1=(win1, HB), mats1=(nxt["mats"], HB))
+        win1 = nxt.win
+        depth = win1.shape[-2]
+        ins.update(h=(nxt.h, VM), gain=(nxt.gain, VM), win1=(win1, HB), mats1=(nxt.mats, HB))
         outs.update(
             result=(struct(tokens, width), VM),
-            win1_all=(struct(2, 2, zh_size, WAYS, *win1.shape[1:], dtype=bf16), HB),
-            mats1_all=(struct(groups, *nxt["mats"].shape, dtype=bf16), HB),
+            win1_all=(struct(2, 2, zh_size, WAYS, depth, 2 * half, dtype=bf16), HB),
+            mats1_all=(struct(groups, *nxt.mats.shape[1:], dtype=bf16), HB),
             xg1=(struct(TP, tokens, width, dtype=bf16), HB),
         )
         scratch.update(
             normed=pltpu.VMEM((tokens, width), bf16), gather_sems=Gather.sems(dma),
-            turned=pltpu.VMEM(win1.shape, bf16), l_sems=[dma((TP - 1,)), dma((TP - 1,)), dma],
+            part=pltpu.VMEM((TP, tokens, width), bf16), scatter_buf=Scatter.buffers((tokens, width)),
+            scatter_sems=Scatter.sems(dma),
+            turned=pltpu.VMEM((TP, depth, 2 * half), bf16), l_sems=[dma((TP - 1,)), dma((TP - 1,))], l_own=dma,
             d1=Spread.sems(dma, zh_size), d2=Spread.sems(dma, zh_size), d3=Spread.sems(dma, zh_size),
         )
 
     def body(r):
         side, far = dp_peers(zh_size)
         greet([p[0] for p in tp_peers()] + [side] + [f[0] for f in far])
-        entry, act, step, beta, kq, y = r["entry"], r["act"], r["step"], r["beta"], r["kq"], r["y"]
-        vec = r["vec"].at[8 * layer : 8 * (layer + 1)]
+        entry, act, step, beta, kq, y = r.entry, r.act, r.step, r.beta, r.kq, r.y
+        vec = r.vec.at[8 * layer : 8 * (layer + 1)]
         index = lambda ref: lambda xx, zz: ref.at[xx * zh_size + zz]
-        early = Spread(zh_size, r["wout"], index(r["wout_all"]), r["d0"])
+        early = Spread(zh_size, r.wout.at[layer], index(r.wout_all), r.d0)
         early.start()
         if last:
-            gouts = Gather(r["gout"], r["gog"], r["gather_sems"])
+            gouts = Gather(r.gout, r.gog, r.gather_sems)
         else:
-            me = total_rank()
-            turned = [pltpu.make_async_copy(r["win1"].at[me], r["turned"].at[me], r["l_sems"][2])]
-            for i, (target, rank, _) in enumerate(tp_peers()):
-                turned.append(
-                    remote(r["win1"].at[rank], r["turned"].at[me], r["l_sems"][0].at[i], r["l_sems"][1].at[i], target)
-                )
-            for copy in turned:
-                copy.start()
-            moves = [Spread(zh_size, r["mats1"], index(r["mats1_all"]), r["d3"])]
+            turned = Turn(zh_size, r.win1, layer + 1, r.turned, lambda rank: rank, r.l_sems)
+            turned.start()
+            for src, dst in turned.pieces(turned.me):
+                pltpu.make_async_copy(src, dst, r.l_own).start()
+            moves = [Spread(zh_size, r.mats1.at[layer + 1], index(r.mats1_all), r.d3)]
             for k in range(2):
-                view = lambda xx, zz, k=k: r["win1_all"].at[xx, k, zz]
-                src = r["turned"].at[k * WAYS : (k + 1) * WAYS]
-                moves.append(Spread(zh_size, src, view, r["d1" if k == 0 else "d2"]))
+                view = lambda xx, zz, k=k: r.win1_all.at[xx, k, zz]
+                src = r.turned.at[k * WAYS : (k + 1) * WAYS]
+                moves.append(Spread(zh_size, src, view, (r.d1 if k == 0 else r.d2)))
 
         entry[:, :halo, :] = jnp.zeros((2 * parts, halo, LANES), f32)
         tile = 2 * LANES
@@ -612,7 +644,7 @@
             def columns(n, carry, p=p):
                 cols = at_block(n, tile)
                 out = jnp.dot(
-                    r["xg"][2 * p : 2 * p + 2].reshape(2 * tokens, width), r["win"][:, cols],
+                    r.xg[2 * p : 2 * p + 2].reshape(2 * tokens, width), r.win[:, cols],
                     preferred_element_type=f32,
                 )
                 for j in range(2):
@@ -623,11 +655,7 @@
                 return carry
 
             lax.fori_loop(0, 2 * half // tile, columns, 0)
-        if not last:
-            for copy in turned:
-                copy.wait()
-
-        total = Sum(r["payload"], r["parts"], r["proj"], r["sum_sems"])
+        total = Sum(r.payload, r.parts, r.proj, r.sum_sems)
 
         def project(b, carry):
             rs = at_block(b, size)
@@ -635,58 +663,64 @@
                 conv = conv_of(entry, vec, b * size, size, c)
                 act[c, rs, :] = (conv * jax.nn.sigmoid(conv)).astype(bf16).astype(f32)
             out = jnp.dot(
-                wide_of(act, rs, parts).astype(bf16), r["mats"][:, RANK:], preferred_element_type=f32
+                wide_of(act, rs, parts).astype(bf16), r.mats[:, RANK:], preferred_element_type=f32
             )
-            r["payload"][b] = encode(out)
+            r.payload[b] = encode(out)
 
             @pl.when(b == total.me)
             def _():
-                r["own"][...] = out
+                r.own[...] = out
 
             return carry
 
         lax.fori_loop(0, blocks, project, 0)
         total.start()
-        total.middle(r["own"][...])
+        if not last:
+            for i in range(TP - 1):
+                turned.arrived(i)
+            mine = r.turned.at[turned.me]
+            pltpu.make_async_copy(mine, mine, r.l_own).wait()
+            moves[0].start()
+            moves[1].start()
+        total.middle(r.own[...])
         total.finish()
-        early.onward()
         if last:
             gouts.start()
         else:
-            moves[0].start()
-            moves[1].start()
-
-        r["stats"][...] = jnp.zeros((2, TP, LANES), f32)
+            turned.sent()
+            moves[2].start()
+
+        r.stats[...] = jnp.zeros((2, TP, LANES), f32)
 
         def rates(b, carry):
             rs = at_block(b, size)
-            tail = decode(r["proj"][b])[:, RANK:]
+            tail = decode(r.proj[b])[:, RANK:]
             keys = tail + pltpu.roll(tail, 32, 1) + pltpu.roll(tail, 64, 1)
             kq[rs, :] = keys
             norm = square_sum(keys)
-            pre = dot(r["proj"][b, :, :RANK], r["mats"][:, :RANK], ((1,), (1,)))
+            pre = dot(r.proj[b, :, :RANK], r.mats[:, :RANK], ((1,), (1,)))
             for c in range(parts):
                 cols = slice(c * LANES, (c + 1) * LANES)
                 rate = jax.nn.sigmoid(pre[:, cols] + vec[CONV + 1 : CONV + 2, cols])
                 beta[c, rs, :] = rate
                 step[c, rs, :] = rate / (1.0 + rate * norm)
-                r["stats"][0] += row_sum(rate)
-                r["stats"][1] = jnp.maximum(
-                    r["stats"][1], jnp.max(rate.reshape(-1, TP, LANES), axis=0)
+                r.stats[0] += row_sum(rate)
+                r.stats[1] = jnp.maximum(
+                    r.stats[1], jnp.max(rate.reshape(-1, TP, LANES), axis=0)
                 )
             return carry
 
         lax.fori_loop(0, blocks, rates, 0)
-        r["stats"][0] = r["stats"][0] * r["scale"][...]
-        r["stats"][1] = r["stats"][1] * r["scale"][...]
+        r.stats[0] = r.stats[0] * r.scale[...]
+        r.stats[1] = r.stats[1] * r.scale[...]
 
         lane = lanes_of((size, LANES))
-        state, wide = r["state"], r["wide"]
+        state, wide = r.state, r.wide
         state[...] = jnp.zeros_like(state)
 
         def block(b, carry):
-            r["keep"][b] = state[...]
-            wide[...] = jnp.dot(spread_keys(kq[at_block(b, size), :], lane), r["e"][...], preferred_element_type=f32)
+            r.keep[b] = state[...]
+            wide[...] = jnp.dot(spread_keys(kq[at_block(b, size), :], lane), r.e[...], preferred_element_type=f32)
 
             def one(j, carry):
                 t = at_block(b * STEPS + j, TP)
@@ -715,54 +749,57 @@
                 skip = vec[CONV + 2 : CONV + 3, cols]
                 step[c, rs, :] = (y[c, rs, :] + skip * act[c, rs, :]) * (gate * jax.nn.sigmoid(gate))
                 for s in range(TP):
-                    r["mixed"][s, here, cols] = step[c, pl.ds(b * size + s, STEPS, stride=TP), :].astype(bf16)
+                    r.mixed[s, here, cols] = step[c, pl.ds(b * size + s, STEPS, stride=TP), :].astype(bf16)
             return carry
 
+        early.onward()
+        lax.fori_loop(0, blocks // 2, block, 0)
         if last:
-            lax.fori_loop(0, blocks, block, 0)
             gouts.relay()
         else:
-            lax.fori_loop(0, blocks // 2, block, 0)
             moves[0].onward()
-            moves[2].start()
-            lax.fori_loop(blocks // 2, blocks, block, 0)
+        lax.fori_loop(blocks // 2, blocks, block, 0)
         early.finish()
-        weight = lambda: r["wout_all"][...].reshape(half, width)
+        weight = lambda: r.wout_all[...].reshape(half, width)
         if last:
 
             def plain(s, carry):
-                r["part"][s] = dot(r["mixed"][s], weight(), ((1,), (0,))).astype(bf16)
+                two = r.mixed[pl.ds(2 * s, 2)].reshape(2 * tokens, half)
+                out = dot(two, weight(), ((1,), (0,))).astype(bf16)
+                r.part[pl.ds(2 * s, 2)] = out.reshape(2, tokens, width)
                 return carry
 
-            lax.fori_loop(0, TP // 2, plain, 0)
+            lax.fori_loop(0, TP // 4, plain, 0)
             gouts.rest()
-            lax.fori_loop(TP // 2, TP, plain, 0)
+            lax.fori_loop(TP // 4, TP // 2, plain, 0)
             gouts.finish()
             return
+        scatter = Scatter(r.part, r.scatter_buf, r.scatter_sems)
+        out_partial(scatter, r.part, r.mixed, weight)
         moves[1].onward()
-        scatter = Scatter(r["part"], r["scatter_buf"], r["scatter_sems"])
-        out_partial(scatter, r["part"], r["mixed"], weight)
-        moves[2].onward()
-        stream = r["h"][...] + scatter.total()
-        r["result"][...] = stream
-        r["normed"][...] = (stream * rms(stream) * r["gain"][layer + 1 : layer + 2, :]).astype(bf16)
-        spread = Gather(r["normed"], r["xg1"], r["gather_sems"])
+        stream = r.h[...] + scatter.total()
+        r.result[...] = stream
+        r.normed[...] = (stream * rms(stream) * r.gain[layer + 1 : layer + 2, :]).astype(bf16)
+        spread = Gather(r.normed, r.xg1, r.gather_sems)
         spread.start()
         spread.relay()
+        moves[2].onward()
         spread.rest()
         spread.finish()
         for move in moves:
             move.finish()
 
-    return call(body, "layer_forward_last" if last else "layer_forward", 7 if last else 6, ins, outs, scratch)
+    return call(body, 7 if last else 6, ins, outs, scratch)
 
 
 def out_partial(scatter, part, left, right, turned=False):
     contract = ((1,), (1,)) if turned else ((1,), (0,))
     for i in range(4):
-        for core in (1 - scatter.core, scatter.core):
-            slot = core * WAYS + scatter.turns[i]
-            part[slot] = dot(left[slot], right(), contract).astype(bf16)
+        slots = [core * WAYS + scatter.turns[i] for core in (1 - scatter.core, scatter.core)]
+        rows = left.shape[1]
+        both = dot(jnp.concatenate([left[slot] for slot in slots], axis=0), right(), contract).astype(bf16)
+        part[slots[0]] = both[:rows]
+        part[slots[1]] = both[rows:]
         scatter.to_sibling(i)
         if i >= 1:
             scatter.across(i - 1)
@@ -832,10 +869,10 @@
     far = max(1, zh_size - 1)
     dma = pltpu.SemaphoreType.DMA
     onward = part is not None
-    ins = {k: (kept[k], VM) for k in ("entry", "beta", "kq", "proj")}
+    ins = dict(entry=(kept.entry, VM), beta=(kept.beta, VM), kq=(kept.kq, VM), proj=(kept.proj, VM))
     ins.update(
         mats=(mats, VM), wout=(wout, HB), vec=(vec, VM), gain=(gain, VM), h=(h, VM), grad=(grad, VM),
-        mixed=(kept["mixed"], HB), e=(spreader(), VM), fold=(folder(), VM), keep=(kept["keep"], HB), gouts=(gog, HB), y=(kept["y"], HB), xg=(xg, HB), win=(win, HB),
+        mixed=(kept.mixed, HB), e=(spreader(), VM), fold=(folder(), VM), keep=(kept.keep, HB), gouts=(gog, HB), y=(kept.y, HB), xg=(xg, HB), win=(win, HB),
     )
     outs = dict(
         prev=(struct(tokens, width), VM), ginner=(struct(groups, 2, deep, half, dtype=bf16), VM),
@@ -864,31 +901,30 @@
         loads=dma((7,)), over=[dma, dma],
     )
     if onward:
-        outs["gog"] = (struct(TP, tokens, width, dtype=bf16), HB)
-        ins["part"] = (part, HB)
-        outs["parts_all"] = (struct(*part.shape, dtype=bf16), HB)
+        outs.update(gog=(struct(TP, tokens, width, dtype=bf16), HB))
+        ins.update(part=(part, HB))
+        outs.update(parts_all=(struct(*part.shape, dtype=bf16), HB))
         scratch.update(part_sems=[dma((TP - 1,)), dma((TP - 1,)), dma])
         scratch.update(gout=pltpu.VMEM((tokens, width), bf16), gather_sems=Gather.sems(dma))
     if late is not None:
-        ins["late"] = (late, HB)
-        outs["late"] = (struct(far, *late.shape[1:], dtype=bf16), HB)
+        ins.update(late_in=(late, HB))
+        outs.update(late=(struct(far, *late.shape[1:], dtype=bf16), HB))
         scratch.update(late_sems=[dma((far,)), dma((far,))])
-        ins["late_in"] = ins.pop("late")
 
     def body(r):
         x, core, zh, q = place()
         side, far_ones = dp_peers(zh_size)
         greet([p[0] for p in tp_peers()] + [side] + [f[0] for f in far_ones])
-        entry, act, step, beta, kq = r["entry"], r["act"], r["step"], r["beta"], r["kq"]
-        gs, gact, sums, gstep = r["gs"], r["gact"], r["sums"], r["gstep"]
-        vec = r["vec"].at[8 * layer : 8 * (layer + 1)]
+        entry, act, step, beta, kq = r.entry, r.act, r.step, r.beta, r.kq
+        gs, gact, sums, gstep = r.gs, r.gact, r.sums, r.gstep
+        vec = r.vec.at[8 * layer : 8 * (layer + 1)]
         loads = [
-            pltpu.make_async_copy(src, dst, r["loads"].at[i])
+            pltpu.make_async_copy(src, dst, r.loads.at[i])
             for i, (src, dst) in enumerate(
                 (
-                    (r["gouts"], r["a"]), (r["mixed"], r["gentry"].at[:, :, :half]),
-                    (r["wout"].at[:, : 2 * half], r["b"].at[:half]), (r["wout"].at[:, 2 * half :], r["b"].at[half : 2 * half]),
-                    (r["y"], gact), (r["xg"], r["a"]), (r["win"], r["b"]),
+                    (r.gouts, r.a), (r.mixed, r.gentry.at[:, :, :half]),
+                    (r.wout.at[:, : 2 * half], r.b.at[:half]), (r.wout.at[:, 2 * half :], r.b.at[half : 2 * half]),
+                    (r.y, gact), (r.xg, r.a), (r.win, r.b),
                 )
             )
         ]
@@ -899,22 +935,22 @@
             me = core * WAYS + q
             for i, (target, rank, _) in enumerate(tp_peers()):
                 copy = remote(
-                    r["part"].at[rank], r["parts_all"].at[me], r["part_sems"][0].at[i], r["part_sems"][1].at[i], target
+                    r.part.at[rank], r.parts_all.at[me], r.part_sems[0].at[i], r.part_sems[1].at[i], target
                 )
                 copy.start()
                 passed.append(copy)
-            passed.append(pltpu.make_async_copy(r["part"].at[me], r["parts_all"].at[me], r["part_sems"][2]))
+            passed.append(pltpu.make_async_copy(r.part.at[me], r.parts_all.at[me], r.part_sems[2]))
             passed[-1].start()
         if late is not None:
             for k, (target, to_z, _) in enumerate(far_ones):
                 copy = remote(
-                    r["late_in"].at[to_z], r["late"].at[k], r["late_sems"][0].at[k], r["late_sems"][1].at[k], target
+                    r.late_in.at[to_z], r.late.at[k], r.late_sems[0].at[k], r.late_sems[1].at[k], target
                 )
                 copy.start()
                 passed.append(copy)
         sums[...] = jnp.zeros_like(sums)
-        r["grate"][...] = jnp.zeros_like(r["grate"])
-        r["gselect"][...] = jnp.zeros_like(r["gselect"])
+        r.grate[...] = jnp.zeros_like(r.grate)
+        r.gselect[...] = jnp.zeros_like(r.gselect)
 
         def again(b, carry):
             rs = at_block(b, size)
@@ -931,14 +967,14 @@
         loads[1].wait()
 
         def outer(c, carry):
-            left = r["gentry"][:, :, at_block(c, LANES)].reshape(rows, LANES)
-            out = dot(left, r["a"][...].reshape(rows, width), ((0,), (0,))).astype(bf16)
+            left = r.gentry[:, :, at_block(c, LANES)].reshape(rows, LANES)
+            out = dot(left, r.a[...].reshape(rows, width), ((0,), (0,))).astype(bf16)
             each = LANES // share
-            r["gwo"][pl.ds(c * each, each)] = out.reshape(each, share, width)
+            r.gwo[pl.ds(c * each, each)] = out.reshape(each, share, width)
             return carry
 
         lax.fori_loop(0, parts, outer, 0)
-        reduce = Reduce(zh_size, r["gwo"], r["reduce_buf"], r["reduce_sems"])
+        reduce = Reduce(zh_size, r.gwo, r.reduce_buf, r.reduce_sems)
         reduce.start()
         loads[2].wait()
         loads[3].wait()
@@ -947,8 +983,8 @@
             def columns(n, carry, p=p):
                 out = 0.0
                 for k in range(2):
-                    left = r["a"][2 * p : 2 * p + 2, :, 2 * half * k : 2 * half * (k + 1)].reshape(2 * tokens, 2 * half)
-                    right = r["b"][pl.ds(pl.multiple_of(half * k + n * 2 * LANES, 2 * LANES), 2 * LANES), :]
+                    left = r.a[2 * p : 2 * p + 2, :, 2 * half * k : 2 * half * (k + 1)].reshape(2 * tokens, 2 * half)
+                    right = r.b[pl.ds(pl.multiple_of(half * k + n * 2 * LANES, 2 * LANES), 2 * LANES), :]
                     out = out + dot(left, right, ((1,), (1,)))
                 for j in range(2):
                     for c in range(2):
@@ -978,7 +1014,7 @@
                 gs[c, rs, :] = down
                 sums[CONV + 2, c] += row_sum(down * a)
                 for s in range(TP):
-                    r["gentry"][s, here, half + c * LANES : half + (c + 1) * LANES] = gstep[
+                    r.gentry[s, here, half + c * LANES : half + (c + 1) * LANES] = gstep[
                         c, pl.ds(s, STEPS, stride=TP), :
                     ].astype(bf16)
             return carry
@@ -988,8 +1024,8 @@
         tile = 2 * LANES
 
         def outer_in(out_ref, first, i, carry):
-            left = r["a"][:, :, at_block(i, tile)].reshape(rows, tile)
-            out = dot(left, r["gentry"][:, :, first : first + half].reshape(rows, half), ((0,), (0,))).astype(bf16)
+            left = r.a[:, :, at_block(i, tile)].reshape(rows, tile)
+            out = dot(left, r.gentry[:, :, first : first + half].reshape(rows, half), ((0,), (0,))).astype(bf16)
             each = tile // deep
             for e in range(each):
                 d = i * each + e
@@ -997,28 +1033,28 @@
                 out_ref[xx * zh_size + zz, cc] = out[e * deep : (e + 1) * deep]
             return carry
 
-        lax.fori_loop(0, width // tile, lambda i, k: outer_in(r["gwg"], half, i, k), 0)
-        gate_reduce = Reduce(zh_size, r["gwg"], r["gate_buf"], r["gate_sems"])
+        lax.fori_loop(0, width // tile, lambda i, k: outer_in(r.gwg, half, i, k), 0)
+        gate_reduce = Reduce(zh_size, r.gwg, r.gate_buf, r.gate_sems)
 
         lane = lanes_of((size, LANES))
-        states, lam, wide = r["states"], r["lam"], r["wide"]
+        states, lam, wide = r.states, r.lam, r.wide
         lam[...] = jnp.zeros_like(lam)
         plus = lambda a, b: b if a is None else a + b
-        total = Sum(r["payload"], r["parts"], r["total"], r["sum_sems"])
+        total = Sum(r.payload, r.parts, r.total, r.sum_sems)
 
         def block(bi, carry):
             b = blocks - 1 - bi
             rs = at_block(b, size)
             slot = lax.rem(b, 2)
-            pltpu.make_async_copy(r["keep"].at[b], r["keeps"].at[slot], r["keep_sems"].at[slot]).wait()
+            pltpu.make_async_copy(r.keep.at[b], r.keeps.at[slot], r.keep_sems.at[slot]).wait()
 
             @pl.when(b > 0)
             def _():
-                ahead = pltpu.make_async_copy(r["keep"].at[b - 1], r["keeps"].at[1 - slot], r["keep_sems"].at[1 - slot])
+                ahead = pltpu.make_async_copy(r.keep.at[b - 1], r.keeps.at[1 - slot], r.keep_sems.at[1 - slot])
                 ahead.start()
 
-            states[0] = r["keeps"][slot]
-            wide[...] = jnp.dot(spread_keys(kq[rs, :], lane), r["e"][...], preferred_element_type=f32)
+            states[0] = r.keeps[slot]
+            wide[...] = jnp.dot(spread_keys(kq[rs, :], lane), r.e[...], preferred_element_type=f32)
 
             def replay(j, carry):
                 t, w = at_block(b * STEPS + j, TP), at_block(j, TP)
@@ -1043,6 +1079,7 @@
                 for n in range(STATE):
                     kcols, qcols = slice(n * LANES, (n + 1) * LANES), slice((STATE + n) * LANES, (STATE + n + 1) * LANES)
                     key, query = wide[w, kcols], wide[w, qcols]
+                    square = key * key
                     key_term, query_term = None, None
                     for c in range(parts):
                         before, after = states[j, n, c], states[j + 1, n, c]
@@ -1050,11 +1087,12 @@
                         u = key * before
                         d = acts[c] - u
                         gk = grad * key
+                        sg = steps[c] * grad
                         first[c] = plus(first[c], gk * d)
                         second[c] = plus(second[c], gk)
-                        key_term = plus(key_term, (steps[c] * grad) * (d - u))
+                        key_term = plus(key_term, sg * (d - u))
                         query_term = plus(query_term, gsums[c] * after)
-                        lam[n, c] = grad - (steps[c] * key) * gk
+                        lam[n, c] = grad - sg * square
                     wide[w, kcols] = key_term
                     wide[w, qcols] = query_term
                 for c in range(parts):
@@ -1066,8 +1104,8 @@
             terms = wide[...]
             high = terms.astype(bf16)
             low = (terms - high.astype(f32)).astype(bf16)
-            gkq = jnp.dot(high, r["fold"][...], preferred_element_type=f32) + jnp.dot(
-                low, r["fold"][...], preferred_element_type=f32
+            gkq = jnp.dot(high, r.fold[...], preferred_element_type=f32) + jnp.dot(
+                low, r.fold[...], preferred_element_type=f32
             )
             keys = kq[rs, :]
             norm = square_sum(keys)
@@ -1085,26 +1123,26 @@
                 grates.append(grate.astype(bf16))
                 gact[c, rs, :] += vec[CONV + 2 : CONV + 3, cols] * gs[c, rs, :]
             grate = jnp.concatenate(grates, axis=1)
-            r["grate"][...] += dot(grate, r["proj"][b, :, :RANK], ((0,), (0,)))
-            grank = dot(grate, r["mats"][:, :RANK], ((1,), (0,)))
+            r.grate[...] += dot(grate, r.proj[b, :, :RANK], ((0,), (0,)))
+            grank = dot(grate, r.mats[:, :RANK], ((1,), (0,)))
             gkq = gkq + jnp.where(lane < STATE, 2.0 * keys * gnorm, 0.0)
             out = jnp.concatenate([grank, gkq], axis=1)
-            r["payload"][b] = encode(out)
+            r.payload[b] = encode(out)
 
             @pl.when(b == total.me)
             def _():
-                r["own"][...] = out
+                r.own[...] = out
 
             return carry
 
         last = (blocks - 1) % 2
-        pltpu.make_async_copy(r["keep"].at[blocks - 1], r["keeps"].at[last], r["keep_sems"].at[last]).start()
+        pltpu.make_async_copy(r.keep.at[blocks - 1], r.keeps.at[last], r.keep_sems.at[last]).start()
         lax.fori_loop(0, blocks // 2, block, 0)
         reduce.middle()
         gate_reduce.start()
         lax.fori_loop(blocks // 2, blocks, block, 0)
         total.start()
-        total.middle(r["own"][...])
+        total.middle(r.own[...])
         total.finish()
         gate_reduce.middle()
         step[:, rows:, :] = jnp.zeros((parts, halo, LANES), f32)
@@ -1112,10 +1150,10 @@
 
         def convs(b, carry):
             rs = at_block(b, size)
-            gp = r["total"][b]
+            gp = r.total[b]
             gp = jnp.where(lanes_of(gp.shape) < RANK + 2 * STATE, gp.astype(f32), 0.0).astype(bf16)
-            r["gselect"][...] += dot(wide_of(act, rs, parts).astype(bf16), gp, ((0,), (0,)))
-            more = dot(gp, r["mats"][:, RANK:], ((1,), (1,)))
+            r.gselect[...] += dot(wide_of(act, rs, parts).astype(bf16), gp, ((0,), (0,)))
+            more = dot(gp, r.mats[:, RANK:], ((1,), (1,)))
             for c in range(parts):
                 conv = conv_of(entry, vec, b * size, size, c)
                 sig = jax.nn.sigmoid(conv)
@@ -1141,37 +1179,37 @@
                 gs[c, rs, :] = value
                 for s in range(TP):
                     at = pl.ds(b * size + s, STEPS, stride=TP)
-                    r["gentry"][s, here, cols] = gs[c, at, :].astype(bf16)
+                    r.gentry[s, here, cols] = gs[c, at, :].astype(bf16)
             return carry
 
         lax.fori_loop(0, blocks, inners, 0)
-        lax.fori_loop(0, width // tile, lambda i, k: outer_in(r["ginner"], 0, i, k), 0)
+        lax.fori_loop(0, width // tile, lambda i, k: outer_in(r.ginner, 0, i, k), 0)
         over = remote(
-            r["ginner"].at[pl.ds((1 - x) * zh_size, zh_size)], r["near"], r["over"][0], r["over"][1], side
+            r.ginner.at[pl.ds((1 - x) * zh_size, zh_size)], r.near, r.over[0], r.over[1], side
         )
         over.start()
         loads[6].wait()
-        scatter = Scatter(r["a"], r["scatter_buf"], r["scatter_sems"])
-        out_partial(scatter, r["a"], r["gentry"], lambda: r["b"][...], turned=True)
-        r["gmats"][:, :RANK] = r["grate"][...].astype(bf16)
-        r["gmats"][:, RANK:] = r["gselect"][...].astype(bf16)
+        scatter = Scatter(r.a, r.scatter_buf, r.scatter_sems)
+        out_partial(scatter, r.a, r.gentry, lambda: r.b[...], turned=True)
+        r.gmats[:, :RANK] = r.grate[...].astype(bf16)
+        r.gmats[:, RANK:] = r.gselect[...].astype(bf16)
         for j in range(8):
             for c in range(parts):
-                r["gvec"][j : j + 1, c * LANES : (c + 1) * LANES] = jnp.sum(sums[j, c], axis=0, keepdims=True)
-        r["gwout"][...] = reduce.total()
-        r["ggate"][...] = gate_reduce.total().astype(bf16)
+                r.gvec[j : j + 1, c * LANES : (c + 1) * LANES] = jnp.sum(sums[j, c], axis=0, keepdims=True)
+        r.gwout[...] = reduce.total()
+        r.ggate[...] = gate_reduce.total().astype(bf16)
         gnormed = scatter.total()
-        stream = r["h"][...]
+        stream = r.h[...]
         scale = rms(stream)
-        r["ggain"][...] = jnp.sum(gnormed * stream * scale, axis=0, keepdims=True)
-        scaled = gnormed * r["gain"][layer : layer + 1, :]
-        grad = r["grad"][...] + scale * scaled - stream * (scale * scale * scale) * jnp.mean(
+        r.ggain[...] = jnp.sum(gnormed * stream * scale, axis=0, keepdims=True)
+        scaled = gnormed * r.gain[layer : layer + 1, :]
+        grad = r.grad[...] + scale * scaled - stream * (scale * scale * scale) * jnp.mean(
             stream * scaled, axis=-1, keepdims=True
         )
-        r["prev"][...] = grad
+        r.prev[...] = grad
         if onward:
-            r["gout"][...] = grad.astype(bf16)
-            spread = Gather(r["gout"], r["gog"], r["gather_sems"])
+            r.gout[...] = grad.astype(bf16)
+            spread = Gather(r.gout, r.gog, r.gather_sems)
             spread.start()
             spread.relay()
             spread.rest()
@@ -1180,51 +1218,45 @@
             copy.wait()
         over.wait()
 
-    return call(body, "layer_backward", 9 if onward else 8, ins, outs, scratch)
-
-
-def closing(zh_size, inner, near, mats, small, stats, gain, turns, gwouts, select):
+    return call(body, 9 if onward else 8, ins, outs, scratch)
+
+
+def closing(zh_size, inner, near, mats, small, stats, gain, turns, share, width, select):
     groups = 2 * zh_size
     count = groups * TP
     far_n = max(1, zh_size - 1)
     dma = pltpu.SemaphoreType.DMA
     depth, half = inner.shape[3] // WAYS, inner.shape[4]
-    share, width = gwouts[0].shape
     gains = width // count
     every = (2, zh_size) + stats.shape
     v = pltpu.VMEM
     ins = dict(
         inner=(inner, VM), near=(near, VM), mats=(mats, VM), small=(small, VM), stats=(stats, VM), gain=(gain, VM),
-        t0=(turns[0], VM), t1=(turns[1], VM), t2=(turns[2], VM), w0=(gwouts[0], VM), w1=(gwouts[1], VM),
+        t0=(turns[0], VM), t1=(turns[1], VM), t2=(turns[2], VM),
     )
     outs = dict(
         gin=(struct(LAYERS, depth, 2 * count * share), VM), gselect=(struct(LAYERS, share, select), VM),
-        grate=(struct(LAYERS, RANK, share), VM), gwout=(struct(LAYERS, share, width), VM),
+        grate=(struct(LAYERS, RANK, share), VM),
         ggain=(struct(LAYERS, gains), VM), gtaps=(struct(LAYERS, CONV, share), VM), gshift=(struct(LAYERS, share), VM),
         grate_shift=(struct(LAYERS, share), VM), gskip=(struct(LAYERS, share), VM), stats_all=(struct(*stats.shape), VM),
     )
-    chunk = lambda shape, dtype: dict(
-        s=v(shape[1:], dtype), z=v((far_n,) + shape[2:], dtype), z_sems=[dma((far_n,)), dma((far_n,))]
-    )
-    shapes = dict(
-        c0=(inner.shape[:2] + inner.shape[3:], bf16), c1=(inner.shape[:2] + inner.shape[3:], bf16),
-        mats=(mats.shape, bf16), small=(small.shape, f32), stats=(every, f32),
-    )
+
+    def chunk(shape, dtype):
+        return [
+            v(shape[1:], dtype), v((far_n,) + shape[2:], dtype), dma((far_n,)), dma((far_n,)), v(shape[1:], dtype), dma, dma
+        ]
+
+    piece = inner.shape[:2] + inner.shape[3:]
     scratch = dict(
         vectors=v(small.shape, f32), stats_v=v(every, f32), stats_t=v((TP - 1,) + stats.shape, f32),
         gain_t=v((TP - 1,) + gain.shape[1:], f32), win_t=v((2, WAYS, depth, half), bf16),
         total=v(small.shape[2:], f32),
         g_sems=[dma((TP - 1,))] * 2, s_sems=[dma((TP - 1,))] * 2,
     )
-    for i in range(4):
-        scratch["b%d" % i] = v((TP, depth, half), bf16)
-        scratch["b%d_sems" % i] = [dma((TP - 1,)), dma((TP - 1,))]
-    for name, (shape, dtype) in shapes.items():
-        for key, value in chunk(shape, dtype).items():
-            scratch[name + "_" + key] = value
-        if name not in ("c0", "c1"):
-            scratch[name + "_near"] = v(shape[1:], dtype)
-            scratch[name + "_x"] = [dma, dma]
+    scratch.update(
+        boxes=v((4, TP, depth, half), bf16), turn_sems=[[dma((TP - 1,)), dma((TP - 1,))] for _ in range(4)],
+        chunks=[chunk(piece, bf16), chunk(piece, bf16), chunk(mats.shape, bf16), chunk(small.shape, f32), chunk(every, f32)],
+    )
 
     def body(r):
         x, core, zh, q = place()
@@ -1242,23 +1274,23 @@
             return a + b
 
         class Chunk:
-            def __init__(self, name, src, near=None):
-                self.name, self.src, self.near, self.peaks = name, src, near, name == "stats"
+            def __init__(self, number, src, near=None):
+                self.src, self.peaks = src, number == 4
+                self.mine, self.buf, self.z_send, self.z_recv, spare, self.x_send, self.x_recv = r.chunks[number]
+                self.near = spare if near is None else near
 
             def start(self):
-                self.near = r[self.name + "_near"]
-                sems = r[self.name + "_x"]
-                self.over = remote(self.src.at[1 - x], self.near, sems[0], sems[1], side)
+                self.over = remote(self.src.at[1 - x], self.near, self.x_send, self.x_recv, side)
                 self.over.start()
                 sent.append(self.over)
 
             def middle(self, arrived=False):
                 if not arrived:
                     self.over.wait_recv()
-                mine, buf, sems = r[self.name + "_s"], r[self.name + "_z"], r[self.name + "_z_sems"]
+                mine, buf = self.mine, self.buf
                 mine[...] = join(self.src[x], self.near[...], self.peaks).astype(mine.dtype)
                 self.along = [
-                    remote(mine.at[to_z], buf.at[k], sems[0].at[k], sems[1].at[k], target)
+                    remote(mine.at[to_z], buf.at[k], self.z_send.at[k], self.z_recv.at[k], target)
                     for k, (target, to_z, _) in enumerate(far)
                 ]
                 for copy in self.along:
@@ -1269,93 +1301,89 @@
                 value = join(self.src[x, zh], self.near[zh], self.peaks)
                 for k, copy in enumerate(self.along):
                     copy.wait_recv()
-                    value = join(value, r[self.name + "_z"][k], self.peaks)
+                    value = join(value, self.buf[k], self.peaks)
                 return value
 
         def turn(src, i):
-            box, sems = r["b%d" % i], r["b%d_sems" % i]
+            box, sems = r.boxes.at[i], r.turn_sems[i]
             for k, (target, rank, _) in enumerate(peers):
                 copy = remote(src(rank), box.at[me], sems[0].at[k], sems[1].at[k], target)
                 copy.start()
                 full.append(copy)
             box[me] = src(me)[...]
 
-        cs = [Chunk("c%d" % c, r["inner"].at[:, :, c], r["near"].at[:, c]) for c in range(2)]
+        cs = [Chunk(c, r.inner.at[:, :, c], r.near.at[:, c]) for c in range(2)]
         cs[0].middle(arrived=True)
         cs[1].middle(arrived=True)
         gained, shown = [], []
         for i, (target, rank, _) in enumerate(peers):
             for src, buf, sems, copies in (
-                (r["gain"].at[rank], r["gain_t"], r["g_sems"], gained),
-                (r["stats"], r["stats_t"], r["s_sems"], shown),
+                (r.gain.at[rank], r.gain_t, r.g_sems, gained),
+                (r.stats, r.stats_t, r.s_sems, shown),
             ):
                 copy = remote(src, buf.at[i], sems[0].at[i], sems[1].at[i], target)
                 copy.start()
                 copies.append(copy)
                 sent.append(copy)
-        mats_c = Chunk("mats", r["mats"])
+        mats_c = Chunk(2, r.mats)
         mats_c.start()
-        for l in range(LAYERS):
-            r["gwout"][l] = r["w%d" % l][...]
+        sources = (r.t0, r.t1, r.t2)
         for i in range(3):
-            turn(lambda rank, i=i: r["t%d" % i].at[rank], i + 1)
-        total = r["gain"][me]
-        seen = r["stats"][...]
+            turn(lambda rank, i=i: sources[i].at[rank], i + 1)
+        total = r.gain[me]
+        seen = r.stats[...]
         for i in range(TP - 1):
             gained[i].wait_recv()
-            total = total + r["gain_t"][i]
+            total = total + r.gain_t[i]
             shown[i].wait_recv()
-            seen = join(seen, r["stats_t"][i], True)
-        r["vectors"][...] = r["small"][...]
+            seen = join(seen, r.stats_t[i], True)
+        r.vectors[...] = r.small[...]
         for l in range(LAYERS):
             for g in range(groups):
                 at = l * groups + g
-                r["vectors"][g // zh_size, g % zh_size, l * 16 + 8 : l * 16 + 9, :] = total[at : at + 1, :]
-        r["stats_v"][...] = jnp.broadcast_to(seen, every)
-        rest = [mats_c, Chunk("small", r["vectors"]), Chunk("stats", r["stats_v"])]
+                r.vectors[g // zh_size, g % zh_size, l * 16 + 8 : l * 16 + 9, :] = total[at : at + 1, :]
+        r.stats_v[...] = jnp.broadcast_to(seen, every)
+        rest = [mats_c, Chunk(3, r.vectors), Chunk(4, r.stats_v)]
         for c in rest[1:]:
             c.start()
         for c in rest:
             c.middle()
         for c in range(2):
-            r["win_t"][c] = cs[c].total().astype(bf16).reshape(WAYS, depth, half)
-        turn(lambda rank: r["win_t"].at[rank // WAYS, lax.rem(rank, WAYS)], 0)
+            r.win_t[c] = cs[c].total().astype(bf16).reshape(WAYS, depth, half)
+        turn(lambda rank: r.win_t.at[rank // WAYS, lax.rem(rank, WAYS)], 0)
         m = rest[0].total()
         for l in range(LAYERS):
             base = 3 * LANES * l
-            r["grate"][l] = m[:, base : base + RANK].T
-            r["gselect"][l] = m[:, base + RANK : base + RANK + select]
-        r["total"][...] = rest[1].total()
+            r.grate[l] = m[:, base : base + RANK].T
+            r.gselect[l] = m[:, base + RANK : base + RANK + select]
+        r.total[...] = rest[1].total()
         for l in range(LAYERS):
-            r["gtaps"][l] = r["total"][16 * l : 16 * l + CONV, :share]
-            for name, j, size in (
-                ("gshift", CONV, share), ("grate_shift", CONV + 1, share), ("gskip", CONV + 2, share), ("ggain", 8, gains)
+            r.gtaps[l] = r.total[16 * l : 16 * l + CONV, :share]
+            for out, j, size in (
+                (r.gshift, CONV, share), (r.grate_shift, CONV + 1, share), (r.gskip, CONV + 2, share), (r.ggain, 8, gains)
             ):
-                r[name][l : l + 1, :] = r["total"][16 * l + j : 16 * l + j + 1, :size]
-        r["stats_all"][...] = rest[2].total()
-
-        def lay(box, l, at):
+                out[l : l + 1, :] = r.total[16 * l + j : 16 * l + j + 1, :size]
+        r.stats_all[...] = rest[2].total()
+
+        def lay(i):
             for rank in range(TP):
                 for g in range(groups):
                     d = ((g // zh_size * 2 + rank // WAYS) * zh_size + g % zh_size) * WAYS + rank % WAYS
-                    r["gin"][l, :, at + d * share : at + (d + 1) * share] = box[
-                        rank, :, g * share : (g + 1) * share
-                    ].astype(f32)
-
-        boxes = {0: (0, 0), 1: (0, count * share), 2: (1, 0), 3: (1, count * share)}
-        done = full[: 3 * (TP - 1)]
-        for copy in done:
+                    first = i % 2 * count * share + d * share
+                    r.gin[i // 2, :, first : first + share] = r.boxes[i, rank, :, g * share : (g + 1) * share].astype(f32)
+
+        early, late = full[: 3 * (TP - 1)], full[3 * (TP - 1) :]
+        for copy in early:
             copy.wait_recv()
         for i in (1, 2, 3):
-            lay(r["b%d" % i], *boxes[i])
-        late = full[3 * (TP - 1) :]
+            lay(i)
         for copy in late:
             copy.wait_recv()
-        lay(r["b0"], *boxes[0])
-        for copy in sent + done + late:
+        lay(0)
+        for copy in sent + full:
             copy.wait_send()
 
-    return call(body, "closing", 5, ins, outs, scratch)
+    return call(body, 5, ins, outs, scratch)
 
 
 def on_device(
@@ -1375,8 +1403,10 @@
     labels = jnp.arange(group_weights.shape[0])
     own_weight = jnp.sum(jnp.where(groups[:, None] == labels[None, :], group_weights[None, :], 0.0))
 
-    wins = input_weight.reshape(LAYERS, depth, 2, 2, 2, zh_size, WAYS, share)
-    wins = wins.transpose(0, 4, 6, 1, 2, 3, 5, 7).reshape(LAYERS, TP, depth, 2 * half)
+    wins = input_weight
+    if share % LANES:
+        wins = wins.reshape(LAYERS, depth, 2, 2, 2, zh_size, WAYS, share)
+        wins = wins.transpose(0, 4, 6, 1, 2, 3, 5, 7).reshape(LAYERS, TP, depth, 2 * half)
     mats = jnp.concatenate([rate_weight.swapaxes(1, 2), select_weight], axis=2)
     mats = jnp.pad(mats, ((0, 0), (0, 0), (0, 3 * LANES - mats.shape[2])))
     vectors = [conv_taps, conv_shift[:, None], rate_shift[:, None], skip_gain[:, None], skip_gain[:, None]]
@@ -1387,55 +1417,58 @@
 
     flat = lambda a: a.reshape(half, -1)
     h0 = hidden[0]
-    start = opening(zh_size, gains, share, wins[0], small, misc, mats[0], h0, cotangent[0])
-    vec, gain, scale = start["vec"], start["gains"], start["scale"]
-    win0, mat0 = start["win_all"].reshape(count * depth, -1), flat(start["mats_all"])
+    start = opening(zh_size, gains, share, wins, small, misc, mats, h0, cotangent[0])
+    vec, gain, scale = start.vec, start.gains, start.scale
+    win0, mat0 = start.win_all.reshape(count * depth, -1), flat(start.mats_all)
     one = forward_layer(
-        zh_size, 0, start["xg"], win0, mat0, output_weight[0], vec, scale,
-        nxt=dict(h=h0, gain=gain, win=wins[1], mats=mats[1]),
-    )
-    win1, mat1 = one["win1_all"].reshape(count * depth, -1), flat(one["mats1_all"])
-    h1 = one["result"]
-    two = forward_layer(zh_size, 1, one["xg1"], win1, mat1, output_weight[1], vec, scale, gout=start["gout"])
+        zh_size, 0, start.xg, win0, mat0, output_weight, vec, scale,
+        nxt=types.SimpleNamespace(h=h0, gain=gain, win=wins, mats=mats),
+    )
+    win1, mat1 = one.win1_all.reshape(count * depth, -1), flat(one.mats1_all)
+    h1 = one.result
+    two = forward_layer(zh_size, 1, one.xg1, win1, mat1, output_weight, vec, scale, gout=start.gout)
 
     down1 = backward_layer(
-        zh_size, 1, two, two["gog"], flat(two["wout_all"]), mat1, vec, one["xg1"], win1, gain, h1, start["grad"],
-        part=two["part"],
-    )
-    stream = h1 + jnp.sum(down1["parts_all"].astype(f32), axis=0)
-    blocks = (2, zh_size) + down1["ginner"].shape[1:]
+        zh_size, 1, two, two.gog, flat(two.wout_all), mat1, vec, one.xg1, win1, gain, h1, start.grad,
+        part=two.part,
+    )
+    stream = h1 + jnp.sum(down1.parts_all.astype(f32), axis=0)
+    blocks = (2, zh_size) + down1.ginner.shape[1:]
     pick = lambda a, i: lax.dynamic_index_in_dim(a, i, 0, keepdims=False)
-    summed = pick(down1["ginner"].reshape(blocks), x).astype(f32) + down1["near"].astype(f32)
+    summed = pick(down1.ginner.reshape(blocks), x).astype(f32) + down1.near.astype(f32)
     down0 = backward_layer(
-        zh_size, 0, one, down1["gog"], flat(one["wout_all"]), mat0, vec, start["xg"], win0, gain, h0, down1["prev"],
+        zh_size, 0, one, down1.gog, flat(one.wout_all), mat0, vec, start.xg, win0, gain, h0, down1.prev,
         late=summed.astype(bf16),
     )
     late = pick(summed, zh)
     for k in range(zh_size - 1):
-        late = late + down0["late"][k].astype(f32)
-
-    sums = [jnp.sum(o["stats"][0]) for o in (one, two)]
-    peaks = [jnp.max(o["stats"][1]) for o in (one, two)]
+        late = late + down0.late[k].astype(f32)
+
+    sums = [jnp.sum(o.stats[0]) for o in (one, two)]
+    peaks = [jnp.max(o.stats[1]) for o in (one, two)]
     pad = [jnp.zeros((), f32)] * (4 - LAYERS)
     own_stats = jnp.broadcast_to(jnp.stack(sums + pad + peaks + pad)[:, None], (8, LANES))
     downs = (down0, down1)
-    small = jnp.stack([down["gvec"] for down in downs]).reshape(LAYERS, 8, group_count, share)
+    small = jnp.stack([down.gvec for down in downs]).reshape(LAYERS, 8, group_count, share)
     small = jnp.pad(small.transpose(2, 0, 1, 3), ((0, 0), (0, 0), (0, 8), (0, LANES - share)))
     small = small.reshape(2, zh_size, 16 * LAYERS, LANES)
-    spread_gain = jnp.stack([down["ggain"][0] for down in downs]).reshape(LAYERS, 2, 2, zh_size, WAYS, gains)
+    spread_gain = jnp.stack([down.ggain[0] for down in downs]).reshape(LAYERS, 2, 2, zh_size, WAYS, gains)
     spread_gain = spread_gain.transpose(2, 4, 0, 1, 3, 5).reshape(TP, LAYERS * group_count, gains)
     spread_gain = jnp.pad(spread_gain, ((0, 0), (0, -LAYERS * group_count % 8), (0, LANES - gains)))
-    mats = jnp.concatenate([down["gmats"] for down in downs], axis=1).reshape(2, zh_size, share, -1)
-    turns = [down0["ggate"], late.astype(bf16), down1["ggate"]]
+    mats = jnp.concatenate([down.gmats for down in downs], axis=1).reshape(2, zh_size, share, -1)
+    turns = [down0.ggate, late.astype(bf16), down1.ggate]
     end = closing(
-        zh_size, down0["ginner"].reshape(blocks), down0["near"], mats, small, own_stats, spread_gain,
-        [t.reshape(TP, depth, half) for t in turns], [down["gwout"] for down in downs], select_weight.shape[2],
-    )
-    stats = end["stats_all"]
+        zh_size, down0.ginner.reshape(blocks), down0.near, mats, small, own_stats, spread_gain,
+        [t.reshape(TP, depth, half) for t in turns], share, output_weight.shape[2], select_weight.shape[2],
+    )
+    stats = end.stats_all
     beta_mean = stats[:LAYERS, 0] / (count * hidden.shape[1] * INNER)
     beta_max = stats[4 : 4 + LAYERS, 0]
-    names = ("gin", "gselect", "grate", "gwout", "ggain", "gtaps", "gshift", "grate_shift", "gskip")
-    return (stream[None], down0["prev"][None]) + tuple(end[n] for n in names) + (beta_mean, beta_max)
+    gwout = jnp.stack([down.gwout for down in downs])
+    return (
+        stream[None], down0.prev[None], end.gin, end.gselect, end.grate, gwout, end.ggain, end.gtaps, end.gshift,
+        end.grate_shift, end.gskip, beta_mean, beta_max,
+    )
 
 
 def solution(mesh):

time: 668 us -> 644 us (0.964)
  local copies, waits for them, and re-layouts: 36.8 us -> 19 us
  Pallas kernels: 606 us -> 594 us
    pallas_call x6, Pallas kernels: 606 us -> 594 us  [call(): pl.pallas_call(kernel, out_shape=[shape for shape, _ in outs.values()], i...]
    unnamed x46 -> x47, local copies, waits for them, and re-layouts: 15.6 us -> 10.3 us
where the time goes in v5:
time: 644 us; the launch traced here: 634 us
  Pallas kernels  594 us (92%)
  other arithmetic  19.4 us (3%)
  local copies, waits for them, and re-layouts  19 us (3%)
    pallas_call x6, Pallas kernels, call(): pl.pallas_call(kernel, out_shape=[shape for shape, _ in outs.values()], i...  594 us

profile of v5, /device:TPU:0, one launch (start us, length us, event | category | flops | bytes accessed | tf_op | source)
XLA Modules:
  0.0 634.1 jit_solution(2382757502453188030)
XLA Ops:
  1.3 1.3 fusion.3
  2.6 0.7 pad_convert_fusion
  3.2 0.7 copy.42
  3.9 0.7 copy.43
  4.6 0.7 copy.44
  5.2 0.7 concatenate.13
  5.9 1.2 concatenate.14.refs_2_
  7.2 0.6 bitcast_convert_fusion.refs_1_
  7.8 0.9 copy.46
  8.7 1.0 copy.47
  9.7 0.7 fusion.2.refs_3_.refs_10_
  10.4 77.2 %shard_map.282 = (bf16[32,64,1024]{2,1,0:T(8,128)(2,1)}, bf16[4,128,384]{2,1,0:T(8,128)(2,1)}, f32[16,512]{1,0:T(8,128)}, f32[8,2048]{1,0:T(8,128)}, f32[8,128]{...) custom-call(bf16[2,64,8192]{2,1,0:T(8,128)(2,1)} %refs_9_.1, ...), custom_call_target="tpu_custom_call" | custom-call | tf_op jit(solution)/shard_map/pallas_call | solution.py:317
  87.6 128.6 %shard_map.283 = (f32[8,1048,128]{2,1,0:T(8,128)}, f32[4,1024,128]{2,1,0:T(8,128)}, f32[1024,128]{1,0:T(8,128)}, bf16[8,128,256]{2,1,0:T(8,128)(2,1)}, f32[4,102...) custom-call(bf16[8,128,2048]{2,1,0:T(8,128)(2,1)} %get-tuple-element, ...), custom_call_target="tpu_custom_call" | custom-call | tf_op jit(solution)/shard_map/pallas_call | solution.py:317
  216.2 1.3 slice_reduce_fusion.1
  217.5 71.0 %shard_map.284 = (f32[8,1048,128]{2,1,0:T(8,128)}, f32[4,1024,128]{2,1,0:T(8,128)}, f32[1024,128]{1,0:T(8,128)}, bf16[8,128,256]{2,1,0:T(8,128)(2,1)}, f32[4,102...) custom-call(bf16[8,128,2048]{2,1,0:T(8,128)(2,1)} %get-tuple-element, ...), custom_call_target="tpu_custom_call" | custom-call | tf_op jit(solution)/shard_map/pallas_call | solution.py:317
  288.5 144.2 %shard_map.285 = (f32[128,2048]{1,0:T(8,128)}, bf16[4,2,256,512]{3,2,1,0:T(8,128)(2,1)}, bf16[2,2,256,512]{3,2,1,0:T(8,128)(2,1)}, bf16[2,256,512]{2,1,0:T(8,128...) custom-call(f32[8,1048,128]{2,1,0:T(8,128)} %get-tuple-element.84.re, ...), custom_call_target="tpu_custom_call" | custom-call | tf_op jit(solution)/shard_map/pallas_call | solution.py:317
  432.7 0.0 copy-start
  432.8 0.0 copy-start.10
  432.8 3.1 convert_reduce_fusion
  435.8 0.0 copy-done
  435.9 0.0 copy-start.3
  435.9 0.0 copy-start.4
  435.9 1.1 add_bitcast_fusion
  437.0 0.0 copy-done.10
  437.0 0.6 slice_reduce_fusion
  437.6 2.7 stack.43
  440.2 0.7 broadcast_in_dim.36.refs_4_
  440.9 0.0 copy-done.3
  440.9 0.0 copy-done.4
  440.9 2.1 fusion.4
  443.0 124.3 %shard_map.286 = (f32[128,2048]{1,0:T(8,128)}, bf16[4,2,256,512]{3,2,1,0:T(8,128)(2,1)}, bf16[2,2,256,512]{3,2,1,0:T(8,128)(2,1)}, bf16[2,256,512]{2,1,0:T(8,128...) custom-call(f32[8,1048,128]{2,1,0:T(8,128)} %get-tuple-element.96.re, ...), custom_call_target="tpu_custom_call" | custom-call | tf_op jit(solution)/shard_map/pallas_call | solution.py:317
  567.3 0.0 copy-start.11
  567.3 0.0 copy-start.12
  567.3 0.0 copy-start.8
  567.3 0.0 copy-start.9
  567.3 0.0 copy-start.5
  567.4 0.0 copy-start.6
  567.4 2.4 add_convert_fusion
  569.8 0.0 copy-done.11
  569.8 0.0 copy-done.12
  569.8 0.1 reshape.105
  569.9 0.6 pad.24.refs_5_
  570.6 0.0 copy-done.8
  570.6 0.0 copy-done.9
  570.6 0.6 pad.23
  571.2 0.0 copy-done.5
  571.2 0.0 copy-done.6
  571.2 0.9 pad_maximum_fusion.1
  572.2 48.7 %shard_map.287 = (f32[2,64,8192]{2,1,0:T(8,128)}, f32[2,128,160]{2,1,0:T(8,128)}, f32[2,128,128]{2,1,0:T(8,128)}, f32[2,64]{1,0:T(2,128)}, f32[2,4,128]{2,1,0:T(...) custom-call(bf16[2,2,2,256,512]{4,3,2,1,0:T(8,128)(2,1)} %bitcast.59, ...), custom_call_target="tpu_custom_call" | custom-call | tf_op jit(solution)/shard_map/pallas_call | solution.py:317
  620.9 1.4 slice_reduce_fusion.4
  622.3 1.8 copy.51
  624.2 3.2 pad_maximum_fusion
  627.4 0.0 copy-done.2
  627.4 1.0 copy.61
  628.4 2.0 copy.62
  630.4 0.0 copy-done.7
  630.4 0.7 copy.63
  631.1 0.0 copy-done.17
  631.1 0.6 copy.64
  631.6 0.6 copy.65
  632.2 0.6 copy.66
  632.8 0.6 copy.67
  633.4 0.0 copy-done.14
  633.4 0.6 copy.68
  (16 shorter events, 0.1 us)
Async XLA Ops:
  432.7 3.1 copy-start
  432.8 4.2 copy-start.10
  435.9 5.1 copy-start.3
  435.9 5.1 copy-start.4
  567.3 2.5 copy-start.11
  567.3 2.5 copy-start.12
  567.3 3.2 copy-start.8
  567.3 3.2 copy-start.9
  567.3 3.9 copy-start.5
  567.4 3.9 copy-start.6
  622.3 5.1 copy-start.2
  624.2 4.2 copy-start.1
  628.4 2.1 copy-start.7
  628.4 2.7 copy-start.17
  628.4 3.3 copy-start.13
  628.4 3.9 copy-start.16
  628.4 4.4 copy-start.15
  628.4 5.0 copy-start.14

commit v6 on v5

--- a/solution.py
+++ b/solution.py
@@ -23,6 +23,7 @@
 bf16 = jnp.bfloat16
 VM = pl.BlockSpec(memory_space=pltpu.VMEM)
 HB = pl.BlockSpec(memory_space=pl.ANY)
+EARLY, LATE = object(), object()
 
 
 def place():
@@ -308,18 +309,38 @@
     def rebuild(kind, refs):
         return [rebuild(each, refs) for each in kind] if isinstance(kind, list) else refs.pop(0)
 
+    early = [key for key, (_, spec) in ins.items() if spec is EARLY]
+    late = [key for key, (_, spec) in outs.items() if spec is LATE]
+    space = lambda spec: HB if spec is EARLY or spec is LATE else spec
+    held = [pltpu.VMEM(ins[key][0].shape, ins[key][0].dtype) for key in early]
+    held += [pltpu.VMEM(outs[key][0].shape, outs[key][0].dtype) for key in late]
+    extra = [held, [pltpu.SemaphoreType.DMA] * len(held)]
+
     def kernel(*refs):
         refs = list(refs)
         named = {key: refs.pop(0) for key in list(ins) + list(outs)}
         named.update({key: rebuild(kind, refs) for key, kind in scratch.items()})
-        body(types.SimpleNamespace(**named))
+        buffers, sems = rebuild(extra, refs)
+        loads, stores = {}, {}
+        for key, buffer, sem in zip(early + late, buffers, sems):
+            if key in early:
+                loads[key] = pltpu.make_async_copy(named[key], buffer, sem)
+            else:
+                stores[key] = pltpu.make_async_copy(buffer, named[key], sem)
+            named[key] = buffer
+        r = types.SimpleNamespace(**named)
+        r.load = lambda: [copy.start() for copy in loads.values()]
+        r.need = types.SimpleNamespace(**{key: copy.wait for key, copy in loads.items()})
+        r.put = types.SimpleNamespace(**{key: copy.start for key, copy in stores.items()})
+        r.done = lambda: [copy.wait() for copy in stores.values()]
+        body(r)
 
     values = pl.pallas_call(
         kernel,
         out_shape=[shape for shape, _ in outs.values()],
-        in_specs=[spec for _, spec in ins.values()],
-        out_specs=[spec for _, spec in outs.values()],
-        scratch_shapes=flatten(list(scratch.values())),
+        in_specs=[space(spec) for _, spec in ins.values()],
+        out_specs=[space(spec) for _, spec in outs.values()],
+        scratch_shapes=flatten(list(scratch.values()) + extra),
         compiler_params=pltpu.CompilerParams(
             collective_id=collective, has_side_effects=True, vmem_limit_bytes=63 * 2**20
         ),
@@ -574,14 +595,14 @@
     last = nxt is None
     groups = 2 * zh_size
     ins = dict(
-        xg=(xg, VM), win=(win, VM), mats=(mats, VM), wout=(wout, HB), vec=(vec, VM),
-        scale=(scale, VM), e=(spreader(), VM),
+        xg=(xg, EARLY), win=(win, EARLY), mats=(mats, EARLY), wout=(wout, HB), vec=(vec, VM),
+        scale=(scale, VM), e=(spreader(), EARLY),
     )
     outs = dict(
-        entry=(struct(2 * parts, halo + rows, LANES), VM), beta=(struct(parts, rows, LANES), VM),
-        kq=(struct(rows, LANES), VM), proj=(struct(TP, size, 2 * LANES, dtype=bf16), VM),
-        y=(struct(parts, rows, LANES), VM), keep=(struct(blocks, STATE, parts, TP, LANES), VM),
-        mixed=(struct(TP, tokens, half, dtype=bf16), VM), stats=(struct(2, TP, LANES), VM),
+        entry=(struct(2 * parts, halo + rows, LANES), LATE), beta=(struct(parts, rows, LANES), LATE),
+        kq=(struct(rows, LANES), LATE), proj=(struct(TP, size, 2 * LANES, dtype=bf16), LATE),
+        y=(struct(parts, rows, LANES), LATE), keep=(struct(blocks, STATE, parts, TP, LANES), LATE),
+        mixed=(struct(TP, tokens, half, dtype=bf16), LATE), stats=(struct(2, TP, LANES), VM),
     )
     scratch = dict(
         act=pltpu.VMEM((parts, rows, LANES), f32), step=pltpu.VMEM((parts, rows, LANES), f32),
@@ -590,18 +611,18 @@
         state=pltpu.VMEM((STATE, parts, TP, LANES), f32), wide=pltpu.VMEM((size, 32 * LANES), f32),
         sum_sems=Sum.sems(dma),
     )
-    outs.update(wout_all=(struct(groups, *wout.shape[1:], dtype=bf16), VM))
+    outs.update(wout_all=(struct(groups, *wout.shape[1:], dtype=bf16), LATE))
     scratch.update(d0=Spread.sems(dma, zh_size))
     if last:
         ins.update(gout=(gout, VM))
         outs.update(
-            gog=(struct(TP, tokens, width, dtype=bf16), HB), part=(struct(TP, tokens, width, dtype=bf16), VM)
+            gog=(struct(TP, tokens, width, dtype=bf16), HB), part=(struct(TP, tokens, width, dtype=bf16), LATE)
         )
         scratch.update(gather_sems=Gather.sems(dma))
     if not last:
         win1 = nxt.win
         depth = win1.shape[-2]
-        ins.update(h=(nxt.h, VM), gain=(nxt.gain, VM), win1=(win1, HB), mats1=(nxt.mats, HB))
+        ins.update(h=(nxt.h, EARLY), gain=(nxt.gain, VM), win1=(win1, HB), mats1=(nxt.mats, HB))
         outs.update(
             result=(struct(tokens, width), VM),
             win1_all=(struct(2, 2, zh_size, WAYS, depth, 2 * half, dtype=bf16), HB),
@@ -617,6 +638,7 @@
         )
 
     def body(r):
+        r.load()
         side, far = dp_peers(zh_size)
         greet([p[0] for p in tp_peers()] + [side] + [f[0] for f in far])
         entry, act, step, beta, kq, y = r.entry, r.act, r.step, r.beta, r.kq, r.y
@@ -637,6 +659,8 @@
                 src = r.turned.at[k * WAYS : (k + 1) * WAYS]
                 moves.append(Spread(zh_size, src, view, (r.d1 if k == 0 else r.d2)))
 
+        r.need.xg()
+        r.need.win()
         entry[:, :halo, :] = jnp.zeros((2 * parts, halo, LANES), f32)
         tile = 2 * LANES
         for p in range(TP // 2):
@@ -655,6 +679,8 @@
                 return carry
 
             lax.fori_loop(0, 2 * half // tile, columns, 0)
+        r.put.entry()
+        r.need.mats()
         total = Sum(r.payload, r.parts, r.proj, r.sum_sems)
 
         def project(b, carry):
@@ -684,6 +710,7 @@
             moves[1].start()
         total.middle(r.own[...])
         total.finish()
+        r.put.proj()
         if last:
             gouts.start()
         else:
@@ -711,6 +738,9 @@
             return carry
 
         lax.fori_loop(0, blocks, rates, 0)
+        r.put.beta()
+        r.put.kq()
+        r.need.e()
         r.stats[0] = r.stats[0] * r.scale[...]
         r.stats[1] = r.stats[1] * r.scale[...]
 
@@ -760,6 +790,8 @@
             moves[0].onward()
         lax.fori_loop(blocks // 2, blocks, block, 0)
         early.finish()
+        for start in (r.put.y, r.put.keep, r.put.mixed, r.put.wout_all):
+            start()
         weight = lambda: r.wout_all[...].reshape(half, width)
         if last:
 
@@ -772,11 +804,14 @@
             lax.fori_loop(0, TP // 4, plain, 0)
             gouts.rest()
             lax.fori_loop(TP // 4, TP // 2, plain, 0)
+            r.put.part()
             gouts.finish()
+            r.done()
             return
         scatter = Scatter(r.part, r.scatter_buf, r.scatter_sems)
         out_partial(scatter, r.part, r.mixed, weight)
         moves[1].onward()
+        r.need.h()
         stream = r.h[...] + scatter.total()
         r.result[...] = stream
         r.normed[...] = (stream * rms(stream) * r.gain[layer + 1 : layer + 2, :]).astype(bf16)
@@ -788,6 +823,7 @@
         spread.finish()
         for move in moves:
             move.finish()
+        r.done()
 
     return call(body, 7 if last else 6, ins, outs, scratch)
 
@@ -869,13 +905,13 @@
     far = max(1, zh_size - 1)
     dma = pltpu.SemaphoreType.DMA
     onward = part is not None
-    ins = dict(entry=(kept.entry, VM), beta=(kept.beta, VM), kq=(kept.kq, VM), proj=(kept.proj, VM))
+    ins = dict(entry=(kept.entry, EARLY), kq=(kept.kq, EARLY), beta=(kept.beta, EARLY), proj=(kept.proj, EARLY))
     ins.update(
-        mats=(mats, VM), wout=(wout, HB), vec=(vec, VM), gain=(gain, VM), h=(h, VM), grad=(grad, VM),
-        mixed=(kept.mixed, HB), e=(spreader(), VM), fold=(folder(), VM), keep=(kept.keep, HB), gouts=(gog, HB), y=(kept.y, HB), xg=(xg, HB), win=(win, HB),
+        mats=(mats, EARLY), wout=(wout, HB), vec=(vec, VM), gain=(gain, VM), h=(h, EARLY), grad=(grad, EARLY),
+        mixed=(kept.mixed, HB), e=(spreader(), EARLY), fold=(folder(), EARLY), keep=(kept.keep, HB), gouts=(gog, HB), y=(kept.y, HB), xg=(xg, HB), win=(win, HB),
     )
     outs = dict(
-        prev=(struct(tokens, width), VM), ginner=(struct(groups, 2, deep, half, dtype=bf16), VM),
+        prev=(struct(tokens, width), VM), ginner=(struct(groups, 2, deep, half, dtype=bf16), LATE),
         near=(struct(zh_size, 2, deep, half, dtype=bf16), HB), ggate=(struct(2, deep, half, dtype=bf16), VM), gwout=(struct(share, width), VM),
         gmats=(struct(half, 3 * LANES, dtype=bf16), VM), gvec=(struct(8, half), VM),
         ggain=(struct(1, width), VM),
@@ -928,8 +964,10 @@
                 )
             )
         ]
-        for copy in loads[:5]:
+        for copy in loads[:4]:
             copy.start()
+        r.load()
+        loads[4].start()
         passed = []
         if onward:
             me = core * WAYS + q
@@ -952,17 +990,6 @@
         r.grate[...] = jnp.zeros_like(r.grate)
         r.gselect[...] = jnp.zeros_like(r.gselect)
 
-        def again(b, carry):
-            rs = at_block(b, size)
-            norm = square_sum(kq[rs, :])
-            for c in range(parts):
-                conv = conv_of(entry, vec, b * size, size, c)
-                act[c, rs, :] = (conv * jax.nn.sigmoid(conv)).astype(bf16).astype(f32)
-                rate = beta[c, rs, :]
-                step[c, rs, :] = rate / (1.0 + rate * norm)
-            return carry
-
-        lax.fori_loop(0, blocks, again, 0)
         loads[0].wait()
         loads[1].wait()
 
@@ -996,6 +1023,21 @@
             lax.fori_loop(0, half // (2 * LANES), columns, 0)
         loads[5].start()
         loads[6].start()
+        r.need.entry()
+        r.need.kq()
+        r.need.beta()
+
+        def again(b, carry):
+            rs = at_block(b, size)
+            norm = square_sum(kq[rs, :])
+            for c in range(parts):
+                conv = conv_of(entry, vec, b * size, size, c)
+                act[c, rs, :] = (conv * jax.nn.sigmoid(conv)).astype(bf16).astype(f32)
+                rate = beta[c, rs, :]
+                step[c, rs, :] = rate / (1.0 + rate * norm)
+            return carry
+
+        lax.fori_loop(0, blocks, again, 0)
         loads[4].wait()
 
         def gates(b, carry):
@@ -1135,6 +1177,8 @@
 
             return carry
 
+        for wait in (r.need.proj, r.need.mats, r.need.e, r.need.fold):
+            wait()
         last = (blocks - 1) % 2
         pltpu.make_async_copy(r.keep.at[blocks - 1], r.keeps.at[last], r.keep_sems.at[last]).start()
         lax.fori_loop(0, blocks // 2, block, 0)
@@ -1188,6 +1232,7 @@
             r.ginner.at[pl.ds((1 - x) * zh_size, zh_size)], r.near, r.over[0], r.over[1], side
         )
         over.start()
+        r.put.ginner()
         loads[6].wait()
         scatter = Scatter(r.a, r.scatter_buf, r.scatter_sems)
         out_partial(scatter, r.a, r.gentry, lambda: r.b[...], turned=True)
@@ -1199,6 +1244,8 @@
         r.gwout[...] = reduce.total()
         r.ggate[...] = gate_reduce.total().astype(bf16)
         gnormed = scatter.total()
+        r.need.h()
+        r.need.grad()
         stream = r.h[...]
         scale = rms(stream)
         r.ggain[...] = jnp.sum(gnormed * stream * scale, axis=0, keepdims=True)
@@ -1217,6 +1264,7 @@
         for copy in passed:
             copy.wait()
         over.wait()
+        r.done()
 
     return call(body, 9 if onward else 8, ins, outs, scratch)
 

time: 644 us -> 624 us (0.969)
  Pallas kernels: 594 us -> 574 us
    pallas_call x6, Pallas kernels: 594 us -> 574 us  [call(): pl.pallas_call(kernel, out_shape=[shape for shape, _ in outs.values()], i...]
where the time goes in v6:
time: 624 us; the launch traced here: 614 us
  Pallas kernels  574 us (92%)
  other arithmetic  19.4 us (3%)
  local copies, waits for them, and re-layouts  19 us (3%)
    pallas_call x6, Pallas kernels, call(): pl.pallas_call(kernel, out_shape=[shape for shape, _ in outs.values()], i...  574 us

profile of v6, /device:TPU:0, one launch (start us, length us, event | category | flops | bytes accessed | tf_op | source)
XLA Modules:
  0.0 614.3 jit_solution(3271691714119640516)
XLA Ops:
  1.3 1.3 fusion.3
  2.6 0.7 pad_convert_fusion
  3.2 0.7 copy.42
  3.9 0.7 copy.43
  4.6 0.7 copy.44
  5.2 0.7 concatenate.13
  5.9 1.2 concatenate.14.refs_2_
  7.2 0.6 bitcast_convert_fusion.refs_1_
  7.8 0.9 copy.46
  8.7 1.0 copy.47
  9.7 0.7 fusion.2.refs_3_.refs_10_
  10.4 77.2 %shard_map.282 = (bf16[32,64,1024]{2,1,0:T(8,128)(2,1)}, bf16[4,128,384]{2,1,0:T(8,128)(2,1)}, f32[16,512]{1,0:T(8,128)}, f32[8,2048]{1,0:T(8,128)}, f32[8,128]{...) custom-call(bf16[2,64,8192]{2,1,0:T(8,128)(2,1)} %refs_9_.1, ...), custom_call_target="tpu_custom_call" | custom-call | tf_op jit(solution)/shard_map/pallas_call | solution.py:338
  87.6 120.8 %shard_map.283 = (f32[8,1048,128]{2,1,0:T(8,128)}, f32[4,1024,128]{2,1,0:T(8,128)}, f32[1024,128]{1,0:T(8,128)}, bf16[8,128,256]{2,1,0:T(8,128)(2,1)}, f32[4,102...) custom-call(bf16[8,128,2048]{2,1,0:T(8,128)(2,1)} %get-tuple-element, ...), custom_call_target="tpu_custom_call" | custom-call | tf_op jit(solution)/shard_map/pallas_call | solution.py:338
  208.4 1.3 slice_reduce_fusion.1
  209.7 65.0 %shard_map.284 = (f32[8,1048,128]{2,1,0:T(8,128)}, f32[4,1024,128]{2,1,0:T(8,128)}, f32[1024,128]{1,0:T(8,128)}, bf16[8,128,256]{2,1,0:T(8,128)(2,1)}, f32[4,102...) custom-call(bf16[8,128,2048]{2,1,0:T(8,128)(2,1)} %get-tuple-element, ...), custom_call_target="tpu_custom_call" | custom-call | tf_op jit(solution)/shard_map/pallas_call | solution.py:338
  274.7 141.0 %shard_map.285 = (f32[128,2048]{1,0:T(8,128)}, bf16[4,2,256,512]{3,2,1,0:T(8,128)(2,1)}, bf16[2,2,256,512]{3,2,1,0:T(8,128)(2,1)}, bf16[2,256,512]{2,1,0:T(8,128...) custom-call(f32[8,1048,128]{2,1,0:T(8,128)} %get-tuple-element.84.re, ...), custom_call_target="tpu_custom_call" | custom-call | tf_op jit(solution)/shard_map/pallas_call | solution.py:338
  415.7 0.0 copy-start
  415.7 0.0 copy-start.10
  415.7 3.1 convert_reduce_fusion
  418.8 0.0 copy-done
  418.8 0.0 copy-start.3
  418.8 0.0 copy-start.4
  418.8 1.1 add_bitcast_fusion
  419.9 0.0 copy-done.10
  419.9 0.6 slice_reduce_fusion
  420.5 2.7 stack.43
  423.2 0.7 broadcast_in_dim.36.refs_4_
  423.9 0.0 copy-done.3
  423.9 0.0 copy-done.4
  423.9 2.1 fusion.4
  425.9 121.6 %shard_map.286 = (f32[128,2048]{1,0:T(8,128)}, bf16[4,2,256,512]{3,2,1,0:T(8,128)(2,1)}, bf16[2,2,256,512]{3,2,1,0:T(8,128)(2,1)}, bf16[2,256,512]{2,1,0:T(8,128...) custom-call(f32[8,1048,128]{2,1,0:T(8,128)} %get-tuple-element.96.re, ...), custom_call_target="tpu_custom_call" | custom-call | tf_op jit(solution)/shard_map/pallas_call | solution.py:338
  547.5 0.0 copy-start.11
  547.6 0.0 copy-start.12
  547.6 0.0 copy-start.8
  547.6 0.0 copy-start.9
  547.6 0.0 copy-start.5
  547.6 0.0 copy-start.6
  547.6 2.4 add_convert_fusion
  550.0 0.0 copy-done.11
  550.0 0.0 copy-done.12
  550.0 0.1 reshape.105
  550.2 0.6 pad.24.refs_5_
  550.8 0.0 copy-done.8
  550.8 0.0 copy-done.9
  550.8 0.6 pad.23
  551.4 0.0 copy-done.5
  551.4 0.0 copy-done.6
  551.5 0.9 pad_maximum_fusion.1
  552.4 48.7 %shard_map.287 = (f32[2,64,8192]{2,1,0:T(8,128)}, f32[2,128,160]{2,1,0:T(8,128)}, f32[2,128,128]{2,1,0:T(8,128)}, f32[2,64]{1,0:T(2,128)}, f32[2,4,128]{2,1,0:T(...) custom-call(bf16[2,2,2,256,512]{4,3,2,1,0:T(8,128)(2,1)} %bitcast.59, ...), custom_call_target="tpu_custom_call" | custom-call | tf_op jit(solution)/shard_map/pallas_call | solution.py:338
  601.1 1.4 slice_reduce_fusion.4
  602.5 1.8 copy.51
  604.4 3.2 pad_maximum_fusion
  607.6 0.0 copy-done.2
  607.6 1.0 copy.61
  608.6 0.0 copy-done.1
  608.6 0.0 copy-start.16
  608.6 0.0 copy-start.15
  608.6 2.0 copy.62
  610.6 0.7 copy.63
  611.3 0.6 copy.64
  611.9 0.6 copy.65
  612.5 0.6 copy.66
  613.0 0.6 copy.67
  613.6 0.6 copy.68
  (16 shorter events, 0.1 us)
Async XLA Ops:
  415.7 3.1 copy-start
  415.7 4.2 copy-start.10
  418.8 5.1 copy-start.3
  418.8 5.1 copy-start.4
  547.5 2.5 copy-start.11
  547.6 2.5 copy-start.12
  547.6 3.2 copy-start.8
  547.6 3.2 copy-start.9
  547.6 3.9 copy-start.5
  547.6 3.9 copy-start.6
  602.5 5.1 copy-start.2
  604.4 4.2 copy-start.1
  608.6 2.1 copy-start.7
  608.6 2.7 copy-start.17
  608.6 3.3 copy-start.13
  608.6 3.9 copy-start.16
  608.6 4.4 copy-start.15
  608.6 5.0 copy-start.14

commit v7 on v6

--- a/solution.py
+++ b/solution.py
@@ -265,40 +265,61 @@
 
 
 class Sum:
-    sems = staticmethod(lambda dma: [dma((TP - 1,))] * 4)
+    sems = staticmethod(
+        lambda dma: [dma, dma, dma((3,)), dma((3,)), dma((4,)), dma((4,)), dma((3,)), dma((3,))]
+    )
 
     def __init__(self, payload, parts, out, sems):
-        self.payload, self.parts, self.out = payload, parts, out
-        self.a_send, self.a_recv, self.b_send, self.b_recv = sems
+        self.payload, self.out = payload, out
+        self.near, self.into = parts.at[:WAYS], parts.at[WAYS:]
+        self.a_send, self.a_recv, self.b_send, self.b_recv, self.c_send, self.c_recv, self.d_send, self.d_recv = sems
         x, core, zh, q = place()
-        self.me = core * WAYS + q
-        self.peers = tp_peers()
+        self.q, self.base, self.me = q, core * WAYS, core * WAYS + q
+        self.other = (1 - core) * WAYS
+        self.sibling = device(x, 1 - core, zh, q)
+        self.chips = [neighbour(q, 1, 1), neighbour(q, 1, 0), neighbour(q, 0, 1)]
+        self.far = [device(x, core, zh, t) for t in self.chips]
 
     def start(self):
-        self.one = [
-            remote(self.payload.at[rank], self.parts.at[i], self.a_send.at[i], self.a_recv.at[i], target)
-            for i, (target, rank, _) in enumerate(self.peers)
-        ]
-        for copy in self.one:
+        swap = remote(
+            self.payload.at[pl.ds(self.other, WAYS)], self.near, self.a_send, self.a_recv, self.sibling
+        )
+        swap.start()
+        swap.wait_recv()
+        self.one = [swap]
+        for i, t in enumerate(self.chips):
+            slot = self.base + t
+            self.payload[slot] = encode(decode(self.payload[slot]) + decode(self.near[t]))
+            copy = remote(self.payload.at[slot], self.into.at[i], self.b_send.at[i], self.b_recv.at[i], self.far[i])
             copy.start()
+            self.one.append(copy)
 
     def middle(self, own):
-        total = own
-        for i in range(TP - 1):
-            self.one[i].wait_recv()
-            total = total + decode(self.parts[i])
+        total = own + decode(self.near[self.q])
+        for i in range(3):
+            self.one[1 + i].wait_recv()
+            total = total + decode(self.into[i])
         self.out[self.me] = encode(total)
+        mine = self.out.at[self.me]
         self.two = [
-            remote(self.out.at[self.me], self.out.at[self.me], self.b_send.at[i], self.b_recv.at[i], target)
-            for i, (target, _, _) in enumerate(self.peers)
+            remote(mine, mine, self.c_send.at[i], self.c_recv.at[i], target)
+            for i, target in enumerate(self.far + [self.sibling])
         ]
         for copy in self.two:
             copy.start()
 
     def finish(self):
-        for copy in self.one:
+        last = []
+        for i in (1, 2, 0):
+            self.two[i].wait_recv()
+            slot = self.out.at[self.base + self.chips[i]]
+            copy = remote(slot, slot, self.d_send.at[i], self.d_recv.at[i], self.sibling)
+            copy.start()
+            last.append(copy)
+        self.two[3].wait_recv()
+        for copy in self.one + self.two:
             copy.wait_send()
-        for copy in self.two:
+        for copy in last:
             copy.wait()
 
 

time: 624 us -> 607 us (0.973)
  Pallas kernels: 574 us -> 558 us
    pallas_call x6, Pallas kernels: 574 us -> 558 us  [call(): pl.pallas_call(kernel, out_shape=[shape for shape, _ in outs.values()], i...]
where the time goes in v7:
time: 607 us; the launch traced here: 598 us
  Pallas kernels  558 us (92%)
  other arithmetic  19.4 us (3%)
  local copies, waits for them, and re-layouts  19 us (3%)
    pallas_call x6, Pallas kernels, call(): pl.pallas_call(kernel, out_shape=[shape for shape, _ in outs.values()], i...  558 us

profile of v7, /device:TPU:0, one launch (start us, length us, event | category | flops | bytes accessed | tf_op | source)
XLA Modules:
  0.0 597.9 jit_solution(15938462073140834470)
XLA Ops:
  1.3 1.3 fusion.3
  2.6 0.7 pad_convert_fusion
  3.2 0.7 copy.42
  3.9 0.7 copy.43
  4.6 0.7 copy.44
  5.2 0.7 concatenate.13
  5.9 1.2 concatenate.14.refs_2_
  7.2 0.6 bitcast_convert_fusion.refs_1_
  7.8 0.9 copy.46
  8.7 1.0 copy.47
  9.7 0.7 fusion.2.refs_3_.refs_10_
  10.4 77.2 %shard_map.282 = (bf16[32,64,1024]{2,1,0:T(8,128)(2,1)}, bf16[4,128,384]{2,1,0:T(8,128)(2,1)}, f32[16,512]{1,0:T(8,128)}, f32[8,2048]{1,0:T(8,128)}, f32[8,128]{...) custom-call(bf16[2,64,8192]{2,1,0:T(8,128)(2,1)} %refs_9_.1, ...), custom_call_target="tpu_custom_call" | custom-call | tf_op jit(solution)/shard_map/pallas_call | solution.py:359
  87.6 118.4 %shard_map.283 = (f32[8,1048,128]{2,1,0:T(8,128)}, f32[4,1024,128]{2,1,0:T(8,128)}, f32[1024,128]{1,0:T(8,128)}, bf16[8,128,256]{2,1,0:T(8,128)(2,1)}, f32[4,102...) custom-call(bf16[8,128,2048]{2,1,0:T(8,128)(2,1)} %get-tuple-element, ...), custom_call_target="tpu_custom_call" | custom-call | tf_op jit(solution)/shard_map/pallas_call | solution.py:359
  206.0 1.3 slice_reduce_fusion.1
  207.3 61.2 %shard_map.284 = (f32[8,1048,128]{2,1,0:T(8,128)}, f32[4,1024,128]{2,1,0:T(8,128)}, f32[1024,128]{1,0:T(8,128)}, bf16[8,128,256]{2,1,0:T(8,128)(2,1)}, f32[4,102...) custom-call(bf16[8,128,2048]{2,1,0:T(8,128)(2,1)} %get-tuple-element, ...), custom_call_target="tpu_custom_call" | custom-call | tf_op jit(solution)/shard_map/pallas_call | solution.py:359
  268.5 135.9 %shard_map.285 = (f32[128,2048]{1,0:T(8,128)}, bf16[4,2,256,512]{3,2,1,0:T(8,128)(2,1)}, bf16[2,2,256,512]{3,2,1,0:T(8,128)(2,1)}, bf16[2,256,512]{2,1,0:T(8,128...) custom-call(f32[8,1048,128]{2,1,0:T(8,128)} %get-tuple-element.84.re, ...), custom_call_target="tpu_custom_call" | custom-call | tf_op jit(solution)/shard_map/pallas_call | solution.py:359
  404.4 0.0 copy-start
  404.4 0.0 copy-start.10
  404.5 3.1 convert_reduce_fusion
  407.5 0.0 copy-done
  407.5 0.0 copy-start.3
  407.6 0.0 copy-start.4
  407.6 1.1 add_bitcast_fusion
  408.7 0.0 copy-done.10
  408.7 0.6 slice_reduce_fusion
  409.3 2.7 stack.43
  411.9 0.7 broadcast_in_dim.36.refs_4_
  412.6 0.0 copy-done.3
  412.6 0.0 copy-done.4
  412.6 2.1 fusion.4
  414.7 116.4 %shard_map.286 = (f32[128,2048]{1,0:T(8,128)}, bf16[4,2,256,512]{3,2,1,0:T(8,128)(2,1)}, bf16[2,2,256,512]{3,2,1,0:T(8,128)(2,1)}, bf16[2,256,512]{2,1,0:T(8,128...) custom-call(f32[8,1048,128]{2,1,0:T(8,128)} %get-tuple-element.96.re, ...), custom_call_target="tpu_custom_call" | custom-call | tf_op jit(solution)/shard_map/pallas_call | solution.py:359
  531.1 0.0 copy-start.11
  531.1 0.0 copy-start.12
  531.1 0.0 copy-start.8
  531.1 0.0 copy-start.9
  531.1 0.0 copy-start.5
  531.1 0.0 copy-start.6
  531.1 2.4 add_convert_fusion
  533.5 0.0 copy-done.11
  533.5 0.0 copy-done.12
  533.6 0.1 reshape.105
  533.7 0.6 pad.24.refs_5_
  534.3 0.0 copy-done.8
  534.3 0.0 copy-done.9
  534.3 0.6 pad.23
  535.0 0.0 copy-done.5
  535.0 0.0 copy-done.6
  535.0 0.9 pad_maximum_fusion.1
  535.9 48.8 %shard_map.287 = (f32[2,64,8192]{2,1,0:T(8,128)}, f32[2,128,160]{2,1,0:T(8,128)}, f32[2,128,128]{2,1,0:T(8,128)}, f32[2,64]{1,0:T(2,128)}, f32[2,4,128]{2,1,0:T(...) custom-call(bf16[2,2,2,256,512]{4,3,2,1,0:T(8,128)(2,1)} %bitcast.59, ...), custom_call_target="tpu_custom_call" | custom-call | tf_op jit(solution)/shard_map/pallas_call | solution.py:359
  584.7 1.4 slice_reduce_fusion.4
  586.1 1.8 copy.51
  587.9 3.2 pad_maximum_fusion
  591.2 0.0 copy-done.2
  591.2 1.0 copy.61
  592.1 0.0 copy-done.1
  592.1 0.0 copy-start.16
  592.2 2.0 copy.62
  594.2 0.7 copy.63
  594.9 0.6 copy.64
  595.4 0.6 copy.65
  596.0 0.0 copy-done.16
  596.0 0.6 copy.66
  596.6 0.6 copy.67
  597.1 0.6 copy.68
  (16 shorter events, 0.1 us)
Async XLA Ops:
  404.4 3.1 copy-start
  404.4 4.2 copy-start.10
  407.5 5.1 copy-start.3
  407.6 5.1 copy-start.4
  531.1 2.5 copy-start.11
  531.1 2.5 copy-start.12
  531.1 3.2 copy-start.8
  531.1 3.2 copy-start.9
  531.1 3.9 copy-start.5
  531.1 3.9 copy-start.6
  586.1 5.1 copy-start.2
  587.9 4.2 copy-start.1
  592.1 2.1 copy-start.7
  592.1 2.7 copy-start.17
  592.1 3.3 copy-start.13
  592.1 3.9 copy-start.16
  592.2 4.4 copy-start.15
  592.2 5.0 copy-start.14

commit v8 on v7

--- a/solution.py
+++ b/solution.py
@@ -1208,8 +1208,11 @@
         lax.fori_loop(blocks // 2, blocks, block, 0)
         total.start()
         total.middle(r.own[...])
+        if onward:
+            gate_reduce.middle()
         total.finish()
-        gate_reduce.middle()
+        if not onward:
+            gate_reduce.middle()
         step[:, rows:, :] = jnp.zeros((parts, halo, LANES), f32)
         gconv = step
 

time: 607 us -> 601 us (level)
  no operation moved by 1% of the time
where the time goes in v8:
time: 601 us; the launch traced here: 592 us
  Pallas kernels  552 us (92%)
  other arithmetic  19.4 us (3%)
  local copies, waits for them, and re-layouts  19 us (3%)
    pallas_call x6, Pallas kernels, call(): pl.pallas_call(kernel, out_shape=[shape for shape, _ in outs.values()], i...  552 us

profile of v8, /device:TPU:0, one launch (start us, length us, event | category | flops | bytes accessed | tf_op | source)
XLA Modules:
  0.0 591.9 jit_solution(14740446633306718759)
XLA Ops:
  1.3 1.3 fusion.3
  2.6 0.7 pad_convert_fusion
  3.2 0.7 copy.42
  3.9 0.7 copy.43
  4.6 0.7 copy.44
  5.2 0.7 concatenate.13
  5.9 1.2 concatenate.14.refs_2_
  7.2 0.6 bitcast_convert_fusion.refs_1_
  7.8 0.9 copy.46
  8.7 1.0 copy.47
  9.7 0.7 fusion.2.refs_3_.refs_10_
  10.4 77.2 %shard_map.282 = (bf16[32,64,1024]{2,1,0:T(8,128)(2,1)}, bf16[4,128,384]{2,1,0:T(8,128)(2,1)}, f32[16,512]{1,0:T(8,128)}, f32[8,2048]{1,0:T(8,128)}, f32[8,128]{...) custom-call(bf16[2,64,8192]{2,1,0:T(8,128)(2,1)} %refs_9_.1, ...), custom_call_target="tpu_custom_call" | custom-call | tf_op jit(solution)/shard_map/pallas_call | solution.py:359
  87.6 118.4 %shard_map.283 = (f32[8,1048,128]{2,1,0:T(8,128)}, f32[4,1024,128]{2,1,0:T(8,128)}, f32[1024,128]{1,0:T(8,128)}, bf16[8,128,256]{2,1,0:T(8,128)(2,1)}, f32[4,102...) custom-call(bf16[8,128,2048]{2,1,0:T(8,128)(2,1)} %get-tuple-element, ...), custom_call_target="tpu_custom_call" | custom-call | tf_op jit(solution)/shard_map/pallas_call | solution.py:359
  206.0 1.3 slice_reduce_fusion.1
  207.3 61.2 %shard_map.284 = (f32[8,1048,128]{2,1,0:T(8,128)}, f32[4,1024,128]{2,1,0:T(8,128)}, f32[1024,128]{1,0:T(8,128)}, bf16[8,128,256]{2,1,0:T(8,128)(2,1)}, f32[4,102...) custom-call(bf16[8,128,2048]{2,1,0:T(8,128)(2,1)} %get-tuple-element, ...), custom_call_target="tpu_custom_call" | custom-call | tf_op jit(solution)/shard_map/pallas_call | solution.py:359
  268.5 129.7 %shard_map.285 = (f32[128,2048]{1,0:T(8,128)}, bf16[4,2,256,512]{3,2,1,0:T(8,128)(2,1)}, bf16[2,2,256,512]{3,2,1,0:T(8,128)(2,1)}, bf16[2,256,512]{2,1,0:T(8,128...) custom-call(f32[8,1048,128]{2,1,0:T(8,128)} %get-tuple-element.84.re, ...), custom_call_target="tpu_custom_call" | custom-call | tf_op jit(solution)/shard_map/pallas_call | solution.py:359
  398.3 0.0 copy-start
  398.3 0.0 copy-start.10
  398.3 3.1 convert_reduce_fusion
  401.4 0.0 copy-done
  401.4 0.0 copy-start.3
  401.4 0.0 copy-start.4
  401.4 1.1 add_bitcast_fusion
  402.5 0.0 copy-done.10
  402.5 0.6 slice_reduce_fusion
  403.1 2.7 stack.43
  405.8 0.7 broadcast_in_dim.36.refs_4_
  406.4 0.0 copy-done.3
  406.4 0.0 copy-done.4
  406.4 2.1 fusion.4
  408.5 116.5 %shard_map.286 = (f32[128,2048]{1,0:T(8,128)}, bf16[4,2,256,512]{3,2,1,0:T(8,128)(2,1)}, bf16[2,2,256,512]{3,2,1,0:T(8,128)(2,1)}, bf16[2,256,512]{2,1,0:T(8,128...) custom-call(f32[8,1048,128]{2,1,0:T(8,128)} %get-tuple-element.96.re, ...), custom_call_target="tpu_custom_call" | custom-call | tf_op jit(solution)/shard_map/pallas_call | solution.py:359
  525.1 0.0 copy-start.11
  525.1 0.0 copy-start.12
  525.1 0.0 copy-start.8
  525.1 0.0 copy-start.9
  525.1 0.0 copy-start.5
  525.1 0.0 copy-start.6
  525.1 2.4 add_convert_fusion
  527.6 0.0 copy-done.11
  527.6 0.0 copy-done.12
  527.6 0.1 reshape.105
  527.7 0.6 pad.24.refs_5_
  528.3 0.0 copy-done.8
  528.3 0.6 pad.23
  529.0 0.0 copy-done.6
  529.0 0.9 pad_maximum_fusion.1
  529.9 48.7 %shard_map.287 = (f32[2,64,8192]{2,1,0:T(8,128)}, f32[2,128,160]{2,1,0:T(8,128)}, f32[2,128,128]{2,1,0:T(8,128)}, f32[2,64]{1,0:T(2,128)}, f32[2,4,128]{2,1,0:T(...) custom-call(bf16[2,2,2,256,512]{4,3,2,1,0:T(8,128)(2,1)} %bitcast.59, ...), custom_call_target="tpu_custom_call" | custom-call | tf_op jit(solution)/shard_map/pallas_call | solution.py:359
  578.7 1.4 slice_reduce_fusion.4
  580.1 1.8 copy.51
  581.9 3.2 pad_maximum_fusion
  585.2 1.0 copy.61
  586.1 0.0 copy-done.1
  586.1 0.0 copy-start.16
  586.1 0.0 copy-start.15
  586.2 0.0 copy-start.14
  586.2 2.0 copy.62
  588.2 0.7 copy.63
  588.8 0.0 copy-done.17
  588.8 0.6 copy.64
  589.4 0.0 copy-done.13
  589.4 0.6 copy.65
  590.0 0.6 copy.66
  590.6 0.6 copy.67
  591.1 0.6 copy.68
  (16 shorter events, 0.1 us)
Async XLA Ops:
  398.3 3.1 copy-start
  398.3 4.2 copy-start.10
  401.4 5.1 copy-start.3
  401.4 5.1 copy-start.4
  525.1 2.5 copy-start.11
  525.1 2.5 copy-start.12
  525.1 3.2 copy-start.8
  525.1 3.2 copy-start.9
  525.1 3.9 copy-start.5
  525.1 3.9 copy-start.6
  580.1 5.1 copy-start.2
  581.9 4.2 copy-start.1
  586.1 2.1 copy-start.7
  586.1 2.7 copy-start.17
  586.1 3.3 copy-start.13
  586.1 3.9 copy-start.16
  586.1 4.4 copy-start.15
  586.2 5.0 copy-start.14
